TPU v7x, 32 devices: a whole 2x2x4 slice. The times are simulated.
32 devices in a mesh: groups: 2 (over x), shard: 16 (over z, y, core).
Axes of the slice: x: 2, y: 2, z: 4, core: 2. Of those that a mesh axis runs over, the one named last changes fastest.
Arguments:
- query_hidden: bfloat16 [128, 32, 768], P(('groups', 'shard')), parts along dimension 0, may hold values from -6 to 6
- query_lengths: int32 [128], P(('groups', 'shard')), parts along dimension 0, may hold values from 8 to 32
- inner_weight: bfloat16 [768, 3072], replicated, may hold values from -0.21875 to 0.21875
- outer_weight: bfloat16 [3072, 768], replicated, may hold values from -0.109375 to 0.109375
- norm_gain: float32 [768], replicated, may hold values from 0.1 to 1.9
- embed_weight: bfloat16 [768, 128], replicated, may hold values from -0.21875 to 0.21875
- passage_vectors: bfloat16 [1536, 128, 128], P(('groups', 'shard')), parts along dimension 0, may hold values from -0.52734375 to 0.52734375
- passage_lengths: int32 [1536], P(('groups', 'shard')), parts along dimension 0, may hold values from 16 to 128
- passage_row: int32 [1536], P('groups'), parts along dimension 0, may hold values from 0 to 767, as said below
- candidates: int32 [128, 64], P(('groups', 'shard')), parts along dimension 0, may hold values from 0 to 767, as said below
Outputs:
- scores: float32 [128, 64], P(('groups', 'shard')), parts along dimension 0
- best_scores: float32 [128, 10], P(('groups', 'shard')), parts along dimension 0
There are 2 independent parts, one for each index of `groups`. A program takes and returns all parts, laid end to end along the dimension named above; an argument that names none is the same for every part. Nothing has to cross between parts.
Inputs may be any that keep to these rules, and one draw needn't show every extreme that they name: A permutation: passage p is stored at row passage_row[p] of passage_vectors and passage_lengths, which lies on shard index passage_row[p] // 48. All candidate entries of the queries of one shard (aligned blocks of 4 queries) name distinct passages; queries of different shards may share candidates. Among the candidate entries of one shard's queries, at most 24 are stored on any one shard, and in every draw one shard stores exactly 24 entries of every shard's queries.
All inputs are finite; a program needn't handle non-finite values.
Results may differ from a plain program's by a relative error of at most 0.00046.
Values may be sent and summed in bfloat16 or wider, within the bound.
No kernel may reach another device: no remote copies, remote signals or barrier semaphores. Data moves between devices by JAX's collectives and lax.ppermute only.
A program may use at most 128 MiB of HBM per device.

v0:
```python
import jax
import jax.numpy as jnp
from jax import lax
from jax.sharding import PartitionSpec as P

TOPN = 10


def encode(query_hidden, inner_weight, outer_weight, norm_gain, embed_weight):
    tokens = query_hidden.reshape(-1, query_hidden.shape[-1])
    inner_sum = jnp.dot(tokens, inner_weight, preferred_element_type=jnp.float32)
    activated = jax.nn.gelu(inner_sum, approximate=False).astype(jnp.bfloat16)
    summed = tokens.astype(jnp.float32) + jnp.dot(
        activated, outer_weight, preferred_element_type=jnp.float32
    )
    center = jnp.mean(summed, axis=-1, keepdims=True)
    spread = jnp.mean(jnp.square(summed - center), axis=-1, keepdims=True)
    layer_out = ((summed - center) * lax.rsqrt(spread + 1e-12) * norm_gain).astype(jnp.bfloat16)
    embedded = jnp.dot(layer_out, embed_weight, preferred_element_type=jnp.float32)
    length = jnp.sum(jnp.square(embedded), axis=-1, keepdims=True)
    vectors = (embedded * lax.rsqrt(length + 1e-06)).astype(jnp.bfloat16)
    return vectors.reshape(query_hidden.shape[0], query_hidden.shape[1], -1)


def maxsim(vectors, query_lens, blocks, block_lens):
    similar = jnp.einsum("bte,bpe->btp", vectors, blocks, preferred_element_type=jnp.float32)
    pass_mask = (
        jnp.arange(blocks.shape[1], dtype=jnp.int32)[None, None, :] < block_lens[:, None, None]
    )
    best_match = jnp.max(jnp.where(pass_mask, similar, -1e30), axis=2)
    token_mask = jnp.arange(vectors.shape[1], dtype=jnp.int32)[None, :] < query_lens[:, None]
    return jnp.sum(jnp.where(token_mask, best_match, 0.0), axis=1)


def blocked_maxsim(vectors, query_lens, blocks, block_lens):
    entry_count = vectors.shape[0]
    group_size = 64
    group_count = entry_count // group_size

    def one_group(packed):
        return maxsim(packed[0], packed[1], packed[2], packed[3])

    result = lax.map(
        one_group,
        (
            vectors.reshape(group_count, group_size, vectors.shape[1], vectors.shape[2]),
            query_lens.reshape(group_count, group_size),
            blocks.reshape(group_count, group_size, blocks.shape[1], blocks.shape[2]),
            block_lens.reshape(group_count, group_size),
        ),
    )
    return result.reshape(entry_count)


def slot_layout(slab_rows, shard_count, capacity, passage_count):
    entry_count = slab_rows.shape[0]
    owner_of = slab_rows // passage_count
    onehot = (owner_of[:, None] == jnp.arange(shard_count, dtype=jnp.int32)[None, :]).astype(
        jnp.int32
    )
    ranking = jnp.sum((jnp.cumsum(onehot, axis=0) - onehot) * onehot, axis=1)
    position = owner_of * capacity + ranking
    filled = (
        jnp.zeros((shard_count * capacity,), jnp.int32)
        .at[position]
        .set(jnp.arange(entry_count, dtype=jnp.int32) + 1)
    )
    return (position, jnp.maximum(filled - 1, 0), filled > 0)


def per_device(
    query_hidden,
    query_lengths,
    inner_weight,
    outer_weight,
    norm_gain,
    embed_weight,
    passage_vectors,
    passage_lengths,
    passage_row,
    candidates,
):
    shard_count = lax.axis_size("shard")
    query_count, cand_count = candidates.shape
    passage_count = passage_vectors.shape[0]
    plen_size = passage_vectors.shape[1]
    embed_size = passage_vectors.shape[2]
    capacity = 3 * query_count * cand_count // (2 * shard_count)
    slab_rows = passage_row[candidates.reshape(-1)]
    position, slot_index, is_filled = slot_layout(slab_rows, shard_count, capacity, passage_count)
    local_rows = jnp.where(is_filled, slab_rows[slot_index] % passage_count, 0).reshape(
        shard_count, capacity
    )
    query_of_slot = slot_index // cand_count
    incoming = lax.all_to_all(local_rows, "shard", split_axis=0, concat_axis=0, tiled=True)
    sent_blocks = passage_vectors[incoming]
    sent_lengths = passage_lengths[incoming]
    arrived, arrived_lens = (
        lax.all_to_all(sent_blocks, "shard", split_axis=0, concat_axis=0, tiled=True),
        lax.all_to_all(sent_lengths, "shard", split_axis=0, concat_axis=0, tiled=True),
    )
    query_vectors = encode(query_hidden, inner_weight, outer_weight, norm_gain, embed_weight)
    buffer_scores = blocked_maxsim(
        query_vectors[query_of_slot],
        query_lengths[query_of_slot],
        arrived.reshape(shard_count * capacity, plen_size, embed_size),
        arrived_lens.reshape(-1),
    )
    scores = buffer_scores[position].reshape(query_count, cand_count)
    best_scores = lax.top_k(scores, TOPN)[0]
    return (scores, best_scores)


def solution(mesh):
    in_specs = (
        P(("groups", "shard"), None, None),
        P(("groups", "shard")),
        P(),
        P(),
        P(),
        P(),
        P(("groups", "shard"), None, None),
        P(("groups", "shard")),
        P("groups"),
        P(("groups", "shard"), None),
    )
    out_specs = (P(("groups", "shard"), None), P(("groups", "shard"), None))
    return jax.shard_map(
        per_device, mesh=mesh, in_specs=in_specs, out_specs=out_specs, check_vma=False
    )
```

profile of v0, /device:TPU:13, one launch (start us, length us, event | category | flops | bytes accessed | tf_op | source)
XLA Modules:
  0.0 345.6 jit_solution(7431916582318794475)
XLA Ops:
  0.6 0.0 copy-start
  0.7 0.9 reshape.220
  1.6 0.0 copy-start.4
  1.6 0.0 copy-start.1
  1.6 1.9 gather_fusion
  3.5 0.6 reduce-window.6
  4.1 0.2 slice_reduce_fusion
  4.4 0.1 fusion.61
  4.5 1.4 scatter_custom_fusion
  5.9 2.8 gather_fusion.1
  8.7 0.0 copy-done.4
  8.7 0.7 fusion.99
  9.4 2.6 compare_select_fusion.3
  12.0 0.1 all_to_all.17
  12.1 10.2 %all_to_all.26 = s32[16,1,24]{2,1,0:T(1,128)S(1)} all-to-all(s32[16,1,24]{2,1,0:T(1,128)S(1)} %all_to_all.17), channel_id=1, replica_groups=mesh['groups'=2,'shard'=16] {'shard'}, dimensions={0} | all-to-all | bytes 3072 | tf_op jit(solution)/shard_map/all_to_all | solution.py:95
  22.2 0.1 reshape.257
  22.3 0.0 copy-done.1
  22.3 2.7 gather_fusion.2
  25.0 0.7 all_to_all.20
  25.7 6.0 %all-to-all-start.1 = ((s32[16,1,24]{2,1,0:T(1,128)}), s32[16,1,24]{2,1,0:T(1,128)S(1)}, u32[]{:S(2)}, u32[]{:S(2)}) async-start(s32[16,1,24]{2,1,0:T(1,128)} %all_to_all.20), calls=%async_computation.1 | async-start | bytes 16384 | tf_op jit(solution)/shard_map/all_to_all | solution.py:100
  31.7 0.0 copy-done
  31.7 11.3 %gather_fusion.4 = bf16[384,128,128]{2,1,0:T(8,128)(2,1)} fusion(bf16[48,128,128]{2,1,0:T(8,128)(2,1)S(1)} %copy-done, s32[1024]{0:T(1024)S(1)} %pad_clamp_fusion.2), kind=kCustom, calls=%fused_computation.4 | custom fusion | bytes 25167360 | tf_op jit(solution)/shard_map/gather | solution.py:96
  43.0 0.0 all-to-all-done.1
  43.0 6.2 %all-to-all-start.2 = ((bf16[16,24,128,128]{3,2,1,0:T(8,128)(2,1)}), bf16[16,24,128,128]{3,2,1,0:T(8,128)(2,1)}, u32[]{:S(2)}, u32[]{:S(2)}) async-start(bf16[16,24,128,128]{3,2,1,0:T(8,128)(2,1)} %bitcast.67), calls=%async_computation.2 | async-start | bytes 25165824 | tf_op jit(solution)/shard_map/all_to_all | solution.py:99
  49.2 0.1 reshape.222
  49.3 0.0 copy-done.6
  49.3 0.0 copy-start.5
  49.3 8.6 %fusion.100 = (f32[128]{0:T(128)S(1)}, f32[128,768]{1,0:T(8,128)S(1)}) fusion(bf16[3072,768]{1,0:T(8,128)(2,1)} %param.15, bf16[128,768]{1,0:T(8,128)(2,1)S(1)} %bitcast.76, bf16[768,3072]{1,0:T(8,128)(2,1)} %param.14), kind=kOutput, calls=%fused_computation.150 | convolution fusion | flops 1233813376 | bytes 10027520 | tf_op jit(solution)/shard_map/dot_general | solution.py:13
  57.8 0.2 multiply_reduce_fusion
  58.0 0.0 copy-done.2
  58.1 0.0 copy-done.5
  58.1 0.3 multiply_reduce_fusion.1
  58.4 0.1 multiply_convert_fusion.2
  58.5 3.3 gather_fusion.3
  61.8 0.5 broadcast.307
  62.3 0.7 reduce.5
  63.0 0.1 reshape_reshape.6
  63.1 258.3 %all-to-all-done.2 = bf16[16,24,128,128]{3,2,1,0:T(8,128)(2,1)} async-done(((bf16[16,24,128,128]{3,2,1,0:T(8,128)(2,1)}), bf16[16,24,128,128]{3,2,1,0:T(8,128)(2,1)}, u32[]{:S(2)}, u32[]{:S(2)}) %all-to-all-start.2) | async-done | bytes 12582944 | tf_op jit(solution)/shard_map/all_to_all | solution.py:99
  321.4 20.3 %while.10 = (s32[]{:T(128)}, f32[6,64]{1,0:T(8,128)S(1)}, s32[6,64]{1,0:T(8,128)S(1)}, s32[6,64]{1,0:T(8,128)S(1)}, bf16[6,64,32,128]{3,2,1,0:T(8,128)(2,1)}, /*...) while((s32[]{:T(128)}, f32[6,64]{1,0:T(8,128)S(1)}, s32[6,64]{1,0:T(8,128)S(1)}, ...), condition=%wide.region_10.11_spmd, body=%wide.region_7.10_spmd.sunk | while | flops 67645376 | bytes 2657629 | solution.py:43
  321.4 0.1 iota_compare_fusion.5
  321.5 3.0 fusion.114
  324.5 0.2 select_reduce_fusion.2
  324.8 0.1 iota_compare_fusion.5
  324.9 3.0 fusion.114
  327.9 0.2 select_reduce_fusion.2
  328.2 0.1 iota_compare_fusion.5
  328.2 3.0 fusion.114
  331.3 0.2 select_reduce_fusion.2
  331.5 0.1 iota_compare_fusion.5
  331.6 3.0 fusion.114
  334.7 0.2 select_reduce_fusion.2
  334.9 0.1 iota_compare_fusion.5
  335.0 3.0 fusion.114
  338.1 0.2 select_reduce_fusion.2
  338.3 0.1 iota_compare_fusion.5
  338.4 3.0 fusion.114
  341.4 0.2 select_reduce_fusion.2
  341.7 0.1 reshape.226
  341.7 1.9 gather_fusion.5
  343.7 0.1 reshape.227
  343.8 0.1 copy.26
  343.9 1.1 top_k.9
  345.0 0.7 copy.27
  345.6 0.0 copy-done.3
  (36 shorter events, 0.4 us)
Async XLA Ops:
  0.6 31.1 %copy-start = (bf16[48,128,128]{2,1,0:T(8,128)(2,1)S(1)}, bf16[48,128,128]{2,1,0:T(8,128)(2,1)}, u32[]{:S(2)}) copy-start(bf16[48,128,128]{2,1,0:T(8,128)(2,1)} %param.18) | copy-start | bytes 4718596
  1.6 7.2 %copy-start.4 = (s32[4]{0:T(128)S(1)}, s32[4]{0:T(128)}, u32[]{:S(2)}) copy-start(s32[4]{0:T(128)} %param.13) | copy-start | bytes 52
  1.6 20.8 %copy-start.1 = (s32[48]{0:T(128)S(1)}, s32[48]{0:T(128)}, u32[]{:S(2)}) copy-start(s32[48]{0:T(128)} %param.19) | copy-start | bytes 580
  25.7 17.3 %all-to-all-start.1 = ((s32[16,1,24]{2,1,0:T(1,128)}), s32[16,1,24]{2,1,0:T(1,128)S(1)}, u32[]{:S(2)}, u32[]{:S(2)}) async-start(s32[16,1,24]{2,1,0:T(1,128)} %all_to_all.20), calls=%async_computation.1 | async-start | bytes 16384 | tf_op jit(solution)/shard_map/all_to_all | solution.py:100
  43.0 6.3 %copy-start.6 = (bf16[4,32,768]{2,1,0:T(8,128)(2,1)S(1)}, bf16[4,32,768]{2,1,0:T(8,128)(2,1)}, u32[]{:S(2)}) copy-start(bf16[4,32,768]{2,1,0:T(8,128)(2,1)} %param.12) | copy-start | bytes 589828
  43.0 278.4 %all-to-all-start.2 = ((bf16[16,24,128,128]{3,2,1,0:T(8,128)(2,1)}), bf16[16,24,128,128]{3,2,1,0:T(8,128)(2,1)}, u32[]{:S(2)}, u32[]{:S(2)}) async-start(bf16[16,24,128,128]{3,2,1,0:T(8,128)(2,1)} %bitcast.67), calls=%async_computation.2 | async-start | bytes 25165824 | tf_op jit(solution)/shard_map/all_to_all | solution.py:99
  49.3 8.8 %copy-start.2 = (bf16[768,128]{1,0:T(8,128)(2,1)S(1)}, bf16[768,128]{1,0:T(8,128)(2,1)}, u32[]{:S(2)}) copy-start(bf16[768,128]{1,0:T(8,128)(2,1)} %param.17) | copy-start | bytes 589828
  49.3 8.8 %copy-start.5 = (f32[768]{0:T(1024)S(1)}, f32[768]{0:T(1024)}, u32[]{:S(2)}) copy-start(f32[768]{0:T(1024)} %param.16) | copy-start | bytes 9220
  343.8 1.9 copy-start.3
where the time goes:
time: 346 us
  waiting for transfers between devices  258 us (75%)
  local copies, waits for them, and re-layouts  29.8 us (9%)
  matrix products  27.2 us (8%)
  starting transfers between devices  12.2 us (4%)
  blocking collectives  10.2 us (3%)
  other arithmetic  6.95 us (2%)
    all_to_all x1, waiting for transfers between devices, per_device(): lax.all_to_all(sent_blocks, 'shard', split_axis=0, concat_axis=0, tiled=T...  258 us
    dot_general x6, matrix products, maxsim(): jnp.einsum('bte,bpe->btp', vectors, blocks, preferred_element_type=jnp.fl...  18.3 us
    gather x1, local copies, waits for them, and re-layouts, per_device(): sent_blocks = passage_vectors[incoming]  11.3 us
    all_to_all x1, blocking collectives, per_device(): lax.all_to_all(local_rows, 'shard', split_axis=0, concat_axis=0, tiled=True)  10.2 us
    dot_general x1, matrix products, encode(): jnp.dot(activated, outer_weight, preferred_element_type=jnp.float32)  8.56 us
  transfers between devices with their start and end apart: 2, of which 1 were waited for; matrix products, arithmetic and copies ran while one was open for 7% of the time, Pallas kernels for 0%

commit v1 on v0

v1 whole, which is shorter than its diff:
```python
import jax
import jax.numpy as jnp
from jax import lax
from jax.experimental import pallas as pl
from jax.experimental.pallas import tpu as pltpu
from jax.sharding import PartitionSpec as P

TOPN = 10
F32 = jnp.float32
BF16 = jnp.bfloat16
NT = (((1,), (1,)), ((), ()))
VMEM = pl.BlockSpec(memory_space=pltpu.VMEM)
SMEM = pl.BlockSpec(memory_space=pltpu.SMEM)
ANY = pl.BlockSpec(memory_space=pl.ANY)


def split3(value):
    high = value.astype(BF16)
    rest = value - high.astype(F32)
    middle = rest.astype(BF16)
    low = (rest - middle.astype(F32)).astype(BF16)
    return high, middle, low


def encode_kernel(lens_ref, x_ref, w1_ref, w2_ref, gain_ref, embed_ref, out_ref, w1_buf, w2_buf, sems):
    chunks, _, width = w1_buf.shape
    copies = []
    for c in range(chunks):
        first = pltpu.make_async_copy(w1_ref.at[:, pl.ds(c * width, width)], w1_buf.at[c], sems.at[0, c])
        second = pltpu.make_async_copy(w2_ref.at[pl.ds(c * width, width), :], w2_buf.at[c], sems.at[1, c])
        first.start()
        second.start()
        copies.append((first, second))
    query_count, token_count, width_in = x_ref.shape
    x = x_ref[...].reshape(query_count * token_count, width_in)
    total = x.astype(F32)
    copies[0][0].wait()
    inner = jnp.dot(x, w1_buf[0], preferred_element_type=F32)
    for c in range(chunks):
        copies[c][1].wait()
        if c + 1 < chunks:
            copies[c + 1][0].wait()
            later = jnp.dot(x, w1_buf[c + 1], preferred_element_type=F32)
        active = (0.5 * inner * (1.0 + lax.erf(inner * (0.5 ** 0.5)))).astype(BF16)
        total = total + jnp.dot(active, w2_buf[c], preferred_element_type=F32)
        if c + 1 < chunks:
            inner = later
    centered = total - jnp.mean(total, axis=-1, keepdims=True)
    spread = jnp.mean(jnp.square(centered), axis=-1, keepdims=True)
    layer_out = (centered * lax.rsqrt(spread + 1e-12) * gain_ref[...]).astype(BF16)
    embedded = jnp.dot(layer_out, embed_ref[...], preferred_element_type=F32)
    length = jnp.sum(jnp.square(embedded), axis=-1, keepdims=True)
    vectors = embedded * lax.rsqrt(length + 1e-06)
    token = lax.broadcasted_iota(jnp.int32, vectors.shape, 0)
    for i in range(query_count):
        padded = (token >= i * token_count + lens_ref[i]) & (token < (i + 1) * token_count)
        vectors = jnp.where(padded, 0.0, vectors)
    out_ref[...] = vectors.astype(BF16)


def encode(query_lengths, query_hidden, inner_weight, outer_weight, norm_gain, embed_weight):
    query_count, token_count, d = query_hidden.shape
    ff = inner_weight.shape[1]
    e = embed_weight.shape[1]
    chunks = 6
    width = ff // chunks
    tokens = query_count * token_count
    return pl.pallas_call(
        encode_kernel,
        out_shape=jax.ShapeDtypeStruct((tokens, e), BF16),
        in_specs=[SMEM, VMEM, ANY, ANY, VMEM, VMEM],
        out_specs=VMEM,
        scratch_shapes=[
            pltpu.VMEM((chunks, d, width), BF16),
            pltpu.VMEM((chunks, width, d), BF16),
            pltpu.SemaphoreType.DMA((2, chunks)),
        ],
        compiler_params=pltpu.CompilerParams(vmem_limit_bytes=40 * 2 ** 20),
        cost_estimate=pl.CostEstimate(
            flops=4 * tokens * d * ff, bytes_accessed=4 * d * ff, transcendentals=tokens * ff
        ),
        name="encode",
    )(query_lengths, query_hidden, inner_weight, outer_weight, norm_gain.reshape(1, d), embed_weight)


def prepare_kernel(
    me_ref, lens_ref, row_ref, own_ref, row_lanes_ref, cand_ref, pass_ref, _, masked_ref, index_ref, rows_ref
):
    passage_count, plen, _ = pass_ref.shape
    query_count, cand_count = own_ref.shape
    shard_count = cand_ref.shape[0] // query_count
    token_count = 32

    def lookup(k, carry):
        for i in range(query_count):
            rows_ref[i, k] = row_ref[own_ref[i, k]]
        return carry

    lax.fori_loop(0, cand_count, lookup, 0, unroll=4)

    position = lax.broadcasted_iota(jnp.int32, (plen, 1), 0)

    def mask(p, carry):
        block = pass_ref[p]
        keep = lax.broadcasted_iota(jnp.int32, block.shape, 0) < lens_ref[p]
        first = jnp.broadcast_to(block[0:1].astype(F32), block.shape)
        masked_ref[p] = jnp.where(keep, block.astype(F32), first).astype(BF16)
        return carry

    lax.fori_loop(0, passage_count, mask, 0, unroll=4)

    base = me_ref[0] * passage_count
    local = lax.broadcasted_iota(jnp.int32, (passage_count, 128), 0) + base
    lane = lax.broadcasted_iota(jnp.int32, (passage_count, 128), 1)

    def find(j, found):
        return jnp.where(row_lanes_ref[pl.ds(j, 1), :] == local, (lane + j * 128).astype(F32), found)

    found = lax.fori_loop(0, row_lanes_ref.shape[0], find, jnp.zeros((passage_count, 128), F32))
    passage_id = jnp.sum(found, axis=1, keepdims=True).astype(jnp.int32)
    passage_id = jnp.broadcast_to(passage_id, (passage_count, cand_count))

    slot_lane = lax.broadcasted_iota(jnp.int32, index_ref.shape, 1)

    def choose(s, index):
        hit = jnp.zeros((passage_count, cand_count), F32)
        for i in range(1, query_count):
            hit = jnp.where(cand_ref[pl.ds(s * query_count + i, 1), :] == passage_id, float(i), hit)
        query = jnp.sum(hit, axis=1, keepdims=True).astype(jnp.int32)
        return jnp.where(slot_lane == s, (s * query_count + query) * token_count, index)

    index_ref[...] = lax.fori_loop(0, shard_count, choose, jnp.zeros(index_ref.shape, jnp.int32))


def prepare(me, passage_lengths, passage_row, candidates, all_candidates, passage_vectors, after):
    passage_count = passage_vectors.shape[0]
    shard_count = all_candidates.shape[0] // candidates.shape[0]
    return pl.pallas_call(
        prepare_kernel,
        out_shape=(
            jax.ShapeDtypeStruct(passage_vectors.shape, BF16),
            jax.ShapeDtypeStruct((passage_count, shard_count), jnp.int32),
            jax.ShapeDtypeStruct(candidates.shape, jnp.int32),
        ),
        in_specs=[SMEM, SMEM, SMEM, SMEM, VMEM, VMEM, VMEM, ANY],
        out_specs=(VMEM, VMEM, SMEM),
        cost_estimate=pl.CostEstimate(
            flops=4 * passage_vectors.size, bytes_accessed=4 * passage_vectors.size, transcendentals=0
        ),
        name="prepare",
    )(
        me,
        passage_lengths,
        passage_row,
        candidates,
        passage_row.reshape(-1, 128),
        all_candidates,
        passage_vectors,
        after,
    )


def score_kernel(index_ref, query_ref, pass_ref, out_ref, best_ref):
    passage_count = pass_ref.shape[0]
    shard_count = index_ref.shape[1]
    token_count = best_ref.shape[1] // shard_count
    group = min(shard_count, 256 // token_count)

    def eight(step, carry):
        for part in range(shard_count // group):
            rows = []
            for j in range(8):
                p = step * 8 + j
                picked = jnp.concatenate(
                    [
                        query_ref[pl.ds(pl.multiple_of(index_ref[p, s], token_count), token_count), :]
                        for s in range(part * group, (part + 1) * group)
                    ],
                    axis=0,
                )
                similar = lax.dot_general(pass_ref[p], picked, NT, preferred_element_type=F32)
                rows.append(jnp.max(similar, axis=0, keepdims=True))
            best_ref[pl.ds(pl.multiple_of(step * 8, 8), 8), pl.ds(part * group * token_count, group * token_count)] = (
                jnp.concatenate(rows, axis=0)
            )
        return carry

    lax.fori_loop(0, passage_count // 8, eight, 0)
    wide = best_ref.shape[1]
    source = lax.broadcasted_iota(jnp.int32, (shard_count, wide), 0)
    column = lax.broadcasted_iota(jnp.int32, (shard_count, wide), 1)
    first = source * token_count
    ones = jnp.where((column >= first) & (column < first + token_count), 1.0, 0.0).astype(BF16)
    total = sum(lax.dot_general(ones, part, NT, preferred_element_type=F32) for part in split3(best_ref[...]))
    out_ref[...] = jnp.zeros(out_ref.shape, F32)
    out_ref[:, pl.ds(0, passage_count)] = total


def score(index, queries, passages, token_count):
    passage_count, plen, e = passages.shape
    shard_count = index.shape[1]
    lanes = -(-passage_count // 128) * 128
    return pl.pallas_call(
        score_kernel,
        out_shape=jax.ShapeDtypeStruct((shard_count, lanes), F32),
        in_specs=[SMEM, VMEM, VMEM],
        out_specs=VMEM,
        scratch_shapes=[pltpu.VMEM((passage_count, shard_count * token_count), F32)],
        compiler_params=pltpu.CompilerParams(vmem_limit_bytes=32 * 2 ** 20),
        cost_estimate=pl.CostEstimate(
            flops=2 * passage_count * shard_count * token_count * plen * e,
            bytes_accessed=2 * (passages.size + queries.size),
            transcendentals=0,
        ),
        name="score",
    )(index, queries, passages)


def finish_kernel(passage_count, got_ref, rows_ref, scores_ref, best_ref):
    shard_count, lanes = got_ref.shape
    query_count, cand_count = scores_ref.shape
    parts = split3(got_ref[...])
    owner_iota = lax.broadcasted_iota(jnp.int32, (shard_count, cand_count), 0)
    local_iota = lax.broadcasted_iota(jnp.int32, (lanes, cand_count), 0)
    row_iota = lax.broadcasted_iota(jnp.int32, (cand_count, cand_count), 0)
    col_iota = lax.broadcasted_iota(jnp.int32, (cand_count, cand_count), 1)
    place = lax.broadcasted_iota(jnp.int32, (cand_count, 128), 1)
    for i in range(query_count):
        row = rows_ref[i:i + 1, :]
        owner = row // passage_count
        local = row - owner * passage_count
        onehot = jnp.where(local_iota == local, 1.0, 0.0).astype(BF16)
        picked = sum(jnp.dot(part, onehot, preferred_element_type=F32) for part in parts)
        score_row = jnp.sum(jnp.where(owner_iota == owner, picked, 0.0), axis=0, keepdims=True)
        scores_ref[i:i + 1, :] = score_row
        across = jnp.broadcast_to(score_row, (cand_count, cand_count))
        score_col = jnp.sum(jnp.where(row_iota == col_iota, across, 0.0), axis=1, keepdims=True)
        ahead = (across > score_col) | ((across == score_col) & (col_iota < row_iota))
        rank = jnp.sum(jnp.where(ahead, 1.0, 0.0), axis=1, keepdims=True).astype(jnp.int32)
        ordered = jnp.sum(jnp.where(rank == place, score_col, 0.0), axis=0, keepdims=True)
        best_ref[i:i + 1, :] = ordered[:, :TOPN]


def finish(got, rows, passage_count):
    def kernel(*refs):
        finish_kernel(passage_count, *refs)

    query_count = rows.shape[0]
    return pl.pallas_call(
        kernel,
        out_shape=(
            jax.ShapeDtypeStruct(rows.shape, F32),
            jax.ShapeDtypeStruct((query_count, TOPN), F32),
        ),
        in_specs=[VMEM, VMEM],
        out_specs=(VMEM, VMEM),
        name="finish",
    )(got, rows)


def per_device(
    query_hidden,
    query_lengths,
    inner_weight,
    outer_weight,
    norm_gain,
    embed_weight,
    passage_vectors,
    passage_lengths,
    passage_row,
    candidates,
):
    passage_count = passage_vectors.shape[0]
    token_count = query_hidden.shape[1]
    me = lax.axis_index("shard").astype(jnp.int32).reshape(1)
    all_candidates = lax.all_gather(candidates, "shard", axis=0, tiled=True)
    vectors = encode(query_lengths, query_hidden, inner_weight, outer_weight, norm_gain, embed_weight)
    all_vectors = lax.all_gather(vectors, "shard", axis=0, tiled=True)
    masked, index, rows = prepare(
        me, passage_lengths, passage_row, candidates, all_candidates, passage_vectors, vectors
    )
    sums = score(index, all_vectors, masked, token_count)
    got = lax.all_to_all(sums, "shard", split_axis=0, concat_axis=0, tiled=True)
    return finish(got, rows, passage_count)


def solution(mesh):
    in_specs = (
        P(("groups", "shard"), None, None),
        P(("groups", "shard")),
        P(),
        P(),
        P(),
        P(),
        P(("groups", "shard"), None, None),
        P(("groups", "shard")),
        P("groups"),
        P(("groups", "shard"), None),
    )
    out_specs = (P(("groups", "shard"), None), P(("groups", "shard"), None))
    return jax.shard_map(
        per_device, mesh=mesh, in_specs=in_specs, out_specs=out_specs, check_vma=False
    )
```

time: 346 us -> 79.3 us (0.23)
  the two profiles are of different devices: /device:TPU:13 before, /device:TPU:0 now
where the time goes in v1:
time: 79.3 us; the launch traced here: 78.8 us
  blocking collectives  53.3 us (67%)
  Pallas kernels  14.8 us (19%)
  local copies, waits for them, and re-layouts  10 us (13%)
    all_gather x1, blocking collectives, per_device(): all_candidates = lax.all_gather(candidates, 'shard', axis=0, tiled=True)  24.8 us
    all_gather x1, blocking collectives, per_device(): all_vectors = lax.all_gather(vectors, 'shard', axis=0, tiled=True)  18.9 us
    all_to_all x1, blocking collectives, per_device(): got = lax.all_to_all(sums, 'shard', split_axis=0, concat_axis=0, tiled=True)  9.67 us
    unnamed x16, local copies, waits for them, and re-layouts  9.32 us
    pallas_call x1, Pallas kernels, prepare(): pl.pallas_call(prepare_kernel, out_shape=(jax.ShapeDtypeStruct(passage_ve...  5.07 us
    pallas_call x1, Pallas kernels, encode(): pl.pallas_call(encode_kernel, out_shape=jax.ShapeDtypeStruct((tokens, e),...  4.24 us
    pallas_call x1, Pallas kernels, score(): pl.pallas_call(score_kernel, out_shape=jax.ShapeDtypeStruct((shard_count,...  3.8 us
    pallas_call x1, Pallas kernels, finish(): pl.pallas_call(kernel, out_shape=(jax.ShapeDtypeStruct(rows.shape, F32),...  1.7 us

profile of v1, /device:TPU:0, one launch (start us, length us, event | category | flops | bytes accessed | tf_op | source)
XLA Modules:
  0.0 78.8 jit_solution(812506412193228902)
XLA Ops:
  0.6 0.7 reshape.17.gain_ref
  1.3 24.8 %all-gather = s32[16,4,64]{2,1,0:T(4,128)} all-gather(s32[1,4,64]{2,1,0:T(4,128)} %bitcast.12), channel_id=1, replica_groups=mesh['groups'=2,'shard'=16] {'shard'}, dimensions={0}, use_global_device_ids=true | all-gather | bytes 17408 | tf_op jit(solution)/shard_map/all_gather | solution.py:276
  26.1 0.0 copy-start
  26.1 2.3 %copy-done = bf16[768,3072]{1,0:T(8,128)(2,1)S(1)} copy-done((bf16[768,3072]{1,0:T(8,128)(2,1)S(1)}, bf16[768,3072]{1,0:T(8,128)(2,1)}, u32[]{:S(2)}) %copy-start) | copy-done | bytes 4718616
  28.5 0.0 copy-start.1
  28.5 2.3 %copy-done.1 = bf16[3072,768]{1,0:T(8,128)(2,1)S(1)} copy-done((bf16[3072,768]{1,0:T(8,128)(2,1)S(1)}, bf16[3072,768]{1,0:T(8,128)(2,1)}, u32[]{:S(2)}) %copy-start.1) | copy-done | bytes 4718616
  30.8 0.0 copy-start.3
  30.8 0.9 %copy-done.3 = bf16[4,32,768]{2,1,0:T(8,128)(2,1)S(1)} copy-done((bf16[4,32,768]{2,1,0:T(8,128)(2,1)S(1)}, bf16[4,32,768]{2,1,0:T(8,128)(2,1)}, u32[]{:S(2)}) %copy-start.3) | copy-done | bytes 196632
  31.7 0.0 copy-start.4
  31.7 0.9 %copy-done.4 = bf16[768,128]{1,0:T(8,128)(2,1)S(1)} copy-done((bf16[768,128]{1,0:T(8,128)(2,1)S(1)}, bf16[768,128]{1,0:T(8,128)(2,1)}, u32[]{:S(2)}) %copy-start.4) | copy-done | bytes 196632
  32.6 0.0 copy-start.5
  32.6 0.7 copy-done.5
  33.3 4.2 %encode.1._ = bf16[128,128]{1,0:T(8,128)(2,1)S(1)} custom-call(s32[4]{0:T(128)S(1)} %copy-done.5, bf16[4,32,768]{2,1,0:T(8,128)(2,1)S(1)} %copy-done.3, bf16[768,3072]{1,0:T(8,128)(2,1)S(1)} %copy-done, bf16[3072,768]{1,0:T(8,128)(2,1)S(1)} %copy-done.1, f32[1,768]{1,0:T(1,128)S(1)} %reshape.17.gain_ref, bf16[768,128]{1,0:T(8,128)(2,1)S(1)} %copy-done.4), custom_call_target="tpu_custom_call" | custom-call | flops 1207959552 | bytes 9437184 | tf_op jit(solution)/shard_map/encode/pallas_call | solution.py:68
  37.6 0.0 copy-start.2
  37.6 18.9 %all_gather.7.query_ref = bf16[2048,128]{1,0:T(8,128)(2,1)S(1)} all-gather(bf16[128,128]{1,0:T(8,128)(2,1)S(1)} %encode.1._), channel_id=1, replica_groups=mesh['groups'=2,'shard'=16] {'shard'}, dimensions={0}, use_global_device_ids=true | all-gather | bytes 557056 | tf_op jit(solution)/shard_map/all_gather | solution.py:278
  56.4 0.0 copy-done.2
  56.4 5.1 %prepare.1 = (bf16[48,128,128]{2,1,0:T(8,128)(2,1)}, s32[48,16]{1,0:T(8,128)}, s32[4,64]{1,0:T(4,128)}) custom-call(s32[1]{0:T(128)} %bitcast.me_ref, s32[48]{0:T(128)} %lens_ref.3, s32[768]{0:T(1024)} %row_ref.1, s32[4,64]{1,0:T(4,128)} %own_ref.1, s32[6,128]{1,0:T(8,128)} %bitcast.11, s32[64,64]{1,0:T(8,128)} %bitcast.9, bf16[48,128,128]{2,1,0:T(8,128)(2,1)} %pass_ref.1, ...), custom_call_target="tpu_custom_call" | custom-call | flops 3145728 | bytes 3145728 | tf_op jit(solution)/shard_map/prepare/pallas_call | solution.py:138
  61.5 0.0 copy-start.6
  61.5 1.4 %copy-done.6 = bf16[48,128,128]{2,1,0:T(8,128)(2,1)S(1)} copy-done((bf16[48,128,128]{2,1,0:T(8,128)(2,1)S(1)}, bf16[48,128,128]{2,1,0:T(8,128)(2,1)}, u32[]{:S(2)}) %copy-start.6) | copy-done | bytes 1572888
  62.9 0.0 copy-start.7
  62.9 0.7 copy-done.7
  63.7 3.8 %score.1 = f32[16,128]{1,0:T(8,128)S(1)} custom-call(s32[48,16]{1,0:T(8,128)S(1)} %copy-done.7, bf16[2048,128]{1,0:T(8,128)(2,1)S(1)} %all_gather.7.query_ref, bf16[48,128,128]{2,1,0:T(8,128)(2,1)S(1)} %copy-done.6), custom_call_target="tpu_custom_call" | custom-call | flops 805306368 | bytes 2097152 | tf_op jit(solution)/shard_map/score/pallas_call | solution.py:203
  67.5 9.7 %all_to_all.11 = f32[16,1,128]{2,1,0:T(1,128)} all-to-all(f32[16,1,128]{2,1,0:T(1,128)S(1)} %bitcast.8), channel_id=1, replica_groups=mesh['groups'=2,'shard'=16] {'shard'}, dimensions={0} | all-to-all | bytes 16384 | tf_op jit(solution)/shard_map/all_to_all | solution.py:283
  77.1 1.7 %finish.1 = (f32[4,64]{1,0:T(4,128)}, f32[4,10]{1,0:T(4,128)}) custom-call(f32[16,128]{1,0:T(8,128)} %bitcast.10, s32[4,64]{1,0:T(4,128)} %get-tuple-element.7.refs_1_), custom_call_target="tpu_custom_call" | custom-call | tf_op jit(solution)/shard_map/finish/pallas_call | solution.py:249
Async XLA Ops:
  26.1 2.3 %copy-start = (bf16[768,3072]{1,0:T(8,128)(2,1)S(1)}, bf16[768,3072]{1,0:T(8,128)(2,1)}, u32[]{:S(2)}) copy-start(bf16[768,3072]{1,0:T(8,128)(2,1)} %w1_ref.1) | copy-start | bytes 14155780
  28.5 2.3 %copy-start.1 = (bf16[3072,768]{1,0:T(8,128)(2,1)S(1)}, bf16[3072,768]{1,0:T(8,128)(2,1)}, u32[]{:S(2)}) copy-start(bf16[3072,768]{1,0:T(8,128)(2,1)} %w2_ref.1) | copy-start | bytes 14155780
  30.8 0.9 %copy-start.3 = (bf16[4,32,768]{2,1,0:T(8,128)(2,1)S(1)}, bf16[4,32,768]{2,1,0:T(8,128)(2,1)}, u32[]{:S(2)}) copy-start(bf16[4,32,768]{2,1,0:T(8,128)(2,1)} %x_ref.1) | copy-start | bytes 589828
  31.7 0.9 %copy-start.4 = (bf16[768,128]{1,0:T(8,128)(2,1)S(1)}, bf16[768,128]{1,0:T(8,128)(2,1)}, u32[]{:S(2)}) copy-start(bf16[768,128]{1,0:T(8,128)(2,1)} %embed_ref.1) | copy-start | bytes 589828
  32.6 0.7 copy-start.5
  37.6 18.9 %copy-start.2 = (bf16[128,128]{1,0:T(8,128)(2,1)}, bf16[128,128]{1,0:T(8,128)(2,1)S(1)}, u32[]{:S(2)}) copy-start(bf16[128,128]{1,0:T(8,128)(2,1)S(1)} %encode.1._) | copy-start | bytes 98308
  61.5 1.4 %copy-start.6 = (bf16[48,128,128]{2,1,0:T(8,128)(2,1)S(1)}, bf16[48,128,128]{2,1,0:T(8,128)(2,1)}, u32[]{:S(2)}) copy-start(bf16[48,128,128]{2,1,0:T(8,128)(2,1)} %get-tuple-element.6.pass_ref) | copy-start | bytes 4718596
  62.9 0.7 copy-start.7

commit v2 on v1

v2 whole, which is shorter than its diff:
```python
import jax
import jax.numpy as jnp
from jax import lax
from jax.experimental import pallas as pl
from jax.experimental.pallas import tpu as pltpu
from jax.sharding import PartitionSpec as P

TOPN = 10
F32 = jnp.float32
BF16 = jnp.bfloat16
NT = (((1,), (1,)), ((), ()))
VMEM = pl.BlockSpec(memory_space=pltpu.VMEM)
SMEM = pl.BlockSpec(memory_space=pltpu.SMEM)
ANY = pl.BlockSpec(memory_space=pl.ANY)


def split3(value):
    high = value.astype(BF16)
    rest = value - high.astype(F32)
    middle = rest.astype(BF16)
    low = (rest - middle.astype(F32)).astype(BF16)
    return high, middle, low


def encode_kernel(lens_ref, x_ref, w1_ref, w2_ref, gain_ref, embed_ref, out_ref, w1_buf, w2_buf, sems):
    chunks, _, width = w1_buf.shape
    copies = []
    for c in range(chunks):
        first = pltpu.make_async_copy(w1_ref.at[:, pl.ds(c * width, width)], w1_buf.at[c], sems.at[0, c])
        second = pltpu.make_async_copy(w2_ref.at[pl.ds(c * width, width), :], w2_buf.at[c], sems.at[1, c])
        first.start()
        second.start()
        copies.append((first, second))
    query_count, token_count, width_in = x_ref.shape
    x = x_ref[...].reshape(query_count * token_count, width_in)
    total = x.astype(F32)
    copies[0][0].wait()
    inner = jnp.dot(x, w1_buf[0], preferred_element_type=F32)
    for c in range(chunks):
        copies[c][1].wait()
        if c + 1 < chunks:
            copies[c + 1][0].wait()
            later = jnp.dot(x, w1_buf[c + 1], preferred_element_type=F32)
        active = (0.5 * inner * (1.0 + lax.erf(inner * (0.5 ** 0.5)))).astype(BF16)
        total = total + jnp.dot(active, w2_buf[c], preferred_element_type=F32)
        if c + 1 < chunks:
            inner = later
    centered = total - jnp.mean(total, axis=-1, keepdims=True)
    spread = jnp.mean(jnp.square(centered), axis=-1, keepdims=True)
    layer_out = (centered * lax.rsqrt(spread + 1e-12) * gain_ref[...]).astype(BF16)
    embedded = jnp.dot(layer_out, embed_ref[...], preferred_element_type=F32)
    length = jnp.sum(jnp.square(embedded), axis=-1, keepdims=True)
    vectors = embedded * lax.rsqrt(length + 1e-06)
    token = lax.broadcasted_iota(jnp.int32, vectors.shape, 0)
    for i in range(query_count):
        padded = (token >= i * token_count + lens_ref[i]) & (token < (i + 1) * token_count)
        vectors = jnp.where(padded, 0.0, vectors)
    out_ref[...] = vectors.astype(BF16)


def encode(query_lengths, query_hidden, inner_weight, outer_weight, norm_gain, embed_weight):
    query_count, token_count, d = query_hidden.shape
    ff = inner_weight.shape[1]
    e = embed_weight.shape[1]
    chunks = 6
    width = ff // chunks
    tokens = query_count * token_count
    return pl.pallas_call(
        encode_kernel,
        out_shape=jax.ShapeDtypeStruct((tokens, e), BF16),
        in_specs=[SMEM, VMEM, ANY, ANY, VMEM, VMEM],
        out_specs=VMEM,
        scratch_shapes=[
            pltpu.VMEM((chunks, d, width), BF16),
            pltpu.VMEM((chunks, width, d), BF16),
            pltpu.SemaphoreType.DMA((2, chunks)),
        ],
        compiler_params=pltpu.CompilerParams(vmem_limit_bytes=56 * 2 ** 20),
        cost_estimate=pl.CostEstimate(
            flops=4 * tokens * d * ff, bytes_accessed=4 * d * ff, transcendentals=tokens * ff
        ),
        name="encode",
    )(query_lengths, query_hidden, inner_weight, outer_weight, norm_gain.reshape(1, d), embed_weight)


def prepare_kernel(slots, token_count, me_ref, row_ref, own_ref, row_lanes_ref, *refs):
    cand_refs = refs[:slots]
    index_ref, rows_ref = refs[slots + 1:]
    passage_count = index_ref.shape[0]
    half = passage_count // 2
    query_count, cand_count = own_ref.shape

    def lookup(k, carry):
        for i in range(query_count):
            rows_ref[i, k] = row_ref[own_ref[i, k]]
        return carry

    lax.fori_loop(0, cand_count, lookup, 0, unroll=4)

    position = lax.broadcasted_iota(jnp.int32, (passage_count, 128), 0)
    local = jnp.where(position < half, position + me_ref[0] * half, position - half + me_ref[1] * half)
    lane = lax.broadcasted_iota(jnp.int32, (passage_count, 128), 1)

    def find(j, found):
        return jnp.where(row_lanes_ref[pl.ds(j, 1), :] == local, (lane + j * 128).astype(F32), found)

    found = lax.fori_loop(0, row_lanes_ref.shape[0], find, jnp.zeros((passage_count, 128), F32))
    passage_id = jnp.sum(found, axis=1, keepdims=True).astype(jnp.int32)
    passage_id = jnp.broadcast_to(passage_id, (passage_count, cand_count))

    slot_lane = lax.broadcasted_iota(jnp.int32, index_ref.shape, 1)
    index = jnp.zeros(index_ref.shape, jnp.int32)
    for s in range(slots):
        hit = jnp.zeros((passage_count, cand_count), F32)
        for i in range(1, query_count):
            hit = jnp.where(cand_refs[s][i:i + 1, :] == passage_id, float(i), hit)
        query = jnp.sum(hit, axis=1, keepdims=True).astype(jnp.int32)
        index = jnp.where(slot_lane == s, query * token_count, index)
    index_ref[...] = index


def prepare(me, passage_row, candidates, passage_count, token_count, after):
    slots = len(candidates)

    def kernel(*refs):
        prepare_kernel(slots, token_count, *refs)

    return pl.pallas_call(
        kernel,
        out_shape=(
            jax.ShapeDtypeStruct((passage_count, slots), jnp.int32),
            jax.ShapeDtypeStruct(candidates[0].shape, jnp.int32),
        ),
        in_specs=[SMEM, SMEM, SMEM, VMEM] + [VMEM] * slots + [ANY],
        out_specs=(VMEM, SMEM),
        cost_estimate=pl.CostEstimate(flops=10 ** 6, bytes_accessed=10 ** 6, transcendentals=0),
        name="prepare",
    )(me, passage_row, candidates[0], passage_row.reshape(-1, 128), *candidates, after)


def score_kernel(slots, index_ref, len0_ref, len1_ref, pass0_ref, pass1_ref, *refs):
    query_refs = refs[:slots]
    out_refs = refs[slots:2 * slots]
    best_ref = refs[2 * slots]
    half, plen, _ = pass0_ref.shape
    token_count = best_ref.shape[1] // slots
    group = min(slots, 256 // token_count)
    position = lax.broadcasted_iota(jnp.int32, (plen, group * token_count), 0)

    for side, (len_ref, pass_ref) in enumerate(((len0_ref, pass0_ref), (len1_ref, pass1_ref))):

        def eight(step, carry):
            for part in range(slots // group):
                rows = []
                for j in range(8):
                    p = step * 8 + j
                    picked = jnp.concatenate(
                        [
                            query_refs[s][
                                pl.ds(pl.multiple_of(index_ref[side * half + p, s], token_count), token_count), :
                            ]
                            for s in range(part * group, (part + 1) * group)
                        ],
                        axis=0,
                    )
                    similar = lax.dot_general(pass_ref[p], picked, NT, preferred_element_type=F32)
                    similar = jnp.where(position < len_ref[p], similar, -1e30)
                    rows.append(jnp.max(similar, axis=0, keepdims=True))
                best_ref[
                    pl.ds(pl.multiple_of(side * half + step * 8, 8), 8),
                    pl.ds(part * group * token_count, group * token_count),
                ] = jnp.concatenate(rows, axis=0)
            return carry

        lax.fori_loop(0, half // 8, eight, 0)
    wide = best_ref.shape[1]
    source = lax.broadcasted_iota(jnp.int32, (slots, wide), 0)
    column = lax.broadcasted_iota(jnp.int32, (slots, wide), 1)
    first = source * token_count
    ones = jnp.where((column >= first) & (column < first + token_count), 1.0, 0.0).astype(BF16)
    total = sum(lax.dot_general(ones, part, NT, preferred_element_type=F32) for part in split3(best_ref[...]))
    for s in range(slots):
        out_refs[s][...] = jnp.zeros(out_refs[s].shape, F32)
        out_refs[s][:, pl.ds(0, 2 * half)] = total[s:s + 1]


def score(index, lengths, passages, queries, token_count):
    half, plen, e = passages[0].shape
    slots = len(queries)
    lanes = -(-2 * half // 128) * 128

    def kernel(*refs):
        score_kernel(slots, *refs)

    return pl.pallas_call(
        kernel,
        out_shape=[jax.ShapeDtypeStruct((1, lanes), F32)] * slots,
        in_specs=[SMEM, SMEM, SMEM, VMEM, VMEM] + [VMEM] * slots,
        out_specs=[VMEM] * slots,
        scratch_shapes=[pltpu.VMEM((2 * half, slots * token_count), F32)],
        cost_estimate=pl.CostEstimate(
            flops=4 * half * slots * token_count * plen * e,
            bytes_accessed=4 * passages[0].size,
            transcendentals=0,
        ),
        name="score",
    )(index, *lengths, *passages, *queries)


def finish_kernel(slots, half, me_ref, rows_ref, *refs):
    got_refs = refs[:slots]
    scores_ref, best_ref = refs[slots:]
    query_count, cand_count = scores_ref.shape
    got = jnp.concatenate([ref[...] for ref in got_refs], axis=0)
    lanes = got.shape[1]
    parts = split3(got)
    slot_iota = lax.broadcasted_iota(jnp.int32, (slots, cand_count), 0)
    local_iota = lax.broadcasted_iota(jnp.int32, (lanes, cand_count), 0)
    row_iota = lax.broadcasted_iota(jnp.int32, (cand_count, cand_count), 0)
    col_iota = lax.broadcasted_iota(jnp.int32, (cand_count, cand_count), 1)
    place = lax.broadcasted_iota(jnp.int32, (cand_count, 128), 1)
    me = me_ref[0]
    for i in range(query_count):
        row = rows_ref[i:i + 1, :]
        owner = row // half
        side = jnp.bitwise_and(jnp.bitwise_xor(owner, me), 1)
        local = row - owner * half + side * half
        slot = jnp.right_shift(jnp.bitwise_xor(owner, me), 1)
        onehot = jnp.where(local_iota == local, 1.0, 0.0).astype(BF16)
        picked = sum(jnp.dot(part, onehot, preferred_element_type=F32) for part in parts)
        score_row = jnp.sum(jnp.where(slot_iota == slot, picked, 0.0), axis=0, keepdims=True)
        scores_ref[i:i + 1, :] = score_row
        across = jnp.broadcast_to(score_row, (cand_count, cand_count))
        score_col = jnp.sum(jnp.where(row_iota == col_iota, across, 0.0), axis=1, keepdims=True)
        ahead = (across > score_col) | ((across == score_col) & (col_iota < row_iota))
        rank = jnp.sum(jnp.where(ahead, 1.0, 0.0), axis=1, keepdims=True).astype(jnp.int32)
        ordered = jnp.sum(jnp.where(rank == place, score_col, 0.0), axis=0, keepdims=True)
        best_ref[i:i + 1, :] = ordered[:, :TOPN]


def finish(me, rows, got, half):
    slots = len(got)

    def kernel(*refs):
        finish_kernel(slots, half, *refs)

    return pl.pallas_call(
        kernel,
        out_shape=(
            jax.ShapeDtypeStruct(rows.shape, F32),
            jax.ShapeDtypeStruct((rows.shape[0], TOPN), F32),
        ),
        in_specs=[SMEM, VMEM] + [VMEM] * slots,
        out_specs=(VMEM, VMEM),
        name="finish",
    )(me, rows, *got)


def swap(value, distance):
    size = lax.axis_size("shard")
    return lax.ppermute(value, "shard", [(i, i ^ distance) for i in range(size)])


def spread(value, slots):
    return [value] + [swap(value, 2 * d) for d in range(1, slots)]


def per_device(
    query_hidden,
    query_lengths,
    inner_weight,
    outer_weight,
    norm_gain,
    embed_weight,
    passage_vectors,
    passage_lengths,
    passage_row,
    candidates,
):
    half = passage_vectors.shape[0]
    token_count = query_hidden.shape[1]
    slots = lax.axis_size("shard") // 2
    shard = lax.axis_index("shard").astype(jnp.int32)
    me = jnp.stack([shard, jnp.bitwise_xor(shard, 1)])
    all_candidates = spread(candidates, slots)
    passages = (passage_vectors, swap(passage_vectors, 1))
    lengths = (passage_lengths, swap(passage_lengths, 1))
    vectors = encode(query_lengths, query_hidden, inner_weight, outer_weight, norm_gain, embed_weight)
    all_vectors = spread(vectors, slots)
    index, rows = prepare(me, passage_row, all_candidates, 2 * half, token_count, vectors)
    sums = score(index, lengths, passages, all_vectors, token_count)
    got = [sums[0]] + [swap(sums[d], 2 * d) for d in range(1, slots)]
    return finish(me, rows, got, half)


def solution(mesh):
    in_specs = (
        P(("groups", "shard"), None, None),
        P(("groups", "shard")),
        P(),
        P(),
        P(),
        P(),
        P(("groups", "shard"), None, None),
        P(("groups", "shard")),
        P("groups"),
        P(("groups", "shard"), None),
    )
    out_specs = (P(("groups", "shard"), None), P(("groups", "shard"), None))
    return jax.shard_map(
        per_device, mesh=mesh, in_specs=in_specs, out_specs=out_specs, check_vma=False
    )
```

time: 79.3 us -> 83.1 us (1.048)
  blocking collectives: 53.3 us -> 0 us
  starting transfers between devices: 0 us -> 37.6 us
  waiting for transfers between devices: 0 us -> 23.6 us
  local copies, waits for them, and re-layouts: 10 us -> 3.01 us
  Pallas kernels: 14.8 us -> 17.1 us
    all_gather x2 -> x0, blocking collectives: 43.7 us -> none  [the longest x1 24.8 us: per_device(): all_candidates = lax.all_gather(candidates, 'shard', axis=0, tiled=True)]
    ppermute x0 -> x23, starting transfers between devices: none -> 37.6 us  [swap(): lax.ppermute(value, 'shard', [(i, i ^ distance) for i in range(size)])]
    ppermute x0 -> x23, waiting for transfers between devices: none -> 23.6 us  [swap(): lax.ppermute(value, 'shard', [(i, i ^ distance) for i in range(size)])]
    all_to_all x1 -> x0, blocking collectives: 9.67 us -> none  [per_device(): got = lax.all_to_all(sums, 'shard', split_axis=0, concat_axis=0, tiled=True)]
    unnamed x16 -> x50, local copies, waits for them, and re-layouts: 9.32 us -> 1.75 us
    pallas_call x1, Pallas kernels: 4.24 us -> 6.33 us  [encode(): pl.pallas_call(encode_kernel, out_shape=jax.ShapeDtypeStruct((tokens, e),...]
  transfers between devices with their start and end apart: 0 -> 23, of which waited for: 0 -> 10; matrix products, arithmetic and copies ran while one was open for 0% -> 2% of each run, Pallas kernels for 0% -> 11%
where the time goes in v2:
time: 83.1 us; the launch traced here: 82.8 us
  starting transfers between devices  37.6 us (45%)
  waiting for transfers between devices  23.6 us (28%)
  Pallas kernels  17.1 us (21%)
  local copies, waits for them, and re-layouts  3.01 us (4%)
  between operations  0.89 us (1%)
    ppermute x23, starting transfers between devices, swap(): lax.ppermute(value, 'shard', [(i, i ^ distance) for i in range(size)])  37.6 us
    ppermute x23, waiting for transfers between devices, swap(): lax.ppermute(value, 'shard', [(i, i ^ distance) for i in range(size)])  23.6 us
    pallas_call x1, Pallas kernels, score(): pl.pallas_call(kernel, out_shape=[jax.ShapeDtypeStruct((1, lanes), F32)]...  6.56 us
    pallas_call x1, Pallas kernels, encode(): pl.pallas_call(encode_kernel, out_shape=jax.ShapeDtypeStruct((tokens, e),...  6.33 us
    pallas_call x1, Pallas kernels, prepare(): pl.pallas_call(kernel, out_shape=(jax.ShapeDtypeStruct((passage_count, sl...  2.37 us
    pallas_call x1, Pallas kernels, finish(): pl.pallas_call(kernel, out_shape=(jax.ShapeDtypeStruct(rows.shape, F32),...  1.81 us
    unnamed x50, local copies, waits for them, and re-layouts  1.75 us
  transfers between devices with their start and end apart: 23, of which 10 were waited for; matrix products, arithmetic and copies ran while one was open for 2% of the time, Pallas kernels for 11%

profile of v2, /device:TPU:0, one launch (start us, length us, event | category | flops | bytes accessed | tf_op | source)
XLA Modules:
  0.0 82.8 jit_solution(14827650170430309591)
XLA Ops:
  0.6 0.5 collective-permute-start.8
  1.1 1.3 %reshape.11.gain_ref = f32[1,768]{1,0:T(1,128)} reshape(f32[768]{0:T(1024)} %param.14) | data formatting | bytes 6144 | tf_op jit(solution)/shard_map/reshape | solution.py:83
  2.4 6.3 %encode.1.refs_12_.refs_5_ = bf16[128,128]{1,0:T(8,128)(2,1)} custom-call(s32[4]{0:T(128)} %lens_ref.1, bf16[4,32,768]{2,1,0:T(8,128)(2,1)} %x_ref.1, bf16[768,3072]{1,0:T(8,128)(2,1)} %w1_ref.1, bf16[3072,768]{1,0:T(8,128)(2,1)} %w2_ref.1, f32[1,768]{1,0:T(1,128)} %reshape.11.gain_ref, bf16[768,128]{1,0:T(8,128)(2,1)} %embed_ref.1), custom_call_target="tpu_custom_call" | custom-call | flops 1207959552 | bytes 9437184 | tf_op jit(solution)/shard_map/encode/pallas_call | solution.py:68
  8.8 5.6 %collective-permute-start.15 = (bf16[128,128]{1,0:T(8,128)(2,1)}, bf16[128,128]{1,0:T(8,128)(2,1)S(1)}, u32[]{:S(2)}, u32[]{:S(2)}) collective-permute-start(bf16[128,128]{1,0:T(8,128)(2,1)} %encode.1.refs_12_.refs_5_), channel_id=1, source_target_pairs={{0,14},{1,15},{2,12},{3,13},{4,10},{5,11},{6,8},{7,9},{8,6},{9,7},... | collective-permute-start | bytes 98312 | tf_op jit(solution)/shard_map/ppermute | solution.py:261
  14.4 0.2 collective-permute-start.14
  14.6 0.7 collective-permute-start.13
  15.3 0.0 copy-done.16
  15.3 0.0 collective-permute-start.7
  15.3 1.1 %collective-permute-done.7.refs_2_ = s32[48]{0:T(128)S(1)} collective-permute-done((s32[48]{0:T(128)S(1)}, s32[48]{0:T(128)S(1)}, u32[]{:S(2)}, u32[]{:S(2)}) %collective-permute-start.7) | collective-permute-done | bytes 224 | tf_op jit(solution)/shard_map/ppermute | solution.py:261
  16.5 0.0 copy-done.8
  16.5 2.9 %collective-permute-start.5 = (s32[4,64]{1,0:T(4,128)S(1)}, s32[4,64]{1,0:T(4,128)S(1)}, u32[]{:S(2)}, u32[]{:S(2)}) collective-permute-start(s32[4,64]{1,0:T(4,128)S(1)} %copy-done.8), channel_id=1, source_target_pairs={{0,12},{1,13},{2,14},{3,15},{4,8},{5,9},{6,10},{7,11},{8,4},{9,5},... | collective-permute-start | bytes 3080 | tf_op jit(solution)/shard_map/ppermute | solution.py:261
  19.3 2.5 %collective-permute-done.5.refs_10_ = s32[4,64]{1,0:T(4,128)S(1)} collective-permute-done((s32[4,64]{1,0:T(4,128)S(1)}, s32[4,64]{1,0:T(4,128)S(1)}, u32[]{:S(2)}, u32[]{:S(2)}) %collective-permute-start.5) | collective-permute-done | bytes 1056 | tf_op jit(solution)/shard_map/ppermute | solution.py:261
  21.9 2.0 %collective-permute-start.4 = (s32[4,64]{1,0:T(4,128)S(1)}, s32[4,64]{1,0:T(4,128)S(1)}, u32[]{:S(2)}, u32[]{:S(2)}) collective-permute-start(s32[4,64]{1,0:T(4,128)S(1)} %copy-done.8), channel_id=1, source_target_pairs={{0,10},{1,11},{2,8},{3,9},{4,14},{5,15},{6,12},{7,13},{8,2},{9,3},... | collective-permute-start | bytes 3080 | tf_op jit(solution)/shard_map/ppermute | solution.py:261
  23.8 3.4 %collective-permute-done.4.refs_9_ = s32[4,64]{1,0:T(4,128)S(1)} collective-permute-done((s32[4,64]{1,0:T(4,128)S(1)}, s32[4,64]{1,0:T(4,128)S(1)}, u32[]{:S(2)}, u32[]{:S(2)}) %collective-permute-start.4) | collective-permute-done | bytes 1056 | tf_op jit(solution)/shard_map/ppermute | solution.py:261
  27.2 1.0 %collective-permute-start.3 = (s32[4,64]{1,0:T(4,128)S(1)}, s32[4,64]{1,0:T(4,128)S(1)}, u32[]{:S(2)}, u32[]{:S(2)}) collective-permute-start(s32[4,64]{1,0:T(4,128)S(1)} %copy-done.8), channel_id=1, source_target_pairs={{0,8},{1,9},{2,10},{3,11},{4,12},{5,13},{6,14},{7,15},{8,0},{9,1},... | collective-permute-start | bytes 3080 | tf_op jit(solution)/shard_map/ppermute | solution.py:261
  28.3 3.5 %collective-permute-done.3.refs_8_ = s32[4,64]{1,0:T(4,128)S(1)} collective-permute-done((s32[4,64]{1,0:T(4,128)S(1)}, s32[4,64]{1,0:T(4,128)S(1)}, u32[]{:S(2)}, u32[]{:S(2)}) %collective-permute-start.3) | collective-permute-done | bytes 1056 | tf_op jit(solution)/shard_map/ppermute | solution.py:261
  31.7 2.5 %collective-permute-start.2 = (s32[4,64]{1,0:T(4,128)S(1)}, s32[4,64]{1,0:T(4,128)S(1)}, u32[]{:S(2)}, u32[]{:S(2)}) collective-permute-start(s32[4,64]{1,0:T(4,128)S(1)} %copy-done.8), channel_id=1, source_target_pairs={{0,6},{1,7},{2,4},{3,5},{4,2},{5,3},{6,0},{7,1},{8,14},{9,15},{10,... | collective-permute-start | bytes 3080 | tf_op jit(solution)/shard_map/ppermute | solution.py:261
  34.3 2.0 %collective-permute-done.2.refs_7_ = s32[4,64]{1,0:T(4,128)S(1)} collective-permute-done((s32[4,64]{1,0:T(4,128)S(1)}, s32[4,64]{1,0:T(4,128)S(1)}, u32[]{:S(2)}, u32[]{:S(2)}) %collective-permute-start.2) | collective-permute-done | bytes 1056 | tf_op jit(solution)/shard_map/ppermute | solution.py:261
  36.2 1.6 %collective-permute-start.1 = (s32[4,64]{1,0:T(4,128)S(1)}, s32[4,64]{1,0:T(4,128)S(1)}, u32[]{:S(2)}, u32[]{:S(2)}) collective-permute-start(s32[4,64]{1,0:T(4,128)S(1)} %copy-done.8), channel_id=1, source_target_pairs={{0,4},{1,5},{2,6},{3,7},{4,0},{5,1},{6,2},{7,3},{8,12},{9,13},{10,... | collective-permute-start | bytes 3080 | tf_op jit(solution)/shard_map/ppermute | solution.py:261
  37.8 2.0 %collective-permute-done.1.refs_6_ = s32[4,64]{1,0:T(4,128)S(1)} collective-permute-done((s32[4,64]{1,0:T(4,128)S(1)}, s32[4,64]{1,0:T(4,128)S(1)}, u32[]{:S(2)}, u32[]{:S(2)}) %collective-permute-start.1) | collective-permute-done | bytes 1056 | tf_op jit(solution)/shard_map/ppermute | solution.py:261
  39.8 1.5 %collective-permute-start = (s32[4,64]{1,0:T(4,128)S(1)}, s32[4,64]{1,0:T(4,128)S(1)}, u32[]{:S(2)}, u32[]{:S(2)}) collective-permute-start(s32[4,64]{1,0:T(4,128)S(1)} %copy-done.8), channel_id=1, source_target_pairs={{0,2},{1,3},{2,0},{3,1},{4,6},{5,7},{6,4},{7,5},{8,10},{9,11},{10,... | collective-permute-start | bytes 3080 | tf_op jit(solution)/shard_map/ppermute | solution.py:261
  41.3 2.1 %collective-permute-done.refs_5_ = s32[4,64]{1,0:T(4,128)S(1)} collective-permute-done((s32[4,64]{1,0:T(4,128)S(1)}, s32[4,64]{1,0:T(4,128)S(1)}, u32[]{:S(2)}, u32[]{:S(2)}) %collective-permute-start) | collective-permute-done | bytes 1056 | tf_op jit(solution)/shard_map/ppermute | solution.py:261
  43.4 2.8 %collective-permute-start.6 = (s32[4,64]{1,0:T(4,128)S(1)}, s32[4,64]{1,0:T(4,128)S(1)}, u32[]{:S(2)}, u32[]{:S(2)}) collective-permute-start(s32[4,64]{1,0:T(4,128)S(1)} %copy-done.8), channel_id=1, source_target_pairs={{0,14},{1,15},{2,12},{3,13},{4,10},{5,11},{6,8},{7,9},{8,6},{9,7},... | collective-permute-start | bytes 3080 | tf_op jit(solution)/shard_map/ppermute | solution.py:261
  46.2 3.5 %collective-permute-done.6.refs_11_ = s32[4,64]{1,0:T(4,128)S(1)} collective-permute-done((s32[4,64]{1,0:T(4,128)S(1)}, s32[4,64]{1,0:T(4,128)S(1)}, u32[]{:S(2)}, u32[]{:S(2)}) %collective-permute-start.6) | collective-permute-done | bytes 1056 | tf_op jit(solution)/shard_map/ppermute | solution.py:261
  49.7 0.0 collective-permute-start.12
  49.7 0.0 collective-permute-done.15.refs_12_
  49.7 0.0 copy-start.1
  49.7 3.4 %collective-permute-start.11 = (bf16[128,128]{1,0:T(8,128)(2,1)}, bf16[128,128]{1,0:T(8,128)(2,1)S(1)}, u32[]{:S(2)}, u32[]{:S(2)}) collective-permute-start(bf16[128,128]{1,0:T(8,128)(2,1)} %encode.1.refs_12_.refs_5_), channel_id=1, source_target_pairs={{0,6},{1,7},{2,4},{3,5},{4,2},{5,3},{6,0},{7,1},{8,14},{9,15},{10,... | collective-permute-start | bytes 98312 | tf_op jit(solution)/shard_map/ppermute | solution.py:261
  53.1 0.0 collective-permute-done.14.refs_11_
  53.1 0.1 collective-permute-start.10
  53.2 0.0 collective-permute-done.13.refs_10_
  53.2 1.5 %collective-permute-start.9 = (bf16[128,128]{1,0:T(8,128)(2,1)}, bf16[128,128]{1,0:T(8,128)(2,1)S(1)}, u32[]{:S(2)}, u32[]{:S(2)}) collective-permute-start(bf16[128,128]{1,0:T(8,128)(2,1)} %encode.1.refs_12_.refs_5_), channel_id=1, source_target_pairs={{0,2},{1,3},{2,0},{3,1},{4,6},{5,7},{6,4},{7,5},{8,10},{9,11},{10,... | collective-permute-start | bytes 98312 | tf_op jit(solution)/shard_map/ppermute | solution.py:261
  54.7 0.6 pad_add_fusion.refs_0_
  55.3 0.0 copy-done.10
  55.3 0.0 copy-done.12
  55.4 2.4 %prepare.1 = (s32[96,8]{1,0:T(8,128)}, s32[4,64]{1,0:T(4,128)}) custom-call(s32[2]{0:T(128)} %pad_add_fusion.refs_0_, s32[768]{0:T(1024)} %refs_1_.2, s32[4,64]{1,0:T(4,128)} %refs_4_.1, s32[6,128]{1,0:T(8,128)} %bitcast.3, s32[4,64]{1,0:T(4,128)} %refs_4_.1, s32[4,64]{1,0:T(4,128)} %copy-done.14, s32[4,64]{1,0:T(4,128)} %copy-done.13, s32[4,64]{1,0:T(4,128)} %copy-done.12, ...), custom_call_target="tpu_custom_call" | custom-call | flops 1000000 | bytes 1000000 | tf_op jit(solution)/shard_map/prepare/pallas_call | solution.py:128
  57.8 0.0 collective-permute-done.12.refs_9_
  57.8 0.0 collective-permute-done.11.refs_8_
  57.8 0.0 collective-permute-done.10.refs_7_
  57.8 0.0 collective-permute-done.9.refs_6_
  57.8 0.0 collective-permute-done.8.refs_4_
  57.9 0.5 copy-done.4
  58.4 0.0 copy-done.5
  58.4 0.0 copy-done.6
  58.4 0.0 copy-done.7
  58.4 0.6 copy-done
  59.0 6.6 %score.1 = (f32[1,128]{1,0:T(1,128)}, f32[1,128]{1,0:T(1,128)}, f32[1,128]{1,0:T(1,128)}, f32[1,128]{1,0:T(1,128)}, f32[1,128]{1,0:T(1,128)}, /*index=5*/f32[1,1...) custom-call(s32[96,8]{1,0:T(8,128)} %get-tuple-element.13.refs_0_, s32[48]{0:T(128)} %refs_1_.3, s32[48]{0:T(128)} %copy-done.17, ...), custom_call_target="tpu_custom_call" | custom-call | flops 805306368 | bytes 3145728 | tf_op jit(solution)/shard_map/score/pallas_call | solution.py:195
  65.6 1.0 %collective-permute-start.16 = (f32[1,128]{1,0:T(1,128)}, f32[1,128]{1,0:T(1,128)S(1)}, u32[]{:S(2)}, u32[]{:S(2)}) collective-permute-start(f32[1,128]{1,0:T(1,128)} %get-tuple-element.15), channel_id=1, source_target_pairs={{0,2},{1,3},{2,0},{3,1},{4,6},{5,7},{6,4},{7,5},{8,10},{9,11},{10,... | collective-permute-start | bytes 1544 | tf_op jit(solution)/shard_map/ppermute | solution.py:261
  66.6 1.9 %collective-permute-start.17 = (f32[1,128]{1,0:T(1,128)}, f32[1,128]{1,0:T(1,128)S(1)}, u32[]{:S(2)}, u32[]{:S(2)}) collective-permute-start(f32[1,128]{1,0:T(1,128)} %get-tuple-element.16), channel_id=1, source_target_pairs={{0,4},{1,5},{2,6},{3,7},{4,0},{5,1},{6,2},{7,3},{8,12},{9,13},{10,... | collective-permute-start | bytes 1544 | tf_op jit(solution)/shard_map/ppermute | solution.py:261
  68.6 0.6 collective-permute-start.18
  69.1 1.9 %collective-permute-start.19 = (f32[1,128]{1,0:T(1,128)}, f32[1,128]{1,0:T(1,128)S(1)}, u32[]{:S(2)}, u32[]{:S(2)}) collective-permute-start(f32[1,128]{1,0:T(1,128)} %get-tuple-element.18), channel_id=1, source_target_pairs={{0,8},{1,9},{2,10},{3,11},{4,12},{5,13},{6,14},{7,15},{8,0},{9,1},... | collective-permute-start | bytes 1544 | tf_op jit(solution)/shard_map/ppermute | solution.py:261
  71.0 1.5 %collective-permute-start.20 = (f32[1,128]{1,0:T(1,128)}, f32[1,128]{1,0:T(1,128)S(1)}, u32[]{:S(2)}, u32[]{:S(2)}) collective-permute-start(f32[1,128]{1,0:T(1,128)} %get-tuple-element.19), channel_id=1, source_target_pairs={{0,10},{1,11},{2,8},{3,9},{4,14},{5,15},{6,12},{7,13},{8,2},{9,3},... | collective-permute-start | bytes 1544 | tf_op jit(solution)/shard_map/ppermute | solution.py:261
  72.5 0.0 collective-permute-done.16.refs_3_
  72.5 1.5 %collective-permute-start.21 = (f32[1,128]{1,0:T(1,128)}, f32[1,128]{1,0:T(1,128)S(1)}, u32[]{:S(2)}, u32[]{:S(2)}) collective-permute-start(f32[1,128]{1,0:T(1,128)} %get-tuple-element.20), channel_id=1, source_target_pairs={{0,12},{1,13},{2,14},{3,15},{4,8},{5,9},{6,10},{7,11},{8,4},{9,5},... | collective-permute-start | bytes 1544 | tf_op jit(solution)/shard_map/ppermute | solution.py:261
  74.0 0.0 collective-permute-done.17.refs_4_
  74.0 2.8 %collective-permute-start.22 = (f32[1,128]{1,0:T(1,128)}, f32[1,128]{1,0:T(1,128)S(1)}, u32[]{:S(2)}, u32[]{:S(2)}) collective-permute-start(f32[1,128]{1,0:T(1,128)} %get-tuple-element.21), channel_id=1, source_target_pairs={{0,14},{1,15},{2,12},{3,13},{4,10},{5,11},{6,8},{7,9},{8,6},{9,7},... | collective-permute-start | bytes 1544 | tf_op jit(solution)/shard_map/ppermute | solution.py:261
  76.8 0.0 collective-permute-done.18.refs_5_
  76.8 0.0 collective-permute-done.19.refs_6_
  76.8 0.0 collective-permute-done.20.refs_7_
  76.8 1.0 %collective-permute-done.21.refs_8_ = f32[1,128]{1,0:T(1,128)S(1)} collective-permute-done((f32[1,128]{1,0:T(1,128)}, f32[1,128]{1,0:T(1,128)S(1)}, u32[]{:S(2)}, u32[]{:S(2)}) %collective-permute-start.21) | collective-permute-done | bytes 544 | tf_op jit(solution)/shard_map/ppermute | solution.py:261
  77.9 2.6 %collective-permute-done.22.refs_9_ = f32[1,128]{1,0:T(1,128)S(1)} collective-permute-done((f32[1,128]{1,0:T(1,128)}, f32[1,128]{1,0:T(1,128)S(1)}, u32[]{:S(2)}, u32[]{:S(2)}) %collective-permute-start.22) | collective-permute-done | bytes 544 | tf_op jit(solution)/shard_map/ppermute | solution.py:261
  80.4 0.0 copy-done.20
  80.5 0.5 copy-done.24
  81.0 1.8 %finish.1 = (f32[4,64]{1,0:T(4,128)}, f32[4,10]{1,0:T(4,128)}) custom-call(s32[2]{0:T(128)} %pad_add_fusion.refs_0_, s32[4,64]{1,0:T(4,128)} %get-tuple-element.12.refs_1_, f32[1,128]{1,0:T(1,128)} %get-tuple-element.14.refs_2_, f32[1,128]{1,0:T(1,128)} %copy-done.18, f32[1,128]{1,0:T(1,128)} %copy-done.19, f32[1,128]{1,0:T(1,128)} %copy-done.20, ...), custom_call_target="tpu_custom_call" | custom-call | tf_op jit(solution)/shard_map/finish/pallas_call | solution.py:247
  (38 shorter events, 0.1 us)
Async XLA Ops:
  0.6 57.2 %collective-permute-start.8 = (bf16[48,128,128]{2,1,0:T(8,128)(2,1)}, bf16[48,128,128]{2,1,0:T(8,128)(2,1)S(1)}, u32[]{:S(2)}, u32[]{:S(2)}) collective-permute-start(bf16[48,128,128]{2,1,0:T(8,128)(2,1)} %refs_3_.1), channel_id=1, source_target_pairs={{0,1},{1,0},{2,3},{3,2},{4,5},{5,4},{6,7},{7,6},{8,9},{9,8},{10,11... | collective-permute-start | bytes 4718600 | tf_op jit(solution)/shard_map/ppermute | solution.py:261
  2.4 12.9 %copy-start.16 = (s32[48]{0:T(128)S(1)}, s32[48]{0:T(128)}, u32[]{:S(2)}) copy-start(s32[48]{0:T(128)} %refs_1_.3) | copy-start | bytes 580
  2.4 14.1 %copy-start.8 = (s32[4,64]{1,0:T(4,128)S(1)}, s32[4,64]{1,0:T(4,128)}, u32[]{:S(2)}) copy-start(s32[4,64]{1,0:T(4,128)} %refs_4_.1) | copy-start | bytes 3076
  8.8 40.9 %collective-permute-start.15 = (bf16[128,128]{1,0:T(8,128)(2,1)}, bf16[128,128]{1,0:T(8,128)(2,1)S(1)}, u32[]{:S(2)}, u32[]{:S(2)}) collective-permute-start(bf16[128,128]{1,0:T(8,128)(2,1)} %encode.1.refs_12_.refs_5_), channel_id=1, source_target_pairs={{0,14},{1,15},{2,12},{3,13},{4,10},{5,11},{6,8},{7,9},{8,6},{9,7},... | collective-permute-start | bytes 98312 | tf_op jit(solution)/shard_map/ppermute | solution.py:261
  14.4 38.7 %collective-permute-start.14 = (bf16[128,128]{1,0:T(8,128)(2,1)}, bf16[128,128]{1,0:T(8,128)(2,1)S(1)}, u32[]{:S(2)}, u32[]{:S(2)}) collective-permute-start(bf16[128,128]{1,0:T(8,128)(2,1)} %encode.1.refs_12_.refs_5_), channel_id=1, source_target_pairs={{0,12},{1,13},{2,14},{3,15},{4,8},{5,9},{6,10},{7,11},{8,4},{9,5},... | collective-permute-start | bytes 98312 | tf_op jit(solution)/shard_map/ppermute | solution.py:261
  14.6 38.6 %collective-permute-start.13 = (bf16[128,128]{1,0:T(8,128)(2,1)}, bf16[128,128]{1,0:T(8,128)(2,1)S(1)}, u32[]{:S(2)}, u32[]{:S(2)}) collective-permute-start(bf16[128,128]{1,0:T(8,128)(2,1)} %encode.1.refs_12_.refs_5_), channel_id=1, source_target_pairs={{0,10},{1,11},{2,8},{3,9},{4,14},{5,15},{6,12},{7,13},{8,2},{9,3},... | collective-permute-start | bytes 98312 | tf_op jit(solution)/shard_map/ppermute | solution.py:261
  15.3 1.1 %collective-permute-start.7 = (s32[48]{0:T(128)S(1)}, s32[48]{0:T(128)S(1)}, u32[]{:S(2)}, u32[]{:S(2)}) collective-permute-start(s32[48]{0:T(128)S(1)} %copy-done.16), channel_id=1, source_target_pairs={{0,1},{1,0},{2,3},{3,2},{4,5},{5,4},{6,7},{7,6},{8,9},{9,8},{10,11... | collective-permute-start | bytes 584 | tf_op jit(solution)/shard_map/ppermute | solution.py:261
  16.5 41.4 %copy-start.17 = (s32[48]{0:T(128)}, s32[48]{0:T(128)S(1)}, u32[]{:S(2)}) copy-start(s32[48]{0:T(128)S(1)} %collective-permute-done.7.refs_2_) | copy-start | bytes 580
  16.5 5.4 %collective-permute-start.5 = (s32[4,64]{1,0:T(4,128)S(1)}, s32[4,64]{1,0:T(4,128)S(1)}, u32[]{:S(2)}, u32[]{:S(2)}) collective-permute-start(s32[4,64]{1,0:T(4,128)S(1)} %copy-done.8), channel_id=1, source_target_pairs={{0,12},{1,13},{2,14},{3,15},{4,8},{5,9},{6,10},{7,11},{8,4},{9,5},... | collective-permute-start | bytes 3080 | tf_op jit(solution)/shard_map/ppermute | solution.py:261
  21.9 33.5 %copy-start.9 = (s32[4,64]{1,0:T(4,128)}, s32[4,64]{1,0:T(4,128)S(1)}, u32[]{:S(2)}) copy-start(s32[4,64]{1,0:T(4,128)S(1)} %collective-permute-done.5.refs_10_) | copy-start | bytes 3076
  21.9 5.4 %collective-permute-start.4 = (s32[4,64]{1,0:T(4,128)S(1)}, s32[4,64]{1,0:T(4,128)S(1)}, u32[]{:S(2)}, u32[]{:S(2)}) collective-permute-start(s32[4,64]{1,0:T(4,128)S(1)} %copy-done.8), channel_id=1, source_target_pairs={{0,10},{1,11},{2,8},{3,9},{4,14},{5,15},{6,12},{7,13},{8,2},{9,3},... | collective-permute-start | bytes 3080 | tf_op jit(solution)/shard_map/ppermute | solution.py:261
  27.2 28.1 %copy-start.10 = (s32[4,64]{1,0:T(4,128)}, s32[4,64]{1,0:T(4,128)S(1)}, u32[]{:S(2)}) copy-start(s32[4,64]{1,0:T(4,128)S(1)} %collective-permute-done.4.refs_9_) | copy-start | bytes 3076
  27.2 4.5 %collective-permute-start.3 = (s32[4,64]{1,0:T(4,128)S(1)}, s32[4,64]{1,0:T(4,128)S(1)}, u32[]{:S(2)}, u32[]{:S(2)}) collective-permute-start(s32[4,64]{1,0:T(4,128)S(1)} %copy-done.8), channel_id=1, source_target_pairs={{0,8},{1,9},{2,10},{3,11},{4,12},{5,13},{6,14},{7,15},{8,0},{9,1},... | collective-permute-start | bytes 3080 | tf_op jit(solution)/shard_map/ppermute | solution.py:261
  31.7 23.6 %copy-start.11 = (s32[4,64]{1,0:T(4,128)}, s32[4,64]{1,0:T(4,128)S(1)}, u32[]{:S(2)}) copy-start(s32[4,64]{1,0:T(4,128)S(1)} %collective-permute-done.3.refs_8_) | copy-start | bytes 3076
  31.7 4.5 %collective-permute-start.2 = (s32[4,64]{1,0:T(4,128)S(1)}, s32[4,64]{1,0:T(4,128)S(1)}, u32[]{:S(2)}, u32[]{:S(2)}) collective-permute-start(s32[4,64]{1,0:T(4,128)S(1)} %copy-done.8), channel_id=1, source_target_pairs={{0,6},{1,7},{2,4},{3,5},{4,2},{5,3},{6,0},{7,1},{8,14},{9,15},{10,... | collective-permute-start | bytes 3080 | tf_op jit(solution)/shard_map/ppermute | solution.py:261
  36.2 19.1 %copy-start.12 = (s32[4,64]{1,0:T(4,128)}, s32[4,64]{1,0:T(4,128)S(1)}, u32[]{:S(2)}) copy-start(s32[4,64]{1,0:T(4,128)S(1)} %collective-permute-done.2.refs_7_) | copy-start | bytes 3076
  36.2 3.6 %collective-permute-start.1 = (s32[4,64]{1,0:T(4,128)S(1)}, s32[4,64]{1,0:T(4,128)S(1)}, u32[]{:S(2)}, u32[]{:S(2)}) collective-permute-start(s32[4,64]{1,0:T(4,128)S(1)} %copy-done.8), channel_id=1, source_target_pairs={{0,4},{1,5},{2,6},{3,7},{4,0},{5,1},{6,2},{7,3},{8,12},{9,13},{10,... | collective-permute-start | bytes 3080 | tf_op jit(solution)/shard_map/ppermute | solution.py:261
  39.8 15.5 %copy-start.13 = (s32[4,64]{1,0:T(4,128)}, s32[4,64]{1,0:T(4,128)S(1)}, u32[]{:S(2)}) copy-start(s32[4,64]{1,0:T(4,128)S(1)} %collective-permute-done.1.refs_6_) | copy-start | bytes 3076
  39.8 3.6 %collective-permute-start = (s32[4,64]{1,0:T(4,128)S(1)}, s32[4,64]{1,0:T(4,128)S(1)}, u32[]{:S(2)}, u32[]{:S(2)}) collective-permute-start(s32[4,64]{1,0:T(4,128)S(1)} %copy-done.8), channel_id=1, source_target_pairs={{0,2},{1,3},{2,0},{3,1},{4,6},{5,7},{6,4},{7,5},{8,10},{9,11},{10,... | collective-permute-start | bytes 3080 | tf_op jit(solution)/shard_map/ppermute | solution.py:261
  43.4 12.0 %copy-start.14 = (s32[4,64]{1,0:T(4,128)}, s32[4,64]{1,0:T(4,128)S(1)}, u32[]{:S(2)}) copy-start(s32[4,64]{1,0:T(4,128)S(1)} %collective-permute-done.refs_5_) | copy-start | bytes 3076
  43.4 6.3 %collective-permute-start.6 = (s32[4,64]{1,0:T(4,128)S(1)}, s32[4,64]{1,0:T(4,128)S(1)}, u32[]{:S(2)}, u32[]{:S(2)}) collective-permute-start(s32[4,64]{1,0:T(4,128)S(1)} %copy-done.8), channel_id=1, source_target_pairs={{0,14},{1,15},{2,12},{3,13},{4,10},{5,11},{6,8},{7,9},{8,6},{9,7},... | collective-permute-start | bytes 3080 | tf_op jit(solution)/shard_map/ppermute | solution.py:261
  49.7 5.7 %copy-start.15 = (s32[4,64]{1,0:T(4,128)}, s32[4,64]{1,0:T(4,128)S(1)}, u32[]{:S(2)}) copy-start(s32[4,64]{1,0:T(4,128)S(1)} %collective-permute-done.6.refs_11_) | copy-start | bytes 3076
  49.7 8.1 %collective-permute-start.12 = (bf16[128,128]{1,0:T(8,128)(2,1)}, bf16[128,128]{1,0:T(8,128)(2,1)S(1)}, u32[]{:S(2)}, u32[]{:S(2)}) collective-permute-start(bf16[128,128]{1,0:T(8,128)(2,1)} %encode.1.refs_12_.refs_5_), channel_id=1, source_target_pairs={{0,8},{1,9},{2,10},{3,11},{4,12},{5,13},{6,14},{7,15},{8,0},{9,1},... | collective-permute-start | bytes 98312 | tf_op jit(solution)/shard_map/ppermute | solution.py:261
  49.7 8.2 %copy-start.1 = (bf16[128,128]{1,0:T(8,128)(2,1)}, bf16[128,128]{1,0:T(8,128)(2,1)S(1)}, u32[]{:S(2)}) copy-start(bf16[128,128]{1,0:T(8,128)(2,1)S(1)} %collective-permute-done.15.refs_12_) | copy-start | bytes 98308
  49.7 8.1 %collective-permute-start.11 = (bf16[128,128]{1,0:T(8,128)(2,1)}, bf16[128,128]{1,0:T(8,128)(2,1)S(1)}, u32[]{:S(2)}, u32[]{:S(2)}) collective-permute-start(bf16[128,128]{1,0:T(8,128)(2,1)} %encode.1.refs_12_.refs_5_), channel_id=1, source_target_pairs={{0,6},{1,7},{2,4},{3,5},{4,2},{5,3},{6,0},{7,1},{8,14},{9,15},{10,... | collective-permute-start | bytes 98312 | tf_op jit(solution)/shard_map/ppermute | solution.py:261
  53.1 4.8 %copy-start.2 = (bf16[128,128]{1,0:T(8,128)(2,1)}, bf16[128,128]{1,0:T(8,128)(2,1)S(1)}, u32[]{:S(2)}) copy-start(bf16[128,128]{1,0:T(8,128)(2,1)S(1)} %collective-permute-done.14.refs_11_) | copy-start | bytes 98308
  53.1 4.7 %collective-permute-start.10 = (bf16[128,128]{1,0:T(8,128)(2,1)}, bf16[128,128]{1,0:T(8,128)(2,1)S(1)}, u32[]{:S(2)}, u32[]{:S(2)}) collective-permute-start(bf16[128,128]{1,0:T(8,128)(2,1)} %encode.1.refs_12_.refs_5_), channel_id=1, source_target_pairs={{0,4},{1,5},{2,6},{3,7},{4,0},{5,1},{6,2},{7,3},{8,12},{9,13},{10,... | collective-permute-start | bytes 98312 | tf_op jit(solution)/shard_map/ppermute | solution.py:261
  53.2 4.7 %copy-start.3 = (bf16[128,128]{1,0:T(8,128)(2,1)}, bf16[128,128]{1,0:T(8,128)(2,1)S(1)}, u32[]{:S(2)}) copy-start(bf16[128,128]{1,0:T(8,128)(2,1)S(1)} %collective-permute-done.13.refs_10_) | copy-start | bytes 98308
  53.2 4.6 %collective-permute-start.9 = (bf16[128,128]{1,0:T(8,128)(2,1)}, bf16[128,128]{1,0:T(8,128)(2,1)S(1)}, u32[]{:S(2)}, u32[]{:S(2)}) collective-permute-start(bf16[128,128]{1,0:T(8,128)(2,1)} %encode.1.refs_12_.refs_5_), channel_id=1, source_target_pairs={{0,2},{1,3},{2,0},{3,1},{4,6},{5,7},{6,4},{7,5},{8,10},{9,11},{10,... | collective-permute-start | bytes 98312 | tf_op jit(solution)/shard_map/ppermute | solution.py:261
  57.8 0.6 copy-start.4
  57.8 0.6 copy-start.5
  57.8 0.6 copy-start.6
  57.8 0.6 copy-start.7
  57.8 1.2 %copy-start = (bf16[48,128,128]{2,1,0:T(8,128)(2,1)}, bf16[48,128,128]{2,1,0:T(8,128)(2,1)S(1)}, u32[]{:S(2)}) copy-start(bf16[48,128,128]{2,1,0:T(8,128)(2,1)S(1)} %collective-permute-done.8.refs_4_) | copy-start | bytes 4718596
  65.6 6.9 %collective-permute-start.16 = (f32[1,128]{1,0:T(1,128)}, f32[1,128]{1,0:T(1,128)S(1)}, u32[]{:S(2)}, u32[]{:S(2)}) collective-permute-start(f32[1,128]{1,0:T(1,128)} %get-tuple-element.15), channel_id=1, source_target_pairs={{0,2},{1,3},{2,0},{3,1},{4,6},{5,7},{6,4},{7,5},{8,10},{9,11},{10,... | collective-permute-start | bytes 1544 | tf_op jit(solution)/shard_map/ppermute | solution.py:261
  66.6 7.4 %collective-permute-start.17 = (f32[1,128]{1,0:T(1,128)}, f32[1,128]{1,0:T(1,128)S(1)}, u32[]{:S(2)}, u32[]{:S(2)}) collective-permute-start(f32[1,128]{1,0:T(1,128)} %get-tuple-element.16), channel_id=1, source_target_pairs={{0,4},{1,5},{2,6},{3,7},{4,0},{5,1},{6,2},{7,3},{8,12},{9,13},{10,... | collective-permute-start | bytes 1544 | tf_op jit(solution)/shard_map/ppermute | solution.py:261
  68.6 8.2 %collective-permute-start.18 = (f32[1,128]{1,0:T(1,128)}, f32[1,128]{1,0:T(1,128)S(1)}, u32[]{:S(2)}, u32[]{:S(2)}) collective-permute-start(f32[1,128]{1,0:T(1,128)} %get-tuple-element.17), channel_id=1, source_target_pairs={{0,6},{1,7},{2,4},{3,5},{4,2},{5,3},{6,0},{7,1},{8,14},{9,15},{10,... | collective-permute-start | bytes 1544 | tf_op jit(solution)/shard_map/ppermute | solution.py:261
  69.1 7.7 %collective-permute-start.19 = (f32[1,128]{1,0:T(1,128)}, f32[1,128]{1,0:T(1,128)S(1)}, u32[]{:S(2)}, u32[]{:S(2)}) collective-permute-start(f32[1,128]{1,0:T(1,128)} %get-tuple-element.18), channel_id=1, source_target_pairs={{0,8},{1,9},{2,10},{3,11},{4,12},{5,13},{6,14},{7,15},{8,0},{9,1},... | collective-permute-start | bytes 1544 | tf_op jit(solution)/shard_map/ppermute | solution.py:261
  71.0 5.8 %collective-permute-start.20 = (f32[1,128]{1,0:T(1,128)}, f32[1,128]{1,0:T(1,128)S(1)}, u32[]{:S(2)}, u32[]{:S(2)}) collective-permute-start(f32[1,128]{1,0:T(1,128)} %get-tuple-element.19), channel_id=1, source_target_pairs={{0,10},{1,11},{2,8},{3,9},{4,14},{5,15},{6,12},{7,13},{8,2},{9,3},... | collective-permute-start | bytes 1544 | tf_op jit(solution)/shard_map/ppermute | solution.py:261
  72.5 8.0 %copy-start.18 = (f32[1,128]{1,0:T(1,128)}, f32[1,128]{1,0:T(1,128)S(1)}, u32[]{:S(2)}) copy-start(f32[1,128]{1,0:T(1,128)S(1)} %collective-permute-done.16.refs_3_) | copy-start | bytes 1540
  72.5 5.4 %collective-permute-start.21 = (f32[1,128]{1,0:T(1,128)}, f32[1,128]{1,0:T(1,128)S(1)}, u32[]{:S(2)}, u32[]{:S(2)}) collective-permute-start(f32[1,128]{1,0:T(1,128)} %get-tuple-element.20), channel_id=1, source_target_pairs={{0,12},{1,13},{2,14},{3,15},{4,8},{5,9},{6,10},{7,11},{8,4},{9,5},... | collective-permute-start | bytes 1544 | tf_op jit(solution)/shard_map/ppermute | solution.py:261
  74.0 6.5 %copy-start.19 = (f32[1,128]{1,0:T(1,128)}, f32[1,128]{1,0:T(1,128)S(1)}, u32[]{:S(2)}) copy-start(f32[1,128]{1,0:T(1,128)S(1)} %collective-permute-done.17.refs_4_) | copy-start | bytes 1540
  74.0 6.4 %collective-permute-start.22 = (f32[1,128]{1,0:T(1,128)}, f32[1,128]{1,0:T(1,128)S(1)}, u32[]{:S(2)}, u32[]{:S(2)}) collective-permute-start(f32[1,128]{1,0:T(1,128)} %get-tuple-element.21), channel_id=1, source_target_pairs={{0,14},{1,15},{2,12},{3,13},{4,10},{5,11},{6,8},{7,9},{8,6},{9,7},... | collective-permute-start | bytes 1544 | tf_op jit(solution)/shard_map/ppermute | solution.py:261
  76.8 3.6 %copy-start.20 = (f32[1,128]{1,0:T(1,128)}, f32[1,128]{1,0:T(1,128)S(1)}, u32[]{:S(2)}) copy-start(f32[1,128]{1,0:T(1,128)S(1)} %collective-permute-done.18.refs_5_) | copy-start | bytes 1540
  76.8 3.6 %copy-start.21 = (f32[1,128]{1,0:T(1,128)}, f32[1,128]{1,0:T(1,128)S(1)}, u32[]{:S(2)}) copy-start(f32[1,128]{1,0:T(1,128)S(1)} %collective-permute-done.19.refs_6_) | copy-start | bytes 1540
  76.8 3.6 %copy-start.22 = (f32[1,128]{1,0:T(1,128)}, f32[1,128]{1,0:T(1,128)S(1)}, u32[]{:S(2)}) copy-start(f32[1,128]{1,0:T(1,128)S(1)} %collective-permute-done.20.refs_7_) | copy-start | bytes 1540
  77.9 2.6 %copy-start.23 = (f32[1,128]{1,0:T(1,128)}, f32[1,128]{1,0:T(1,128)S(1)}, u32[]{:S(2)}) copy-start(f32[1,128]{1,0:T(1,128)S(1)} %collective-permute-done.21.refs_8_) | copy-start | bytes 1540
  80.4 0.6 copy-start.24

commit v3 on v2

v3 whole, which is shorter than its diff:
```python
import jax
import jax.numpy as jnp
from jax import lax
from jax.experimental import pallas as pl
from jax.experimental.pallas import tpu as pltpu
from jax.sharding import PartitionSpec as P

TOPN = 10
F32 = jnp.float32
BF16 = jnp.bfloat16
NT = (((1,), (1,)), ((), ()))
VMEM = pl.BlockSpec(memory_space=pltpu.VMEM)
SMEM = pl.BlockSpec(memory_space=pltpu.SMEM)
ANY = pl.BlockSpec(memory_space=pl.ANY)


def split3(value):
    high = value.astype(BF16)
    rest = value - high.astype(F32)
    middle = rest.astype(BF16)
    low = (rest - middle.astype(F32)).astype(BF16)
    return high, middle, low


def encode_kernel(
    inverse,
    lens_ref,
    me_ref,
    row_ref,
    cand_ref,
    plen_ref,
    x_ref,
    w1_ref,
    w2_ref,
    gain_ref,
    embed_ref,
    pass_ref,
    out_ref,
    masked_ref,
    spot_ref,
    w1_buf,
    w2_buf,
    pass_buf,
    table,
    table_v,
    sems,
    pass_sem,
    table_sem,
):
    chunks, _, width = w1_buf.shape
    half, plen, _ = pass_buf.shape
    slots, lanes = table_v.shape
    query_count, token_count, width_in = x_ref.shape
    cand_count = cand_ref.shape[1]
    table_v[...] = jnp.zeros(table_v.shape, jnp.int32)
    clear = pltpu.make_async_copy(table_v, table, table_sem)
    clear.start()
    copies = []
    for c in range(chunks):
        first = pltpu.make_async_copy(w1_ref.at[:, pl.ds(c * width, width)], w1_buf.at[c], sems.at[0, c])
        second = pltpu.make_async_copy(w2_ref.at[pl.ds(c * width, width), :], w2_buf.at[c], sems.at[1, c])
        first.start()
        second.start()
        copies.append((first, second))
    load = pltpu.make_async_copy(pass_ref, pass_buf, pass_sem)
    load.start()
    clear.wait()

    side = jnp.bitwise_and(me_ref[0], 1)

    def enter(k, carry):
        for i in range(query_count):
            row = row_ref[cand_ref[i, k]]
            owner = inverse(row)
            chip = jnp.right_shift(owner, 1)
            place = row - owner * half + jnp.bitwise_xor(jnp.bitwise_and(owner, 1), side) * half
            table[chip, place] = i
            spot_ref[i, k] = chip * lanes + place
        return carry

    lax.fori_loop(0, cand_count, enter, 0, unroll=4)
    fetch = pltpu.make_async_copy(table, table_v, table_sem)
    fetch.start()

    x = x_ref[...].reshape(query_count * token_count, width_in)
    total = x.astype(F32)
    copies[0][0].wait()
    inner = jnp.dot(x, w1_buf[0], preferred_element_type=F32)
    for c in range(chunks):
        copies[c][1].wait()
        if c + 1 < chunks:
            copies[c + 1][0].wait()
            later = jnp.dot(x, w1_buf[c + 1], preferred_element_type=F32)
        active = (0.5 * inner * (1.0 + lax.erf(inner * (0.5 ** 0.5)))).astype(BF16)
        total = total + jnp.dot(active, w2_buf[c], preferred_element_type=F32)
        if c + 1 < chunks:
            inner = later

    load.wait()

    def mask(p, carry):
        block = pass_buf[p]
        keep = lax.broadcasted_iota(jnp.int32, block.shape, 0) < plen_ref[p]
        block = block.astype(F32)
        pass_buf[p] = jnp.where(keep, block, jnp.broadcast_to(block[0:1], block.shape)).astype(BF16)
        return carry

    lax.fori_loop(0, half, mask, 0, unroll=4)
    save = pltpu.make_async_copy(pass_buf, masked_ref, pass_sem)
    save.start()

    centered = total - jnp.mean(total, axis=-1, keepdims=True)
    variance = jnp.mean(jnp.square(centered), axis=-1, keepdims=True)
    layer_out = (centered * lax.rsqrt(variance + 1e-12) * gain_ref[...]).astype(BF16)
    embedded = jnp.dot(layer_out, embed_ref[...], preferred_element_type=F32)
    length = jnp.sum(jnp.square(embedded), axis=-1, keepdims=True)
    vectors = embedded * lax.rsqrt(length + 1e-06)
    token = lax.broadcasted_iota(jnp.int32, vectors.shape, 0)
    for i in range(query_count):
        padded = (token >= i * token_count + lens_ref[i]) & (token < (i + 1) * token_count)
        vectors = jnp.where(padded, 0.0, vectors)
    vectors = vectors.astype(BF16)
    fetch.wait()
    tokens = query_count * token_count
    tail = out_ref.shape[1] - tokens
    for s in range(slots):
        out_ref[s, pl.ds(0, tokens), :] = vectors
        out_ref[s, pl.ds(tokens, tail), :] = jnp.broadcast_to(
            table_v[s:s + 1, :].astype(F32), (tail, lanes)
        ).astype(BF16)
    save.wait()


def divider(divisor, limit):
    magic = -(-(2 ** 20) // divisor)
    if limit * magic < 2 ** 31 and all((v * magic) >> 20 == v // divisor for v in range(limit)):
        return lambda value: jnp.right_shift(value * magic, 20)
    return lambda value: value // divisor


def encode(
    me,
    query_hidden,
    query_lengths,
    inner_weight,
    outer_weight,
    norm_gain,
    embed_weight,
    passage_vectors,
    passage_lengths,
    passage_row,
    candidates,
    slots,
):
    query_count, token_count, d = query_hidden.shape
    ff = inner_weight.shape[1]
    e = embed_weight.shape[1]
    half = passage_vectors.shape[0]
    assert 2 * half <= e
    chunks = 6
    width = ff // chunks
    tokens = query_count * token_count
    inverse = divider(half, passage_row.shape[0])

    def kernel(*refs):
        encode_kernel(inverse, *refs)

    return pl.pallas_call(
        kernel,
        out_shape=(
            jax.ShapeDtypeStruct((slots, tokens + 16, e), BF16),
            jax.ShapeDtypeStruct(passage_vectors.shape, BF16),
            jax.ShapeDtypeStruct(candidates.shape, jnp.int32),
        ),
        in_specs=[SMEM] * 5 + [VMEM, ANY, ANY, VMEM, VMEM, ANY],
        out_specs=(VMEM, ANY, SMEM),
        scratch_shapes=[
            pltpu.VMEM((chunks, d, width), BF16),
            pltpu.VMEM((chunks, width, d), BF16),
            pltpu.VMEM(passage_vectors.shape, BF16),
            pltpu.SMEM((slots, e), jnp.int32),
            pltpu.VMEM((slots, e), jnp.int32),
            pltpu.SemaphoreType.DMA((2, chunks)),
            pltpu.SemaphoreType.DMA,
            pltpu.SemaphoreType.DMA,
        ],
        compiler_params=pltpu.CompilerParams(vmem_limit_bytes=56 * 2 ** 20),
        cost_estimate=pl.CostEstimate(
            flops=4 * tokens * d * ff, bytes_accessed=4 * d * ff, transcendentals=tokens * ff
        ),
        name="encode",
    )(
        query_lengths,
        me,
        passage_row,
        candidates,
        passage_lengths,
        query_hidden,
        inner_weight,
        outer_weight,
        norm_gain.reshape(1, d),
        embed_weight,
        passage_vectors,
    )


def score_kernel(token_count, got_ref, pass0_ref, pass1_ref, out_ref, best_ref, index_v, index, sem):
    slots, message, lanes = got_ref.shape
    half = pass0_ref.shape[0]
    tokens = message - 16
    group = min(slots, 256 // token_count)
    for s in range(slots):
        index_v[s:s + 1, :] = got_ref[s, pl.ds(tokens, 16), :].astype(F32)[0:1].astype(jnp.int32) * token_count
    copy = pltpu.make_async_copy(index_v, index, sem)
    copy.start()
    copy.wait()

    for side, pass_ref in enumerate((pass0_ref, pass1_ref)):

        def eight(step, carry):
            for part in range(slots // group):
                rows = []
                for j in range(8):
                    p = step * 8 + j
                    picked = jnp.concatenate(
                        [
                            got_ref[s, pl.ds(pl.multiple_of(index[s, side * half + p], token_count), token_count), :]
                            for s in range(part * group, (part + 1) * group)
                        ],
                        axis=0,
                    )
                    similar = lax.dot_general(pass_ref[p], picked, NT, preferred_element_type=F32)
                    rows.append(jnp.max(similar, axis=0, keepdims=True))
                best_ref[
                    pl.ds(pl.multiple_of(side * half + step * 8, 8), 8),
                    pl.ds(part * group * token_count, group * token_count),
                ] = jnp.concatenate(rows, axis=0)
            return carry

        lax.fori_loop(0, half // 8, eight, 0)
    wide = best_ref.shape[1]
    source = lax.broadcasted_iota(jnp.int32, (slots, wide), 0)
    column = lax.broadcasted_iota(jnp.int32, (slots, wide), 1)
    first = source * token_count
    ones = jnp.where((column >= first) & (column < first + token_count), 1.0, 0.0).astype(BF16)
    total = sum(lax.dot_general(ones, part, NT, preferred_element_type=F32) for part in split3(best_ref[...]))
    out_ref[...] = jnp.zeros(out_ref.shape, F32)
    out_ref[:, pl.ds(0, 2 * half)] = total


def score(got, own, other, token_count):
    half, plen, e = own.shape
    slots = got.shape[0]

    def kernel(*refs):
        score_kernel(token_count, *refs)

    return pl.pallas_call(
        kernel,
        out_shape=jax.ShapeDtypeStruct((slots, e), F32),
        in_specs=[VMEM] * 3,
        out_specs=VMEM,
        scratch_shapes=[
            pltpu.VMEM((2 * half, slots * token_count), F32),
            pltpu.VMEM((slots, e), jnp.int32),
            pltpu.SMEM((slots, e), jnp.int32),
            pltpu.SemaphoreType.DMA,
        ],
        cost_estimate=pl.CostEstimate(
            flops=4 * half * slots * token_count * plen * e, bytes_accessed=4 * own.size, transcendentals=0
        ),
        name="score",
    )(got, own, other)


def finish_kernel(got_ref, spot_ref, scores_ref, best_ref):
    slots, lanes = got_ref.shape
    query_count, cand_count = scores_ref.shape
    parts = split3(got_ref[...])
    slot_iota = lax.broadcasted_iota(jnp.int32, (slots, cand_count), 0) * lanes
    lane_iota = lax.broadcasted_iota(jnp.int32, (lanes, cand_count), 0)
    row_iota = lax.broadcasted_iota(jnp.int32, (cand_count, cand_count), 0)
    col_iota = lax.broadcasted_iota(jnp.int32, (cand_count, cand_count), 1)
    place = lax.broadcasted_iota(jnp.int32, (cand_count, 128), 1)
    for i in range(query_count):
        spot = spot_ref[i:i + 1, :]
        lane = jnp.bitwise_and(spot, lanes - 1)
        onehot = jnp.where(lane_iota == lane, 1.0, 0.0).astype(BF16)
        picked = sum(jnp.dot(part, onehot, preferred_element_type=F32) for part in parts)
        score_row = jnp.sum(jnp.where(slot_iota == spot - lane, picked, 0.0), axis=0, keepdims=True)
        scores_ref[i:i + 1, :] = score_row
        across = jnp.broadcast_to(score_row, (cand_count, cand_count))
        score_col = jnp.sum(jnp.where(row_iota == col_iota, across, 0.0), axis=1, keepdims=True)
        ahead = (across > score_col) | ((across == score_col) & (col_iota < row_iota))
        rank = jnp.sum(jnp.where(ahead, 1.0, 0.0), axis=1, keepdims=True).astype(jnp.int32)
        ordered = jnp.sum(jnp.where(rank == place, score_col, 0.0), axis=0, keepdims=True)
        best_ref[i:i + 1, :] = ordered[:, :TOPN]


def finish(got, spots):
    return pl.pallas_call(
        finish_kernel,
        out_shape=(
            jax.ShapeDtypeStruct(spots.shape, F32),
            jax.ShapeDtypeStruct((spots.shape[0], TOPN), F32),
        ),
        in_specs=[VMEM, VMEM],
        out_specs=(VMEM, VMEM),
        name="finish",
    )(got, spots)


def per_device(
    query_hidden,
    query_lengths,
    inner_weight,
    outer_weight,
    norm_gain,
    embed_weight,
    passage_vectors,
    passage_lengths,
    passage_row,
    candidates,
):
    size = lax.axis_size("shard")
    slots = size // 2
    groups = [list(range(core, size, 2)) for core in range(2)]
    me = lax.axis_index("shard").astype(jnp.int32).reshape(1)
    message, own, spots = encode(
        me,
        query_hidden,
        query_lengths,
        inner_weight,
        outer_weight,
        norm_gain,
        embed_weight,
        passage_vectors,
        passage_lengths,
        passage_row,
        candidates,
        slots,
    )
    other = lax.ppermute(own, "shard", [(i, i ^ 1) for i in range(size)])
    got = lax.all_to_all(message, "shard", split_axis=0, concat_axis=0, axis_index_groups=groups, tiled=True)
    sums = score(got, own, other, query_hidden.shape[1])
    back = lax.all_to_all(sums, "shard", split_axis=0, concat_axis=0, axis_index_groups=groups, tiled=True)
    return finish(back, spots)


def solution(mesh):
    in_specs = (
        P(("groups", "shard"), None, None),
        P(("groups", "shard")),
        P(),
        P(),
        P(),
        P(),
        P(("groups", "shard"), None, None),
        P(("groups", "shard")),
        P("groups"),
        P(("groups", "shard"), None),
    )
    out_specs = (P(("groups", "shard"), None), P(("groups", "shard"), None))
    return jax.shard_map(
        per_device, mesh=mesh, in_specs=in_specs, out_specs=out_specs, check_vma=False
    )
```

time: 83.1 us -> 49.4 us (0.59)
  starting transfers between devices: 37.6 us -> 0.51 us
  blocking collectives: 0 us -> 28.3 us
  waiting for transfers between devices: 23.6 us -> 0.01 us
    ppermute x23 -> x1, starting transfers between devices: 37.6 us -> 0.51 us  [per_device(): other = lax.ppermute(own, 'shard', [(i, i ^ 1) for i in range(size)])]
    all_to_all x0 -> x2, blocking collectives: none -> 28.3 us  [the longest x1 17.9 us: per_device(): lax.all_to_all(message, 'shard', split_axis=0, concat_axis=0, axis_index_...]
    ppermute x23 -> x1, waiting for transfers between devices: 23.6 us -> 0.01 us  [per_device(): other = lax.ppermute(own, 'shard', [(i, i ^ 1) for i in range(size)])]
    unnamed x50 -> x2, local copies, waits for them, and re-layouts: 1.75 us -> 1.16 us
    pallas_call x4 -> x3, Pallas kernels: 17.1 us -> 17.2 us  [the longest x1 8.25 us: encode(): pl.pallas_call(kernel, out_shape=(jax.ShapeDtypeStruct((slots, tokens + 1...]
  transfers between devices with their start and end apart: 23 -> 1, of which waited for: 10 -> 0; matrix products, arithmetic and copies ran while one was open for 2% -> 0% of each run, Pallas kernels for 11% -> 0%
where the time goes in v3:
time: 49.4 us; the launch traced here: 49.1 us
  blocking collectives  28.3 us (57%)
  Pallas kernels  17.2 us (35%)
  local copies, waits for them, and re-layouts  2.44 us (5%)
  between operations  0.65 us (1%)
  starting transfers between devices  0.51 us (1%)
    all_to_all x1, blocking collectives, per_device(): lax.all_to_all(message, 'shard', split_axis=0, concat_axis=0, axis_index_...  17.9 us
    all_to_all x1, blocking collectives, per_device(): lax.all_to_all(sums, 'shard', split_axis=0, concat_axis=0, axis_index_gro...  10.4 us
    pallas_call x1, Pallas kernels, encode(): pl.pallas_call(kernel, out_shape=(jax.ShapeDtypeStruct((slots, tokens + 1...  8.25 us
    pallas_call x1, Pallas kernels, score(): pl.pallas_call(kernel, out_shape=jax.ShapeDtypeStruct((slots, e), F32), i...  7.24 us
    pallas_call x1, Pallas kernels, finish(): pl.pallas_call(finish_kernel, out_shape=(jax.ShapeDtypeStruct(spots.shape...  1.67 us
    reshape x1, local copies, waits for them, and re-layouts, encode(): norm_gain.reshape(1, d)  1.28 us
    unnamed x2, local copies, waits for them, and re-layouts  1.16 us
  transfers between devices with their start and end apart: 1, of which 0 were waited for; matrix products, arithmetic and copies ran while one was open for 0% of the time, Pallas kernels for 0%

profile of v3, /device:TPU:0, one launch (start us, length us, event | category | flops | bytes accessed | tf_op | source)
XLA Modules:
  0.0 49.1 jit_solution(6764423179749714314)
XLA Ops:
  0.6 1.3 %reshape.13.refs_8_ = f32[1,768]{1,0:T(1,128)} reshape(f32[768]{0:T(1024)} %param.14) | data formatting | bytes 6144 | tf_op jit(solution)/shard_map/reshape | solution.py:201
  1.9 8.3 %encode.1 = (bf16[8,144,128]{2,1,0:T(8,128)(2,1)}, bf16[48,128,128]{2,1,0:T(8,128)(2,1)}, s32[4,64]{1,0:T(4,128)}) custom-call(s32[4]{0:T(128)} %refs_0_.1, s32[1]{0:T(128)} %bitcast.refs_1_, s32[768]{0:T(1024)} %refs_2_.1, s32[4,64]{1,0:T(4,128)} %refs_3_.1, s32[48]{0:T(128)} %refs_4_.1, bf16[4,32,768]{2,1,0:T(8,128)(2,1)} %refs_5_.1, ...), custom_call_target="tpu_custom_call" | custom-call | flops 1207959552 | bytes 9437184 | tf_op jit(solution)/shard_map/encode/pallas_call | solution.py:168
  10.2 0.5 %collective-permute-start = (bf16[48,128,128]{2,1,0:T(8,128)(2,1)}, bf16[48,128,128]{2,1,0:T(8,128)(2,1)S(1)}, u32[]{:S(2)}, u32[]{:S(2)}) collective-permute-start(bf16[48,128,128]{2,1,0:T(8,128)(2,1)} %get-tuple-element.6.refs_1_), channel_id=1, source_target_pairs={{0,1},{1,0},{2,3},{3,2},{4,5},{5,4},{6,7},{7,6},{8,9},{9,8},{10,11... | collective-permute-start | bytes 4718600 | tf_op jit(solution)/shard_map/ppermute | solution.py:343
  10.7 17.9 %all_to_all.16.refs_0_ = bf16[8,144,128]{2,1,0:T(8,128)(2,1)} all-to-all(bf16[8,144,128]{2,1,0:T(8,128)(2,1)} %get-tuple-element.5), channel_id=1, replica_groups={{0,2,4,6,8,10,12,14},{1,3,5,7,9,11,13,15},{16,18,20,22,24,26,28,30},{17..., dimensions={0} | all-to-all | bytes 589824 | tf_op jit(solution)/shard_map/all_to_all | solution.py:344
  28.6 0.0 collective-permute-done.refs_2_
  28.6 0.0 copy-start
  28.6 1.2 %copy-done = bf16[48,128,128]{2,1,0:T(8,128)(2,1)} copy-done((bf16[48,128,128]{2,1,0:T(8,128)(2,1)}, bf16[48,128,128]{2,1,0:T(8,128)(2,1)S(1)}, u32[]{:S(2)}) %copy-start) | copy-done | bytes 1572888
  29.8 7.2 %score.1 = f32[8,128]{1,0:T(8,128)} custom-call(bf16[8,144,128]{2,1,0:T(8,128)(2,1)} %all_to_all.16.refs_0_, bf16[48,128,128]{2,1,0:T(8,128)(2,1)} %get-tuple-element.6.refs_1_, bf16[48,128,128]{2,1,0:T(8,128)(2,1)} %copy-done), custom_call_target="tpu_custom_call" | custom-call | flops 805306368 | bytes 3145728 | tf_op jit(solution)/shard_map/score/pallas_call | solution.py:258
  37.0 10.4 %all_to_all.17 = f32[8,1,128]{2,1,0:T(1,128)} all-to-all(f32[8,1,128]{2,1,0:T(1,128)} %bitcast.5), channel_id=1, replica_groups={{0,2,4,6,8,10,12,14},{1,3,5,7,9,11,13,15},{16,18,20,22,24,26,28,30},{17..., dimensions={0} | all-to-all | bytes 8192 | tf_op jit(solution)/shard_map/all_to_all | solution.py:346
  47.4 1.7 %finish.1 = (f32[4,64]{1,0:T(4,128)}, f32[4,10]{1,0:T(4,128)}) custom-call(f32[8,128]{1,0:T(8,128)} %bitcast.6, s32[4,64]{1,0:T(4,128)} %get-tuple-element.7.spot_ref), custom_call_target="tpu_custom_call" | custom-call | tf_op jit(solution)/shard_map/finish/pallas_call | solution.py:301
Async XLA Ops:
  10.2 18.5 %collective-permute-start = (bf16[48,128,128]{2,1,0:T(8,128)(2,1)}, bf16[48,128,128]{2,1,0:T(8,128)(2,1)S(1)}, u32[]{:S(2)}, u32[]{:S(2)}) collective-permute-start(bf16[48,128,128]{2,1,0:T(8,128)(2,1)} %get-tuple-element.6.refs_1_), channel_id=1, source_target_pairs={{0,1},{1,0},{2,3},{3,2},{4,5},{5,4},{6,7},{7,6},{8,9},{9,8},{10,11... | collective-permute-start | bytes 4718600 | tf_op jit(solution)/shard_map/ppermute | solution.py:343
  28.6 1.2 %copy-start = (bf16[48,128,128]{2,1,0:T(8,128)(2,1)}, bf16[48,128,128]{2,1,0:T(8,128)(2,1)S(1)}, u32[]{:S(2)}) copy-start(bf16[48,128,128]{2,1,0:T(8,128)(2,1)S(1)} %collective-permute-done.refs_2_) | copy-start | bytes 4718596

commit v4 on v3

--- a/solution.py
+++ b/solution.py
@@ -24,31 +24,33 @@
 
 def encode_kernel(
     inverse,
-    lens_ref,
+    half,
     me_ref,
-    row_ref,
-    cand_ref,
-    plen_ref,
-    x_ref,
+    lens_hbm,
+    row_hbm,
+    cand_hbm,
+    x_hbm,
     w1_ref,
     w2_ref,
-    gain_ref,
-    embed_ref,
-    pass_ref,
+    gain_hbm,
+    embed_hbm,
     out_ref,
-    masked_ref,
     spot_ref,
     w1_buf,
     w2_buf,
-    pass_buf,
+    lens_ref,
+    row_ref,
+    cand_ref,
+    x_ref,
+    gain_ref,
+    embed_ref,
     table,
     table_v,
     sems,
-    pass_sem,
+    small_sems,
     table_sem,
 ):
     chunks, _, width = w1_buf.shape
-    half, plen, _ = pass_buf.shape
     slots, lanes = table_v.shape
     query_count, token_count, width_in = x_ref.shape
     cand_count = cand_ref.shape[1]
@@ -59,12 +61,31 @@
     for c in range(chunks):
         first = pltpu.make_async_copy(w1_ref.at[:, pl.ds(c * width, width)], w1_buf.at[c], sems.at[0, c])
         second = pltpu.make_async_copy(w2_ref.at[pl.ds(c * width, width), :], w2_buf.at[c], sems.at[1, c])
+        copies.append((first, second))
+    small = [
+        pltpu.make_async_copy(source, target, small_sems.at[n])
+        for n, (source, target) in enumerate(
+            (
+                (row_hbm, row_ref),
+                (cand_hbm, cand_ref),
+                (x_hbm, x_ref),
+                (lens_hbm, lens_ref),
+                (gain_hbm, gain_ref),
+                (embed_hbm, embed_ref),
+            )
+        )
+    ]
+    for copy in small[:3]:
+        copy.start()
+    for first, _ in copies:
         first.start()
+    for _, second in copies:
         second.start()
-        copies.append((first, second))
-    load = pltpu.make_async_copy(pass_ref, pass_buf, pass_sem)
-    load.start()
+    for copy in small[3:]:
+        copy.start()
     clear.wait()
+    small[0].wait()
+    small[1].wait()
 
     side = jnp.bitwise_and(me_ref[0], 1)
 
@@ -82,36 +103,23 @@
     fetch = pltpu.make_async_copy(table, table_v, table_sem)
     fetch.start()
 
+    small[2].wait()
     x = x_ref[...].reshape(query_count * token_count, width_in)
+    actives = []
+    for c in range(chunks):
+        copies[c][0].wait()
+        inner = jnp.dot(x, w1_buf[c], preferred_element_type=F32)
+        actives.append((0.5 * inner * (1.0 + lax.erf(inner * (0.5 ** 0.5)))).astype(BF16))
     total = x.astype(F32)
-    copies[0][0].wait()
-    inner = jnp.dot(x, w1_buf[0], preferred_element_type=F32)
     for c in range(chunks):
         copies[c][1].wait()
-        if c + 1 < chunks:
-            copies[c + 1][0].wait()
-            later = jnp.dot(x, w1_buf[c + 1], preferred_element_type=F32)
-        active = (0.5 * inner * (1.0 + lax.erf(inner * (0.5 ** 0.5)))).astype(BF16)
-        total = total + jnp.dot(active, w2_buf[c], preferred_element_type=F32)
-        if c + 1 < chunks:
-            inner = later
-
-    load.wait()
-
-    def mask(p, carry):
-        block = pass_buf[p]
-        keep = lax.broadcasted_iota(jnp.int32, block.shape, 0) < plen_ref[p]
-        block = block.astype(F32)
-        pass_buf[p] = jnp.where(keep, block, jnp.broadcast_to(block[0:1], block.shape)).astype(BF16)
-        return carry
-
-    lax.fori_loop(0, half, mask, 0, unroll=4)
-    save = pltpu.make_async_copy(pass_buf, masked_ref, pass_sem)
-    save.start()
-
+        total = total + jnp.dot(actives[c], w2_buf[c], preferred_element_type=F32)
+
+    for copy in small[3:]:
+        copy.wait()
     centered = total - jnp.mean(total, axis=-1, keepdims=True)
     variance = jnp.mean(jnp.square(centered), axis=-1, keepdims=True)
-    layer_out = (centered * lax.rsqrt(variance + 1e-12) * gain_ref[...]).astype(BF16)
+    layer_out = (centered * lax.rsqrt(variance + 1e-12) * gain_ref[...].reshape(1, width_in)).astype(BF16)
     embedded = jnp.dot(layer_out, embed_ref[...], preferred_element_type=F32)
     length = jnp.sum(jnp.square(embedded), axis=-1, keepdims=True)
     vectors = embedded * lax.rsqrt(length + 1e-06)
@@ -128,7 +136,6 @@
         out_ref[s, pl.ds(tokens, tail), :] = jnp.broadcast_to(
             table_v[s:s + 1, :].astype(F32), (tail, lanes)
         ).astype(BF16)
-    save.wait()
 
 
 def divider(divisor, limit):
@@ -146,16 +153,14 @@
     outer_weight,
     norm_gain,
     embed_weight,
-    passage_vectors,
-    passage_lengths,
     passage_row,
     candidates,
     slots,
+    half,
 ):
     query_count, token_count, d = query_hidden.shape
     ff = inner_weight.shape[1]
     e = embed_weight.shape[1]
-    half = passage_vectors.shape[0]
     assert 2 * half <= e
     chunks = 6
     width = ff // chunks
@@ -163,50 +168,81 @@
     inverse = divider(half, passage_row.shape[0])
 
     def kernel(*refs):
-        encode_kernel(inverse, *refs)
+        encode_kernel(inverse, half, *refs)
 
     return pl.pallas_call(
         kernel,
         out_shape=(
             jax.ShapeDtypeStruct((slots, tokens + 16, e), BF16),
-            jax.ShapeDtypeStruct(passage_vectors.shape, BF16),
             jax.ShapeDtypeStruct(candidates.shape, jnp.int32),
         ),
-        in_specs=[SMEM] * 5 + [VMEM, ANY, ANY, VMEM, VMEM, ANY],
-        out_specs=(VMEM, ANY, SMEM),
+        in_specs=[SMEM] + [ANY] * 8,
+        out_specs=(VMEM, SMEM),
         scratch_shapes=[
             pltpu.VMEM((chunks, d, width), BF16),
             pltpu.VMEM((chunks, width, d), BF16),
-            pltpu.VMEM(passage_vectors.shape, BF16),
+            pltpu.SMEM(query_lengths.shape, jnp.int32),
+            pltpu.SMEM(passage_row.shape, jnp.int32),
+            pltpu.SMEM(candidates.shape, jnp.int32),
+            pltpu.VMEM(query_hidden.shape, BF16),
+            pltpu.VMEM(norm_gain.shape, F32),
+            pltpu.VMEM(embed_weight.shape, BF16),
             pltpu.SMEM((slots, e), jnp.int32),
             pltpu.VMEM((slots, e), jnp.int32),
             pltpu.SemaphoreType.DMA((2, chunks)),
-            pltpu.SemaphoreType.DMA,
+            pltpu.SemaphoreType.DMA((6,)),
             pltpu.SemaphoreType.DMA,
         ],
-        compiler_params=pltpu.CompilerParams(vmem_limit_bytes=56 * 2 ** 20),
+        compiler_params=pltpu.CompilerParams(vmem_limit_bytes=60 * 2 ** 20),
         cost_estimate=pl.CostEstimate(
             flops=4 * tokens * d * ff, bytes_accessed=4 * d * ff, transcendentals=tokens * ff
         ),
         name="encode",
     )(
+        me,
         query_lengths,
-        me,
         passage_row,
         candidates,
-        passage_lengths,
         query_hidden,
         inner_weight,
         outer_weight,
-        norm_gain.reshape(1, d),
+        norm_gain,
         embed_weight,
-        passage_vectors,
     )
 
 
-def score_kernel(token_count, got_ref, pass0_ref, pass1_ref, out_ref, best_ref, index_v, index, sem):
+def mask_kernel(len0_ref, len1_ref, pass0_ref, pass1_ref, _, out_ref):
+    half = pass0_ref.shape[0]
+    for side, (len_ref, pass_ref) in enumerate(((len0_ref, pass0_ref), (len1_ref, pass1_ref))):
+
+        def mask(p, carry):
+            block = pass_ref[p]
+            keep = lax.broadcasted_iota(jnp.int32, block.shape, 0) < len_ref[p]
+            block = block.astype(F32)
+            out_ref[side * half + p] = jnp.where(keep, block, jnp.broadcast_to(block[0:1], block.shape)).astype(BF16)
+            return carry
+
+        lax.fori_loop(0, half, mask, 0, unroll=4)
+
+
+def mask(lengths, passages, after):
+    half, plen, e = passages[0].shape
+    return pl.pallas_call(
+        mask_kernel,
+        out_shape=jax.ShapeDtypeStruct((2 * half, plen, e), BF16),
+        in_specs=[SMEM, SMEM, VMEM, VMEM, ANY],
+        out_specs=VMEM,
+        compiler_params=pltpu.CompilerParams(vmem_limit_bytes=8 * 2 ** 20),
+        cost_estimate=pl.CostEstimate(
+            flops=8 * half * plen * e, bytes_accessed=8 * half * plen * e, transcendentals=0
+        ),
+        name="mask",
+    )(*lengths, *passages, after)
+
+
+def score_kernel(token_count, got_ref, pass_ref, out_ref, best_ref, index_v, index, sem):
     slots, message, lanes = got_ref.shape
-    half = pass0_ref.shape[0]
+    passage_count = pass_ref.shape[0]
     tokens = message - 16
     group = min(slots, 256 // token_count)
     for s in range(slots):
@@ -215,29 +251,27 @@
     copy.start()
     copy.wait()
 
-    for side, pass_ref in enumerate((pass0_ref, pass1_ref)):
-
-        def eight(step, carry):
-            for part in range(slots // group):
-                rows = []
-                for j in range(8):
-                    p = step * 8 + j
-                    picked = jnp.concatenate(
-                        [
-                            got_ref[s, pl.ds(pl.multiple_of(index[s, side * half + p], token_count), token_count), :]
-                            for s in range(part * group, (part + 1) * group)
-                        ],
-                        axis=0,
-                    )
-                    similar = lax.dot_general(pass_ref[p], picked, NT, preferred_element_type=F32)
-                    rows.append(jnp.max(similar, axis=0, keepdims=True))
-                best_ref[
-                    pl.ds(pl.multiple_of(side * half + step * 8, 8), 8),
-                    pl.ds(part * group * token_count, group * token_count),
-                ] = jnp.concatenate(rows, axis=0)
-            return carry
-
-        lax.fori_loop(0, half // 8, eight, 0)
+    def eight(step, carry):
+        for part in range(slots // group):
+            rows = []
+            for j in range(8):
+                p = step * 8 + j
+                picked = jnp.concatenate(
+                    [
+                        got_ref[s, pl.ds(pl.multiple_of(index[s, p], token_count), token_count), :]
+                        for s in range(part * group, (part + 1) * group)
+                    ],
+                    axis=0,
+                )
+                similar = lax.dot_general(pass_ref[p], picked, NT, preferred_element_type=F32)
+                rows.append(jnp.max(similar, axis=0, keepdims=True))
+            best_ref[
+                pl.ds(pl.multiple_of(step * 8, 8), 8),
+                pl.ds(part * group * token_count, group * token_count),
+            ] = jnp.concatenate(rows, axis=0)
+        return carry
+
+    lax.fori_loop(0, passage_count // 8, eight, 0)
     wide = best_ref.shape[1]
     source = lax.broadcasted_iota(jnp.int32, (slots, wide), 0)
     column = lax.broadcasted_iota(jnp.int32, (slots, wide), 1)
@@ -245,11 +279,11 @@
     ones = jnp.where((column >= first) & (column < first + token_count), 1.0, 0.0).astype(BF16)
     total = sum(lax.dot_general(ones, part, NT, preferred_element_type=F32) for part in split3(best_ref[...]))
     out_ref[...] = jnp.zeros(out_ref.shape, F32)
-    out_ref[:, pl.ds(0, 2 * half)] = total
-
-
-def score(got, own, other, token_count):
-    half, plen, e = own.shape
+    out_ref[:, pl.ds(0, passage_count)] = total
+
+
+def score(got, passages, token_count):
+    passage_count, plen, e = passages.shape
     slots = got.shape[0]
 
     def kernel(*refs):
@@ -258,19 +292,22 @@
     return pl.pallas_call(
         kernel,
         out_shape=jax.ShapeDtypeStruct((slots, e), F32),
-        in_specs=[VMEM] * 3,
+        in_specs=[VMEM] * 2,
         out_specs=VMEM,
         scratch_shapes=[
-            pltpu.VMEM((2 * half, slots * token_count), F32),
+            pltpu.VMEM((passage_count, slots * token_count), F32),
             pltpu.VMEM((slots, e), jnp.int32),
             pltpu.SMEM((slots, e), jnp.int32),
             pltpu.SemaphoreType.DMA,
         ],
+        compiler_params=pltpu.CompilerParams(vmem_limit_bytes=12 * 2 ** 20),
         cost_estimate=pl.CostEstimate(
-            flops=4 * half * slots * token_count * plen * e, bytes_accessed=4 * own.size, transcendentals=0
+            flops=2 * passage_count * slots * token_count * plen * e,
+            bytes_accessed=2 * passages.size,
+            transcendentals=0,
         ),
         name="score",
-    )(got, own, other)
+    )(got, passages)
 
 
 def finish_kernel(got_ref, spot_ref, scores_ref, best_ref):
@@ -306,6 +343,7 @@
         ),
         in_specs=[VMEM, VMEM],
         out_specs=(VMEM, VMEM),
+        compiler_params=pltpu.CompilerParams(vmem_limit_bytes=2 ** 21),
         name="finish",
     )(got, spots)
 
@@ -326,7 +364,11 @@
     slots = size // 2
     groups = [list(range(core, size, 2)) for core in range(2)]
     me = lax.axis_index("shard").astype(jnp.int32).reshape(1)
-    message, own, spots = encode(
+    half = passage_vectors.shape[0]
+    across = [(i, i ^ 1) for i in range(size)]
+    passages = (passage_vectors, lax.ppermute(passage_vectors, "shard", across))
+    lengths = (passage_lengths, lax.ppermute(passage_lengths, "shard", across))
+    message, spots = encode(
         me,
         query_hidden,
         query_lengths,
@@ -334,15 +376,14 @@
         outer_weight,
         norm_gain,
         embed_weight,
-        passage_vectors,
-        passage_lengths,
         passage_row,
         candidates,
         slots,
+        half,
     )
-    other = lax.ppermute(own, "shard", [(i, i ^ 1) for i in range(size)])
     got = lax.all_to_all(message, "shard", split_axis=0, concat_axis=0, axis_index_groups=groups, tiled=True)
-    sums = score(got, own, other, query_hidden.shape[1])
+    masked = mask(lengths, passages, spots)
+    sums = score(got, masked, query_hidden.shape[1])
     back = lax.all_to_all(sums, "shard", split_axis=0, concat_axis=0, axis_index_groups=groups, tiled=True)
     return finish(back, spots)
 

time: 49.4 us -> 41.6 us (0.84)
  blocking collectives: 28.3 us -> 9.89 us
  starting transfers between devices: 0.51 us -> 7.65 us
  waiting for transfers between devices: 0.01 us -> 3.88 us
  Pallas kernels: 17.2 us -> 14.4 us
  local copies, waits for them, and re-layouts: 2.44 us -> 4.66 us
    all_to_all x1 -> x0, blocking collectives: 17.9 us -> none  [per_device(): lax.all_to_all(message, 'shard', split_axis=0, concat_axis=0, axis_index_...]
    all_to_all x0 -> x1, starting transfers between devices: none -> 6.86 us  [per_device(): lax.all_to_all(message, 'shard', split_axis=0, concat_axis=0, axis_index_...]
    unnamed x2 -> x12, local copies, waits for them, and re-layouts: 1.16 us -> 4.66 us
    all_to_all x0 -> x1, waiting for transfers between devices: none -> 2.97 us  [per_device(): lax.all_to_all(message, 'shard', split_axis=0, concat_axis=0, axis_index_...]
    pallas_call x1, Pallas kernels: 7.24 us -> 4.67 us  [score(): pl.pallas_call(kernel, out_shape=jax.ShapeDtypeStruct((slots, e), F32), i...]
    pallas_call x0 -> x1, Pallas kernels: none -> 1.39 us  [mask(): pl.pallas_call(mask_kernel, out_shape=jax.ShapeDtypeStruct((2 * half, ple...]
    reshape x1 -> x0, local copies, waits for them, and re-layouts: 1.28 us -> none  [encode(): norm_gain.reshape(1, d)]
    ppermute x1 -> x2, waiting for transfers between devices: 0.01 us -> 0.92 us  [the longest x1 0.91 us: per_device(): lengths = (passage_lengths, lax.ppermute(passage_lengths, 'shard', across))]
  transfers between devices with their start and end apart: 1 -> 3, of which waited for: 0 -> 2; matrix products, arithmetic and copies ran while one was open for 0% -> 0% of each run, Pallas kernels for 0% -> 21%
where the time goes in v4:
time: 41.6 us; the launch traced here: 41.2 us
  Pallas kernels  14.4 us (35%)
  blocking collectives  9.89 us (24%)
  starting transfers between devices  7.65 us (18%)
  local copies, waits for them, and re-layouts  4.66 us (11%)
  waiting for transfers between devices  3.88 us (9%)
  between operations  0.68 us (2%)
    all_to_all x1, blocking collectives, per_device(): lax.all_to_all(sums, 'shard', split_axis=0, concat_axis=0, axis_index_gro...  9.89 us
    pallas_call x1, Pallas kernels, encode(): pl.pallas_call(kernel, out_shape=(jax.ShapeDtypeStruct((slots, tokens + 1...  7.4 us
    all_to_all x1, starting transfers between devices, per_device(): lax.all_to_all(message, 'shard', split_axis=0, concat_axis=0, axis_index_...  6.86 us
    pallas_call x1, Pallas kernels, score(): pl.pallas_call(kernel, out_shape=jax.ShapeDtypeStruct((slots, e), F32), i...  4.67 us
    unnamed x12, local copies, waits for them, and re-layouts  4.66 us
    all_to_all x1, waiting for transfers between devices, per_device(): lax.all_to_all(message, 'shard', split_axis=0, concat_axis=0, axis_index_...  2.97 us
    pallas_call x1, Pallas kernels, mask(): pl.pallas_call(mask_kernel, out_shape=jax.ShapeDtypeStruct((2 * half, ple...  1.39 us
    pallas_call x1, Pallas kernels, finish(): pl.pallas_call(finish_kernel, out_shape=(jax.ShapeDtypeStruct(spots.shape...  0.99 us
  transfers between devices with their start and end apart: 3, of which 2 were waited for; matrix products, arithmetic and copies ran while one was open for 0% of the time, Pallas kernels for 21%

profile of v4, /device:TPU:0, one launch (start us, length us, event | category | flops | bytes accessed | tf_op | source)
XLA Modules:
  0.0 41.2 jit_solution(1729742843309546650)
XLA Ops:
  0.6 0.5 %collective-permute-start.1 = (bf16[48,128,128]{2,1,0:T(8,128)(2,1)}, bf16[48,128,128]{2,1,0:T(8,128)(2,1)S(1)}, u32[]{:S(2)}, u32[]{:S(2)}) collective-permute-start(bf16[48,128,128]{2,1,0:T(8,128)(2,1)} %pass0_ref.1), channel_id=1, source_target_pairs={{0,1},{1,0},{2,3},{3,2},{4,5},{5,4},{6,7},{7,6},{8,9},{9,8},{10,11... | collective-permute-start | bytes 4718600 | tf_op jit(solution)/shard_map/ppermute | solution.py:369
  1.2 0.0 copy-start.5
  1.2 7.4 %encode.1 = (bf16[8,144,128]{2,1,0:T(8,128)(2,1)}, s32[4,64]{1,0:T(4,128)}) custom-call(s32[1]{0:T(128)} %bitcast.refs_0_, s32[4]{0:T(128)} %refs_1_.1, s32[768]{0:T(1024)} %refs_2_.1, s32[4,64]{1,0:T(4,128)} %refs_3_.1, bf16[4,32,768]{2,1,0:T(8,128)(2,1)} %refs_4_.1, bf16[768,3072]{1,0:T(8,128)(2,1)} %refs_5_.1, bf16[3072,768]{1,0:T(8,128)(2,1)} %refs_6_.1, ...), custom_call_target="tpu_custom_call" | custom-call | flops 1207959552 | bytes 9437184 | tf_op jit(solution)/shard_map/encode/pallas_call | solution.py:173
  8.6 6.9 %all-to-all-start = ((bf16[8,144,128]{2,1,0:T(8,128)(2,1)}), bf16[8,144,128]{2,1,0:T(8,128)(2,1)S(1)}, u32[]{:S(2)}, u32[]{:S(2)}) async-start(bf16[8,144,128]{2,1,0:T(8,128)(2,1)} %get-tuple-element.4), calls=%async_computation | async-start | bytes 589824 | tf_op jit(solution)/shard_map/all_to_all | solution.py:384
  15.4 0.0 copy-done.5
  15.4 0.3 collective-permute-start
  15.7 0.9 %collective-permute-done.len1_ref = s32[48]{0:T(128)S(1)} collective-permute-done((s32[48]{0:T(128)S(1)}, s32[48]{0:T(128)S(1)}, u32[]{:S(2)}, u32[]{:S(2)}) %collective-permute-start) | collective-permute-done | bytes 224 | tf_op jit(solution)/shard_map/ppermute | solution.py:370
  16.6 0.0 collective-permute-done.1.pass1_ref
  16.6 0.0 copy-start.1
  16.6 1.2 %copy-done.1 = bf16[48,128,128]{2,1,0:T(8,128)(2,1)} copy-done((bf16[48,128,128]{2,1,0:T(8,128)(2,1)}, bf16[48,128,128]{2,1,0:T(8,128)(2,1)S(1)}, u32[]{:S(2)}) %copy-start.1) | copy-done | bytes 1572888
  17.8 0.0 copy-start
  17.8 1.4 %copy-done = bf16[48,128,128]{2,1,0:T(8,128)(2,1)S(1)} copy-done((bf16[48,128,128]{2,1,0:T(8,128)(2,1)S(1)}, bf16[48,128,128]{2,1,0:T(8,128)(2,1)}, u32[]{:S(2)}) %copy-start) | copy-done | bytes 1572888
  19.2 0.0 copy-start.2
  19.2 1.4 %copy-done.2 = bf16[48,128,128]{2,1,0:T(8,128)(2,1)S(1)} copy-done((bf16[48,128,128]{2,1,0:T(8,128)(2,1)S(1)}, bf16[48,128,128]{2,1,0:T(8,128)(2,1)}, u32[]{:S(2)}) %copy-start.2) | copy-done | bytes 1572888
  20.6 0.0 copy-start.3
  20.6 0.7 %copy-done.3 = s32[4,64]{1,0:T(4,128)S(1)} copy-done((s32[4,64]{1,0:T(4,128)S(1)}, s32[4,64]{1,0:T(4,128)}, u32[]{:S(2)}) %copy-start.3) | copy-done | bytes 1048
  21.3 1.4 %mask.1.refs_1_ = bf16[96,128,128]{2,1,0:T(8,128)(2,1)S(1)} custom-call(s32[48]{0:T(128)S(1)} %copy-done.5, s32[48]{0:T(128)S(1)} %collective-permute-done.len1_ref, bf16[48,128,128]{2,1,0:T(8,128)(2,1)S(1)} %copy-done, bf16[48,128,128]{2,1,0:T(8,128)(2,1)S(1)} %copy-done.2, s32[4,64]{1,0:T(4,128)S(1)} %copy-done.3), custom_call_target="tpu_custom_call" | custom-call | flops 6291456 | bytes 6291456 | tf_op jit(solution)/shard_map/mask/pallas_call | solution.py:230
  22.7 0.0 copy-start.4
  22.7 3.0 %all-to-all-done.refs_0_ = bf16[8,144,128]{2,1,0:T(8,128)(2,1)S(1)} async-done(((bf16[8,144,128]{2,1,0:T(8,128)(2,1)}), bf16[8,144,128]{2,1,0:T(8,128)(2,1)S(1)}, u32[]{:S(2)}, u32[]{:S(2)}) %all-to-all-start) | async-done | bytes 294944 | tf_op jit(solution)/shard_map/all_to_all | solution.py:384
  25.7 4.7 %score.1 = f32[8,128]{1,0:T(8,128)S(1)} custom-call(bf16[8,144,128]{2,1,0:T(8,128)(2,1)S(1)} %all-to-all-done.refs_0_, bf16[96,128,128]{2,1,0:T(8,128)(2,1)S(1)} %mask.1.refs_1_), custom_call_target="tpu_custom_call" | custom-call | flops 805306368 | bytes 3145728 | tf_op jit(solution)/shard_map/score/pallas_call | solution.py:292
  30.3 9.9 %all_to_all.16 = f32[8,1,128]{2,1,0:T(1,128)S(1)} all-to-all(f32[8,1,128]{2,1,0:T(1,128)S(1)} %bitcast.5), channel_id=1, replica_groups={{0,2,4,6,8,10,12,14},{1,3,5,7,9,11,13,15},{16,18,20,22,24,26,28,30},{17..., dimensions={0} | all-to-all | bytes 8192 | tf_op jit(solution)/shard_map/all_to_all | solution.py:387
  40.2 0.0 copy-done.4
  40.2 1.0 %finish.1 = (f32[4,64]{1,0:T(4,128)}, f32[4,10]{1,0:T(4,128)}) custom-call(f32[8,128]{1,0:T(8,128)S(1)} %bitcast.6, s32[4,64]{1,0:T(4,128)S(1)} %copy-done.4), custom_call_target="tpu_custom_call" | custom-call | tf_op jit(solution)/shard_map/finish/pallas_call | solution.py:338
Async XLA Ops:
  0.6 16.0 %collective-permute-start.1 = (bf16[48,128,128]{2,1,0:T(8,128)(2,1)}, bf16[48,128,128]{2,1,0:T(8,128)(2,1)S(1)}, u32[]{:S(2)}, u32[]{:S(2)}) collective-permute-start(bf16[48,128,128]{2,1,0:T(8,128)(2,1)} %pass0_ref.1), channel_id=1, source_target_pairs={{0,1},{1,0},{2,3},{3,2},{4,5},{5,4},{6,7},{7,6},{8,9},{9,8},{10,11... | collective-permute-start | bytes 4718600 | tf_op jit(solution)/shard_map/ppermute | solution.py:369
  1.2 14.3 %copy-start.5 = (s32[48]{0:T(128)S(1)}, s32[48]{0:T(128)}, u32[]{:S(2)}) copy-start(s32[48]{0:T(128)} %len0_ref.1) | copy-start | bytes 580
  8.6 17.1 %all-to-all-start = ((bf16[8,144,128]{2,1,0:T(8,128)(2,1)}), bf16[8,144,128]{2,1,0:T(8,128)(2,1)S(1)}, u32[]{:S(2)}, u32[]{:S(2)}) async-start(bf16[8,144,128]{2,1,0:T(8,128)(2,1)} %get-tuple-element.4), calls=%async_computation | async-start | bytes 589824 | tf_op jit(solution)/shard_map/all_to_all | solution.py:384
  15.4 1.2 %collective-permute-start = (s32[48]{0:T(128)S(1)}, s32[48]{0:T(128)S(1)}, u32[]{:S(2)}, u32[]{:S(2)}) collective-permute-start(s32[48]{0:T(128)S(1)} %copy-done.5), channel_id=1, source_target_pairs={{0,1},{1,0},{2,3},{3,2},{4,5},{5,4},{6,7},{7,6},{8,9},{9,8},{10,11... | collective-permute-start | bytes 584 | tf_op jit(solution)/shard_map/ppermute | solution.py:370
  16.6 1.2 %copy-start.1 = (bf16[48,128,128]{2,1,0:T(8,128)(2,1)}, bf16[48,128,128]{2,1,0:T(8,128)(2,1)S(1)}, u32[]{:S(2)}) copy-start(bf16[48,128,128]{2,1,0:T(8,128)(2,1)S(1)} %collective-permute-done.1.pass1_ref) | copy-start | bytes 4718596
  17.8 1.4 %copy-start = (bf16[48,128,128]{2,1,0:T(8,128)(2,1)S(1)}, bf16[48,128,128]{2,1,0:T(8,128)(2,1)}, u32[]{:S(2)}) copy-start(bf16[48,128,128]{2,1,0:T(8,128)(2,1)} %pass0_ref.1) | copy-start | bytes 4718596
  19.2 1.4 %copy-start.2 = (bf16[48,128,128]{2,1,0:T(8,128)(2,1)S(1)}, bf16[48,128,128]{2,1,0:T(8,128)(2,1)}, u32[]{:S(2)}) copy-start(bf16[48,128,128]{2,1,0:T(8,128)(2,1)} %copy-done.1) | copy-start | bytes 4718596
  20.6 0.7 %copy-start.3 = (s32[4,64]{1,0:T(4,128)S(1)}, s32[4,64]{1,0:T(4,128)}, u32[]{:S(2)}) copy-start(s32[4,64]{1,0:T(4,128)} %get-tuple-element.5._.spot_ref) | copy-start | bytes 3076
  22.7 17.5 %copy-start.4 = (s32[4,64]{1,0:T(4,128)S(1)}, s32[4,64]{1,0:T(4,128)}, u32[]{:S(2)}) copy-start(s32[4,64]{1,0:T(4,128)} %get-tuple-element.5._.spot_ref) | copy-start | bytes 3076

commit v5 on v4

--- a/solution.py
+++ b/solution.py
@@ -89,30 +89,34 @@
 
     side = jnp.bitwise_and(me_ref[0], 1)
 
-    def enter(k, carry):
-        for i in range(query_count):
+    entries = [(i, k) for k in range(cand_count) for i in range(query_count)]
+    share = -(-len(entries) // (2 * chunks - 2))
+
+    def enter():
+        for i, k in entries[:share]:
             row = row_ref[cand_ref[i, k]]
             owner = inverse(row)
             chip = jnp.right_shift(owner, 1)
             place = row - owner * half + jnp.bitwise_xor(jnp.bitwise_and(owner, 1), side) * half
             table[chip, place] = i
             spot_ref[i, k] = chip * lanes + place
-        return carry
-
-    lax.fori_loop(0, cand_count, enter, 0, unroll=4)
-    fetch = pltpu.make_async_copy(table, table_v, table_sem)
-    fetch.start()
+        del entries[:share]
 
     small[2].wait()
     x = x_ref[...].reshape(query_count * token_count, width_in)
     actives = []
     for c in range(chunks):
         copies[c][0].wait()
+        enter()
         inner = jnp.dot(x, w1_buf[c], preferred_element_type=F32)
         actives.append((0.5 * inner * (1.0 + lax.erf(inner * (0.5 ** 0.5)))).astype(BF16))
     total = x.astype(F32)
     for c in range(chunks):
         copies[c][1].wait()
+        enter()
+        if c == chunks - 2:
+            fetch = pltpu.make_async_copy(table, table_v, table_sem)
+            fetch.start()
         total = total + jnp.dot(actives[c], w2_buf[c], preferred_element_type=F32)
 
     for copy in small[3:]:
@@ -211,38 +215,32 @@
     )
 
 
-def mask_kernel(len0_ref, len1_ref, pass0_ref, pass1_ref, _, out_ref):
-    half = pass0_ref.shape[0]
-    for side, (len_ref, pass_ref) in enumerate(((len0_ref, pass0_ref), (len1_ref, pass1_ref))):
-
-        def mask(p, carry):
-            block = pass_ref[p]
-            keep = lax.broadcasted_iota(jnp.int32, block.shape, 0) < len_ref[p]
-            block = block.astype(F32)
-            out_ref[side * half + p] = jnp.where(keep, block, jnp.broadcast_to(block[0:1], block.shape)).astype(BF16)
-            return carry
-
-        lax.fori_loop(0, half, mask, 0, unroll=4)
+def mask_kernel(len_ref, pass_ref, _, out_ref):
+    def mask(p, carry):
+        block = pass_ref[p]
+        keep = lax.broadcasted_iota(jnp.int32, block.shape, 0) < len_ref[p]
+        block = block.astype(F32)
+        out_ref[p] = jnp.where(keep, block, jnp.broadcast_to(block[0:1], block.shape)).astype(BF16)
+        return carry
+
+    lax.fori_loop(0, pass_ref.shape[0], mask, 0, unroll=4)
 
 
 def mask(lengths, passages, after):
-    half, plen, e = passages[0].shape
     return pl.pallas_call(
         mask_kernel,
-        out_shape=jax.ShapeDtypeStruct((2 * half, plen, e), BF16),
-        in_specs=[SMEM, SMEM, VMEM, VMEM, ANY],
+        out_shape=jax.ShapeDtypeStruct(passages.shape, BF16),
+        in_specs=[SMEM, VMEM, ANY],
         out_specs=VMEM,
         compiler_params=pltpu.CompilerParams(vmem_limit_bytes=8 * 2 ** 20),
-        cost_estimate=pl.CostEstimate(
-            flops=8 * half * plen * e, bytes_accessed=8 * half * plen * e, transcendentals=0
-        ),
+        cost_estimate=pl.CostEstimate(flops=8 * passages.size, bytes_accessed=4 * passages.size, transcendentals=0),
         name="mask",
-    )(*lengths, *passages, after)
-
-
-def score_kernel(token_count, got_ref, pass_ref, out_ref, best_ref, index_v, index, sem):
+    )(lengths, passages, after)
+
+
+def score_kernel(token_count, got_ref, pass0_ref, pass1_ref, out_ref, best_ref, index_v, index, sem):
     slots, message, lanes = got_ref.shape
-    passage_count = pass_ref.shape[0]
+    half = pass0_ref.shape[0]
     tokens = message - 16
     group = min(slots, 256 // token_count)
     for s in range(slots):
@@ -251,27 +249,29 @@
     copy.start()
     copy.wait()
 
-    def eight(step, carry):
-        for part in range(slots // group):
-            rows = []
-            for j in range(8):
-                p = step * 8 + j
-                picked = jnp.concatenate(
-                    [
-                        got_ref[s, pl.ds(pl.multiple_of(index[s, p], token_count), token_count), :]
-                        for s in range(part * group, (part + 1) * group)
-                    ],
-                    axis=0,
-                )
-                similar = lax.dot_general(pass_ref[p], picked, NT, preferred_element_type=F32)
-                rows.append(jnp.max(similar, axis=0, keepdims=True))
-            best_ref[
-                pl.ds(pl.multiple_of(step * 8, 8), 8),
-                pl.ds(part * group * token_count, group * token_count),
-            ] = jnp.concatenate(rows, axis=0)
-        return carry
-
-    lax.fori_loop(0, passage_count // 8, eight, 0)
+    for side, pass_ref in enumerate((pass0_ref, pass1_ref)):
+
+        def eight(step, carry):
+            for part in range(slots // group):
+                rows = []
+                for j in range(8):
+                    p = step * 8 + j
+                    picked = jnp.concatenate(
+                        [
+                            got_ref[s, pl.ds(pl.multiple_of(index[s, side * half + p], token_count), token_count), :]
+                            for s in range(part * group, (part + 1) * group)
+                        ],
+                        axis=0,
+                    )
+                    similar = lax.dot_general(pass_ref[p], picked, NT, preferred_element_type=F32)
+                    rows.append(jnp.max(similar, axis=0, keepdims=True))
+                best_ref[
+                    pl.ds(pl.multiple_of(side * half + step * 8, 8), 8),
+                    pl.ds(part * group * token_count, group * token_count),
+                ] = jnp.concatenate(rows, axis=0)
+            return carry
+
+        lax.fori_loop(0, half // 8, eight, 0)
     wide = best_ref.shape[1]
     source = lax.broadcasted_iota(jnp.int32, (slots, wide), 0)
     column = lax.broadcasted_iota(jnp.int32, (slots, wide), 1)
@@ -279,11 +279,12 @@
     ones = jnp.where((column >= first) & (column < first + token_count), 1.0, 0.0).astype(BF16)
     total = sum(lax.dot_general(ones, part, NT, preferred_element_type=F32) for part in split3(best_ref[...]))
     out_ref[...] = jnp.zeros(out_ref.shape, F32)
-    out_ref[:, pl.ds(0, passage_count)] = total
-
-
-def score(got, passages, token_count):
-    passage_count, plen, e = passages.shape
+    out_ref[:, pl.ds(0, 2 * half)] = total
+
+
+def score(got, own, other, token_count):
+    half, plen, e = own.shape
+    passage_count = 2 * half
     slots = got.shape[0]
 
     def kernel(*refs):
@@ -292,7 +293,7 @@
     return pl.pallas_call(
         kernel,
         out_shape=jax.ShapeDtypeStruct((slots, e), F32),
-        in_specs=[VMEM] * 2,
+        in_specs=[VMEM] * 3,
         out_specs=VMEM,
         scratch_shapes=[
             pltpu.VMEM((passage_count, slots * token_count), F32),
@@ -303,17 +304,18 @@
         compiler_params=pltpu.CompilerParams(vmem_limit_bytes=12 * 2 ** 20),
         cost_estimate=pl.CostEstimate(
             flops=2 * passage_count * slots * token_count * plen * e,
-            bytes_accessed=2 * passages.size,
+            bytes_accessed=4 * own.size,
             transcendentals=0,
         ),
         name="score",
-    )(got, passages)
-
-
-def finish_kernel(got_ref, spot_ref, scores_ref, best_ref):
-    slots, lanes = got_ref.shape
+    )(got, own, other)
+
+
+def finish_kernel(me_ref, got_ref, spot_ref, scores_ref, best_ref):
+    slots, _, lanes = got_ref.shape
     query_count, cand_count = scores_ref.shape
-    parts = split3(got_ref[...])
+    chip = jnp.right_shift(me_ref[0], 1)
+    parts = split3(jnp.concatenate([got_ref[s, pl.ds(chip, 1), :] for s in range(slots)], axis=0))
     slot_iota = lax.broadcasted_iota(jnp.int32, (slots, cand_count), 0) * lanes
     lane_iota = lax.broadcasted_iota(jnp.int32, (lanes, cand_count), 0)
     row_iota = lax.broadcasted_iota(jnp.int32, (cand_count, cand_count), 0)
@@ -334,18 +336,18 @@
         best_ref[i:i + 1, :] = ordered[:, :TOPN]
 
 
-def finish(got, spots):
+def finish(me, got, spots):
     return pl.pallas_call(
         finish_kernel,
         out_shape=(
             jax.ShapeDtypeStruct(spots.shape, F32),
             jax.ShapeDtypeStruct((spots.shape[0], TOPN), F32),
         ),
-        in_specs=[VMEM, VMEM],
+        in_specs=[SMEM, VMEM, VMEM],
         out_specs=(VMEM, VMEM),
         compiler_params=pltpu.CompilerParams(vmem_limit_bytes=2 ** 21),
         name="finish",
-    )(got, spots)
+    )(me, got, spots)
 
 
 def per_device(
@@ -366,8 +368,6 @@
     me = lax.axis_index("shard").astype(jnp.int32).reshape(1)
     half = passage_vectors.shape[0]
     across = [(i, i ^ 1) for i in range(size)]
-    passages = (passage_vectors, lax.ppermute(passage_vectors, "shard", across))
-    lengths = (passage_lengths, lax.ppermute(passage_lengths, "shard", across))
     message, spots = encode(
         me,
         query_hidden,
@@ -382,10 +382,11 @@
         half,
     )
     got = lax.all_to_all(message, "shard", split_axis=0, concat_axis=0, axis_index_groups=groups, tiled=True)
-    masked = mask(lengths, passages, spots)
-    sums = score(got, masked, query_hidden.shape[1])
-    back = lax.all_to_all(sums, "shard", split_axis=0, concat_axis=0, axis_index_groups=groups, tiled=True)
-    return finish(back, spots)
+    own = mask(passage_lengths, passage_vectors, spots)
+    other = lax.ppermute(own, "shard", across)
+    sums = score(got, own, other, query_hidden.shape[1])
+    back = lax.all_gather(sums, "shard", axis=0, axis_index_groups=groups)
+    return finish(me, back, spots)
 
 
 def solution(mesh):

time: 41.6 us -> 64.2 us (1.54)
  blocking collectives: 9.89 us -> 48 us
  starting transfers between devices: 7.65 us -> 0.52 us
  local copies, waits for them, and re-layouts: 4.66 us -> 0.69 us
  waiting for transfers between devices: 3.88 us -> 0.01 us
    all_gather x0 -> x1, blocking collectives: none -> 30.4 us  [per_device(): back = lax.all_gather(sums, 'shard', axis=0, axis_index_groups=groups)]
    all_to_all x1, blocking collectives: 9.89 us -> 17.6 us  [per_device(): lax.all_to_all(message, 'shard', split_axis=0, concat_axis=0, axis_index_...]
    all_to_all x1 -> x0, starting transfers between devices: 6.86 us -> none  [per_device(): lax.all_to_all(message, 'shard', split_axis=0, concat_axis=0, axis_index_...]
    unnamed x12 -> x10, local copies, waits for them, and re-layouts: 4.66 us -> 0.69 us
    all_to_all x1 -> x0, waiting for transfers between devices: 2.97 us -> none  [per_device(): lax.all_to_all(message, 'shard', split_axis=0, concat_axis=0, axis_index_...]
    ppermute x2 -> x1, waiting for transfers between devices: 0.92 us -> 0.01 us  [per_device(): other = lax.ppermute(own, 'shard', across)]
  transfers between devices with their start and end apart: 3 -> 1, of which waited for: 2 -> 0; matrix products, arithmetic and copies ran while one was open for 0% -> 0% of each run, Pallas kernels for 21% -> 0%
where the time goes in v5:
time: 64.2 us; the launch traced here: 64 us
  blocking collectives  48 us (75%)
  Pallas kernels  14.1 us (22%)
  between operations  0.71 us (1%)
  local copies, waits for them, and re-layouts  0.69 us (1%)
    all_gather x1, blocking collectives, per_device(): back = lax.all_gather(sums, 'shard', axis=0, axis_index_groups=groups)  30.4 us
    all_to_all x1, blocking collectives, per_device(): lax.all_to_all(message, 'shard', split_axis=0, concat_axis=0, axis_index_...  17.6 us
    pallas_call x1, Pallas kernels, encode(): pl.pallas_call(kernel, out_shape=(jax.ShapeDtypeStruct((slots, tokens + 1...  7.44 us
    pallas_call x1, Pallas kernels, score(): pl.pallas_call(kernel, out_shape=jax.ShapeDtypeStruct((slots, e), F32), i...  4.66 us
  transfers between devices with their start and end apart: 1, of which 0 were waited for; matrix products, arithmetic and copies ran while one was open for 0% of the time, Pallas kernels for 0%

profile of v5, /device:TPU:0, one launch (start us, length us, event | category | flops | bytes accessed | tf_op | source)
XLA Modules:
  0.0 64.0 jit_solution(7292631103749035390)
XLA Ops:
  0.6 0.0 copy-start
  0.6 0.0 copy-start.3
  0.7 7.4 %encode.1 = (bf16[8,144,128]{2,1,0:T(8,128)(2,1)}, s32[4,64]{1,0:T(4,128)}) custom-call(s32[1]{0:T(128)} %bitcast.refs_0_.me_ref, s32[4]{0:T(128)} %refs_1_.1, s32[768]{0:T(1024)} %refs_2_.1, s32[4,64]{1,0:T(4,128)} %refs_3_.1, bf16[4,32,768]{2,1,0:T(8,128)(2,1)} %refs_4_.1, bf16[768,3072]{1,0:T(8,128)(2,1)} %refs_5_.1, bf16[3072,768]{1,0:T(8,128)(2,1)} %refs_6_.1, ...), custom_call_target="tpu_custom_call" | custom-call | flops 1207959552 | bytes 9437184 | tf_op jit(solution)/shard_map/encode/pallas_call | solution.py:177
  8.1 0.0 copy-done
  8.1 0.0 copy-done.3
  8.1 0.0 copy-start.1
  8.1 0.7 %copy-done.1 = s32[4,64]{1,0:T(4,128)S(1)} copy-done((s32[4,64]{1,0:T(4,128)S(1)}, s32[4,64]{1,0:T(4,128)}, u32[]{:S(2)}) %copy-start.1) | copy-done | bytes 1048
  8.8 0.0 copy-start.4
  8.8 1.0 %mask.1.refs_1_ = bf16[48,128,128]{2,1,0:T(8,128)(2,1)S(1)} custom-call(s32[48]{0:T(128)S(1)} %copy-done.3, bf16[48,128,128]{2,1,0:T(8,128)(2,1)S(1)} %copy-done, s32[4,64]{1,0:T(4,128)S(1)} %copy-done.1), custom_call_target="tpu_custom_call" | custom-call | flops 6291456 | bytes 3145728 | tf_op jit(solution)/shard_map/mask/pallas_call | solution.py:230
  9.8 0.5 collective-permute-start
  10.3 0.0 copy-done.4
  10.3 17.6 %all_to_all.5.refs_0_ = bf16[8,144,128]{2,1,0:T(8,128)(2,1)S(1)} all-to-all(bf16[8,144,128]{2,1,0:T(8,128)(2,1)S(1)} %copy-done.4), channel_id=1, replica_groups={{0,2,4,6,8,10,12,14},{1,3,5,7,9,11,13,15},{16,18,20,22,24,26,28,30},{17..., dimensions={0} | all-to-all | bytes 589824 | tf_op jit(solution)/shard_map/all_to_all | solution.py:384
  27.9 0.0 copy-start.2
  27.9 0.0 collective-permute-done.refs_2_
  27.9 4.7 %score.1 = f32[8,128]{1,0:T(8,128)S(1)} custom-call(bf16[8,144,128]{2,1,0:T(8,128)(2,1)S(1)} %all_to_all.5.refs_0_, bf16[48,128,128]{2,1,0:T(8,128)(2,1)S(1)} %mask.1.refs_1_, bf16[48,128,128]{2,1,0:T(8,128)(2,1)S(1)} %collective-permute-done.refs_2_), custom_call_target="tpu_custom_call" | custom-call | flops 805306368 | bytes 3145728 | tf_op jit(solution)/shard_map/score/pallas_call | solution.py:293
  32.6 30.4 %all-gather = f32[64,128]{1,0:T(8,128)S(1)} all-gather(f32[8,128]{1,0:T(8,128)S(1)} %score.1), channel_id=2, replica_groups={{0,2,4,6,8,10,12,14},{1,3,5,7,9,11,13,15},{16,18,20,22,24,26,28,30},{17..., dimensions={0}, use_global_device_ids=true | all-gather | bytes 36864 | tf_op jit(solution)/shard_map/all_gather | solution.py:388
  63.0 0.0 copy-done.2
  63.0 1.0 %finish.1 = (f32[4,64]{1,0:T(4,128)}, f32[4,10]{1,0:T(4,128)}) custom-call(s32[1]{0:T(128)} %bitcast.refs_0_.me_ref, f32[8,8,128]{2,1,0:T(8,128)S(1)} %bitcast.2, s32[4,64]{1,0:T(4,128)S(1)} %copy-done.2), custom_call_target="tpu_custom_call" | custom-call | tf_op jit(solution)/shard_map/finish/pallas_call | solution.py:340
Async XLA Ops:
  0.6 7.5 %copy-start = (bf16[48,128,128]{2,1,0:T(8,128)(2,1)S(1)}, bf16[48,128,128]{2,1,0:T(8,128)(2,1)}, u32[]{:S(2)}) copy-start(bf16[48,128,128]{2,1,0:T(8,128)(2,1)} %pass_ref.1) | copy-start | bytes 4718596
  0.6 7.5 %copy-start.3 = (s32[48]{0:T(128)S(1)}, s32[48]{0:T(128)}, u32[]{:S(2)}) copy-start(s32[48]{0:T(128)} %len_ref.1) | copy-start | bytes 580
  8.1 0.7 %copy-start.1 = (s32[4,64]{1,0:T(4,128)S(1)}, s32[4,64]{1,0:T(4,128)}, u32[]{:S(2)}) copy-start(s32[4,64]{1,0:T(4,128)} %get-tuple-element.5._.spot_ref) | copy-start | bytes 3076
  8.8 1.5 %copy-start.4 = (bf16[8,144,128]{2,1,0:T(8,128)(2,1)S(1)}, bf16[8,144,128]{2,1,0:T(8,128)(2,1)}, u32[]{:S(2)}) copy-start(bf16[8,144,128]{2,1,0:T(8,128)(2,1)} %get-tuple-element.4) | copy-start | bytes 884740
  9.8 18.1 %collective-permute-start = (bf16[48,128,128]{2,1,0:T(8,128)(2,1)S(1)}, bf16[48,128,128]{2,1,0:T(8,128)(2,1)S(1)}, u32[]{:S(2)}, u32[]{:S(2)}) collective-permute-start(bf16[48,128,128]{2,1,0:T(8,128)(2,1)S(1)} %mask.1.refs_1_), channel_id=1, source_target_pairs={{0,1},{1,0},{2,3},{3,2},{4,5},{5,4},{6,7},{7,6},{8,9},{9,8},{10,11... | collective-permute-start | bytes 4718600 | tf_op jit(solution)/shard_map/ppermute | solution.py:386
  27.9 35.1 %copy-start.2 = (s32[4,64]{1,0:T(4,128)S(1)}, s32[4,64]{1,0:T(4,128)}, u32[]{:S(2)}) copy-start(s32[4,64]{1,0:T(4,128)} %get-tuple-element.5._.spot_ref) | copy-start | bytes 3076

commit v6 on v5

--- a/solution.py
+++ b/solution.py
@@ -27,6 +27,7 @@
     half,
     me_ref,
     lens_hbm,
+    plen_hbm,
     row_hbm,
     cand_hbm,
     x_hbm,
@@ -34,11 +35,15 @@
     w2_ref,
     gain_hbm,
     embed_hbm,
+    pass_hbm,
     out_ref,
+    masked_hbm,
     spot_ref,
     w1_buf,
     w2_buf,
+    pass_buf,
     lens_ref,
+    plen_ref,
     row_ref,
     cand_ref,
     x_ref,
@@ -49,6 +54,7 @@
     sems,
     small_sems,
     table_sem,
+    pass_sems,
 ):
     chunks, _, width = w1_buf.shape
     slots, lanes = table_v.shape
@@ -69,19 +75,32 @@
                 (row_hbm, row_ref),
                 (cand_hbm, cand_ref),
                 (x_hbm, x_ref),
+                (plen_hbm, plen_ref),
                 (lens_hbm, lens_ref),
                 (gain_hbm, gain_ref),
                 (embed_hbm, embed_ref),
             )
         )
     ]
-    for copy in small[:3]:
+    for copy in small[:4]:
         copy.start()
-    for first, _ in copies:
-        first.start()
-    for _, second in copies:
-        second.start()
-    for copy in small[3:]:
+    batch = half // chunks
+    loads, saves = [], []
+    for c in range(chunks):
+        rows = pl.ds(c * batch, batch)
+        loads.append(pltpu.make_async_copy(pass_hbm.at[rows], pass_buf.at[rows], pass_sems.at[0, c]))
+        saves.append(pltpu.make_async_copy(pass_buf.at[rows], masked_hbm.at[rows], pass_sems.at[1, c]))
+    copies[0][0].start()
+    copies[1][0].start()
+    copies[0][1].start()
+    for c in range(2, chunks):
+        loads[c - 2].start()
+        copies[c][0].start()
+        copies[c - 1][1].start()
+    copies[-1][1].start()
+    loads[-2].start()
+    loads[-1].start()
+    for copy in small[4:]:
         copy.start()
     clear.wait()
     small[0].wait()
@@ -90,7 +109,7 @@
     side = jnp.bitwise_and(me_ref[0], 1)
 
     entries = [(i, k) for k in range(cand_count) for i in range(query_count)]
-    share = -(-len(entries) // (2 * chunks - 2))
+    share = -(-len(entries) // (chunks + 1))
 
     def enter():
         for i, k in entries[:share]:
@@ -102,24 +121,41 @@
             spot_ref[i, k] = chip * lanes + place
         del entries[:share]
 
+    def mask(c):
+        loads[c].wait()
+        for p in range(c * batch, (c + 1) * batch):
+            block = pass_buf[p]
+            keep = lax.broadcasted_iota(jnp.int32, block.shape, 0) < plen_ref[p]
+            block = block.astype(F32)
+            pass_buf[p] = jnp.where(keep, block, jnp.broadcast_to(block[0:1], block.shape)).astype(BF16)
+        saves[c].start()
+
     small[2].wait()
+    small[3].wait()
     x = x_ref[...].reshape(query_count * token_count, width_in)
-    actives = []
-    for c in range(chunks):
-        copies[c][0].wait()
+    total = x.astype(F32)
+    inner = active = None
+    for step in range(chunks + 2):
+        if step < chunks:
+            copies[step][0].wait()
+        if step >= 2:
+            copies[step - 2][1].wait()
+        if 2 <= step < chunks:
+            mask(step - 2)
         enter()
-        inner = jnp.dot(x, w1_buf[c], preferred_element_type=F32)
-        actives.append((0.5 * inner * (1.0 + lax.erf(inner * (0.5 ** 0.5)))).astype(BF16))
-    total = x.astype(F32)
-    for c in range(chunks):
-        copies[c][1].wait()
-        enter()
-        if c == chunks - 2:
+        later = jnp.dot(x, w1_buf[step], preferred_element_type=F32) if step < chunks else None
+        if step >= 2:
+            total = total + jnp.dot(active, w2_buf[step - 2], preferred_element_type=F32)
+        if 1 <= step <= chunks:
+            active = (0.5 * inner * (1.0 + lax.erf(inner * (0.5 ** 0.5)))).astype(BF16)
+        inner = later
+        if step == chunks:
             fetch = pltpu.make_async_copy(table, table_v, table_sem)
             fetch.start()
-        total = total + jnp.dot(actives[c], w2_buf[c], preferred_element_type=F32)
-
-    for copy in small[3:]:
+    mask(chunks - 2)
+    mask(chunks - 1)
+
+    for copy in small[4:]:
         copy.wait()
     centered = total - jnp.mean(total, axis=-1, keepdims=True)
     variance = jnp.mean(jnp.square(centered), axis=-1, keepdims=True)
@@ -134,12 +170,10 @@
     vectors = vectors.astype(BF16)
     fetch.wait()
     tokens = query_count * token_count
-    tail = out_ref.shape[1] - tokens
-    for s in range(slots):
-        out_ref[s, pl.ds(0, tokens), :] = vectors
-        out_ref[s, pl.ds(tokens, tail), :] = jnp.broadcast_to(
-            table_v[s:s + 1, :].astype(F32), (tail, lanes)
-        ).astype(BF16)
+    out_ref[pl.ds(0, tokens), :] = vectors
+    out_ref[pl.ds(tokens, slots), :] = table_v[...].astype(F32).astype(BF16)
+    for save in saves:
+        save.wait()
 
 
 def divider(divisor, limit):
@@ -157,14 +191,17 @@
     outer_weight,
     norm_gain,
     embed_weight,
+    passage_vectors,
+    passage_lengths,
     passage_row,
     candidates,
     slots,
-    half,
 ):
     query_count, token_count, d = query_hidden.shape
     ff = inner_weight.shape[1]
     e = embed_weight.shape[1]
+    half = passage_vectors.shape[0]
+    slots = -(-slots // 16) * 16
     assert 2 * half <= e
     chunks = 6
     width = ff // chunks
@@ -177,15 +214,18 @@
     return pl.pallas_call(
         kernel,
         out_shape=(
-            jax.ShapeDtypeStruct((slots, tokens + 16, e), BF16),
+            jax.ShapeDtypeStruct((tokens + slots, e), BF16),
+            jax.ShapeDtypeStruct(passage_vectors.shape, BF16),
             jax.ShapeDtypeStruct(candidates.shape, jnp.int32),
         ),
-        in_specs=[SMEM] + [ANY] * 8,
-        out_specs=(VMEM, SMEM),
+        in_specs=[SMEM] + [ANY] * 10,
+        out_specs=(VMEM, ANY, SMEM),
         scratch_shapes=[
             pltpu.VMEM((chunks, d, width), BF16),
             pltpu.VMEM((chunks, width, d), BF16),
+            pltpu.VMEM(passage_vectors.shape, BF16),
             pltpu.SMEM(query_lengths.shape, jnp.int32),
+            pltpu.SMEM(passage_lengths.shape, jnp.int32),
             pltpu.SMEM(passage_row.shape, jnp.int32),
             pltpu.SMEM(candidates.shape, jnp.int32),
             pltpu.VMEM(query_hidden.shape, BF16),
@@ -194,8 +234,9 @@
             pltpu.SMEM((slots, e), jnp.int32),
             pltpu.VMEM((slots, e), jnp.int32),
             pltpu.SemaphoreType.DMA((2, chunks)),
-            pltpu.SemaphoreType.DMA((6,)),
+            pltpu.SemaphoreType.DMA((7,)),
             pltpu.SemaphoreType.DMA,
+            pltpu.SemaphoreType.DMA((2, chunks)),
         ],
         compiler_params=pltpu.CompilerParams(vmem_limit_bytes=60 * 2 ** 20),
         cost_estimate=pl.CostEstimate(
@@ -205,6 +246,7 @@
     )(
         me,
         query_lengths,
+        passage_lengths,
         passage_row,
         candidates,
         query_hidden,
@@ -212,39 +254,24 @@
         outer_weight,
         norm_gain,
         embed_weight,
+        passage_vectors,
     )
 
 
-def mask_kernel(len_ref, pass_ref, _, out_ref):
-    def mask(p, carry):
-        block = pass_ref[p]
-        keep = lax.broadcasted_iota(jnp.int32, block.shape, 0) < len_ref[p]
-        block = block.astype(F32)
-        out_ref[p] = jnp.where(keep, block, jnp.broadcast_to(block[0:1], block.shape)).astype(BF16)
-        return carry
-
-    lax.fori_loop(0, pass_ref.shape[0], mask, 0, unroll=4)
-
-
-def mask(lengths, passages, after):
-    return pl.pallas_call(
-        mask_kernel,
-        out_shape=jax.ShapeDtypeStruct(passages.shape, BF16),
-        in_specs=[SMEM, VMEM, ANY],
-        out_specs=VMEM,
-        compiler_params=pltpu.CompilerParams(vmem_limit_bytes=8 * 2 ** 20),
-        cost_estimate=pl.CostEstimate(flops=8 * passages.size, bytes_accessed=4 * passages.size, transcendentals=0),
-        name="mask",
-    )(lengths, passages, after)
-
-
-def score_kernel(token_count, got_ref, pass0_ref, pass1_ref, out_ref, best_ref, index_v, index, sem):
-    slots, message, lanes = got_ref.shape
+def score_kernel(slots, token_count, me_ref, pass0_ref, pass1_ref, *refs):
+    got_refs = refs[:slots]
+    out_ref, best_ref, index_v, index, sem = refs[slots:]
+    message, lanes = got_refs[0].shape
     half = pass0_ref.shape[0]
-    tokens = message - 16
+    rows = -(-slots // 16) * 16
+    tokens = message - rows
     group = min(slots, 256 // token_count)
+    chip = jnp.right_shift(me_ref[0], 1)
+    mine = lax.broadcasted_iota(jnp.int32, (rows, lanes), 0) == chip
     for s in range(slots):
-        index_v[s:s + 1, :] = got_ref[s, pl.ds(tokens, 16), :].astype(F32)[0:1].astype(jnp.int32) * token_count
+        table = got_refs[s][pl.ds(tokens, rows), :].astype(F32)
+        query = jnp.sum(jnp.where(mine, table, 0.0), axis=0, keepdims=True)
+        index_v[s:s + 1, :] = query.astype(jnp.int32) * token_count
     copy = pltpu.make_async_copy(index_v, index, sem)
     copy.start()
     copy.wait()
@@ -258,7 +285,7 @@
                     p = step * 8 + j
                     picked = jnp.concatenate(
                         [
-                            got_ref[s, pl.ds(pl.multiple_of(index[s, side * half + p], token_count), token_count), :]
+                            got_refs[s][pl.ds(pl.multiple_of(index[s, side * half + p], token_count), token_count), :]
                             for s in range(part * group, (part + 1) * group)
                         ],
                         axis=0,
@@ -279,21 +306,22 @@
     ones = jnp.where((column >= first) & (column < first + token_count), 1.0, 0.0).astype(BF16)
     total = sum(lax.dot_general(ones, part, NT, preferred_element_type=F32) for part in split3(best_ref[...]))
     out_ref[...] = jnp.zeros(out_ref.shape, F32)
-    out_ref[:, pl.ds(0, 2 * half)] = total
-
-
-def score(got, own, other, token_count):
+    for s in range(slots):
+        out_ref[pl.ds(jnp.bitwise_xor(chip, s), 1), pl.ds(0, 2 * half)] = total[s:s + 1]
+
+
+def score(me, got, own, other, token_count):
     half, plen, e = own.shape
     passage_count = 2 * half
-    slots = got.shape[0]
+    slots = len(got)
 
     def kernel(*refs):
-        score_kernel(token_count, *refs)
+        score_kernel(slots, token_count, *refs)
 
     return pl.pallas_call(
         kernel,
         out_shape=jax.ShapeDtypeStruct((slots, e), F32),
-        in_specs=[VMEM] * 3,
+        in_specs=[SMEM] + [VMEM] * (2 + slots),
         out_specs=VMEM,
         scratch_shapes=[
             pltpu.VMEM((passage_count, slots * token_count), F32),
@@ -308,14 +336,13 @@
             transcendentals=0,
         ),
         name="score",
-    )(got, own, other)
-
-
-def finish_kernel(me_ref, got_ref, spot_ref, scores_ref, best_ref):
-    slots, _, lanes = got_ref.shape
+    )(me, own, other, *got)
+
+
+def finish_kernel(got_ref, spot_ref, scores_ref, best_ref):
+    slots, lanes = got_ref.shape
     query_count, cand_count = scores_ref.shape
-    chip = jnp.right_shift(me_ref[0], 1)
-    parts = split3(jnp.concatenate([got_ref[s, pl.ds(chip, 1), :] for s in range(slots)], axis=0))
+    parts = split3(got_ref[...])
     slot_iota = lax.broadcasted_iota(jnp.int32, (slots, cand_count), 0) * lanes
     lane_iota = lax.broadcasted_iota(jnp.int32, (lanes, cand_count), 0)
     row_iota = lax.broadcasted_iota(jnp.int32, (cand_count, cand_count), 0)
@@ -336,18 +363,23 @@
         best_ref[i:i + 1, :] = ordered[:, :TOPN]
 
 
-def finish(me, got, spots):
+def finish(got, spots):
     return pl.pallas_call(
         finish_kernel,
         out_shape=(
             jax.ShapeDtypeStruct(spots.shape, F32),
             jax.ShapeDtypeStruct((spots.shape[0], TOPN), F32),
         ),
-        in_specs=[SMEM, VMEM, VMEM],
+        in_specs=[VMEM, VMEM],
         out_specs=(VMEM, VMEM),
         compiler_params=pltpu.CompilerParams(vmem_limit_bytes=2 ** 21),
         name="finish",
-    )(me, got, spots)
+    )(got, spots)
+
+
+def swap(value, distance):
+    size = lax.axis_size("shard")
+    return lax.ppermute(value, "shard", [(i, i ^ distance) for i in range(size)])
 
 
 def per_device(
@@ -366,9 +398,7 @@
     slots = size // 2
     groups = [list(range(core, size, 2)) for core in range(2)]
     me = lax.axis_index("shard").astype(jnp.int32).reshape(1)
-    half = passage_vectors.shape[0]
-    across = [(i, i ^ 1) for i in range(size)]
-    message, spots = encode(
+    message, own, spots = encode(
         me,
         query_hidden,
         query_lengths,
@@ -376,17 +406,17 @@
         outer_weight,
         norm_gain,
         embed_weight,
+        passage_vectors,
+        passage_lengths,
         passage_row,
         candidates,
         slots,
-        half,
     )
-    got = lax.all_to_all(message, "shard", split_axis=0, concat_axis=0, axis_index_groups=groups, tiled=True)
-    own = mask(passage_lengths, passage_vectors, spots)
-    other = lax.ppermute(own, "shard", across)
-    sums = score(got, own, other, query_hidden.shape[1])
-    back = lax.all_gather(sums, "shard", axis=0, axis_index_groups=groups)
-    return finish(me, back, spots)
+    got = [message] + [swap(message, 2 * d) for d in range(1, slots)]
+    other = swap(own, 1)
+    sums = score(me, got, own, other, query_hidden.shape[1])
+    back = lax.all_to_all(sums, "shard", split_axis=0, concat_axis=0, axis_index_groups=groups, tiled=True)
+    return finish(back, spots)
 
 
 def solution(mesh):

time: 64.2 us -> 44.1 us (0.69)
  blocking collectives: 48 us -> 10.5 us
  starting transfers between devices: 0.52 us -> 12.5 us
  waiting for transfers between devices: 0.01 us -> 5.09 us
  local copies, waits for them, and re-layouts: 0.69 us -> 2.18 us
  Pallas kernels: 14.1 us -> 12.8 us
    all_gather x1 -> x0, blocking collectives: 30.4 us -> none  [per_device(): back = lax.all_gather(sums, 'shard', axis=0, axis_index_groups=groups)]
    ppermute x1 -> x8, starting transfers between devices: 0.52 us -> 12.5 us  [swap(): lax.ppermute(value, 'shard', [(i, i ^ distance) for i in range(size)])]
    all_to_all x1, blocking collectives: 17.6 us -> 10.5 us  [per_device(): lax.all_to_all(sums, 'shard', split_axis=0, concat_axis=0, axis_index_gro...]
    ppermute x1 -> x8, waiting for transfers between devices: 0.01 us -> 5.09 us  [swap(): lax.ppermute(value, 'shard', [(i, i ^ distance) for i in range(size)])]
    unnamed x10 -> x6, local copies, waits for them, and re-layouts: 0.69 us -> 2.18 us
    pallas_call x2 -> x1, Pallas kernels: 8.41 us -> 7.17 us  [encode(): pl.pallas_call(kernel, out_shape=(jax.ShapeDtypeStruct((tokens + slots, e...]
  transfers between devices with their start and end apart: 1 -> 8, of which waited for: 0 -> 5; matrix products, arithmetic and copies ran while one was open for 0% -> 0% of each run, Pallas kernels for 0% -> 0%
where the time goes in v6:
time: 44.1 us; the launch traced here: 43.8 us
  Pallas kernels  12.8 us (29%)
  starting transfers between devices  12.5 us (28%)
  blocking collectives  10.5 us (24%)
  waiting for transfers between devices  5.09 us (12%)
  local copies, waits for them, and re-layouts  2.18 us (5%)
  between operations  0.67 us (2%)
    ppermute x8, starting transfers between devices, swap(): lax.ppermute(value, 'shard', [(i, i ^ distance) for i in range(size)])  12.5 us
    all_to_all x1, blocking collectives, per_device(): lax.all_to_all(sums, 'shard', split_axis=0, concat_axis=0, axis_index_gro...  10.5 us
    pallas_call x1, Pallas kernels, encode(): pl.pallas_call(kernel, out_shape=(jax.ShapeDtypeStruct((tokens + slots, e...  7.17 us
    ppermute x8, waiting for transfers between devices, swap(): lax.ppermute(value, 'shard', [(i, i ^ distance) for i in range(size)])  5.09 us
    pallas_call x1, Pallas kernels, score(): pl.pallas_call(kernel, out_shape=jax.ShapeDtypeStruct((slots, e), F32), i...  4.68 us
    unnamed x6, local copies, waits for them, and re-layouts  2.18 us
    pallas_call x1, Pallas kernels, finish(): pl.pallas_call(finish_kernel, out_shape=(jax.ShapeDtypeStruct(spots.shape...  0.99 us
  transfers between devices with their start and end apart: 8, of which 5 were waited for; matrix products, arithmetic and copies ran while one was open for 0% of the time, Pallas kernels for 0%

profile of v6, /device:TPU:0, one launch (start us, length us, event | category | flops | bytes accessed | tf_op | source)
XLA Modules:
  0.0 43.8 jit_solution(11504479955854824584)
XLA Ops:
  0.6 7.2 %encode.1 = (bf16[144,128]{1,0:T(8,128)(2,1)}, bf16[48,128,128]{2,1,0:T(8,128)(2,1)}, s32[4,64]{1,0:T(4,128)}) custom-call(s32[1]{0:T(128)} %bitcast.refs_0_, s32[4]{0:T(128)} %refs_1_.1, s32[48]{0:T(128)} %refs_2_.1, s32[768]{0:T(1024)} %refs_3_.1, s32[4,64]{1,0:T(4,128)} %refs_4_.1, bf16[4,32,768]{2,1,0:T(8,128)(2,1)} %refs_5_.1, ...), custom_call_target="tpu_custom_call" | custom-call | flops 1207959552 | bytes 9437184 | tf_op jit(solution)/shard_map/encode/pallas_call | solution.py:214
  7.8 0.0 copy-start.2
  7.8 0.5 %collective-permute-start = (bf16[48,128,128]{2,1,0:T(8,128)(2,1)}, bf16[48,128,128]{2,1,0:T(8,128)(2,1)S(1)}, u32[]{:S(2)}, u32[]{:S(2)}) collective-permute-start(bf16[48,128,128]{2,1,0:T(8,128)(2,1)} %get-tuple-element.5.refs_1_), channel_id=1, source_target_pairs={{0,1},{1,0},{2,3},{3,2},{4,5},{5,4},{6,7},{7,6},{8,9},{9,8},{10,11... | collective-permute-start | bytes 4718600 | tf_op jit(solution)/shard_map/ppermute | solution.py:382
  8.3 5.6 %collective-permute-start.7 = (bf16[144,128]{1,0:T(8,128)(2,1)}, bf16[144,128]{1,0:T(8,128)(2,1)S(1)}, u32[]{:S(2)}, u32[]{:S(2)}) collective-permute-start(bf16[144,128]{1,0:T(8,128)(2,1)} %get-tuple-element.6.refs_3_), channel_id=1, source_target_pairs={{0,14},{1,15},{2,12},{3,13},{4,10},{5,11},{6,8},{7,9},{8,6},{9,7},... | collective-permute-start | bytes 110600 | tf_op jit(solution)/shard_map/ppermute | solution.py:382
  14.0 0.2 collective-permute-start.6
  14.2 0.7 %collective-permute-start.5 = (bf16[144,128]{1,0:T(8,128)(2,1)}, bf16[144,128]{1,0:T(8,128)(2,1)S(1)}, u32[]{:S(2)}, u32[]{:S(2)}) collective-permute-start(bf16[144,128]{1,0:T(8,128)(2,1)} %get-tuple-element.6.refs_3_), channel_id=1, source_target_pairs={{0,10},{1,11},{2,8},{3,9},{4,14},{5,15},{6,12},{7,13},{8,2},{9,3},... | collective-permute-start | bytes 110600 | tf_op jit(solution)/shard_map/ppermute | solution.py:382
  14.9 2.1 %collective-permute-start.4 = (bf16[144,128]{1,0:T(8,128)(2,1)}, bf16[144,128]{1,0:T(8,128)(2,1)S(1)}, u32[]{:S(2)}, u32[]{:S(2)}) collective-permute-start(bf16[144,128]{1,0:T(8,128)(2,1)} %get-tuple-element.6.refs_3_), channel_id=1, source_target_pairs={{0,8},{1,9},{2,10},{3,11},{4,12},{5,13},{6,14},{7,15},{8,0},{9,1},... | collective-permute-start | bytes 110600 | tf_op jit(solution)/shard_map/ppermute | solution.py:382
  17.0 0.0 collective-permute-done.7.refs_10_
  17.0 2.3 %collective-permute-start.3 = (bf16[144,128]{1,0:T(8,128)(2,1)}, bf16[144,128]{1,0:T(8,128)(2,1)S(1)}, u32[]{:S(2)}, u32[]{:S(2)}) collective-permute-start(bf16[144,128]{1,0:T(8,128)(2,1)} %get-tuple-element.6.refs_3_), channel_id=1, source_target_pairs={{0,6},{1,7},{2,4},{3,5},{4,2},{5,3},{6,0},{7,1},{8,14},{9,15},{10,... | collective-permute-start | bytes 110600 | tf_op jit(solution)/shard_map/ppermute | solution.py:382
  19.3 0.8 %collective-permute-done.6.refs_9_ = bf16[144,128]{1,0:T(8,128)(2,1)S(1)} collective-permute-done((bf16[144,128]{1,0:T(8,128)(2,1)}, bf16[144,128]{1,0:T(8,128)(2,1)S(1)}, u32[]{:S(2)}, u32[]{:S(2)}) %collective-permute-start.6) | collective-permute-done | bytes 36896 | tf_op jit(solution)/shard_map/ppermute | solution.py:382
  20.0 0.0 collective-permute-start.2
  20.1 1.2 %collective-permute-done.5.refs_8_ = bf16[144,128]{1,0:T(8,128)(2,1)S(1)} collective-permute-done((bf16[144,128]{1,0:T(8,128)(2,1)}, bf16[144,128]{1,0:T(8,128)(2,1)S(1)}, u32[]{:S(2)}, u32[]{:S(2)}) %collective-permute-start.5) | collective-permute-done | bytes 36896 | tf_op jit(solution)/shard_map/ppermute | solution.py:382
  21.2 1.0 %collective-permute-start.1 = (bf16[144,128]{1,0:T(8,128)(2,1)}, bf16[144,128]{1,0:T(8,128)(2,1)S(1)}, u32[]{:S(2)}, u32[]{:S(2)}) collective-permute-start(bf16[144,128]{1,0:T(8,128)(2,1)} %get-tuple-element.6.refs_3_), channel_id=1, source_target_pairs={{0,2},{1,3},{2,0},{3,1},{4,6},{5,7},{6,4},{7,5},{8,10},{9,11},{10,... | collective-permute-start | bytes 110600 | tf_op jit(solution)/shard_map/ppermute | solution.py:382
  22.3 0.0 collective-permute-done.4.refs_7_
  22.3 0.5 %collective-permute-done.3.refs_6_ = bf16[144,128]{1,0:T(8,128)(2,1)S(1)} collective-permute-done((bf16[144,128]{1,0:T(8,128)(2,1)}, bf16[144,128]{1,0:T(8,128)(2,1)S(1)}, u32[]{:S(2)}, u32[]{:S(2)}) %collective-permute-start.3) | collective-permute-done | bytes 36896 | tf_op jit(solution)/shard_map/ppermute | solution.py:382
  22.7 1.5 %collective-permute-done.2.refs_5_ = bf16[144,128]{1,0:T(8,128)(2,1)S(1)} collective-permute-done((bf16[144,128]{1,0:T(8,128)(2,1)}, bf16[144,128]{1,0:T(8,128)(2,1)S(1)}, u32[]{:S(2)}, u32[]{:S(2)}) %collective-permute-start.2) | collective-permute-done | bytes 36896 | tf_op jit(solution)/shard_map/ppermute | solution.py:382
  24.2 1.2 %collective-permute-done.1.refs_4_ = bf16[144,128]{1,0:T(8,128)(2,1)S(1)} collective-permute-done((bf16[144,128]{1,0:T(8,128)(2,1)}, bf16[144,128]{1,0:T(8,128)(2,1)S(1)}, u32[]{:S(2)}, u32[]{:S(2)}) %collective-permute-start.1) | collective-permute-done | bytes 36896 | tf_op jit(solution)/shard_map/ppermute | solution.py:382
  25.4 0.0 collective-permute-done.refs_2_
  25.4 0.0 copy-start
  25.4 1.4 %copy-done = bf16[48,128,128]{2,1,0:T(8,128)(2,1)S(1)} copy-done((bf16[48,128,128]{2,1,0:T(8,128)(2,1)S(1)}, bf16[48,128,128]{2,1,0:T(8,128)(2,1)}, u32[]{:S(2)}) %copy-start) | copy-done | bytes 1572888
  26.8 0.0 copy-start.1
  26.8 0.8 %copy-done.1 = bf16[144,128]{1,0:T(8,128)(2,1)S(1)} copy-done((bf16[144,128]{1,0:T(8,128)(2,1)S(1)}, bf16[144,128]{1,0:T(8,128)(2,1)}, u32[]{:S(2)}) %copy-start.1) | copy-done | bytes 36888
  27.6 4.7 %score.1 = f32[8,128]{1,0:T(8,128)S(1)} custom-call(s32[1]{0:T(128)} %bitcast.refs_0_, bf16[48,128,128]{2,1,0:T(8,128)(2,1)S(1)} %copy-done, bf16[48,128,128]{2,1,0:T(8,128)(2,1)S(1)} %collective-permute-done.refs_2_, bf16[144,128]{1,0:T(8,128)(2,1)S(1)} %copy-done.1, bf16[144,128]{1,0:T(8,128)(2,1)S(1)} %collective-permute-done.1.refs_4_, ...), custom_call_target="tpu_custom_call" | custom-call | flops 805306368 | bytes 3145728 | tf_op jit(solution)/shard_map/score/pallas_call | solution.py:321
  32.3 10.5 %all_to_all.11 = f32[8,1,128]{2,1,0:T(1,128)S(1)} all-to-all(f32[8,1,128]{2,1,0:T(1,128)S(1)} %bitcast.5), channel_id=1, replica_groups={{0,2,4,6,8,10,12,14},{1,3,5,7,9,11,13,15},{16,18,20,22,24,26,28,30},{17..., dimensions={0} | all-to-all | bytes 8192 | tf_op jit(solution)/shard_map/all_to_all | solution.py:418
  42.8 0.0 copy-done.2
  42.8 1.0 %finish.1 = (f32[4,64]{1,0:T(4,128)}, f32[4,10]{1,0:T(4,128)}) custom-call(f32[8,128]{1,0:T(8,128)S(1)} %bitcast.6, s32[4,64]{1,0:T(4,128)S(1)} %copy-done.2), custom_call_target="tpu_custom_call" | custom-call | tf_op jit(solution)/shard_map/finish/pallas_call | solution.py:367
Async XLA Ops:
  7.8 35.0 %copy-start.2 = (s32[4,64]{1,0:T(4,128)S(1)}, s32[4,64]{1,0:T(4,128)}, u32[]{:S(2)}) copy-start(s32[4,64]{1,0:T(4,128)} %get-tuple-element.7.spot_ref) | copy-start | bytes 3076
  7.8 17.6 %collective-permute-start = (bf16[48,128,128]{2,1,0:T(8,128)(2,1)}, bf16[48,128,128]{2,1,0:T(8,128)(2,1)S(1)}, u32[]{:S(2)}, u32[]{:S(2)}) collective-permute-start(bf16[48,128,128]{2,1,0:T(8,128)(2,1)} %get-tuple-element.5.refs_1_), channel_id=1, source_target_pairs={{0,1},{1,0},{2,3},{3,2},{4,5},{5,4},{6,7},{7,6},{8,9},{9,8},{10,11... | collective-permute-start | bytes 4718600 | tf_op jit(solution)/shard_map/ppermute | solution.py:382
  8.3 8.7 %collective-permute-start.7 = (bf16[144,128]{1,0:T(8,128)(2,1)}, bf16[144,128]{1,0:T(8,128)(2,1)S(1)}, u32[]{:S(2)}, u32[]{:S(2)}) collective-permute-start(bf16[144,128]{1,0:T(8,128)(2,1)} %get-tuple-element.6.refs_3_), channel_id=1, source_target_pairs={{0,14},{1,15},{2,12},{3,13},{4,10},{5,11},{6,8},{7,9},{8,6},{9,7},... | collective-permute-start | bytes 110600 | tf_op jit(solution)/shard_map/ppermute | solution.py:382
  14.0 6.1 %collective-permute-start.6 = (bf16[144,128]{1,0:T(8,128)(2,1)}, bf16[144,128]{1,0:T(8,128)(2,1)S(1)}, u32[]{:S(2)}, u32[]{:S(2)}) collective-permute-start(bf16[144,128]{1,0:T(8,128)(2,1)} %get-tuple-element.6.refs_3_), channel_id=1, source_target_pairs={{0,12},{1,13},{2,14},{3,15},{4,8},{5,9},{6,10},{7,11},{8,4},{9,5},... | collective-permute-start | bytes 110600 | tf_op jit(solution)/shard_map/ppermute | solution.py:382
  14.2 7.0 %collective-permute-start.5 = (bf16[144,128]{1,0:T(8,128)(2,1)}, bf16[144,128]{1,0:T(8,128)(2,1)S(1)}, u32[]{:S(2)}, u32[]{:S(2)}) collective-permute-start(bf16[144,128]{1,0:T(8,128)(2,1)} %get-tuple-element.6.refs_3_), channel_id=1, source_target_pairs={{0,10},{1,11},{2,8},{3,9},{4,14},{5,15},{6,12},{7,13},{8,2},{9,3},... | collective-permute-start | bytes 110600 | tf_op jit(solution)/shard_map/ppermute | solution.py:382
  14.9 7.3 %collective-permute-start.4 = (bf16[144,128]{1,0:T(8,128)(2,1)}, bf16[144,128]{1,0:T(8,128)(2,1)S(1)}, u32[]{:S(2)}, u32[]{:S(2)}) collective-permute-start(bf16[144,128]{1,0:T(8,128)(2,1)} %get-tuple-element.6.refs_3_), channel_id=1, source_target_pairs={{0,8},{1,9},{2,10},{3,11},{4,12},{5,13},{6,14},{7,15},{8,0},{9,1},... | collective-permute-start | bytes 110600 | tf_op jit(solution)/shard_map/ppermute | solution.py:382
  17.0 5.7 %collective-permute-start.3 = (bf16[144,128]{1,0:T(8,128)(2,1)}, bf16[144,128]{1,0:T(8,128)(2,1)S(1)}, u32[]{:S(2)}, u32[]{:S(2)}) collective-permute-start(bf16[144,128]{1,0:T(8,128)(2,1)} %get-tuple-element.6.refs_3_), channel_id=1, source_target_pairs={{0,6},{1,7},{2,4},{3,5},{4,2},{5,3},{6,0},{7,1},{8,14},{9,15},{10,... | collective-permute-start | bytes 110600 | tf_op jit(solution)/shard_map/ppermute | solution.py:382
  20.0 4.2 %collective-permute-start.2 = (bf16[144,128]{1,0:T(8,128)(2,1)}, bf16[144,128]{1,0:T(8,128)(2,1)S(1)}, u32[]{:S(2)}, u32[]{:S(2)}) collective-permute-start(bf16[144,128]{1,0:T(8,128)(2,1)} %get-tuple-element.6.refs_3_), channel_id=1, source_target_pairs={{0,4},{1,5},{2,6},{3,7},{4,0},{5,1},{6,2},{7,3},{8,12},{9,13},{10,... | collective-permute-start | bytes 110600 | tf_op jit(solution)/shard_map/ppermute | solution.py:382
  21.2 4.2 %collective-permute-start.1 = (bf16[144,128]{1,0:T(8,128)(2,1)}, bf16[144,128]{1,0:T(8,128)(2,1)S(1)}, u32[]{:S(2)}, u32[]{:S(2)}) collective-permute-start(bf16[144,128]{1,0:T(8,128)(2,1)} %get-tuple-element.6.refs_3_), channel_id=1, source_target_pairs={{0,2},{1,3},{2,0},{3,1},{4,6},{5,7},{6,4},{7,5},{8,10},{9,11},{10,... | collective-permute-start | bytes 110600 | tf_op jit(solution)/shard_map/ppermute | solution.py:382
  25.4 1.4 %copy-start = (bf16[48,128,128]{2,1,0:T(8,128)(2,1)S(1)}, bf16[48,128,128]{2,1,0:T(8,128)(2,1)}, u32[]{:S(2)}) copy-start(bf16[48,128,128]{2,1,0:T(8,128)(2,1)} %get-tuple-element.5.refs_1_) | copy-start | bytes 4718596
  26.8 0.8 %copy-start.1 = (bf16[144,128]{1,0:T(8,128)(2,1)S(1)}, bf16[144,128]{1,0:T(8,128)(2,1)}, u32[]{:S(2)}) copy-start(bf16[144,128]{1,0:T(8,128)(2,1)} %get-tuple-element.6.refs_3_) | copy-start | bytes 110596

commit v7 on v6

--- a/solution.py
+++ b/solution.py
@@ -20,6 +20,31 @@
     middle = rest.astype(BF16)
     low = (rest - middle.astype(F32)).astype(BF16)
     return high, middle, low
+
+
+def gelu(value):
+    size = jnp.abs(value)
+    inverse = 1.0 / (1.0 + (0.3275911 * 0.5 ** 0.5) * size)
+    tail = 0.5 * 1.061405429
+    for factor in (-1.453152027, 1.421413741, -0.284496736, 0.254829592):
+        tail = tail * inverse + 0.5 * factor
+    tail = tail * inverse * jnp.exp(-0.5 * value * value)
+    return jnp.maximum(value, 0.0) - size * tail
+
+
+def mask_into(out_ref, pass_ref, len_ref, first, count):
+    def mask(p, carry):
+        block = pass_ref[p]
+        keep = lax.broadcasted_iota(jnp.int32, block.shape, 0) < len_ref[p]
+        block = block.astype(F32)
+        out_ref[p] = jnp.where(keep, block, jnp.broadcast_to(block[0:1], block.shape)).astype(BF16)
+        return carry
+
+    if count <= 8:
+        for p in range(first, first + count):
+            mask(p, 0)
+    else:
+        lax.fori_loop(first, first + count, mask, 0, unroll=8)
 
 
 def encode_kernel(
@@ -123,11 +148,7 @@
 
     def mask(c):
         loads[c].wait()
-        for p in range(c * batch, (c + 1) * batch):
-            block = pass_buf[p]
-            keep = lax.broadcasted_iota(jnp.int32, block.shape, 0) < plen_ref[p]
-            block = block.astype(F32)
-            pass_buf[p] = jnp.where(keep, block, jnp.broadcast_to(block[0:1], block.shape)).astype(BF16)
+        mask_into(pass_buf, pass_buf, plen_ref, c * batch, batch)
         saves[c].start()
 
     small[2].wait()
@@ -147,7 +168,7 @@
         if step >= 2:
             total = total + jnp.dot(active, w2_buf[step - 2], preferred_element_type=F32)
         if 1 <= step <= chunks:
-            active = (0.5 * inner * (1.0 + lax.erf(inner * (0.5 ** 0.5)))).astype(BF16)
+            active = gelu(inner).astype(BF16)
         inner = later
         if step == chunks:
             fetch = pltpu.make_async_copy(table, table_v, table_sem)
@@ -170,8 +191,10 @@
     vectors = vectors.astype(BF16)
     fetch.wait()
     tokens = query_count * token_count
-    out_ref[pl.ds(0, tokens), :] = vectors
-    out_ref[pl.ds(tokens, slots), :] = table_v[...].astype(F32).astype(BF16)
+    wanted = table_v[...].astype(F32).astype(BF16)
+    for z in range(out_ref.shape[0]):
+        out_ref[z, pl.ds(0, tokens), :] = vectors
+        out_ref[z, pl.ds(tokens, slots), :] = wanted
     for save in saves:
         save.wait()
 
@@ -196,6 +219,7 @@
     passage_row,
     candidates,
     slots,
+    outer,
 ):
     query_count, token_count, d = query_hidden.shape
     ff = inner_weight.shape[1]
@@ -214,7 +238,7 @@
     return pl.pallas_call(
         kernel,
         out_shape=(
-            jax.ShapeDtypeStruct((tokens + slots, e), BF16),
+            jax.ShapeDtypeStruct((outer, tokens + slots, e), BF16),
             jax.ShapeDtypeStruct(passage_vectors.shape, BF16),
             jax.ShapeDtypeStruct(candidates.shape, jnp.int32),
         ),
@@ -258,25 +282,27 @@
     )
 
 
-def score_kernel(slots, token_count, me_ref, pass0_ref, pass1_ref, *refs):
-    got_refs = refs[:slots]
-    out_ref, best_ref, index_v, index, sem = refs[slots:]
-    message, lanes = got_refs[0].shape
-    half = pass0_ref.shape[0]
+def score_kernel(inner, token_count, me_ref, len_ref, raw_ref, other_ref, *refs):
+    got_refs = refs[:inner]
+    out_ref, best_ref, own_ref, index_v, index, sem = refs[inner:]
+    outer, message, lanes = got_refs[0].shape
+    half = own_ref.shape[0]
+    slots = inner * outer
     rows = -(-slots // 16) * 16
     tokens = message - rows
     group = min(slots, 256 // token_count)
     chip = jnp.right_shift(me_ref[0], 1)
     mine = lax.broadcasted_iota(jnp.int32, (rows, lanes), 0) == chip
     for s in range(slots):
-        table = got_refs[s][pl.ds(tokens, rows), :].astype(F32)
+        table = got_refs[s // outer][s % outer, pl.ds(tokens, rows), :].astype(F32)
         query = jnp.sum(jnp.where(mine, table, 0.0), axis=0, keepdims=True)
         index_v[s:s + 1, :] = query.astype(jnp.int32) * token_count
     copy = pltpu.make_async_copy(index_v, index, sem)
     copy.start()
+    mask_into(own_ref, raw_ref, len_ref, 0, half)
     copy.wait()
 
-    for side, pass_ref in enumerate((pass0_ref, pass1_ref)):
+    for first, pass_ref in ((half, other_ref), (0, own_ref)):
 
         def eight(step, carry):
             for part in range(slots // group):
@@ -285,7 +311,9 @@
                     p = step * 8 + j
                     picked = jnp.concatenate(
                         [
-                            got_refs[s][pl.ds(pl.multiple_of(index[s, side * half + p], token_count), token_count), :]
+                            got_refs[s // outer][
+                                s % outer, pl.ds(pl.multiple_of(index[s, first + p], token_count), token_count), :
+                            ]
                             for s in range(part * group, (part + 1) * group)
                         ],
                         axis=0,
@@ -293,7 +321,7 @@
                     similar = lax.dot_general(pass_ref[p], picked, NT, preferred_element_type=F32)
                     rows.append(jnp.max(similar, axis=0, keepdims=True))
                 best_ref[
-                    pl.ds(pl.multiple_of(side * half + step * 8, 8), 8),
+                    pl.ds(pl.multiple_of(first + step * 8, 8), 8),
                     pl.ds(part * group * token_count, group * token_count),
                 ] = jnp.concatenate(rows, axis=0)
             return carry
@@ -302,29 +330,32 @@
     wide = best_ref.shape[1]
     source = lax.broadcasted_iota(jnp.int32, (slots, wide), 0)
     column = lax.broadcasted_iota(jnp.int32, (slots, wide), 1)
-    first = source * token_count
-    ones = jnp.where((column >= first) & (column < first + token_count), 1.0, 0.0).astype(BF16)
+    start = source * token_count
+    ones = jnp.where((column >= start) & (column < start + token_count), 1.0, 0.0).astype(BF16)
     total = sum(lax.dot_general(ones, part, NT, preferred_element_type=F32) for part in split3(best_ref[...]))
     out_ref[...] = jnp.zeros(out_ref.shape, F32)
     for s in range(slots):
-        out_ref[pl.ds(jnp.bitwise_xor(chip, s), 1), pl.ds(0, 2 * half)] = total[s:s + 1]
-
-
-def score(me, got, own, other, token_count):
+        out_ref[s % outer, s // outer:s // outer + 1, pl.ds(0, 2 * half)] = total[s:s + 1]
+
+
+def score(me, lengths, got, own, other, token_count):
     half, plen, e = own.shape
     passage_count = 2 * half
-    slots = len(got)
+    inner = len(got)
+    outer = got[0].shape[0]
+    slots = inner * outer
 
     def kernel(*refs):
-        score_kernel(slots, token_count, *refs)
+        score_kernel(inner, token_count, *refs)
 
     return pl.pallas_call(
         kernel,
-        out_shape=jax.ShapeDtypeStruct((slots, e), F32),
-        in_specs=[SMEM] + [VMEM] * (2 + slots),
+        out_shape=jax.ShapeDtypeStruct((outer, inner, e), F32),
+        in_specs=[SMEM, SMEM, VMEM, VMEM] + [VMEM] * inner,
         out_specs=VMEM,
         scratch_shapes=[
             pltpu.VMEM((passage_count, slots * token_count), F32),
+            pltpu.VMEM(own.shape, BF16),
             pltpu.VMEM((slots, e), jnp.int32),
             pltpu.SMEM((slots, e), jnp.int32),
             pltpu.SemaphoreType.DMA,
@@ -336,20 +367,24 @@
             transcendentals=0,
         ),
         name="score",
-    )(me, own, other, *got)
-
-
-def finish_kernel(got_ref, spot_ref, scores_ref, best_ref):
-    slots, lanes = got_ref.shape
+    )(me, lengths, own, other, *got)
+
+
+def finish_kernel(inner, me_ref, *refs):
+    got_refs = refs[:inner]
+    spot_ref, scores_ref, best_ref = refs[inner:]
+    outer, _, lanes = got_refs[0].shape
+    slots = inner * outer
     query_count, cand_count = scores_ref.shape
-    parts = split3(got_ref[...])
+    chip = jnp.right_shift(me_ref[0], 1)
+    parts = split3(jnp.concatenate([got_refs[d][z, d:d + 1, :] for z in range(outer) for d in range(inner)], axis=0))
     slot_iota = lax.broadcasted_iota(jnp.int32, (slots, cand_count), 0) * lanes
     lane_iota = lax.broadcasted_iota(jnp.int32, (lanes, cand_count), 0)
     row_iota = lax.broadcasted_iota(jnp.int32, (cand_count, cand_count), 0)
     col_iota = lax.broadcasted_iota(jnp.int32, (cand_count, cand_count), 1)
     place = lax.broadcasted_iota(jnp.int32, (cand_count, 128), 1)
     for i in range(query_count):
-        spot = spot_ref[i:i + 1, :]
+        spot = jnp.bitwise_xor(spot_ref[i:i + 1, :], jnp.bitwise_and(chip, inner - 1) * lanes)
         lane = jnp.bitwise_and(spot, lanes - 1)
         onehot = jnp.where(lane_iota == lane, 1.0, 0.0).astype(BF16)
         picked = sum(jnp.dot(part, onehot, preferred_element_type=F32) for part in parts)
@@ -363,18 +398,23 @@
         best_ref[i:i + 1, :] = ordered[:, :TOPN]
 
 
-def finish(got, spots):
+def finish(me, got, spots):
+    inner = len(got)
+
+    def kernel(*refs):
+        finish_kernel(inner, *refs)
+
     return pl.pallas_call(
-        finish_kernel,
+        kernel,
         out_shape=(
             jax.ShapeDtypeStruct(spots.shape, F32),
             jax.ShapeDtypeStruct((spots.shape[0], TOPN), F32),
         ),
-        in_specs=[VMEM, VMEM],
+        in_specs=[SMEM] + [VMEM] * (inner + 1),
         out_specs=(VMEM, VMEM),
         compiler_params=pltpu.CompilerParams(vmem_limit_bytes=2 ** 21),
         name="finish",
-    )(got, spots)
+    )(me, *got, spots)
 
 
 def swap(value, distance):
@@ -396,9 +436,13 @@
 ):
     size = lax.axis_size("shard")
     slots = size // 2
-    groups = [list(range(core, size, 2)) for core in range(2)]
+    inner = 1
+    while 4 * inner * inner <= slots:
+        inner *= 2
+    outer = slots // inner
+    lines = [[(z * inner + y) * 2 + core for z in range(outer)] for y in range(inner) for core in range(2)]
     me = lax.axis_index("shard").astype(jnp.int32).reshape(1)
-    message, own, spots = encode(
+    message, masked, spots = encode(
         me,
         query_hidden,
         query_lengths,
@@ -411,12 +455,17 @@
         passage_row,
         candidates,
         slots,
+        outer,
     )
-    got = [message] + [swap(message, 2 * d) for d in range(1, slots)]
-    other = swap(own, 1)
-    sums = score(me, got, own, other, query_hidden.shape[1])
-    back = lax.all_to_all(sums, "shard", split_axis=0, concat_axis=0, axis_index_groups=groups, tiled=True)
-    return finish(back, spots)
+    other = swap(masked, 1)
+
+    def exchange(value):
+        line = lax.all_to_all(value, "shard", split_axis=0, concat_axis=0, axis_index_groups=lines, tiled=True)
+        return [line] + [swap(line, 2 * d) for d in range(1, inner)]
+
+    got = exchange(message)
+    sums = score(me, passage_lengths, got, passage_vectors, other, query_hidden.shape[1])
+    return finish(me, exchange(sums), spots)
 
 
 def solution(mesh):

time: 44.1 us -> 46.3 us (1.050)
  blocking collectives: 10.5 us -> 21.4 us
  starting transfers between devices: 12.5 us -> 3.52 us
  local copies, waits for them, and re-layouts: 2.18 us -> 0.01 us
  Pallas kernels: 12.8 us -> 14.7 us
  waiting for transfers between devices: 5.09 us -> 5.72 us
    all_to_all x1 -> x2, blocking collectives: 10.5 us -> 21.4 us  [exchange(): lax.all_to_all(value, 'shard', split_axis=0, concat_axis=0, axis_index_gr...]
    ppermute x8 -> x3, starting transfers between devices: 12.5 us -> 3.52 us  [swap(): lax.ppermute(value, 'shard', [(i, i ^ distance) for i in range(size)])]
    unnamed x6, local copies, waits for them, and re-layouts: 2.18 us -> 0.01 us
    pallas_call x3, Pallas kernels: 12.8 us -> 14.7 us  [the longest x1 8.55 us: encode(): pl.pallas_call(kernel, out_shape=(jax.ShapeDtypeStruct((outer, tokens + s...]
    ppermute x8 -> x3, waiting for transfers between devices: 5.09 us -> 5.72 us  [swap(): lax.ppermute(value, 'shard', [(i, i ^ distance) for i in range(size)])]
  transfers between devices with their start and end apart: 8 -> 3, of which waited for: 5 -> 2; matrix products, arithmetic and copies ran while one was open for 0% -> 0% of each run, Pallas kernels for 0% -> 0%
where the time goes in v7:
time: 46.3 us; the launch traced here: 46.1 us
  blocking collectives  21.4 us (46%)
  Pallas kernels  14.7 us (32%)
  waiting for transfers between devices  5.72 us (12%)
  starting transfers between devices  3.52 us (8%)
  between operations  0.68 us (1%)
    all_to_all x2, blocking collectives, exchange(): lax.all_to_all(value, 'shard', split_axis=0, concat_axis=0, axis_index_gr...  21.4 us
    pallas_call x1, Pallas kernels, encode(): pl.pallas_call(kernel, out_shape=(jax.ShapeDtypeStruct((outer, tokens + s...  8.55 us
    ppermute x3, waiting for transfers between devices, swap(): lax.ppermute(value, 'shard', [(i, i ^ distance) for i in range(size)])  5.72 us
    pallas_call x1, Pallas kernels, score(): pl.pallas_call(kernel, out_shape=jax.ShapeDtypeStruct((outer, inner, e),...  5.18 us
    ppermute x3, starting transfers between devices, swap(): lax.ppermute(value, 'shard', [(i, i ^ distance) for i in range(size)])  3.52 us
    pallas_call x1, Pallas kernels, finish(): pl.pallas_call(kernel, out_shape=(jax.ShapeDtypeStruct(spots.shape, F32),...  0.99 us
  transfers between devices with their start and end apart: 3, of which 2 were waited for; matrix products, arithmetic and copies ran while one was open for 0% of the time, Pallas kernels for 0%

profile of v7, /device:TPU:0, one launch (start us, length us, event | category | flops | bytes accessed | tf_op | source)
XLA Modules:
  0.0 46.1 jit_solution(14274126725585374422)
XLA Ops:
  0.6 0.0 copy-start
  0.6 0.0 copy-start.1
  0.7 8.6 %encode.1 = (bf16[4,144,128]{2,1,0:T(8,128)(2,1)}, bf16[48,128,128]{2,1,0:T(8,128)(2,1)}, s32[4,64]{1,0:T(4,128)}) custom-call(s32[1]{0:T(128)} %bitcast.refs_0_, s32[4]{0:T(128)} %refs_1_.2, s32[48]{0:T(128)} %refs_1_.3, s32[768]{0:T(1024)} %refs_3_.1, s32[4,64]{1,0:T(4,128)} %refs_4_.1, bf16[4,32,768]{2,1,0:T(8,128)(2,1)} %refs_5_.1, ...), custom_call_target="tpu_custom_call" | custom-call | flops 1207959552 | bytes 9437184 | tf_op jit(solution)/shard_map/encode/pallas_call | solution.py:238
  9.2 0.5 %collective-permute-start = (bf16[48,128,128]{2,1,0:T(8,128)(2,1)}, bf16[48,128,128]{2,1,0:T(8,128)(2,1)S(1)}, u32[]{:S(2)}, u32[]{:S(2)}) collective-permute-start(bf16[48,128,128]{2,1,0:T(8,128)(2,1)} %get-tuple-element.5), channel_id=1, source_target_pairs={{0,1},{1,0},{2,3},{3,2},{4,5},{5,4},{6,7},{7,6},{8,9},{9,8},{10,11... | collective-permute-start | bytes 4718600 | tf_op jit(solution)/shard_map/ppermute | solution.py:422
  9.7 13.0 %all_to_all.10.refs_4_ = bf16[4,144,128]{2,1,0:T(8,128)(2,1)S(1)} all-to-all(bf16[4,144,128]{2,1,0:T(8,128)(2,1)} %get-tuple-element.6), channel_id=1, replica_groups={{0,4,8,12},{1,5,9,13},{2,6,10,14},{3,7,11,15},{16,20,24,28},{17,21,25,2..., dimensions={0} | all-to-all | bytes 294912 | tf_op jit(solution)/shard_map/all_to_all | solution.py:463
  22.7 0.0 copy-start.2
  22.7 1.5 %collective-permute-start.1 = (bf16[4,144,128]{2,1,0:T(8,128)(2,1)S(1)}, bf16[4,144,128]{2,1,0:T(8,128)(2,1)S(1)}, u32[]{:S(2)}, u32[]{:S(2)}) collective-permute-start(bf16[4,144,128]{2,1,0:T(8,128)(2,1)S(1)} %all_to_all.10.refs_4_), channel_id=1, source_target_pairs={{0,2},{1,3},{2,0},{3,1},{4,6},{5,7},{6,4},{7,5},{8,10},{9,11},{10,... | collective-permute-start | bytes 442376 | tf_op jit(solution)/shard_map/ppermute | solution.py:422
  24.2 3.6 %collective-permute-done.1.refs_5_ = bf16[4,144,128]{2,1,0:T(8,128)(2,1)S(1)} collective-permute-done((bf16[4,144,128]{2,1,0:T(8,128)(2,1)S(1)}, bf16[4,144,128]{2,1,0:T(8,128)(2,1)S(1)}, u32[]{:S(2)}, u32[]{:S(2)}) %collective-permute-start.1) | collective-permute-done | bytes 147488 | tf_op jit(solution)/shard_map/ppermute | solution.py:422
  27.8 0.0 collective-permute-done.refs_3_
  27.8 0.0 copy-done
  27.8 0.0 copy-done.1
  27.8 5.2 %score.1 = f32[4,2,128]{2,1,0:T(2,128)S(1)} custom-call(s32[1]{0:T(128)} %bitcast.refs_0_, s32[48]{0:T(128)S(1)} %copy-done.1, bf16[48,128,128]{2,1,0:T(8,128)(2,1)S(1)} %copy-done, bf16[48,128,128]{2,1,0:T(8,128)(2,1)S(1)} %collective-permute-done.refs_3_, bf16[4,144,128]{2,1,0:T(8,128)(2,1)S(1)} %all_to_all.10.refs_4_, ...), custom_call_target="tpu_custom_call" | custom-call | flops 805306368 | bytes 3145728 | tf_op jit(solution)/shard_map/score/pallas_call | solution.py:351
  33.0 8.5 %all_to_all.11.refs_1_ = f32[4,2,128]{2,1,0:T(2,128)S(1)} all-to-all(f32[4,2,128]{2,1,0:T(2,128)S(1)} %score.1), channel_id=1, replica_groups={{0,4,8,12},{1,5,9,13},{2,6,10,14},{3,7,11,15},{16,20,24,28},{17,21,25,2..., dimensions={0} | all-to-all | bytes 8192 | tf_op jit(solution)/shard_map/all_to_all | solution.py:463
  41.5 1.5 %collective-permute-start.2 = (f32[4,2,128]{2,1,0:T(2,128)S(1)}, f32[4,2,128]{2,1,0:T(2,128)S(1)}, u32[]{:S(2)}, u32[]{:S(2)}) collective-permute-start(f32[4,2,128]{2,1,0:T(2,128)S(1)} %all_to_all.11.refs_1_), channel_id=1, source_target_pairs={{0,2},{1,3},{2,0},{3,1},{4,6},{5,7},{6,4},{7,5},{8,10},{9,11},{10,... | collective-permute-start | bytes 12296 | tf_op jit(solution)/shard_map/ppermute | solution.py:422
  43.0 2.1 %collective-permute-done.2.refs_2_ = f32[4,2,128]{2,1,0:T(2,128)S(1)} collective-permute-done((f32[4,2,128]{2,1,0:T(2,128)S(1)}, f32[4,2,128]{2,1,0:T(2,128)S(1)}, u32[]{:S(2)}, u32[]{:S(2)}) %collective-permute-start.2) | collective-permute-done | bytes 4128 | tf_op jit(solution)/shard_map/ppermute | solution.py:422
  45.1 0.0 copy-done.2
  45.1 1.0 %finish.1 = (f32[4,64]{1,0:T(4,128)}, f32[4,10]{1,0:T(4,128)}) custom-call(s32[1]{0:T(128)} %bitcast.refs_0_, f32[4,2,128]{2,1,0:T(2,128)S(1)} %all_to_all.11.refs_1_, f32[4,2,128]{2,1,0:T(2,128)S(1)} %collective-permute-done.2.refs_2_, s32[4,64]{1,0:T(4,128)S(1)} %copy-done.2), custom_call_target="tpu_custom_call" | custom-call | tf_op jit(solution)/shard_map/finish/pallas_call | solution.py:407
Async XLA Ops:
  0.6 27.2 %copy-start = (bf16[48,128,128]{2,1,0:T(8,128)(2,1)S(1)}, bf16[48,128,128]{2,1,0:T(8,128)(2,1)}, u32[]{:S(2)}) copy-start(bf16[48,128,128]{2,1,0:T(8,128)(2,1)} %refs_2_.3) | copy-start | bytes 4718596
  0.6 27.2 %copy-start.1 = (s32[48]{0:T(128)S(1)}, s32[48]{0:T(128)}, u32[]{:S(2)}) copy-start(s32[48]{0:T(128)} %refs_1_.3) | copy-start | bytes 580
  9.2 18.6 %collective-permute-start = (bf16[48,128,128]{2,1,0:T(8,128)(2,1)}, bf16[48,128,128]{2,1,0:T(8,128)(2,1)S(1)}, u32[]{:S(2)}, u32[]{:S(2)}) collective-permute-start(bf16[48,128,128]{2,1,0:T(8,128)(2,1)} %get-tuple-element.5), channel_id=1, source_target_pairs={{0,1},{1,0},{2,3},{3,2},{4,5},{5,4},{6,7},{7,6},{8,9},{9,8},{10,11... | collective-permute-start | bytes 4718600 | tf_op jit(solution)/shard_map/ppermute | solution.py:422
  22.7 22.4 %copy-start.2 = (s32[4,64]{1,0:T(4,128)S(1)}, s32[4,64]{1,0:T(4,128)}, u32[]{:S(2)}) copy-start(s32[4,64]{1,0:T(4,128)} %get-tuple-element.7.refs_3_) | copy-start | bytes 3076
  22.7 5.1 %collective-permute-start.1 = (bf16[4,144,128]{2,1,0:T(8,128)(2,1)S(1)}, bf16[4,144,128]{2,1,0:T(8,128)(2,1)S(1)}, u32[]{:S(2)}, u32[]{:S(2)}) collective-permute-start(bf16[4,144,128]{2,1,0:T(8,128)(2,1)S(1)} %all_to_all.10.refs_4_), channel_id=1, source_target_pairs={{0,2},{1,3},{2,0},{3,1},{4,6},{5,7},{6,4},{7,5},{8,10},{9,11},{10,... | collective-permute-start | bytes 442376 | tf_op jit(solution)/shard_map/ppermute | solution.py:422
  41.5 3.6 %collective-permute-start.2 = (f32[4,2,128]{2,1,0:T(2,128)S(1)}, f32[4,2,128]{2,1,0:T(2,128)S(1)}, u32[]{:S(2)}, u32[]{:S(2)}) collective-permute-start(f32[4,2,128]{2,1,0:T(2,128)S(1)} %all_to_all.11.refs_1_), channel_id=1, source_target_pairs={{0,2},{1,3},{2,0},{3,1},{4,6},{5,7},{6,4},{7,5},{8,10},{9,11},{10,... | collective-permute-start | bytes 12296 | tf_op jit(solution)/shard_map/ppermute | solution.py:422

commit v8 on v6

--- a/solution.py
+++ b/solution.py
@@ -20,6 +20,21 @@
     middle = rest.astype(BF16)
     low = (rest - middle.astype(F32)).astype(BF16)
     return high, middle, low
+
+
+def mask_into(out_ref, pass_ref, len_ref, first, count):
+    def mask(p, carry):
+        block = pass_ref[p]
+        keep = lax.broadcasted_iota(jnp.int32, block.shape, 0) < len_ref[p]
+        block = block.astype(F32)
+        out_ref[p] = jnp.where(keep, block, jnp.broadcast_to(block[0:1], block.shape)).astype(BF16)
+        return carry
+
+    if count <= 8:
+        for p in range(first, first + count):
+            mask(p, 0)
+    else:
+        lax.fori_loop(first, first + count, mask, 0, unroll=8)
 
 
 def encode_kernel(
@@ -123,11 +138,7 @@
 
     def mask(c):
         loads[c].wait()
-        for p in range(c * batch, (c + 1) * batch):
-            block = pass_buf[p]
-            keep = lax.broadcasted_iota(jnp.int32, block.shape, 0) < plen_ref[p]
-            block = block.astype(F32)
-            pass_buf[p] = jnp.where(keep, block, jnp.broadcast_to(block[0:1], block.shape)).astype(BF16)
+        mask_into(pass_buf, pass_buf, plen_ref, c * batch, batch)
         saves[c].start()
 
     small[2].wait()
@@ -170,8 +181,9 @@
     vectors = vectors.astype(BF16)
     fetch.wait()
     tokens = query_count * token_count
+    wanted = table_v[...].astype(F32).astype(BF16)
     out_ref[pl.ds(0, tokens), :] = vectors
-    out_ref[pl.ds(tokens, slots), :] = table_v[...].astype(F32).astype(BF16)
+    out_ref[pl.ds(tokens, slots), :] = wanted
     for save in saves:
         save.wait()
 
@@ -258,11 +270,11 @@
     )
 
 
-def score_kernel(slots, token_count, me_ref, pass0_ref, pass1_ref, *refs):
+def score_kernel(slots, token_count, me_ref, len_ref, raw_ref, other_ref, *refs):
     got_refs = refs[:slots]
-    out_ref, best_ref, index_v, index, sem = refs[slots:]
+    out_ref, best_ref, own_ref, index_v, index, sem = refs[slots:]
     message, lanes = got_refs[0].shape
-    half = pass0_ref.shape[0]
+    half = own_ref.shape[0]
     rows = -(-slots // 16) * 16
     tokens = message - rows
     group = min(slots, 256 // token_count)
@@ -274,9 +286,10 @@
         index_v[s:s + 1, :] = query.astype(jnp.int32) * token_count
     copy = pltpu.make_async_copy(index_v, index, sem)
     copy.start()
+    mask_into(own_ref, raw_ref, len_ref, 0, half)
     copy.wait()
 
-    for side, pass_ref in enumerate((pass0_ref, pass1_ref)):
+    for first, pass_ref in ((half, other_ref), (0, own_ref)):
 
         def eight(step, carry):
             for part in range(slots // group):
@@ -285,7 +298,7 @@
                     p = step * 8 + j
                     picked = jnp.concatenate(
                         [
-                            got_refs[s][pl.ds(pl.multiple_of(index[s, side * half + p], token_count), token_count), :]
+                            got_refs[s][pl.ds(pl.multiple_of(index[s, first + p], token_count), token_count), :]
                             for s in range(part * group, (part + 1) * group)
                         ],
                         axis=0,
@@ -293,7 +306,7 @@
                     similar = lax.dot_general(pass_ref[p], picked, NT, preferred_element_type=F32)
                     rows.append(jnp.max(similar, axis=0, keepdims=True))
                 best_ref[
-                    pl.ds(pl.multiple_of(side * half + step * 8, 8), 8),
+                    pl.ds(pl.multiple_of(first + step * 8, 8), 8),
                     pl.ds(part * group * token_count, group * token_count),
                 ] = jnp.concatenate(rows, axis=0)
             return carry
@@ -302,15 +315,15 @@
     wide = best_ref.shape[1]
     source = lax.broadcasted_iota(jnp.int32, (slots, wide), 0)
     column = lax.broadcasted_iota(jnp.int32, (slots, wide), 1)
-    first = source * token_count
-    ones = jnp.where((column >= first) & (column < first + token_count), 1.0, 0.0).astype(BF16)
+    start = source * token_count
+    ones = jnp.where((column >= start) & (column < start + token_count), 1.0, 0.0).astype(BF16)
     total = sum(lax.dot_general(ones, part, NT, preferred_element_type=F32) for part in split3(best_ref[...]))
     out_ref[...] = jnp.zeros(out_ref.shape, F32)
     for s in range(slots):
         out_ref[pl.ds(jnp.bitwise_xor(chip, s), 1), pl.ds(0, 2 * half)] = total[s:s + 1]
 
 
-def score(me, got, own, other, token_count):
+def score(me, lengths, got, own, other, token_count):
     half, plen, e = own.shape
     passage_count = 2 * half
     slots = len(got)
@@ -321,10 +334,11 @@
     return pl.pallas_call(
         kernel,
         out_shape=jax.ShapeDtypeStruct((slots, e), F32),
-        in_specs=[SMEM] + [VMEM] * (2 + slots),
+        in_specs=[SMEM, SMEM, VMEM, VMEM] + [VMEM] * slots,
         out_specs=VMEM,
         scratch_shapes=[
             pltpu.VMEM((passage_count, slots * token_count), F32),
+            pltpu.VMEM(own.shape, BF16),
             pltpu.VMEM((slots, e), jnp.int32),
             pltpu.SMEM((slots, e), jnp.int32),
             pltpu.SemaphoreType.DMA,
@@ -336,7 +350,7 @@
             transcendentals=0,
         ),
         name="score",
-    )(me, own, other, *got)
+    )(me, lengths, own, other, *got)
 
 
 def finish_kernel(got_ref, spot_ref, scores_ref, best_ref):
@@ -396,9 +410,12 @@
 ):
     size = lax.axis_size("shard")
     slots = size // 2
+    inner = 1
+    while 4 * inner * inner <= slots:
+        inner *= 2
     groups = [list(range(core, size, 2)) for core in range(2)]
     me = lax.axis_index("shard").astype(jnp.int32).reshape(1)
-    message, own, spots = encode(
+    message, masked, spots = encode(
         me,
         query_hidden,
         query_lengths,
@@ -412,9 +429,11 @@
         candidates,
         slots,
     )
-    got = [message] + [swap(message, 2 * d) for d in range(1, slots)]
-    other = swap(own, 1)
-    sums = score(me, got, own, other, query_hidden.shape[1])
+    other = swap(masked, 1)
+
+    line = [message] + [swap(message, 2 * d) for d in range(slots - inner, 0, -inner)][::-1]
+    got = [line[s // inner] if s % inner == 0 else swap(line[s // inner], 2 * (s % inner)) for s in range(slots)]
+    sums = score(me, passage_lengths, got, passage_vectors, other, query_hidden.shape[1])
     back = lax.all_to_all(sums, "shard", split_axis=0, concat_axis=0, axis_index_groups=groups, tiled=True)
     return finish(back, spots)
 

time: 44.1 us -> 40.7 us (0.923)
  starting transfers between devices: 12.5 us -> 10.8 us
  local copies, waits for them, and re-layouts: 2.18 us -> 0.78 us
  Pallas kernels: 12.8 us -> 13.7 us
  blocking collectives: 10.5 us -> 9.63 us
    ppermute x8, starting transfers between devices: 12.5 us -> 10.8 us  [swap(): lax.ppermute(value, 'shard', [(i, i ^ distance) for i in range(size)])]
    unnamed x6 -> x8, local copies, waits for them, and re-layouts: 2.18 us -> 0.78 us
    all_to_all x1, blocking collectives: 10.5 us -> 9.63 us  [per_device(): lax.all_to_all(sums, 'shard', split_axis=0, concat_axis=0, axis_index_gro...]
    pallas_call x1, Pallas kernels: 4.68 us -> 5.17 us  [score(): pl.pallas_call(kernel, out_shape=jax.ShapeDtypeStruct((slots, e), F32), i...]
  transfers between devices with their start and end apart: 8 -> 8, of which waited for: 5 -> 3; matrix products, arithmetic and copies ran while one was open for 0% -> 0% of each run, Pallas kernels for 0% -> 0%
where the time goes in v8:
time: 40.7 us; the launch traced here: 40.5 us
  Pallas kernels  13.7 us (34%)
  starting transfers between devices  10.8 us (27%)
  blocking collectives  9.63 us (24%)
  waiting for transfers between devices  4.85 us (12%)
  local copies, waits for them, and re-layouts  0.78 us (2%)
  between operations  0.7 us (2%)
    ppermute x8, starting transfers between devices, swap(): lax.ppermute(value, 'shard', [(i, i ^ distance) for i in range(size)])  10.8 us
    all_to_all x1, blocking collectives, per_device(): lax.all_to_all(sums, 'shard', split_axis=0, concat_axis=0, axis_index_gro...  9.63 us
    pallas_call x1, Pallas kernels, encode(): pl.pallas_call(kernel, out_shape=(jax.ShapeDtypeStruct((tokens + slots, e...  7.54 us
    pallas_call x1, Pallas kernels, score(): pl.pallas_call(kernel, out_shape=jax.ShapeDtypeStruct((slots, e), F32), i...  5.17 us
    ppermute x8, waiting for transfers between devices, swap(): lax.ppermute(value, 'shard', [(i, i ^ distance) for i in range(size)])  4.85 us
    pallas_call x1, Pallas kernels, finish(): pl.pallas_call(finish_kernel, out_shape=(jax.ShapeDtypeStruct(spots.shape...  0.99 us
  transfers between devices with their start and end apart: 8, of which 3 were waited for; matrix products, arithmetic and copies ran while one was open for 0% of the time, Pallas kernels for 0%

profile of v8, /device:TPU:0, one launch (start us, length us, event | category | flops | bytes accessed | tf_op | source)
XLA Modules:
  0.0 40.5 jit_solution(14781982050877064725)
XLA Ops:
  0.6 0.0 copy-start
  0.6 0.0 copy-start.2
  0.7 7.5 %encode.1 = (bf16[144,128]{1,0:T(8,128)(2,1)}, bf16[48,128,128]{2,1,0:T(8,128)(2,1)}, s32[4,64]{1,0:T(4,128)}) custom-call(s32[1]{0:T(128)} %bitcast.refs_0_, s32[4]{0:T(128)} %refs_1_.2, s32[48]{0:T(128)} %refs_1_.3, s32[768]{0:T(1024)} %refs_3_.1, s32[4,64]{1,0:T(4,128)} %refs_4_.1, bf16[4,32,768]{2,1,0:T(8,128)(2,1)} %refs_5_.1, ...), custom_call_target="tpu_custom_call" | custom-call | flops 1207959552 | bytes 9437184 | tf_op jit(solution)/shard_map/encode/pallas_call | solution.py:226
  8.2 0.0 copy-start.3
  8.2 0.5 %collective-permute-start = (bf16[48,128,128]{2,1,0:T(8,128)(2,1)}, bf16[48,128,128]{2,1,0:T(8,128)(2,1)S(1)}, u32[]{:S(2)}, u32[]{:S(2)}) collective-permute-start(bf16[48,128,128]{2,1,0:T(8,128)(2,1)} %get-tuple-element.5), channel_id=1, source_target_pairs={{0,1},{1,0},{2,3},{3,2},{4,5},{5,4},{6,7},{7,6},{8,9},{9,8},{10,11... | collective-permute-start | bytes 4718600 | tf_op jit(solution)/shard_map/ppermute | solution.py:396
  8.7 2.6 %collective-permute-start.2 = (bf16[144,128]{1,0:T(8,128)(2,1)}, bf16[144,128]{1,0:T(8,128)(2,1)S(1)}, u32[]{:S(2)}, u32[]{:S(2)}) collective-permute-start(bf16[144,128]{1,0:T(8,128)(2,1)} %get-tuple-element.6.refs_4_), channel_id=1, source_target_pairs={{0,4},{1,5},{2,6},{3,7},{4,0},{5,1},{6,2},{7,3},{8,12},{9,13},{10,... | collective-permute-start | bytes 110600 | tf_op jit(solution)/shard_map/ppermute | solution.py:396
  11.3 2.6 %collective-permute-start.4 = (bf16[144,128]{1,0:T(8,128)(2,1)}, bf16[144,128]{1,0:T(8,128)(2,1)S(1)}, u32[]{:S(2)}, u32[]{:S(2)}) collective-permute-start(bf16[144,128]{1,0:T(8,128)(2,1)} %get-tuple-element.6.refs_4_), channel_id=1, source_target_pairs={{0,8},{1,9},{2,10},{3,11},{4,12},{5,13},{6,14},{7,15},{8,0},{9,1},... | collective-permute-start | bytes 110600 | tf_op jit(solution)/shard_map/ppermute | solution.py:396
  14.0 0.0 collective-permute-start.6
  14.0 1.8 %collective-permute-start.1 = (bf16[144,128]{1,0:T(8,128)(2,1)}, bf16[144,128]{1,0:T(8,128)(2,1)S(1)}, u32[]{:S(2)}, u32[]{:S(2)}) collective-permute-start(bf16[144,128]{1,0:T(8,128)(2,1)} %get-tuple-element.6.refs_4_), channel_id=1, source_target_pairs={{0,2},{1,3},{2,0},{3,1},{4,6},{5,7},{6,4},{7,5},{8,10},{9,11},{10,... | collective-permute-start | bytes 110600 | tf_op jit(solution)/shard_map/ppermute | solution.py:396
  15.7 0.0 collective-permute-done.2.refs_6_
  15.7 0.3 collective-permute-start.3
  16.0 1.2 %collective-permute-done.4.refs_8_ = bf16[144,128]{1,0:T(8,128)(2,1)S(1)} collective-permute-done((bf16[144,128]{1,0:T(8,128)(2,1)}, bf16[144,128]{1,0:T(8,128)(2,1)S(1)}, u32[]{:S(2)}, u32[]{:S(2)}) %collective-permute-start.4) | collective-permute-done | bytes 36896 | tf_op jit(solution)/shard_map/ppermute | solution.py:396
  17.1 1.5 %collective-permute-start.5 = (bf16[144,128]{1,0:T(8,128)(2,1)S(1)}, bf16[144,128]{1,0:T(8,128)(2,1)S(1)}, u32[]{:S(2)}, u32[]{:S(2)}) collective-permute-start(bf16[144,128]{1,0:T(8,128)(2,1)S(1)} %collective-permute-done.4.refs_8_), channel_id=1, source_target_pairs={{0,2},{1,3},{2,0},{3,1},{4,6},{5,7},{6,4},{7,5},{8,10},{9,11},{10,... | collective-permute-start | bytes 110600 | tf_op jit(solution)/shard_map/ppermute | solution.py:396
  18.7 1.2 %collective-permute-done.6.refs_10_ = bf16[144,128]{1,0:T(8,128)(2,1)S(1)} collective-permute-done((bf16[144,128]{1,0:T(8,128)(2,1)}, bf16[144,128]{1,0:T(8,128)(2,1)S(1)}, u32[]{:S(2)}, u32[]{:S(2)}) %collective-permute-start.6) | collective-permute-done | bytes 36896 | tf_op jit(solution)/shard_map/ppermute | solution.py:396
  19.9 1.5 %collective-permute-start.7 = (bf16[144,128]{1,0:T(8,128)(2,1)S(1)}, bf16[144,128]{1,0:T(8,128)(2,1)S(1)}, u32[]{:S(2)}, u32[]{:S(2)}) collective-permute-start(bf16[144,128]{1,0:T(8,128)(2,1)S(1)} %collective-permute-done.6.refs_10_), channel_id=1, source_target_pairs={{0,2},{1,3},{2,0},{3,1},{4,6},{5,7},{6,4},{7,5},{8,10},{9,11},{10,... | collective-permute-start | bytes 110600 | tf_op jit(solution)/shard_map/ppermute | solution.py:396
  21.4 0.0 collective-permute-done.1.refs_5_
  21.4 0.0 collective-permute-done.3.refs_7_
  21.4 0.0 collective-permute-done.5.refs_9_
  21.4 2.4 %collective-permute-done.7.refs_11_ = bf16[144,128]{1,0:T(8,128)(2,1)S(1)} collective-permute-done((bf16[144,128]{1,0:T(8,128)(2,1)S(1)}, bf16[144,128]{1,0:T(8,128)(2,1)S(1)}, u32[]{:S(2)}, u32[]{:S(2)}) %collective-permute-start.7) | collective-permute-done | bytes 36896 | tf_op jit(solution)/shard_map/ppermute | solution.py:396
  23.9 0.0 collective-permute-done.refs_3_
  23.9 0.0 copy-done
  23.9 0.0 copy-done.2
  23.9 0.0 copy-start.1
  23.9 0.8 %copy-done.1 = bf16[144,128]{1,0:T(8,128)(2,1)S(1)} copy-done((bf16[144,128]{1,0:T(8,128)(2,1)S(1)}, bf16[144,128]{1,0:T(8,128)(2,1)}, u32[]{:S(2)}) %copy-start.1) | copy-done | bytes 36888
  24.7 5.2 %score.1 = f32[8,128]{1,0:T(8,128)S(1)} custom-call(s32[1]{0:T(128)} %bitcast.refs_0_, s32[48]{0:T(128)S(1)} %copy-done.2, bf16[48,128,128]{2,1,0:T(8,128)(2,1)S(1)} %copy-done, bf16[48,128,128]{2,1,0:T(8,128)(2,1)S(1)} %collective-permute-done.refs_3_, bf16[144,128]{1,0:T(8,128)(2,1)S(1)} %copy-done.1, bf16[144,128]{1,0:T(8,128)(2,1)S(1)} %collective-permute-done.1.refs_5_, ...), custom_call_target="tpu_custom_call" | custom-call | flops 805306368 | bytes 3145728 | tf_op jit(solution)/shard_map/score/pallas_call | solution.py:334
  29.8 9.6 %all_to_all.11 = f32[8,1,128]{2,1,0:T(1,128)S(1)} all-to-all(f32[8,1,128]{2,1,0:T(1,128)S(1)} %bitcast.5), channel_id=1, replica_groups={{0,2,4,6,8,10,12,14},{1,3,5,7,9,11,13,15},{16,18,20,22,24,26,28,30},{17..., dimensions={0} | all-to-all | bytes 8192 | tf_op jit(solution)/shard_map/all_to_all | solution.py:437
  39.5 0.0 copy-done.3
  39.5 1.0 %finish.1 = (f32[4,64]{1,0:T(4,128)}, f32[4,10]{1,0:T(4,128)}) custom-call(f32[8,128]{1,0:T(8,128)S(1)} %bitcast.6, s32[4,64]{1,0:T(4,128)S(1)} %copy-done.3), custom_call_target="tpu_custom_call" | custom-call | tf_op jit(solution)/shard_map/finish/pallas_call | solution.py:381
Async XLA Ops:
  0.6 23.3 %copy-start = (bf16[48,128,128]{2,1,0:T(8,128)(2,1)S(1)}, bf16[48,128,128]{2,1,0:T(8,128)(2,1)}, u32[]{:S(2)}) copy-start(bf16[48,128,128]{2,1,0:T(8,128)(2,1)} %refs_2_.3) | copy-start | bytes 4718596
  0.6 23.2 %copy-start.2 = (s32[48]{0:T(128)S(1)}, s32[48]{0:T(128)}, u32[]{:S(2)}) copy-start(s32[48]{0:T(128)} %refs_1_.3) | copy-start | bytes 580
  8.2 31.3 %copy-start.3 = (s32[4,64]{1,0:T(4,128)S(1)}, s32[4,64]{1,0:T(4,128)}, u32[]{:S(2)}) copy-start(s32[4,64]{1,0:T(4,128)} %get-tuple-element.7.spot_ref) | copy-start | bytes 3076
  8.2 15.7 %collective-permute-start = (bf16[48,128,128]{2,1,0:T(8,128)(2,1)}, bf16[48,128,128]{2,1,0:T(8,128)(2,1)S(1)}, u32[]{:S(2)}, u32[]{:S(2)}) collective-permute-start(bf16[48,128,128]{2,1,0:T(8,128)(2,1)} %get-tuple-element.5), channel_id=1, source_target_pairs={{0,1},{1,0},{2,3},{3,2},{4,5},{5,4},{6,7},{7,6},{8,9},{9,8},{10,11... | collective-permute-start | bytes 4718600 | tf_op jit(solution)/shard_map/ppermute | solution.py:396
  8.7 7.0 %collective-permute-start.2 = (bf16[144,128]{1,0:T(8,128)(2,1)}, bf16[144,128]{1,0:T(8,128)(2,1)S(1)}, u32[]{:S(2)}, u32[]{:S(2)}) collective-permute-start(bf16[144,128]{1,0:T(8,128)(2,1)} %get-tuple-element.6.refs_4_), channel_id=1, source_target_pairs={{0,4},{1,5},{2,6},{3,7},{4,0},{5,1},{6,2},{7,3},{8,12},{9,13},{10,... | collective-permute-start | bytes 110600 | tf_op jit(solution)/shard_map/ppermute | solution.py:396
  11.3 5.8 %collective-permute-start.4 = (bf16[144,128]{1,0:T(8,128)(2,1)}, bf16[144,128]{1,0:T(8,128)(2,1)S(1)}, u32[]{:S(2)}, u32[]{:S(2)}) collective-permute-start(bf16[144,128]{1,0:T(8,128)(2,1)} %get-tuple-element.6.refs_4_), channel_id=1, source_target_pairs={{0,8},{1,9},{2,10},{3,11},{4,12},{5,13},{6,14},{7,15},{8,0},{9,1},... | collective-permute-start | bytes 110600 | tf_op jit(solution)/shard_map/ppermute | solution.py:396
  14.0 6.0 %collective-permute-start.6 = (bf16[144,128]{1,0:T(8,128)(2,1)}, bf16[144,128]{1,0:T(8,128)(2,1)S(1)}, u32[]{:S(2)}, u32[]{:S(2)}) collective-permute-start(bf16[144,128]{1,0:T(8,128)(2,1)} %get-tuple-element.6.refs_4_), channel_id=1, source_target_pairs={{0,12},{1,13},{2,14},{3,15},{4,8},{5,9},{6,10},{7,11},{8,4},{9,5},... | collective-permute-start | bytes 110600 | tf_op jit(solution)/shard_map/ppermute | solution.py:396
  14.0 7.5 %collective-permute-start.1 = (bf16[144,128]{1,0:T(8,128)(2,1)}, bf16[144,128]{1,0:T(8,128)(2,1)S(1)}, u32[]{:S(2)}, u32[]{:S(2)}) collective-permute-start(bf16[144,128]{1,0:T(8,128)(2,1)} %get-tuple-element.6.refs_4_), channel_id=1, source_target_pairs={{0,2},{1,3},{2,0},{3,1},{4,6},{5,7},{6,4},{7,5},{8,10},{9,11},{10,... | collective-permute-start | bytes 110600 | tf_op jit(solution)/shard_map/ppermute | solution.py:396
  15.7 5.7 %collective-permute-start.3 = (bf16[144,128]{1,0:T(8,128)(2,1)S(1)}, bf16[144,128]{1,0:T(8,128)(2,1)S(1)}, u32[]{:S(2)}, u32[]{:S(2)}) collective-permute-start(bf16[144,128]{1,0:T(8,128)(2,1)S(1)} %collective-permute-done.2.refs_6_), channel_id=1, source_target_pairs={{0,2},{1,3},{2,0},{3,1},{4,6},{5,7},{6,4},{7,5},{8,10},{9,11},{10,... | collective-permute-start | bytes 110600 | tf_op jit(solution)/shard_map/ppermute | solution.py:396
  17.1 4.3 %collective-permute-start.5 = (bf16[144,128]{1,0:T(8,128)(2,1)S(1)}, bf16[144,128]{1,0:T(8,128)(2,1)S(1)}, u32[]{:S(2)}, u32[]{:S(2)}) collective-permute-start(bf16[144,128]{1,0:T(8,128)(2,1)S(1)} %collective-permute-done.4.refs_8_), channel_id=1, source_target_pairs={{0,2},{1,3},{2,0},{3,1},{4,6},{5,7},{6,4},{7,5},{8,10},{9,11},{10,... | collective-permute-start | bytes 110600 | tf_op jit(solution)/shard_map/ppermute | solution.py:396
  19.9 4.0 %collective-permute-start.7 = (bf16[144,128]{1,0:T(8,128)(2,1)S(1)}, bf16[144,128]{1,0:T(8,128)(2,1)S(1)}, u32[]{:S(2)}, u32[]{:S(2)}) collective-permute-start(bf16[144,128]{1,0:T(8,128)(2,1)S(1)} %collective-permute-done.6.refs_10_), channel_id=1, source_target_pairs={{0,2},{1,3},{2,0},{3,1},{4,6},{5,7},{6,4},{7,5},{8,10},{9,11},{10,... | collective-permute-start | bytes 110600 | tf_op jit(solution)/shard_map/ppermute | solution.py:396
  23.9 0.8 %copy-start.1 = (bf16[144,128]{1,0:T(8,128)(2,1)S(1)}, bf16[144,128]{1,0:T(8,128)(2,1)}, u32[]{:S(2)}) copy-start(bf16[144,128]{1,0:T(8,128)(2,1)} %get-tuple-element.6.refs_4_) | copy-start | bytes 110596

commit v9 on v8

--- a/solution.py
+++ b/solution.py
@@ -38,7 +38,6 @@
 
 
 def encode_kernel(
-    inverse,
     half,
     me_ref,
     lens_hbm,
@@ -60,6 +59,7 @@
     lens_ref,
     plen_ref,
     row_ref,
+    place_ref,
     cand_ref,
     x_ref,
     gain_ref,
@@ -68,6 +68,7 @@
     table_v,
     sems,
     small_sems,
+    place_sem,
     table_sem,
     pass_sems,
 ):
@@ -87,9 +88,9 @@
         pltpu.make_async_copy(source, target, small_sems.at[n])
         for n, (source, target) in enumerate(
             (
+                (x_hbm, x_ref),
                 (row_hbm, row_ref),
                 (cand_hbm, cand_ref),
-                (x_hbm, x_ref),
                 (plen_hbm, plen_ref),
                 (lens_hbm, lens_ref),
                 (gain_hbm, gain_ref),
@@ -97,15 +98,16 @@
             )
         )
     ]
-    for copy in small[:4]:
+    for copy in small[:3]:
         copy.start()
+    copies[0][0].start()
+    small[3].start()
     batch = half // chunks
     loads, saves = [], []
     for c in range(chunks):
         rows = pl.ds(c * batch, batch)
         loads.append(pltpu.make_async_copy(pass_hbm.at[rows], pass_buf.at[rows], pass_sems.at[0, c]))
         saves.append(pltpu.make_async_copy(pass_buf.at[rows], masked_hbm.at[rows], pass_sems.at[1, c]))
-    copies[0][0].start()
     copies[1][0].start()
     copies[0][1].start()
     for c in range(2, chunks):
@@ -118,22 +120,25 @@
     for copy in small[4:]:
         copy.start()
     clear.wait()
-    small[0].wait()
+    side = jnp.bitwise_and(me_ref[0], 1)
     small[1].wait()
-
-    side = jnp.bitwise_and(me_ref[0], 1)
+    row = row_ref[...]
+    owner = jnp.floor((row.astype(F32) + 0.5) * (1.0 / half)).astype(jnp.int32)
+    opposite = jnp.bitwise_xor(jnp.bitwise_and(owner, 1), side)
+    row_ref[...] = jnp.right_shift(owner, 1) * lanes + row - owner * half + opposite * half
+    placed = pltpu.make_async_copy(row_ref, place_ref, place_sem)
+    placed.start()
+    small[2].wait()
+    placed.wait()
 
     entries = [(i, k) for k in range(cand_count) for i in range(query_count)]
     share = -(-len(entries) // (chunks + 1))
 
     def enter():
         for i, k in entries[:share]:
-            row = row_ref[cand_ref[i, k]]
-            owner = inverse(row)
-            chip = jnp.right_shift(owner, 1)
-            place = row - owner * half + jnp.bitwise_xor(jnp.bitwise_and(owner, 1), side) * half
-            table[chip, place] = i
-            spot_ref[i, k] = chip * lanes + place
+            spot = place_ref[cand_ref[i, k]]
+            table[jnp.right_shift(spot, 7), jnp.bitwise_and(spot, 127)] = i
+            spot_ref[i, k] = spot
         del entries[:share]
 
     def mask(c):
@@ -141,7 +146,7 @@
         mask_into(pass_buf, pass_buf, plen_ref, c * batch, batch)
         saves[c].start()
 
-    small[2].wait()
+    small[0].wait()
     small[3].wait()
     x = x_ref[...].reshape(query_count * token_count, width_in)
     total = x.astype(F32)
@@ -188,13 +193,6 @@
         save.wait()
 
 
-def divider(divisor, limit):
-    magic = -(-(2 ** 20) // divisor)
-    if limit * magic < 2 ** 31 and all((v * magic) >> 20 == v // divisor for v in range(limit)):
-        return lambda value: jnp.right_shift(value * magic, 20)
-    return lambda value: value // divisor
-
-
 def encode(
     me,
     query_hidden,
@@ -214,14 +212,13 @@
     e = embed_weight.shape[1]
     half = passage_vectors.shape[0]
     slots = -(-slots // 16) * 16
-    assert 2 * half <= e
+    assert 2 * half <= e == 128
     chunks = 6
     width = ff // chunks
     tokens = query_count * token_count
-    inverse = divider(half, passage_row.shape[0])
 
     def kernel(*refs):
-        encode_kernel(inverse, half, *refs)
+        encode_kernel(half, *refs)
 
     return pl.pallas_call(
         kernel,
@@ -238,6 +235,7 @@
             pltpu.VMEM(passage_vectors.shape, BF16),
             pltpu.SMEM(query_lengths.shape, jnp.int32),
             pltpu.SMEM(passage_lengths.shape, jnp.int32),
+            pltpu.VMEM(passage_row.shape, jnp.int32),
             pltpu.SMEM(passage_row.shape, jnp.int32),
             pltpu.SMEM(candidates.shape, jnp.int32),
             pltpu.VMEM(query_hidden.shape, BF16),
@@ -247,6 +245,7 @@
             pltpu.VMEM((slots, e), jnp.int32),
             pltpu.SemaphoreType.DMA((2, chunks)),
             pltpu.SemaphoreType.DMA((7,)),
+            pltpu.SemaphoreType.DMA,
             pltpu.SemaphoreType.DMA,
             pltpu.SemaphoreType.DMA((2, chunks)),
         ],
@@ -270,9 +269,25 @@
     )
 
 
-def score_kernel(slots, token_count, me_ref, len_ref, raw_ref, other_ref, *refs):
+def mask_kernel(len_ref, pass_ref, *refs):
+    mask_into(refs[-1], pass_ref, len_ref, 0, pass_ref.shape[0])
+
+
+def mask(lengths, passages, late):
+    return pl.pallas_call(
+        mask_kernel,
+        out_shape=jax.ShapeDtypeStruct(passages.shape, BF16),
+        in_specs=[SMEM, VMEM, VMEM],
+        out_specs=VMEM,
+        compiler_params=pltpu.CompilerParams(vmem_limit_bytes=2 ** 22),
+        cost_estimate=pl.CostEstimate(flops=8 * passages.size, bytes_accessed=4 * passages.size, transcendentals=0),
+        name="mask",
+    )(lengths, passages, late)
+
+
+def score_kernel(slots, token_count, me_ref, own_ref, other_ref, *refs):
     got_refs = refs[:slots]
-    out_ref, best_ref, own_ref, index_v, index, sem = refs[slots:]
+    out_ref, best_ref, index_v, index, sem = refs[slots:]
     message, lanes = got_refs[0].shape
     half = own_ref.shape[0]
     rows = -(-slots // 16) * 16
@@ -286,7 +301,6 @@
         index_v[s:s + 1, :] = query.astype(jnp.int32) * token_count
     copy = pltpu.make_async_copy(index_v, index, sem)
     copy.start()
-    mask_into(own_ref, raw_ref, len_ref, 0, half)
     copy.wait()
 
     for first, pass_ref in ((half, other_ref), (0, own_ref)):
@@ -323,7 +337,7 @@
         out_ref[pl.ds(jnp.bitwise_xor(chip, s), 1), pl.ds(0, 2 * half)] = total[s:s + 1]
 
 
-def score(me, lengths, got, own, other, token_count):
+def score(me, got, own, other, token_count):
     half, plen, e = own.shape
     passage_count = 2 * half
     slots = len(got)
@@ -334,11 +348,10 @@
     return pl.pallas_call(
         kernel,
         out_shape=jax.ShapeDtypeStruct((slots, e), F32),
-        in_specs=[SMEM, SMEM, VMEM, VMEM] + [VMEM] * slots,
+        in_specs=[SMEM, VMEM, VMEM] + [VMEM] * slots,
         out_specs=VMEM,
         scratch_shapes=[
             pltpu.VMEM((passage_count, slots * token_count), F32),
-            pltpu.VMEM(own.shape, BF16),
             pltpu.VMEM((slots, e), jnp.int32),
             pltpu.SMEM((slots, e), jnp.int32),
             pltpu.SemaphoreType.DMA,
@@ -350,7 +363,7 @@
             transcendentals=0,
         ),
         name="score",
-    )(me, lengths, own, other, *got)
+    )(me, own, other, *got)
 
 
 def finish_kernel(got_ref, spot_ref, scores_ref, best_ref):
@@ -433,7 +446,8 @@
 
     line = [message] + [swap(message, 2 * d) for d in range(slots - inner, 0, -inner)][::-1]
     got = [line[s // inner] if s % inner == 0 else swap(line[s // inner], 2 * (s % inner)) for s in range(slots)]
-    sums = score(me, passage_lengths, got, passage_vectors, other, query_hidden.shape[1])
+    own = mask(passage_lengths, passage_vectors, got[inner + 1])
+    sums = score(me, got, own, other, query_hidden.shape[1])
     back = lax.all_to_all(sums, "shard", split_axis=0, concat_axis=0, axis_index_groups=groups, tiled=True)
     return finish(back, spots)
 

time: 40.7 us -> 39.5 us (0.971)
  waiting for transfers between devices: 4.85 us -> 3.89 us
  local copies, waits for them, and re-layouts: 0.78 us -> 0.02 us
  Pallas kernels: 13.7 us -> 14.2 us
    ppermute x8, waiting for transfers between devices: 4.85 us -> 3.89 us  [swap(): lax.ppermute(value, 'shard', [(i, i ^ distance) for i in range(size)])]
    pallas_call x0 -> x1, Pallas kernels: none -> 0.94 us  [mask(): pl.pallas_call(mask_kernel, out_shape=jax.ShapeDtypeStruct(passages.shape...]
    unnamed x8, local copies, waits for them, and re-layouts: 0.78 us -> 0.02 us
    pallas_call x1, Pallas kernels: 5.17 us -> 4.64 us  [score(): pl.pallas_call(kernel, out_shape=jax.ShapeDtypeStruct((slots, e), F32), i...]
  transfers between devices with their start and end apart: 8 -> 8, of which waited for: 3 -> 3; matrix products, arithmetic and copies ran while one was open for 0% -> 0% of each run, Pallas kernels for 0% -> 2%
where the time goes in v9:
time: 39.5 us; the launch traced here: 39.3 us
  Pallas kernels  14.2 us (36%)
  starting transfers between devices  10.8 us (27%)
  blocking collectives  9.66 us (24%)
  waiting for transfers between devices  3.89 us (10%)
  between operations  0.71 us (2%)
    ppermute x8, starting transfers between devices, swap(): lax.ppermute(value, 'shard', [(i, i ^ distance) for i in range(size)])  10.8 us
    all_to_all x1, blocking collectives, per_device(): lax.all_to_all(sums, 'shard', split_axis=0, concat_axis=0, axis_index_gro...  9.66 us
    pallas_call x1, Pallas kernels, encode(): pl.pallas_call(kernel, out_shape=(jax.ShapeDtypeStruct((tokens + slots, e...  7.61 us
    pallas_call x1, Pallas kernels, score(): pl.pallas_call(kernel, out_shape=jax.ShapeDtypeStruct((slots, e), F32), i...  4.64 us
    ppermute x8, waiting for transfers between devices, swap(): lax.ppermute(value, 'shard', [(i, i ^ distance) for i in range(size)])  3.89 us
    pallas_call x1, Pallas kernels, finish(): pl.pallas_call(finish_kernel, out_shape=(jax.ShapeDtypeStruct(spots.shape...  0.99 us
    pallas_call x1, Pallas kernels, mask(): pl.pallas_call(mask_kernel, out_shape=jax.ShapeDtypeStruct(passages.shape...  0.94 us
  transfers between devices with their start and end apart: 8, of which 3 were waited for; matrix products, arithmetic and copies ran while one was open for 0% of the time, Pallas kernels for 2%

profile of v9, /device:TPU:0, one launch (start us, length us, event | category | flops | bytes accessed | tf_op | source)
XLA Modules:
  0.0 39.3 jit_solution(7695615208856555942)
XLA Ops:
  0.6 0.0 copy-start
  0.6 0.0 copy-start.3
  0.7 7.6 %encode.1 = (bf16[144,128]{1,0:T(8,128)(2,1)}, bf16[48,128,128]{2,1,0:T(8,128)(2,1)}, s32[4,64]{1,0:T(4,128)}) custom-call(s32[1]{0:T(128)} %bitcast.refs_0_, s32[4]{0:T(128)} %refs_1_.1, s32[48]{0:T(128)} %len_ref.1, s32[768]{0:T(1024)} %refs_3_.1, s32[4,64]{1,0:T(4,128)} %refs_4_.1, bf16[4,32,768]{2,1,0:T(8,128)(2,1)} %refs_5_.1, ...), custom_call_target="tpu_custom_call" | custom-call | flops 1207959552 | bytes 9437184 | tf_op jit(solution)/shard_map/encode/pallas_call | solution.py:223
  8.3 0.5 %collective-permute-start.2 = (bf16[48,128,128]{2,1,0:T(8,128)(2,1)}, bf16[48,128,128]{2,1,0:T(8,128)(2,1)S(1)}, u32[]{:S(2)}, u32[]{:S(2)}) collective-permute-start(bf16[48,128,128]{2,1,0:T(8,128)(2,1)} %get-tuple-element.6), channel_id=1, source_target_pairs={{0,1},{1,0},{2,3},{3,2},{4,5},{5,4},{6,7},{7,6},{8,9},{9,8},{10,11... | collective-permute-start | bytes 4718600 | tf_op jit(solution)/shard_map/ppermute | solution.py:409
  8.8 0.0 copy-start.1
  8.8 2.7 %collective-permute-start = (bf16[144,128]{1,0:T(8,128)(2,1)}, bf16[144,128]{1,0:T(8,128)(2,1)S(1)}, u32[]{:S(2)}, u32[]{:S(2)}) collective-permute-start(bf16[144,128]{1,0:T(8,128)(2,1)} %get-tuple-element.5.refs_3_), channel_id=1, source_target_pairs={{0,4},{1,5},{2,6},{3,7},{4,0},{5,1},{6,2},{7,3},{8,12},{9,13},{10,... | collective-permute-start | bytes 110600 | tf_op jit(solution)/shard_map/ppermute | solution.py:409
  11.5 2.6 %collective-permute-start.4 = (bf16[144,128]{1,0:T(8,128)(2,1)}, bf16[144,128]{1,0:T(8,128)(2,1)S(1)}, u32[]{:S(2)}, u32[]{:S(2)}) collective-permute-start(bf16[144,128]{1,0:T(8,128)(2,1)} %get-tuple-element.5.refs_3_), channel_id=1, source_target_pairs={{0,8},{1,9},{2,10},{3,11},{4,12},{5,13},{6,14},{7,15},{8,0},{9,1},... | collective-permute-start | bytes 110600 | tf_op jit(solution)/shard_map/ppermute | solution.py:409
  14.1 0.0 collective-permute-start.6
  14.1 0.0 collective-permute-done.refs_5_
  14.1 1.7 %collective-permute-start.1 = (bf16[144,128]{1,0:T(8,128)(2,1)S(1)}, bf16[144,128]{1,0:T(8,128)(2,1)S(1)}, u32[]{:S(2)}, u32[]{:S(2)}) collective-permute-start(bf16[144,128]{1,0:T(8,128)(2,1)S(1)} %collective-permute-done.refs_5_), channel_id=1, source_target_pairs={{0,2},{1,3},{2,0},{3,1},{4,6},{5,7},{6,4},{7,5},{8,10},{9,11},{10,... | collective-permute-start | bytes 110600 | tf_op jit(solution)/shard_map/ppermute | solution.py:409
  15.8 0.3 collective-permute-start.3
  16.1 1.2 %collective-permute-done.4.refs_7_ = bf16[144,128]{1,0:T(8,128)(2,1)S(1)} collective-permute-done((bf16[144,128]{1,0:T(8,128)(2,1)}, bf16[144,128]{1,0:T(8,128)(2,1)S(1)}, u32[]{:S(2)}, u32[]{:S(2)}) %collective-permute-start.4) | collective-permute-done | bytes 36896 | tf_op jit(solution)/shard_map/ppermute | solution.py:409
  17.3 1.5 %collective-permute-start.5 = (bf16[144,128]{1,0:T(8,128)(2,1)S(1)}, bf16[144,128]{1,0:T(8,128)(2,1)S(1)}, u32[]{:S(2)}, u32[]{:S(2)}) collective-permute-start(bf16[144,128]{1,0:T(8,128)(2,1)S(1)} %collective-permute-done.4.refs_7_), channel_id=1, source_target_pairs={{0,2},{1,3},{2,0},{3,1},{4,6},{5,7},{6,4},{7,5},{8,10},{9,11},{10,... | collective-permute-start | bytes 110600 | tf_op jit(solution)/shard_map/ppermute | solution.py:409
  18.8 1.2 %collective-permute-done.6.refs_9_ = bf16[144,128]{1,0:T(8,128)(2,1)S(1)} collective-permute-done((bf16[144,128]{1,0:T(8,128)(2,1)}, bf16[144,128]{1,0:T(8,128)(2,1)S(1)}, u32[]{:S(2)}, u32[]{:S(2)}) %collective-permute-start.6) | collective-permute-done | bytes 36896 | tf_op jit(solution)/shard_map/ppermute | solution.py:409
  20.0 1.5 %collective-permute-start.7 = (bf16[144,128]{1,0:T(8,128)(2,1)S(1)}, bf16[144,128]{1,0:T(8,128)(2,1)S(1)}, u32[]{:S(2)}, u32[]{:S(2)}) collective-permute-start(bf16[144,128]{1,0:T(8,128)(2,1)S(1)} %collective-permute-done.6.refs_9_), channel_id=1, source_target_pairs={{0,2},{1,3},{2,0},{3,1},{4,6},{5,7},{6,4},{7,5},{8,10},{9,11},{10,... | collective-permute-start | bytes 110600 | tf_op jit(solution)/shard_map/ppermute | solution.py:409
  21.5 0.0 collective-permute-done.1.refs_0_.refs_6_
  21.5 0.0 copy-done
  21.5 0.0 copy-done.3
  21.6 0.9 %mask.1.refs_1_ = bf16[48,128,128]{2,1,0:T(8,128)(2,1)S(1)} custom-call(s32[48]{0:T(128)S(1)} %copy-done.3, bf16[48,128,128]{2,1,0:T(8,128)(2,1)S(1)} %copy-done, bf16[144,128]{1,0:T(8,128)(2,1)S(1)} %collective-permute-done.1.refs_0_.refs_6_), custom_call_target="tpu_custom_call" | custom-call | flops 6291456 | bytes 3145728 | tf_op jit(solution)/shard_map/mask/pallas_call | solution.py:277
  22.5 0.0 copy-start.2
  22.5 0.0 collective-permute-done.3.refs_4_
  22.5 0.0 collective-permute-done.5.refs_8_
  22.5 1.5 %collective-permute-done.7.refs_10_ = bf16[144,128]{1,0:T(8,128)(2,1)S(1)} collective-permute-done((bf16[144,128]{1,0:T(8,128)(2,1)S(1)}, bf16[144,128]{1,0:T(8,128)(2,1)S(1)}, u32[]{:S(2)}, u32[]{:S(2)}) %collective-permute-start.7) | collective-permute-done | bytes 36896 | tf_op jit(solution)/shard_map/ppermute | solution.py:409
  24.0 0.0 collective-permute-done.2.refs_2_
  24.0 0.0 copy-done.1
  24.0 4.6 %score.1 = f32[8,128]{1,0:T(8,128)S(1)} custom-call(s32[1]{0:T(128)} %bitcast.refs_0_, bf16[48,128,128]{2,1,0:T(8,128)(2,1)S(1)} %mask.1.refs_1_, bf16[48,128,128]{2,1,0:T(8,128)(2,1)S(1)} %collective-permute-done.2.refs_2_, bf16[144,128]{1,0:T(8,128)(2,1)S(1)} %copy-done.1, bf16[144,128]{1,0:T(8,128)(2,1)S(1)} %collective-permute-done.3.refs_4_, ...), custom_call_target="tpu_custom_call" | custom-call | flops 805306368 | bytes 3145728 | tf_op jit(solution)/shard_map/score/pallas_call | solution.py:348
  28.6 9.7 %all_to_all.11 = f32[8,1,128]{2,1,0:T(1,128)S(1)} all-to-all(f32[8,1,128]{2,1,0:T(1,128)S(1)} %bitcast.5), channel_id=1, replica_groups={{0,2,4,6,8,10,12,14},{1,3,5,7,9,11,13,15},{16,18,20,22,24,26,28,30},{17..., dimensions={0} | all-to-all | bytes 8192 | tf_op jit(solution)/shard_map/all_to_all | solution.py:451
  38.3 0.0 copy-done.2
  38.3 1.0 %finish.1 = (f32[4,64]{1,0:T(4,128)}, f32[4,10]{1,0:T(4,128)}) custom-call(f32[8,128]{1,0:T(8,128)S(1)} %bitcast.6, s32[4,64]{1,0:T(4,128)S(1)} %copy-done.2), custom_call_target="tpu_custom_call" | custom-call | tf_op jit(solution)/shard_map/finish/pallas_call | solution.py:394
Async XLA Ops:
  0.6 20.9 %copy-start = (bf16[48,128,128]{2,1,0:T(8,128)(2,1)S(1)}, bf16[48,128,128]{2,1,0:T(8,128)(2,1)}, u32[]{:S(2)}) copy-start(bf16[48,128,128]{2,1,0:T(8,128)(2,1)} %pass_ref.1) | copy-start | bytes 4718596
  0.6 20.9 %copy-start.3 = (s32[48]{0:T(128)S(1)}, s32[48]{0:T(128)}, u32[]{:S(2)}) copy-start(s32[48]{0:T(128)} %len_ref.1) | copy-start | bytes 580
  8.3 15.7 %collective-permute-start.2 = (bf16[48,128,128]{2,1,0:T(8,128)(2,1)}, bf16[48,128,128]{2,1,0:T(8,128)(2,1)S(1)}, u32[]{:S(2)}, u32[]{:S(2)}) collective-permute-start(bf16[48,128,128]{2,1,0:T(8,128)(2,1)} %get-tuple-element.6), channel_id=1, source_target_pairs={{0,1},{1,0},{2,3},{3,2},{4,5},{5,4},{6,7},{7,6},{8,9},{9,8},{10,11... | collective-permute-start | bytes 4718600 | tf_op jit(solution)/shard_map/ppermute | solution.py:409
  8.8 15.2 %copy-start.1 = (bf16[144,128]{1,0:T(8,128)(2,1)S(1)}, bf16[144,128]{1,0:T(8,128)(2,1)}, u32[]{:S(2)}) copy-start(bf16[144,128]{1,0:T(8,128)(2,1)} %get-tuple-element.5.refs_3_) | copy-start | bytes 110596
  8.8 5.3 %collective-permute-start = (bf16[144,128]{1,0:T(8,128)(2,1)}, bf16[144,128]{1,0:T(8,128)(2,1)S(1)}, u32[]{:S(2)}, u32[]{:S(2)}) collective-permute-start(bf16[144,128]{1,0:T(8,128)(2,1)} %get-tuple-element.5.refs_3_), channel_id=1, source_target_pairs={{0,4},{1,5},{2,6},{3,7},{4,0},{5,1},{6,2},{7,3},{8,12},{9,13},{10,... | collective-permute-start | bytes 110600 | tf_op jit(solution)/shard_map/ppermute | solution.py:409
  11.5 5.8 %collective-permute-start.4 = (bf16[144,128]{1,0:T(8,128)(2,1)}, bf16[144,128]{1,0:T(8,128)(2,1)S(1)}, u32[]{:S(2)}, u32[]{:S(2)}) collective-permute-start(bf16[144,128]{1,0:T(8,128)(2,1)} %get-tuple-element.5.refs_3_), channel_id=1, source_target_pairs={{0,8},{1,9},{2,10},{3,11},{4,12},{5,13},{6,14},{7,15},{8,0},{9,1},... | collective-permute-start | bytes 110600 | tf_op jit(solution)/shard_map/ppermute | solution.py:409
  14.1 6.0 %collective-permute-start.6 = (bf16[144,128]{1,0:T(8,128)(2,1)}, bf16[144,128]{1,0:T(8,128)(2,1)S(1)}, u32[]{:S(2)}, u32[]{:S(2)}) collective-permute-start(bf16[144,128]{1,0:T(8,128)(2,1)} %get-tuple-element.5.refs_3_), channel_id=1, source_target_pairs={{0,12},{1,13},{2,14},{3,15},{4,8},{5,9},{6,10},{7,11},{8,4},{9,5},... | collective-permute-start | bytes 110600 | tf_op jit(solution)/shard_map/ppermute | solution.py:409
  14.1 7.5 %collective-permute-start.1 = (bf16[144,128]{1,0:T(8,128)(2,1)S(1)}, bf16[144,128]{1,0:T(8,128)(2,1)S(1)}, u32[]{:S(2)}, u32[]{:S(2)}) collective-permute-start(bf16[144,128]{1,0:T(8,128)(2,1)S(1)} %collective-permute-done.refs_5_), channel_id=1, source_target_pairs={{0,2},{1,3},{2,0},{3,1},{4,6},{5,7},{6,4},{7,5},{8,10},{9,11},{10,... | collective-permute-start | bytes 110600 | tf_op jit(solution)/shard_map/ppermute | solution.py:409
  15.8 6.7 %collective-permute-start.3 = (bf16[144,128]{1,0:T(8,128)(2,1)}, bf16[144,128]{1,0:T(8,128)(2,1)S(1)}, u32[]{:S(2)}, u32[]{:S(2)}) collective-permute-start(bf16[144,128]{1,0:T(8,128)(2,1)} %get-tuple-element.5.refs_3_), channel_id=1, source_target_pairs={{0,2},{1,3},{2,0},{3,1},{4,6},{5,7},{6,4},{7,5},{8,10},{9,11},{10,... | collective-permute-start | bytes 110600 | tf_op jit(solution)/shard_map/ppermute | solution.py:409
  17.3 5.2 %collective-permute-start.5 = (bf16[144,128]{1,0:T(8,128)(2,1)S(1)}, bf16[144,128]{1,0:T(8,128)(2,1)S(1)}, u32[]{:S(2)}, u32[]{:S(2)}) collective-permute-start(bf16[144,128]{1,0:T(8,128)(2,1)S(1)} %collective-permute-done.4.refs_7_), channel_id=1, source_target_pairs={{0,2},{1,3},{2,0},{3,1},{4,6},{5,7},{6,4},{7,5},{8,10},{9,11},{10,... | collective-permute-start | bytes 110600 | tf_op jit(solution)/shard_map/ppermute | solution.py:409
  20.0 4.0 %collective-permute-start.7 = (bf16[144,128]{1,0:T(8,128)(2,1)S(1)}, bf16[144,128]{1,0:T(8,128)(2,1)S(1)}, u32[]{:S(2)}, u32[]{:S(2)}) collective-permute-start(bf16[144,128]{1,0:T(8,128)(2,1)S(1)} %collective-permute-done.6.refs_9_), channel_id=1, source_target_pairs={{0,2},{1,3},{2,0},{3,1},{4,6},{5,7},{6,4},{7,5},{8,10},{9,11},{10,... | collective-permute-start | bytes 110600 | tf_op jit(solution)/shard_map/ppermute | solution.py:409
  22.5 15.8 %copy-start.2 = (s32[4,64]{1,0:T(4,128)S(1)}, s32[4,64]{1,0:T(4,128)}, u32[]{:S(2)}) copy-start(s32[4,64]{1,0:T(4,128)} %get-tuple-element.7.spot_ref) | copy-start | bytes 3076

commit v10 on v9

--- a/solution.py
+++ b/solution.py
@@ -39,6 +39,7 @@
 
 def encode_kernel(
     half,
+    color,
     me_ref,
     lens_hbm,
     plen_hbm,
@@ -120,19 +121,16 @@
     for copy in small[4:]:
         copy.start()
     clear.wait()
-    side = jnp.bitwise_and(me_ref[0], 1)
     small[1].wait()
     row = row_ref[...]
     owner = jnp.floor((row.astype(F32) + 0.5) * (1.0 / half)).astype(jnp.int32)
-    opposite = jnp.bitwise_xor(jnp.bitwise_and(owner, 1), side)
+    opposite = jnp.bitwise_xor(color(owner), color(me_ref[0]))
     row_ref[...] = jnp.right_shift(owner, 1) * lanes + row - owner * half + opposite * half
     placed = pltpu.make_async_copy(row_ref, place_ref, place_sem)
     placed.start()
-    small[2].wait()
-    placed.wait()
 
     entries = [(i, k) for k in range(cand_count) for i in range(query_count)]
-    share = -(-len(entries) // (chunks + 1))
+    share = -(-len(entries) // chunks)
 
     def enter():
         for i, k in entries[:share]:
@@ -158,7 +156,11 @@
             copies[step - 2][1].wait()
         if 2 <= step < chunks:
             mask(step - 2)
-        enter()
+        if step == 1:
+            small[2].wait()
+            placed.wait()
+        if step >= 1:
+            enter()
         later = jnp.dot(x, w1_buf[step], preferred_element_type=F32) if step < chunks else None
         if step >= 2:
             total = total + jnp.dot(active, w2_buf[step - 2], preferred_element_type=F32)
@@ -206,6 +208,7 @@
     passage_row,
     candidates,
     slots,
+    color,
 ):
     query_count, token_count, d = query_hidden.shape
     ff = inner_weight.shape[1]
@@ -218,7 +221,7 @@
     tokens = query_count * token_count
 
     def kernel(*refs):
-        encode_kernel(half, *refs)
+        encode_kernel(half, color, *refs)
 
     return pl.pallas_call(
         kernel,
@@ -426,7 +429,16 @@
     inner = 1
     while 4 * inner * inner <= slots:
         inner *= 2
-    groups = [list(range(core, size, 2)) for core in range(2)]
+    shift = inner.bit_length()
+
+    def color(index):
+        return (index ^ (index >> 1) ^ (index >> shift)) & 1
+
+    groups = [[i for i in range(size) if color(i) == c] for c in range(2)]
+
+    def send(value, distance):
+        return swap(value, 2 * distance + color(2 * distance))
+
     me = lax.axis_index("shard").astype(jnp.int32).reshape(1)
     message, masked, spots = encode(
         me,
@@ -441,11 +453,12 @@
         passage_row,
         candidates,
         slots,
+        color,
     )
     other = swap(masked, 1)
 
-    line = [message] + [swap(message, 2 * d) for d in range(slots - inner, 0, -inner)][::-1]
-    got = [line[s // inner] if s % inner == 0 else swap(line[s // inner], 2 * (s % inner)) for s in range(slots)]
+    line = [message] + [send(message, d) for d in range(slots - inner, 0, -inner)][::-1]
+    got = [line[s // inner] if s % inner == 0 else send(line[s // inner], s % inner) for s in range(slots)]
     own = mask(passage_lengths, passage_vectors, got[inner + 1])
     sums = score(me, got, own, other, query_hidden.shape[1])
     back = lax.all_to_all(sums, "shard", split_axis=0, concat_axis=0, axis_index_groups=groups, tiled=True)

time: 39.5 us -> 39 us (0.987)
  starting transfers between devices: 10.8 us -> 9.07 us
  waiting for transfers between devices: 3.89 us -> 5.02 us
    ppermute x8, starting transfers between devices: 10.8 us -> 9.07 us  [swap(): lax.ppermute(value, 'shard', [(i, i ^ distance) for i in range(size)])]
    ppermute x8, waiting for transfers between devices: 3.89 us -> 5.02 us  [swap(): lax.ppermute(value, 'shard', [(i, i ^ distance) for i in range(size)])]
where the time goes in v10:
time: 39 us; the launch traced here: 38.8 us
  Pallas kernels  14.2 us (36%)
  blocking collectives  9.83 us (25%)
  starting transfers between devices  9.07 us (23%)
  waiting for transfers between devices  5.02 us (13%)
  between operations  0.71 us (2%)
    all_to_all x1, blocking collectives, per_device(): lax.all_to_all(sums, 'shard', split_axis=0, concat_axis=0, axis_index_gro...  9.83 us
    ppermute x8, starting transfers between devices, swap(): lax.ppermute(value, 'shard', [(i, i ^ distance) for i in range(size)])  9.07 us
    pallas_call x1, Pallas kernels, encode(): pl.pallas_call(kernel, out_shape=(jax.ShapeDtypeStruct((tokens + slots, e...  7.62 us
    ppermute x8, waiting for transfers between devices, swap(): lax.ppermute(value, 'shard', [(i, i ^ distance) for i in range(size)])  5.02 us
    pallas_call x1, Pallas kernels, score(): pl.pallas_call(kernel, out_shape=jax.ShapeDtypeStruct((slots, e), F32), i...  4.64 us
    pallas_call x1, Pallas kernels, finish(): pl.pallas_call(finish_kernel, out_shape=(jax.ShapeDtypeStruct(spots.shape...  0.99 us
    pallas_call x1, Pallas kernels, mask(): pl.pallas_call(mask_kernel, out_shape=jax.ShapeDtypeStruct(passages.shape...  0.94 us
  transfers between devices with their start and end apart: 8, of which 3 were waited for; matrix products, arithmetic and copies ran while one was open for 0% of the time, Pallas kernels for 2%

profile of v10, /device:TPU:0, one launch (start us, length us, event | category | flops | bytes accessed | tf_op | source)
XLA Modules:
  0.0 38.8 jit_solution(16839539423366237336)
XLA Ops:
  0.6 0.0 copy-start
  0.6 0.0 copy-start.3
  0.7 7.6 %encode.1 = (bf16[144,128]{1,0:T(8,128)(2,1)}, bf16[48,128,128]{2,1,0:T(8,128)(2,1)}, s32[4,64]{1,0:T(4,128)}) custom-call(s32[1]{0:T(128)} %bitcast.refs_0_, s32[4]{0:T(128)} %refs_1_.1, s32[48]{0:T(128)} %len_ref.1, s32[768]{0:T(1024)} %refs_3_.1, s32[4,64]{1,0:T(4,128)} %refs_4_.1, bf16[4,32,768]{2,1,0:T(8,128)(2,1)} %refs_5_.1, ...), custom_call_target="tpu_custom_call" | custom-call | flops 1207959552 | bytes 9437184 | tf_op jit(solution)/shard_map/encode/pallas_call | solution.py:226
  8.3 0.5 %collective-permute-start.2 = (bf16[48,128,128]{2,1,0:T(8,128)(2,1)}, bf16[48,128,128]{2,1,0:T(8,128)(2,1)S(1)}, u32[]{:S(2)}, u32[]{:S(2)}) collective-permute-start(bf16[48,128,128]{2,1,0:T(8,128)(2,1)} %get-tuple-element.6), channel_id=1, source_target_pairs={{0,1},{1,0},{2,3},{3,2},{4,5},{5,4},{6,7},{7,6},{8,9},{9,8},{10,11... | collective-permute-start | bytes 4718600 | tf_op jit(solution)/shard_map/ppermute | solution.py:412
  8.8 0.0 copy-start.1
  8.8 2.7 %collective-permute-start = (bf16[144,128]{1,0:T(8,128)(2,1)}, bf16[144,128]{1,0:T(8,128)(2,1)S(1)}, u32[]{:S(2)}, u32[]{:S(2)}) collective-permute-start(bf16[144,128]{1,0:T(8,128)(2,1)} %get-tuple-element.5.refs_3_), channel_id=1, source_target_pairs={{0,5},{1,4},{2,7},{3,6},{4,1},{5,0},{6,3},{7,2},{8,13},{9,12},{10,... | collective-permute-start | bytes 110600 | tf_op jit(solution)/shard_map/ppermute | solution.py:412
  11.5 2.6 %collective-permute-start.4 = (bf16[144,128]{1,0:T(8,128)(2,1)}, bf16[144,128]{1,0:T(8,128)(2,1)S(1)}, u32[]{:S(2)}, u32[]{:S(2)}) collective-permute-start(bf16[144,128]{1,0:T(8,128)(2,1)} %get-tuple-element.5.refs_3_), channel_id=1, source_target_pairs={{0,8},{1,9},{2,10},{3,11},{4,12},{5,13},{6,14},{7,15},{8,0},{9,1},... | collective-permute-start | bytes 110600 | tf_op jit(solution)/shard_map/ppermute | solution.py:412
  14.1 0.0 collective-permute-start.6
  14.1 0.0 collective-permute-done.refs_5_
  14.1 1.5 %collective-permute-start.1 = (bf16[144,128]{1,0:T(8,128)(2,1)S(1)}, bf16[144,128]{1,0:T(8,128)(2,1)S(1)}, u32[]{:S(2)}, u32[]{:S(2)}) collective-permute-start(bf16[144,128]{1,0:T(8,128)(2,1)S(1)} %collective-permute-done.refs_5_), channel_id=1, source_target_pairs={{0,3},{1,2},{2,1},{3,0},{4,7},{5,6},{6,5},{7,4},{8,11},{9,10},{10,... | collective-permute-start | bytes 110600 | tf_op jit(solution)/shard_map/ppermute | solution.py:412
  15.6 0.3 collective-permute-start.3
  15.8 1.2 %collective-permute-done.4.refs_7_ = bf16[144,128]{1,0:T(8,128)(2,1)S(1)} collective-permute-done((bf16[144,128]{1,0:T(8,128)(2,1)}, bf16[144,128]{1,0:T(8,128)(2,1)S(1)}, u32[]{:S(2)}, u32[]{:S(2)}) %collective-permute-start.4) | collective-permute-done | bytes 36896 | tf_op jit(solution)/shard_map/ppermute | solution.py:412
  17.0 0.3 collective-permute-start.5
  17.3 2.5 %collective-permute-done.6.refs_9_ = bf16[144,128]{1,0:T(8,128)(2,1)S(1)} collective-permute-done((bf16[144,128]{1,0:T(8,128)(2,1)}, bf16[144,128]{1,0:T(8,128)(2,1)S(1)}, u32[]{:S(2)}, u32[]{:S(2)}) %collective-permute-start.6) | collective-permute-done | bytes 36896 | tf_op jit(solution)/shard_map/ppermute | solution.py:412
  19.9 1.2 %collective-permute-start.7 = (bf16[144,128]{1,0:T(8,128)(2,1)S(1)}, bf16[144,128]{1,0:T(8,128)(2,1)S(1)}, u32[]{:S(2)}, u32[]{:S(2)}) collective-permute-start(bf16[144,128]{1,0:T(8,128)(2,1)S(1)} %collective-permute-done.6.refs_9_), channel_id=1, source_target_pairs={{0,3},{1,2},{2,1},{3,0},{4,7},{5,6},{6,5},{7,4},{8,11},{9,10},{10,... | collective-permute-start | bytes 110600 | tf_op jit(solution)/shard_map/ppermute | solution.py:412
  21.1 0.0 collective-permute-done.1.refs_0_.refs_6_
  21.1 0.0 copy-done
  21.1 0.0 copy-done.3
  21.1 0.9 %mask.1.refs_1_ = bf16[48,128,128]{2,1,0:T(8,128)(2,1)S(1)} custom-call(s32[48]{0:T(128)S(1)} %copy-done.3, bf16[48,128,128]{2,1,0:T(8,128)(2,1)S(1)} %copy-done, bf16[144,128]{1,0:T(8,128)(2,1)S(1)} %collective-permute-done.1.refs_0_.refs_6_), custom_call_target="tpu_custom_call" | custom-call | flops 6291456 | bytes 3145728 | tf_op jit(solution)/shard_map/mask/pallas_call | solution.py:280
  22.0 0.0 copy-start.2
  22.0 0.0 collective-permute-done.3.refs_4_
  22.0 0.0 collective-permute-done.5.refs_8_
  22.1 1.3 %collective-permute-done.7.refs_10_ = bf16[144,128]{1,0:T(8,128)(2,1)S(1)} collective-permute-done((bf16[144,128]{1,0:T(8,128)(2,1)S(1)}, bf16[144,128]{1,0:T(8,128)(2,1)S(1)}, u32[]{:S(2)}, u32[]{:S(2)}) %collective-permute-start.7) | collective-permute-done | bytes 36896 | tf_op jit(solution)/shard_map/ppermute | solution.py:412
  23.4 0.0 collective-permute-done.2.refs_2_
  23.4 0.0 copy-done.1
  23.4 4.6 %score.1 = f32[8,128]{1,0:T(8,128)S(1)} custom-call(s32[1]{0:T(128)} %bitcast.refs_0_, bf16[48,128,128]{2,1,0:T(8,128)(2,1)S(1)} %mask.1.refs_1_, bf16[48,128,128]{2,1,0:T(8,128)(2,1)S(1)} %collective-permute-done.2.refs_2_, bf16[144,128]{1,0:T(8,128)(2,1)S(1)} %copy-done.1, bf16[144,128]{1,0:T(8,128)(2,1)S(1)} %collective-permute-done.3.refs_4_, ...), custom_call_target="tpu_custom_call" | custom-call | flops 805306368 | bytes 3145728 | tf_op jit(solution)/shard_map/score/pallas_call | solution.py:351
  28.0 9.8 %all_to_all.11 = f32[8,1,128]{2,1,0:T(1,128)S(1)} all-to-all(f32[8,1,128]{2,1,0:T(1,128)S(1)} %bitcast.5), channel_id=1, replica_groups={{0,3,5,6,8,11,13,14},{1,2,4,7,9,10,12,15},{16,19,21,22,24,27,29,30},{17..., dimensions={0} | all-to-all | bytes 8192 | tf_op jit(solution)/shard_map/all_to_all | solution.py:464
  37.9 0.0 copy-done.2
  37.9 1.0 %finish.1 = (f32[4,64]{1,0:T(4,128)}, f32[4,10]{1,0:T(4,128)}) custom-call(f32[8,128]{1,0:T(8,128)S(1)} %bitcast.6, s32[4,64]{1,0:T(4,128)S(1)} %copy-done.2), custom_call_target="tpu_custom_call" | custom-call | tf_op jit(solution)/shard_map/finish/pallas_call | solution.py:397
Async XLA Ops:
  0.6 20.4 %copy-start = (bf16[48,128,128]{2,1,0:T(8,128)(2,1)S(1)}, bf16[48,128,128]{2,1,0:T(8,128)(2,1)}, u32[]{:S(2)}) copy-start(bf16[48,128,128]{2,1,0:T(8,128)(2,1)} %pass_ref.1) | copy-start | bytes 4718596
  0.6 20.4 %copy-start.3 = (s32[48]{0:T(128)S(1)}, s32[48]{0:T(128)}, u32[]{:S(2)}) copy-start(s32[48]{0:T(128)} %len_ref.1) | copy-start | bytes 580
  8.3 15.1 %collective-permute-start.2 = (bf16[48,128,128]{2,1,0:T(8,128)(2,1)}, bf16[48,128,128]{2,1,0:T(8,128)(2,1)S(1)}, u32[]{:S(2)}, u32[]{:S(2)}) collective-permute-start(bf16[48,128,128]{2,1,0:T(8,128)(2,1)} %get-tuple-element.6), channel_id=1, source_target_pairs={{0,1},{1,0},{2,3},{3,2},{4,5},{5,4},{6,7},{7,6},{8,9},{9,8},{10,11... | collective-permute-start | bytes 4718600 | tf_op jit(solution)/shard_map/ppermute | solution.py:412
  8.8 14.6 %copy-start.1 = (bf16[144,128]{1,0:T(8,128)(2,1)S(1)}, bf16[144,128]{1,0:T(8,128)(2,1)}, u32[]{:S(2)}) copy-start(bf16[144,128]{1,0:T(8,128)(2,1)} %get-tuple-element.5.refs_3_) | copy-start | bytes 110596
  8.8 5.3 %collective-permute-start = (bf16[144,128]{1,0:T(8,128)(2,1)}, bf16[144,128]{1,0:T(8,128)(2,1)S(1)}, u32[]{:S(2)}, u32[]{:S(2)}) collective-permute-start(bf16[144,128]{1,0:T(8,128)(2,1)} %get-tuple-element.5.refs_3_), channel_id=1, source_target_pairs={{0,5},{1,4},{2,7},{3,6},{4,1},{5,0},{6,3},{7,2},{8,13},{9,12},{10,... | collective-permute-start | bytes 110600 | tf_op jit(solution)/shard_map/ppermute | solution.py:412
  11.5 5.5 %collective-permute-start.4 = (bf16[144,128]{1,0:T(8,128)(2,1)}, bf16[144,128]{1,0:T(8,128)(2,1)S(1)}, u32[]{:S(2)}, u32[]{:S(2)}) collective-permute-start(bf16[144,128]{1,0:T(8,128)(2,1)} %get-tuple-element.5.refs_3_), channel_id=1, source_target_pairs={{0,8},{1,9},{2,10},{3,11},{4,12},{5,13},{6,14},{7,15},{8,0},{9,1},... | collective-permute-start | bytes 110600 | tf_op jit(solution)/shard_map/ppermute | solution.py:412
  14.1 5.8 %collective-permute-start.6 = (bf16[144,128]{1,0:T(8,128)(2,1)}, bf16[144,128]{1,0:T(8,128)(2,1)S(1)}, u32[]{:S(2)}, u32[]{:S(2)}) collective-permute-start(bf16[144,128]{1,0:T(8,128)(2,1)} %get-tuple-element.5.refs_3_), channel_id=1, source_target_pairs={{0,13},{1,12},{2,15},{3,14},{4,9},{5,8},{6,11},{7,10},{8,5},{9,4},... | collective-permute-start | bytes 110600 | tf_op jit(solution)/shard_map/ppermute | solution.py:412
  14.1 7.0 %collective-permute-start.1 = (bf16[144,128]{1,0:T(8,128)(2,1)S(1)}, bf16[144,128]{1,0:T(8,128)(2,1)S(1)}, u32[]{:S(2)}, u32[]{:S(2)}) collective-permute-start(bf16[144,128]{1,0:T(8,128)(2,1)S(1)} %collective-permute-done.refs_5_), channel_id=1, source_target_pairs={{0,3},{1,2},{2,1},{3,0},{4,7},{5,6},{6,5},{7,4},{8,11},{9,10},{10,... | collective-permute-start | bytes 110600 | tf_op jit(solution)/shard_map/ppermute | solution.py:412
  15.6 6.5 %collective-permute-start.3 = (bf16[144,128]{1,0:T(8,128)(2,1)}, bf16[144,128]{1,0:T(8,128)(2,1)S(1)}, u32[]{:S(2)}, u32[]{:S(2)}) collective-permute-start(bf16[144,128]{1,0:T(8,128)(2,1)} %get-tuple-element.5.refs_3_), channel_id=1, source_target_pairs={{0,3},{1,2},{2,1},{3,0},{4,7},{5,6},{6,5},{7,4},{8,11},{9,10},{10,... | collective-permute-start | bytes 110600 | tf_op jit(solution)/shard_map/ppermute | solution.py:412
  17.0 5.0 %collective-permute-start.5 = (bf16[144,128]{1,0:T(8,128)(2,1)S(1)}, bf16[144,128]{1,0:T(8,128)(2,1)S(1)}, u32[]{:S(2)}, u32[]{:S(2)}) collective-permute-start(bf16[144,128]{1,0:T(8,128)(2,1)S(1)} %collective-permute-done.4.refs_7_), channel_id=1, source_target_pairs={{0,3},{1,2},{2,1},{3,0},{4,7},{5,6},{6,5},{7,4},{8,11},{9,10},{10,... | collective-permute-start | bytes 110600 | tf_op jit(solution)/shard_map/ppermute | solution.py:412
  19.9 3.5 %collective-permute-start.7 = (bf16[144,128]{1,0:T(8,128)(2,1)S(1)}, bf16[144,128]{1,0:T(8,128)(2,1)S(1)}, u32[]{:S(2)}, u32[]{:S(2)}) collective-permute-start(bf16[144,128]{1,0:T(8,128)(2,1)S(1)} %collective-permute-done.6.refs_9_), channel_id=1, source_target_pairs={{0,3},{1,2},{2,1},{3,0},{4,7},{5,6},{6,5},{7,4},{8,11},{9,10},{10,... | collective-permute-start | bytes 110600 | tf_op jit(solution)/shard_map/ppermute | solution.py:412
  22.0 15.8 %copy-start.2 = (s32[4,64]{1,0:T(4,128)S(1)}, s32[4,64]{1,0:T(4,128)}, u32[]{:S(2)}) copy-start(s32[4,64]{1,0:T(4,128)} %get-tuple-element.7.spot_ref) | copy-start | bytes 3076

commit v11 on v10

--- a/solution.py
+++ b/solution.py
@@ -133,10 +133,13 @@
     share = -(-len(entries) // chunks)
 
     def enter():
-        for i, k in entries[:share]:
-            spot = place_ref[cand_ref[i, k]]
-            table[jnp.right_shift(spot, 7), jnp.bitwise_and(spot, 127)] = i
-            spot_ref[i, k] = spot
+        for first in range(0, share, 12):
+            batch = entries[first:min(first + 12, share)]
+            names = [cand_ref[i, k] for i, k in batch]
+            spots = [place_ref[name] for name in names]
+            for (i, k), spot in zip(batch, spots):
+                table[jnp.right_shift(spot, 7), jnp.bitwise_and(spot, 127)] = i
+                spot_ref[i, k] = spot
         del entries[:share]
 
     def mask(c):

time: 39 us -> 39.1 us (level)
  no operation moved by 1% of the time
where the time goes in v11:
time: 39.1 us; the launch traced here: 38.9 us
  Pallas kernels  14.2 us (36%)
  blocking collectives  9.88 us (25%)
  starting transfers between devices  9.11 us (23%)
  waiting for transfers between devices  4.99 us (13%)
  between operations  0.71 us (2%)
    all_to_all x1, blocking collectives, per_device(): lax.all_to_all(sums, 'shard', split_axis=0, concat_axis=0, axis_index_gro...  9.88 us
    ppermute x8, starting transfers between devices, swap(): lax.ppermute(value, 'shard', [(i, i ^ distance) for i in range(size)])  9.11 us
    pallas_call x1, Pallas kernels, encode(): pl.pallas_call(kernel, out_shape=(jax.ShapeDtypeStruct((tokens + slots, e...  7.62 us
    ppermute x8, waiting for transfers between devices, swap(): lax.ppermute(value, 'shard', [(i, i ^ distance) for i in range(size)])  4.99 us
    pallas_call x1, Pallas kernels, score(): pl.pallas_call(kernel, out_shape=jax.ShapeDtypeStruct((slots, e), F32), i...  4.64 us
    pallas_call x1, Pallas kernels, finish(): pl.pallas_call(finish_kernel, out_shape=(jax.ShapeDtypeStruct(spots.shape...  0.99 us
    pallas_call x1, Pallas kernels, mask(): pl.pallas_call(mask_kernel, out_shape=jax.ShapeDtypeStruct(passages.shape...  0.94 us
  transfers between devices with their start and end apart: 8, of which 3 were waited for; matrix products, arithmetic and copies ran while one was open for 0% of the time, Pallas kernels for 2%

profile of v11, /device:TPU:0, one launch (start us, length us, event | category | flops | bytes accessed | tf_op | source)
XLA Modules:
  0.0 38.9 jit_solution(4487058546334152196)
XLA Ops:
  0.6 0.0 copy-start
  0.6 0.0 copy-start.3
  0.7 7.6 %encode.1 = (bf16[144,128]{1,0:T(8,128)(2,1)}, bf16[48,128,128]{2,1,0:T(8,128)(2,1)}, s32[4,64]{1,0:T(4,128)}) custom-call(s32[1]{0:T(128)} %bitcast.refs_0_, s32[4]{0:T(128)} %refs_1_.1, s32[48]{0:T(128)} %len_ref.1, s32[768]{0:T(1024)} %refs_3_.1, s32[4,64]{1,0:T(4,128)} %refs_4_.1, bf16[4,32,768]{2,1,0:T(8,128)(2,1)} %refs_5_.1, ...), custom_call_target="tpu_custom_call" | custom-call | flops 1207959552 | bytes 9437184 | tf_op jit(solution)/shard_map/encode/pallas_call | solution.py:229
  8.3 0.5 %collective-permute-start.2 = (bf16[48,128,128]{2,1,0:T(8,128)(2,1)}, bf16[48,128,128]{2,1,0:T(8,128)(2,1)S(1)}, u32[]{:S(2)}, u32[]{:S(2)}) collective-permute-start(bf16[48,128,128]{2,1,0:T(8,128)(2,1)} %get-tuple-element.6), channel_id=1, source_target_pairs={{0,1},{1,0},{2,3},{3,2},{4,5},{5,4},{6,7},{7,6},{8,9},{9,8},{10,11... | collective-permute-start | bytes 4718600 | tf_op jit(solution)/shard_map/ppermute | solution.py:415
  8.8 0.0 copy-start.1
  8.8 2.7 %collective-permute-start = (bf16[144,128]{1,0:T(8,128)(2,1)}, bf16[144,128]{1,0:T(8,128)(2,1)S(1)}, u32[]{:S(2)}, u32[]{:S(2)}) collective-permute-start(bf16[144,128]{1,0:T(8,128)(2,1)} %get-tuple-element.5.refs_3_), channel_id=1, source_target_pairs={{0,5},{1,4},{2,7},{3,6},{4,1},{5,0},{6,3},{7,2},{8,13},{9,12},{10,... | collective-permute-start | bytes 110600 | tf_op jit(solution)/shard_map/ppermute | solution.py:415
  11.5 2.6 %collective-permute-start.4 = (bf16[144,128]{1,0:T(8,128)(2,1)}, bf16[144,128]{1,0:T(8,128)(2,1)S(1)}, u32[]{:S(2)}, u32[]{:S(2)}) collective-permute-start(bf16[144,128]{1,0:T(8,128)(2,1)} %get-tuple-element.5.refs_3_), channel_id=1, source_target_pairs={{0,8},{1,9},{2,10},{3,11},{4,12},{5,13},{6,14},{7,15},{8,0},{9,1},... | collective-permute-start | bytes 110600 | tf_op jit(solution)/shard_map/ppermute | solution.py:415
  14.1 0.0 collective-permute-start.6
  14.1 0.0 collective-permute-done.refs_5_
  14.1 1.5 %collective-permute-start.1 = (bf16[144,128]{1,0:T(8,128)(2,1)S(1)}, bf16[144,128]{1,0:T(8,128)(2,1)S(1)}, u32[]{:S(2)}, u32[]{:S(2)}) collective-permute-start(bf16[144,128]{1,0:T(8,128)(2,1)S(1)} %collective-permute-done.refs_5_), channel_id=1, source_target_pairs={{0,3},{1,2},{2,1},{3,0},{4,7},{5,6},{6,5},{7,4},{8,11},{9,10},{10,... | collective-permute-start | bytes 110600 | tf_op jit(solution)/shard_map/ppermute | solution.py:415
  15.6 0.3 collective-permute-start.3
  15.8 1.1 %collective-permute-done.4.refs_7_ = bf16[144,128]{1,0:T(8,128)(2,1)S(1)} collective-permute-done((bf16[144,128]{1,0:T(8,128)(2,1)}, bf16[144,128]{1,0:T(8,128)(2,1)S(1)}, u32[]{:S(2)}, u32[]{:S(2)}) %collective-permute-start.4) | collective-permute-done | bytes 36896 | tf_op jit(solution)/shard_map/ppermute | solution.py:415
  17.0 0.3 collective-permute-start.5
  17.3 2.5 %collective-permute-done.6.refs_9_ = bf16[144,128]{1,0:T(8,128)(2,1)S(1)} collective-permute-done((bf16[144,128]{1,0:T(8,128)(2,1)}, bf16[144,128]{1,0:T(8,128)(2,1)S(1)}, u32[]{:S(2)}, u32[]{:S(2)}) %collective-permute-start.6) | collective-permute-done | bytes 36896 | tf_op jit(solution)/shard_map/ppermute | solution.py:415
  19.9 1.2 %collective-permute-start.7 = (bf16[144,128]{1,0:T(8,128)(2,1)S(1)}, bf16[144,128]{1,0:T(8,128)(2,1)S(1)}, u32[]{:S(2)}, u32[]{:S(2)}) collective-permute-start(bf16[144,128]{1,0:T(8,128)(2,1)S(1)} %collective-permute-done.6.refs_9_), channel_id=1, source_target_pairs={{0,3},{1,2},{2,1},{3,0},{4,7},{5,6},{6,5},{7,4},{8,11},{9,10},{10,... | collective-permute-start | bytes 110600 | tf_op jit(solution)/shard_map/ppermute | solution.py:415
  21.1 0.0 collective-permute-done.1.refs_0_.refs_6_
  21.1 0.0 copy-done
  21.1 0.0 copy-done.3
  21.1 0.9 %mask.1.refs_1_ = bf16[48,128,128]{2,1,0:T(8,128)(2,1)S(1)} custom-call(s32[48]{0:T(128)S(1)} %copy-done.3, bf16[48,128,128]{2,1,0:T(8,128)(2,1)S(1)} %copy-done, bf16[144,128]{1,0:T(8,128)(2,1)S(1)} %collective-permute-done.1.refs_0_.refs_6_), custom_call_target="tpu_custom_call" | custom-call | flops 6291456 | bytes 3145728 | tf_op jit(solution)/shard_map/mask/pallas_call | solution.py:283
  22.0 0.0 copy-start.2
  22.0 0.0 collective-permute-done.3.refs_4_
  22.0 0.0 collective-permute-done.5.refs_8_
  22.1 1.3 %collective-permute-done.7.refs_10_ = bf16[144,128]{1,0:T(8,128)(2,1)S(1)} collective-permute-done((bf16[144,128]{1,0:T(8,128)(2,1)S(1)}, bf16[144,128]{1,0:T(8,128)(2,1)S(1)}, u32[]{:S(2)}, u32[]{:S(2)}) %collective-permute-start.7) | collective-permute-done | bytes 36896 | tf_op jit(solution)/shard_map/ppermute | solution.py:415
  23.4 0.0 collective-permute-done.2.refs_2_
  23.4 0.0 copy-done.1
  23.4 4.6 %score.1 = f32[8,128]{1,0:T(8,128)S(1)} custom-call(s32[1]{0:T(128)} %bitcast.refs_0_, bf16[48,128,128]{2,1,0:T(8,128)(2,1)S(1)} %mask.1.refs_1_, bf16[48,128,128]{2,1,0:T(8,128)(2,1)S(1)} %collective-permute-done.2.refs_2_, bf16[144,128]{1,0:T(8,128)(2,1)S(1)} %copy-done.1, bf16[144,128]{1,0:T(8,128)(2,1)S(1)} %collective-permute-done.3.refs_4_, ...), custom_call_target="tpu_custom_call" | custom-call | flops 805306368 | bytes 3145728 | tf_op jit(solution)/shard_map/score/pallas_call | solution.py:354
  28.0 9.9 %all_to_all.11 = f32[8,1,128]{2,1,0:T(1,128)S(1)} all-to-all(f32[8,1,128]{2,1,0:T(1,128)S(1)} %bitcast.5), channel_id=1, replica_groups={{0,3,5,6,8,11,13,14},{1,2,4,7,9,10,12,15},{16,19,21,22,24,27,29,30},{17..., dimensions={0} | all-to-all | bytes 8192 | tf_op jit(solution)/shard_map/all_to_all | solution.py:467
  37.9 0.0 copy-done.2
  37.9 1.0 %finish.1 = (f32[4,64]{1,0:T(4,128)}, f32[4,10]{1,0:T(4,128)}) custom-call(f32[8,128]{1,0:T(8,128)S(1)} %bitcast.6, s32[4,64]{1,0:T(4,128)S(1)} %copy-done.2), custom_call_target="tpu_custom_call" | custom-call | tf_op jit(solution)/shard_map/finish/pallas_call | solution.py:400
Async XLA Ops:
  0.6 20.4 %copy-start = (bf16[48,128,128]{2,1,0:T(8,128)(2,1)S(1)}, bf16[48,128,128]{2,1,0:T(8,128)(2,1)}, u32[]{:S(2)}) copy-start(bf16[48,128,128]{2,1,0:T(8,128)(2,1)} %pass_ref.1) | copy-start | bytes 4718596
  0.6 20.4 %copy-start.3 = (s32[48]{0:T(128)S(1)}, s32[48]{0:T(128)}, u32[]{:S(2)}) copy-start(s32[48]{0:T(128)} %len_ref.1) | copy-start | bytes 580
  8.3 15.1 %collective-permute-start.2 = (bf16[48,128,128]{2,1,0:T(8,128)(2,1)}, bf16[48,128,128]{2,1,0:T(8,128)(2,1)S(1)}, u32[]{:S(2)}, u32[]{:S(2)}) collective-permute-start(bf16[48,128,128]{2,1,0:T(8,128)(2,1)} %get-tuple-element.6), channel_id=1, source_target_pairs={{0,1},{1,0},{2,3},{3,2},{4,5},{5,4},{6,7},{7,6},{8,9},{9,8},{10,11... | collective-permute-start | bytes 4718600 | tf_op jit(solution)/shard_map/ppermute | solution.py:415
  8.8 14.6 %copy-start.1 = (bf16[144,128]{1,0:T(8,128)(2,1)S(1)}, bf16[144,128]{1,0:T(8,128)(2,1)}, u32[]{:S(2)}) copy-start(bf16[144,128]{1,0:T(8,128)(2,1)} %get-tuple-element.5.refs_3_) | copy-start | bytes 110596
  8.8 5.3 %collective-permute-start = (bf16[144,128]{1,0:T(8,128)(2,1)}, bf16[144,128]{1,0:T(8,128)(2,1)S(1)}, u32[]{:S(2)}, u32[]{:S(2)}) collective-permute-start(bf16[144,128]{1,0:T(8,128)(2,1)} %get-tuple-element.5.refs_3_), channel_id=1, source_target_pairs={{0,5},{1,4},{2,7},{3,6},{4,1},{5,0},{6,3},{7,2},{8,13},{9,12},{10,... | collective-permute-start | bytes 110600 | tf_op jit(solution)/shard_map/ppermute | solution.py:415
  11.5 5.5 %collective-permute-start.4 = (bf16[144,128]{1,0:T(8,128)(2,1)}, bf16[144,128]{1,0:T(8,128)(2,1)S(1)}, u32[]{:S(2)}, u32[]{:S(2)}) collective-permute-start(bf16[144,128]{1,0:T(8,128)(2,1)} %get-tuple-element.5.refs_3_), channel_id=1, source_target_pairs={{0,8},{1,9},{2,10},{3,11},{4,12},{5,13},{6,14},{7,15},{8,0},{9,1},... | collective-permute-start | bytes 110600 | tf_op jit(solution)/shard_map/ppermute | solution.py:415
  14.1 5.8 %collective-permute-start.6 = (bf16[144,128]{1,0:T(8,128)(2,1)}, bf16[144,128]{1,0:T(8,128)(2,1)S(1)}, u32[]{:S(2)}, u32[]{:S(2)}) collective-permute-start(bf16[144,128]{1,0:T(8,128)(2,1)} %get-tuple-element.5.refs_3_), channel_id=1, source_target_pairs={{0,13},{1,12},{2,15},{3,14},{4,9},{5,8},{6,11},{7,10},{8,5},{9,4},... | collective-permute-start | bytes 110600 | tf_op jit(solution)/shard_map/ppermute | solution.py:415
  14.1 7.0 %collective-permute-start.1 = (bf16[144,128]{1,0:T(8,128)(2,1)S(1)}, bf16[144,128]{1,0:T(8,128)(2,1)S(1)}, u32[]{:S(2)}, u32[]{:S(2)}) collective-permute-start(bf16[144,128]{1,0:T(8,128)(2,1)S(1)} %collective-permute-done.refs_5_), channel_id=1, source_target_pairs={{0,3},{1,2},{2,1},{3,0},{4,7},{5,6},{6,5},{7,4},{8,11},{9,10},{10,... | collective-permute-start | bytes 110600 | tf_op jit(solution)/shard_map/ppermute | solution.py:415
  15.6 6.5 %collective-permute-start.3 = (bf16[144,128]{1,0:T(8,128)(2,1)}, bf16[144,128]{1,0:T(8,128)(2,1)S(1)}, u32[]{:S(2)}, u32[]{:S(2)}) collective-permute-start(bf16[144,128]{1,0:T(8,128)(2,1)} %get-tuple-element.5.refs_3_), channel_id=1, source_target_pairs={{0,3},{1,2},{2,1},{3,0},{4,7},{5,6},{6,5},{7,4},{8,11},{9,10},{10,... | collective-permute-start | bytes 110600 | tf_op jit(solution)/shard_map/ppermute | solution.py:415
  17.0 5.1 %collective-permute-start.5 = (bf16[144,128]{1,0:T(8,128)(2,1)S(1)}, bf16[144,128]{1,0:T(8,128)(2,1)S(1)}, u32[]{:S(2)}, u32[]{:S(2)}) collective-permute-start(bf16[144,128]{1,0:T(8,128)(2,1)S(1)} %collective-permute-done.4.refs_7_), channel_id=1, source_target_pairs={{0,3},{1,2},{2,1},{3,0},{4,7},{5,6},{6,5},{7,4},{8,11},{9,10},{10,... | collective-permute-start | bytes 110600 | tf_op jit(solution)/shard_map/ppermute | solution.py:415
  19.9 3.5 %collective-permute-start.7 = (bf16[144,128]{1,0:T(8,128)(2,1)S(1)}, bf16[144,128]{1,0:T(8,128)(2,1)S(1)}, u32[]{:S(2)}, u32[]{:S(2)}) collective-permute-start(bf16[144,128]{1,0:T(8,128)(2,1)S(1)} %collective-permute-done.6.refs_9_), channel_id=1, source_target_pairs={{0,3},{1,2},{2,1},{3,0},{4,7},{5,6},{6,5},{7,4},{8,11},{9,10},{10,... | collective-permute-start | bytes 110600 | tf_op jit(solution)/shard_map/ppermute | solution.py:415
  22.0 15.9 %copy-start.2 = (s32[4,64]{1,0:T(4,128)S(1)}, s32[4,64]{1,0:T(4,128)}, u32[]{:S(2)}) copy-start(s32[4,64]{1,0:T(4,128)} %get-tuple-element.7.spot_ref) | copy-start | bytes 3076

commit v12 on v11

--- a/solution.py
+++ b/solution.py
@@ -42,7 +42,6 @@
     color,
     me_ref,
     lens_hbm,
-    plen_hbm,
     row_hbm,
     cand_hbm,
     x_hbm,
@@ -50,15 +49,11 @@
     w2_ref,
     gain_hbm,
     embed_hbm,
-    pass_hbm,
     out_ref,
-    masked_hbm,
     spot_ref,
     w1_buf,
     w2_buf,
-    pass_buf,
     lens_ref,
-    plen_ref,
     row_ref,
     place_ref,
     cand_ref,
@@ -71,7 +66,6 @@
     small_sems,
     place_sem,
     table_sem,
-    pass_sems,
 ):
     chunks, _, width = w1_buf.shape
     slots, lanes = table_v.shape
@@ -92,7 +86,6 @@
                 (x_hbm, x_ref),
                 (row_hbm, row_ref),
                 (cand_hbm, cand_ref),
-                (plen_hbm, plen_ref),
                 (lens_hbm, lens_ref),
                 (gain_hbm, gain_ref),
                 (embed_hbm, embed_ref),
@@ -102,23 +95,13 @@
     for copy in small[:3]:
         copy.start()
     copies[0][0].start()
-    small[3].start()
-    batch = half // chunks
-    loads, saves = [], []
-    for c in range(chunks):
-        rows = pl.ds(c * batch, batch)
-        loads.append(pltpu.make_async_copy(pass_hbm.at[rows], pass_buf.at[rows], pass_sems.at[0, c]))
-        saves.append(pltpu.make_async_copy(pass_buf.at[rows], masked_hbm.at[rows], pass_sems.at[1, c]))
     copies[1][0].start()
     copies[0][1].start()
     for c in range(2, chunks):
-        loads[c - 2].start()
         copies[c][0].start()
         copies[c - 1][1].start()
     copies[-1][1].start()
-    loads[-2].start()
-    loads[-1].start()
-    for copy in small[4:]:
+    for copy in small[3:]:
         copy.start()
     clear.wait()
     small[1].wait()
@@ -142,13 +125,7 @@
                 spot_ref[i, k] = spot
         del entries[:share]
 
-    def mask(c):
-        loads[c].wait()
-        mask_into(pass_buf, pass_buf, plen_ref, c * batch, batch)
-        saves[c].start()
-
     small[0].wait()
-    small[3].wait()
     x = x_ref[...].reshape(query_count * token_count, width_in)
     total = x.astype(F32)
     inner = active = None
@@ -157,8 +134,6 @@
             copies[step][0].wait()
         if step >= 2:
             copies[step - 2][1].wait()
-        if 2 <= step < chunks:
-            mask(step - 2)
         if step == 1:
             small[2].wait()
             placed.wait()
@@ -173,10 +148,8 @@
         if step == chunks:
             fetch = pltpu.make_async_copy(table, table_v, table_sem)
             fetch.start()
-    mask(chunks - 2)
-    mask(chunks - 1)
-
-    for copy in small[4:]:
+
+    for copy in small[3:]:
         copy.wait()
     centered = total - jnp.mean(total, axis=-1, keepdims=True)
     variance = jnp.mean(jnp.square(centered), axis=-1, keepdims=True)
@@ -194,8 +167,6 @@
     wanted = table_v[...].astype(F32).astype(BF16)
     out_ref[pl.ds(0, tokens), :] = vectors
     out_ref[pl.ds(tokens, slots), :] = wanted
-    for save in saves:
-        save.wait()
 
 
 def encode(
@@ -206,8 +177,7 @@
     outer_weight,
     norm_gain,
     embed_weight,
-    passage_vectors,
-    passage_lengths,
+    half,
     passage_row,
     candidates,
     slots,
@@ -216,7 +186,6 @@
     query_count, token_count, d = query_hidden.shape
     ff = inner_weight.shape[1]
     e = embed_weight.shape[1]
-    half = passage_vectors.shape[0]
     slots = -(-slots // 16) * 16
     assert 2 * half <= e == 128
     chunks = 6
@@ -230,17 +199,14 @@
         kernel,
         out_shape=(
             jax.ShapeDtypeStruct((tokens + slots, e), BF16),
-            jax.ShapeDtypeStruct(passage_vectors.shape, BF16),
             jax.ShapeDtypeStruct(candidates.shape, jnp.int32),
         ),
-        in_specs=[SMEM] + [ANY] * 10,
-        out_specs=(VMEM, ANY, SMEM),
+        in_specs=[SMEM] + [ANY] * 8,
+        out_specs=(VMEM, SMEM),
         scratch_shapes=[
             pltpu.VMEM((chunks, d, width), BF16),
             pltpu.VMEM((chunks, width, d), BF16),
-            pltpu.VMEM(passage_vectors.shape, BF16),
             pltpu.SMEM(query_lengths.shape, jnp.int32),
-            pltpu.SMEM(passage_lengths.shape, jnp.int32),
             pltpu.VMEM(passage_row.shape, jnp.int32),
             pltpu.SMEM(passage_row.shape, jnp.int32),
             pltpu.SMEM(candidates.shape, jnp.int32),
@@ -250,10 +216,9 @@
             pltpu.SMEM((slots, e), jnp.int32),
             pltpu.VMEM((slots, e), jnp.int32),
             pltpu.SemaphoreType.DMA((2, chunks)),
-            pltpu.SemaphoreType.DMA((7,)),
+            pltpu.SemaphoreType.DMA((6,)),
             pltpu.SemaphoreType.DMA,
             pltpu.SemaphoreType.DMA,
-            pltpu.SemaphoreType.DMA((2, chunks)),
         ],
         compiler_params=pltpu.CompilerParams(vmem_limit_bytes=60 * 2 ** 20),
         cost_estimate=pl.CostEstimate(
@@ -263,7 +228,6 @@
     )(
         me,
         query_lengths,
-        passage_lengths,
         passage_row,
         candidates,
         query_hidden,
@@ -271,24 +235,26 @@
         outer_weight,
         norm_gain,
         embed_weight,
-        passage_vectors,
     )
 
 
-def mask_kernel(len_ref, pass_ref, *refs):
-    mask_into(refs[-1], pass_ref, len_ref, 0, pass_ref.shape[0])
+def mask_kernel(len0_ref, len1_ref, pass0_ref, pass1_ref, _, out0_ref, out1_ref):
+    mask_into(out0_ref, pass0_ref, len0_ref, 0, pass0_ref.shape[0])
+    mask_into(out1_ref, pass1_ref, len1_ref, 0, pass1_ref.shape[0])
 
 
 def mask(lengths, passages, late):
+    shape = passages[0].shape
+    size = 2 * passages[0].size
     return pl.pallas_call(
         mask_kernel,
-        out_shape=jax.ShapeDtypeStruct(passages.shape, BF16),
-        in_specs=[SMEM, VMEM, VMEM],
-        out_specs=VMEM,
+        out_shape=[jax.ShapeDtypeStruct(shape, BF16)] * 2,
+        in_specs=[SMEM, SMEM, VMEM, VMEM, VMEM],
+        out_specs=[VMEM, VMEM],
         compiler_params=pltpu.CompilerParams(vmem_limit_bytes=2 ** 22),
-        cost_estimate=pl.CostEstimate(flops=8 * passages.size, bytes_accessed=4 * passages.size, transcendentals=0),
+        cost_estimate=pl.CostEstimate(flops=8 * size, bytes_accessed=4 * size, transcendentals=0),
         name="mask",
-    )(lengths, passages, late)
+    )(*lengths, *passages, late)
 
 
 def score_kernel(slots, token_count, me_ref, own_ref, other_ref, *refs):
@@ -443,7 +409,8 @@
         return swap(value, 2 * distance + color(2 * distance))
 
     me = lax.axis_index("shard").astype(jnp.int32).reshape(1)
-    message, masked, spots = encode(
+    across = swap(passage_lengths, 1)
+    message, spots = encode(
         me,
         query_hidden,
         query_lengths,
@@ -451,18 +418,18 @@
         outer_weight,
         norm_gain,
         embed_weight,
-        passage_vectors,
-        passage_lengths,
+        passage_vectors.shape[0],
         passage_row,
         candidates,
         slots,
         color,
     )
-    other = swap(masked, 1)
+    message, across, raw = lax.optimization_barrier((message, across, passage_vectors))
+    raw = swap(raw, 1)
 
     line = [message] + [send(message, d) for d in range(slots - inner, 0, -inner)][::-1]
     got = [line[s // inner] if s % inner == 0 else send(line[s // inner], s % inner) for s in range(slots)]
-    own = mask(passage_lengths, passage_vectors, got[inner + 1])
+    own, other = mask((passage_lengths, across), (passage_vectors, raw), got[inner + 1])
     sums = score(me, got, own, other, query_hidden.shape[1])
     back = lax.all_to_all(sums, "shard", split_axis=0, concat_axis=0, axis_index_groups=groups, tiled=True)
     return finish(back, spots)

time: 39.1 us -> 38 us (0.972)
  Pallas kernels: 14.2 us -> 13.5 us
    pallas_call x1, Pallas kernels: 7.62 us -> 6.5 us  [encode(): pl.pallas_call(kernel, out_shape=(jax.ShapeDtypeStruct((tokens + slots, e...]
    pallas_call x1, Pallas kernels: 0.94 us -> 1.34 us  [mask(): pl.pallas_call(mask_kernel, out_shape=[jax.ShapeDtypeStruct(shape, BF16)]...]
    ppermute x8 -> x9, waiting for transfers between devices: 4.99 us -> 4.67 us  [swap(): lax.ppermute(value, 'shard', [(i, i ^ distance) for i in range(size)])]
    ppermute x8 -> x9, starting transfers between devices: 9.11 us -> 8.92 us  [swap(): lax.ppermute(value, 'shard', [(i, i ^ distance) for i in range(size)])]
  transfers between devices with their start and end apart: 8 -> 9, of which waited for: 3 -> 3; matrix products, arithmetic and copies ran while one was open for 0% -> 0% of each run, Pallas kernels for 2% -> 21%
where the time goes in v12:
time: 38 us; the launch traced here: 37.8 us
  Pallas kernels  13.5 us (36%)
  blocking collectives  10.1 us (27%)
  starting transfers between devices  8.92 us (23%)
  waiting for transfers between devices  4.67 us (12%)
  between operations  0.71 us (2%)
    all_to_all x1, blocking collectives, per_device(): lax.all_to_all(sums, 'shard', split_axis=0, concat_axis=0, axis_index_gro...  10.1 us
    ppermute x9, starting transfers between devices, swap(): lax.ppermute(value, 'shard', [(i, i ^ distance) for i in range(size)])  8.92 us
    pallas_call x1, Pallas kernels, encode(): pl.pallas_call(kernel, out_shape=(jax.ShapeDtypeStruct((tokens + slots, e...  6.5 us
    ppermute x9, waiting for transfers between devices, swap(): lax.ppermute(value, 'shard', [(i, i ^ distance) for i in range(size)])  4.67 us
    pallas_call x1, Pallas kernels, score(): pl.pallas_call(kernel, out_shape=jax.ShapeDtypeStruct((slots, e), F32), i...  4.64 us
    pallas_call x1, Pallas kernels, mask(): pl.pallas_call(mask_kernel, out_shape=[jax.ShapeDtypeStruct(shape, BF16)]...  1.34 us
    pallas_call x1, Pallas kernels, finish(): pl.pallas_call(finish_kernel, out_shape=(jax.ShapeDtypeStruct(spots.shape...  0.99 us
  transfers between devices with their start and end apart: 9, of which 3 were waited for; matrix products, arithmetic and copies ran while one was open for 0% of the time, Pallas kernels for 21%

profile of v12, /device:TPU:0, one launch (start us, length us, event | category | flops | bytes accessed | tf_op | source)
XLA Modules:
  0.0 37.8 jit_solution(973028296738073197)
XLA Ops:
  0.6 0.5 %collective-permute-start = (s32[48]{0:T(128)}, s32[48]{0:T(128)S(1)}, u32[]{:S(2)}, u32[]{:S(2)}) collective-permute-start(s32[48]{0:T(128)} %len0_ref.1), channel_id=1, source_target_pairs={{0,1},{1,0},{2,3},{3,2},{4,5},{5,4},{6,7},{7,6},{8,9},{9,8},{10,11... | collective-permute-start | bytes 584 | tf_op jit(solution)/shard_map/ppermute | solution.py:381
  1.2 0.0 copy-start
  1.2 0.0 copy-start.3
  1.2 6.5 %encode.1 = (bf16[144,128]{1,0:T(8,128)(2,1)}, s32[4,64]{1,0:T(4,128)}) custom-call(s32[1]{0:T(128)} %bitcast.refs_0_, s32[4]{0:T(128)} %refs_1_.1, s32[768]{0:T(1024)} %refs_2_.1, s32[4,64]{1,0:T(4,128)} %refs_3_.1, bf16[4,32,768]{2,1,0:T(8,128)(2,1)} %refs_4_.1, bf16[768,3072]{1,0:T(8,128)(2,1)} %refs_5_.1, bf16[3072,768]{1,0:T(8,128)(2,1)} %refs_6_.1, ...), custom_call_target="tpu_custom_call" | custom-call | flops 1207959552 | bytes 9437184 | tf_op jit(solution)/shard_map/encode/pallas_call | solution.py:198
  7.7 0.0 collective-permute-done.len1_ref
  7.7 0.0 copy-done
  7.7 0.0 copy-start.1
  7.7 0.1 collective-permute-start.1
  7.8 2.7 %collective-permute-start.2 = (bf16[144,128]{1,0:T(8,128)(2,1)}, bf16[144,128]{1,0:T(8,128)(2,1)S(1)}, u32[]{:S(2)}, u32[]{:S(2)}) collective-permute-start(bf16[144,128]{1,0:T(8,128)(2,1)} %get-tuple-element.12.refs_3_), channel_id=1, source_target_pairs={{0,5},{1,4},{2,7},{3,6},{4,1},{5,0},{6,3},{7,2},{8,13},{9,12},{10,... | collective-permute-start | bytes 110600 | tf_op jit(solution)/shard_map/ppermute | solution.py:381
  10.5 2.6 %collective-permute-start.5 = (bf16[144,128]{1,0:T(8,128)(2,1)}, bf16[144,128]{1,0:T(8,128)(2,1)S(1)}, u32[]{:S(2)}, u32[]{:S(2)}) collective-permute-start(bf16[144,128]{1,0:T(8,128)(2,1)} %get-tuple-element.12.refs_3_), channel_id=1, source_target_pairs={{0,8},{1,9},{2,10},{3,11},{4,12},{5,13},{6,14},{7,15},{8,0},{9,1},... | collective-permute-start | bytes 110600 | tf_op jit(solution)/shard_map/ppermute | solution.py:381
  13.1 0.0 collective-permute-start.7
  13.1 0.0 collective-permute-done.2.refs_5_
  13.1 1.5 %collective-permute-start.3 = (bf16[144,128]{1,0:T(8,128)(2,1)S(1)}, bf16[144,128]{1,0:T(8,128)(2,1)S(1)}, u32[]{:S(2)}, u32[]{:S(2)}) collective-permute-start(bf16[144,128]{1,0:T(8,128)(2,1)S(1)} %collective-permute-done.2.refs_5_), channel_id=1, source_target_pairs={{0,3},{1,2},{2,1},{3,0},{4,7},{5,6},{6,5},{7,4},{8,11},{9,10},{10,... | collective-permute-start | bytes 110600 | tf_op jit(solution)/shard_map/ppermute | solution.py:381
  14.6 0.3 collective-permute-start.4
  14.9 1.5 %collective-permute-done.5.refs_7_ = bf16[144,128]{1,0:T(8,128)(2,1)S(1)} collective-permute-done((bf16[144,128]{1,0:T(8,128)(2,1)}, bf16[144,128]{1,0:T(8,128)(2,1)S(1)}, u32[]{:S(2)}, u32[]{:S(2)}) %collective-permute-start.5) | collective-permute-done | bytes 36896 | tf_op jit(solution)/shard_map/ppermute | solution.py:381
  16.4 0.0 collective-permute-start.6
  16.4 2.3 %collective-permute-done.7.refs_9_ = bf16[144,128]{1,0:T(8,128)(2,1)S(1)} collective-permute-done((bf16[144,128]{1,0:T(8,128)(2,1)}, bf16[144,128]{1,0:T(8,128)(2,1)S(1)}, u32[]{:S(2)}, u32[]{:S(2)}) %collective-permute-start.7) | collective-permute-done | bytes 36896 | tf_op jit(solution)/shard_map/ppermute | solution.py:381
  18.6 1.2 %collective-permute-start.8 = (bf16[144,128]{1,0:T(8,128)(2,1)S(1)}, bf16[144,128]{1,0:T(8,128)(2,1)S(1)}, u32[]{:S(2)}, u32[]{:S(2)}) collective-permute-start(bf16[144,128]{1,0:T(8,128)(2,1)S(1)} %collective-permute-done.7.refs_9_), channel_id=1, source_target_pairs={{0,3},{1,2},{2,1},{3,0},{4,7},{5,6},{6,5},{7,4},{8,11},{9,10},{10,... | collective-permute-start | bytes 110600 | tf_op jit(solution)/shard_map/ppermute | solution.py:381
  19.9 0.0 collective-permute-done.3._.refs_6_
  19.9 0.0 collective-permute-done.1.pass1_ref
  19.9 0.0 copy-done.3
  19.9 1.3 %mask.1 = (bf16[48,128,128]{2,1,0:T(8,128)(2,1)S(1)}, bf16[48,128,128]{2,1,0:T(8,128)(2,1)S(1)}) custom-call(s32[48]{0:T(128)S(1)} %copy-done.3, s32[48]{0:T(128)S(1)} %collective-permute-done.len1_ref, bf16[48,128,128]{2,1,0:T(8,128)(2,1)S(1)} %copy-done, bf16[48,128,128]{2,1,0:T(8,128)(2,1)S(1)} %collective-permute-done.1.pass1_ref, ...), custom_call_target="tpu_custom_call" | custom-call | flops 12582912 | bytes 6291456 | tf_op jit(solution)/shard_map/mask/pallas_call | solution.py:249
  21.2 0.0 collective-permute-done.4.refs_4_
  21.2 0.0 collective-permute-done.6.refs_8_
  21.3 0.9 %collective-permute-done.8.refs_10_ = bf16[144,128]{1,0:T(8,128)(2,1)S(1)} collective-permute-done((bf16[144,128]{1,0:T(8,128)(2,1)S(1)}, bf16[144,128]{1,0:T(8,128)(2,1)S(1)}, u32[]{:S(2)}, u32[]{:S(2)}) %collective-permute-start.8) | collective-permute-done | bytes 36896 | tf_op jit(solution)/shard_map/ppermute | solution.py:381
  22.1 0.0 copy-done.1
  22.1 0.0 copy-start.2
  22.1 4.6 %score.1 = f32[8,128]{1,0:T(8,128)S(1)} custom-call(s32[1]{0:T(128)} %bitcast.refs_0_, bf16[48,128,128]{2,1,0:T(8,128)(2,1)S(1)} %get-tuple-element.13.refs_1_, bf16[48,128,128]{2,1,0:T(8,128)(2,1)S(1)} %get-tuple-element.14.refs_2_, bf16[144,128]{1,0:T(8,128)(2,1)S(1)} %copy-done.1, bf16[144,128]{1,0:T(8,128)(2,1)S(1)} %collective-permute-done.4.refs_4_, ...), custom_call_target="tpu_custom_call" | custom-call | flops 805306368 | bytes 3145728 | tf_op jit(solution)/shard_map/score/pallas_call | solution.py:320
  26.8 10.1 %all_to_all.11 = f32[8,1,128]{2,1,0:T(1,128)S(1)} all-to-all(f32[8,1,128]{2,1,0:T(1,128)S(1)} %bitcast.5), channel_id=1, replica_groups={{0,3,5,6,8,11,13,14},{1,2,4,7,9,10,12,15},{16,19,21,22,24,27,29,30},{17..., dimensions={0} | all-to-all | bytes 8192 | tf_op jit(solution)/shard_map/all_to_all | solution.py:434
  36.8 0.0 copy-done.2
  36.8 1.0 %finish.1 = (f32[4,64]{1,0:T(4,128)}, f32[4,10]{1,0:T(4,128)}) custom-call(f32[8,128]{1,0:T(8,128)S(1)} %bitcast.6, s32[4,64]{1,0:T(4,128)S(1)} %copy-done.2), custom_call_target="tpu_custom_call" | custom-call | tf_op jit(solution)/shard_map/finish/pallas_call | solution.py:366
Async XLA Ops:
  0.6 7.0 %collective-permute-start = (s32[48]{0:T(128)}, s32[48]{0:T(128)S(1)}, u32[]{:S(2)}, u32[]{:S(2)}) collective-permute-start(s32[48]{0:T(128)} %len0_ref.1), channel_id=1, source_target_pairs={{0,1},{1,0},{2,3},{3,2},{4,5},{5,4},{6,7},{7,6},{8,9},{9,8},{10,11... | collective-permute-start | bytes 584 | tf_op jit(solution)/shard_map/ppermute | solution.py:381
  1.2 6.5 %copy-start = (bf16[48,128,128]{2,1,0:T(8,128)(2,1)S(1)}, bf16[48,128,128]{2,1,0:T(8,128)(2,1)}, u32[]{:S(2)}) copy-start(bf16[48,128,128]{2,1,0:T(8,128)(2,1)} %pass0_ref.1) | copy-start | bytes 4718596
  1.2 18.7 %copy-start.3 = (s32[48]{0:T(128)S(1)}, s32[48]{0:T(128)}, u32[]{:S(2)}) copy-start(s32[48]{0:T(128)} %len0_ref.1) | copy-start | bytes 580
  7.7 14.4 %copy-start.1 = (bf16[144,128]{1,0:T(8,128)(2,1)S(1)}, bf16[144,128]{1,0:T(8,128)(2,1)}, u32[]{:S(2)}) copy-start(bf16[144,128]{1,0:T(8,128)(2,1)} %get-tuple-element.12.refs_3_) | copy-start | bytes 110596
  7.7 12.2 %collective-permute-start.1 = (bf16[48,128,128]{2,1,0:T(8,128)(2,1)S(1)}, bf16[48,128,128]{2,1,0:T(8,128)(2,1)S(1)}, u32[]{:S(2)}, u32[]{:S(2)}) collective-permute-start(bf16[48,128,128]{2,1,0:T(8,128)(2,1)S(1)} %copy-done), channel_id=1, source_target_pairs={{0,1},{1,0},{2,3},{3,2},{4,5},{5,4},{6,7},{7,6},{8,9},{9,8},{10,11... | collective-permute-start | bytes 4718600 | tf_op jit(solution)/shard_map/ppermute | solution.py:381
  7.8 5.3 %collective-permute-start.2 = (bf16[144,128]{1,0:T(8,128)(2,1)}, bf16[144,128]{1,0:T(8,128)(2,1)S(1)}, u32[]{:S(2)}, u32[]{:S(2)}) collective-permute-start(bf16[144,128]{1,0:T(8,128)(2,1)} %get-tuple-element.12.refs_3_), channel_id=1, source_target_pairs={{0,5},{1,4},{2,7},{3,6},{4,1},{5,0},{6,3},{7,2},{8,13},{9,12},{10,... | collective-permute-start | bytes 110600 | tf_op jit(solution)/shard_map/ppermute | solution.py:381
  10.5 5.9 %collective-permute-start.5 = (bf16[144,128]{1,0:T(8,128)(2,1)}, bf16[144,128]{1,0:T(8,128)(2,1)S(1)}, u32[]{:S(2)}, u32[]{:S(2)}) collective-permute-start(bf16[144,128]{1,0:T(8,128)(2,1)} %get-tuple-element.12.refs_3_), channel_id=1, source_target_pairs={{0,8},{1,9},{2,10},{3,11},{4,12},{5,13},{6,14},{7,15},{8,0},{9,1},... | collective-permute-start | bytes 110600 | tf_op jit(solution)/shard_map/ppermute | solution.py:381
  13.1 5.5 %collective-permute-start.7 = (bf16[144,128]{1,0:T(8,128)(2,1)}, bf16[144,128]{1,0:T(8,128)(2,1)S(1)}, u32[]{:S(2)}, u32[]{:S(2)}) collective-permute-start(bf16[144,128]{1,0:T(8,128)(2,1)} %get-tuple-element.12.refs_3_), channel_id=1, source_target_pairs={{0,13},{1,12},{2,15},{3,14},{4,9},{5,8},{6,11},{7,10},{8,5},{9,4},... | collective-permute-start | bytes 110600 | tf_op jit(solution)/shard_map/ppermute | solution.py:381
  13.1 6.8 %collective-permute-start.3 = (bf16[144,128]{1,0:T(8,128)(2,1)S(1)}, bf16[144,128]{1,0:T(8,128)(2,1)S(1)}, u32[]{:S(2)}, u32[]{:S(2)}) collective-permute-start(bf16[144,128]{1,0:T(8,128)(2,1)S(1)} %collective-permute-done.2.refs_5_), channel_id=1, source_target_pairs={{0,3},{1,2},{2,1},{3,0},{4,7},{5,6},{6,5},{7,4},{8,11},{9,10},{10,... | collective-permute-start | bytes 110600 | tf_op jit(solution)/shard_map/ppermute | solution.py:381
  14.6 6.6 %collective-permute-start.4 = (bf16[144,128]{1,0:T(8,128)(2,1)}, bf16[144,128]{1,0:T(8,128)(2,1)S(1)}, u32[]{:S(2)}, u32[]{:S(2)}) collective-permute-start(bf16[144,128]{1,0:T(8,128)(2,1)} %get-tuple-element.12.refs_3_), channel_id=1, source_target_pairs={{0,3},{1,2},{2,1},{3,0},{4,7},{5,6},{6,5},{7,4},{8,11},{9,10},{10,... | collective-permute-start | bytes 110600 | tf_op jit(solution)/shard_map/ppermute | solution.py:381
  16.4 4.9 %collective-permute-start.6 = (bf16[144,128]{1,0:T(8,128)(2,1)S(1)}, bf16[144,128]{1,0:T(8,128)(2,1)S(1)}, u32[]{:S(2)}, u32[]{:S(2)}) collective-permute-start(bf16[144,128]{1,0:T(8,128)(2,1)S(1)} %collective-permute-done.5.refs_7_), channel_id=1, source_target_pairs={{0,3},{1,2},{2,1},{3,0},{4,7},{5,6},{6,5},{7,4},{8,11},{9,10},{10,... | collective-permute-start | bytes 110600 | tf_op jit(solution)/shard_map/ppermute | solution.py:381
  18.6 3.5 %collective-permute-start.8 = (bf16[144,128]{1,0:T(8,128)(2,1)S(1)}, bf16[144,128]{1,0:T(8,128)(2,1)S(1)}, u32[]{:S(2)}, u32[]{:S(2)}) collective-permute-start(bf16[144,128]{1,0:T(8,128)(2,1)S(1)} %collective-permute-done.7.refs_9_), channel_id=1, source_target_pairs={{0,3},{1,2},{2,1},{3,0},{4,7},{5,6},{6,5},{7,4},{8,11},{9,10},{10,... | collective-permute-start | bytes 110600 | tf_op jit(solution)/shard_map/ppermute | solution.py:381
  22.1 14.7 %copy-start.2 = (s32[4,64]{1,0:T(4,128)S(1)}, s32[4,64]{1,0:T(4,128)}, u32[]{:S(2)}) copy-start(s32[4,64]{1,0:T(4,128)} %get-tuple-element.15.spot_ref) | copy-start | bytes 3076

commit v13 on v12

--- a/solution.py
+++ b/solution.py
@@ -427,8 +427,12 @@
     message, across, raw = lax.optimization_barrier((message, across, passage_vectors))
     raw = swap(raw, 1)
 
-    line = [message] + [send(message, d) for d in range(slots - inner, 0, -inner)][::-1]
-    got = [line[s // inner] if s % inner == 0 else send(line[s // inner], s % inner) for s in range(slots)]
+    got = {0: message}
+    distance = slots
+    while distance > 1:
+        distance //= 2
+        got.update({s + distance: send(value, distance) for s, value in got.items()})
+    got = [got[s] for s in range(slots)]
     own, other = mask((passage_lengths, across), (passage_vectors, raw), got[inner + 1])
     sums = score(me, got, own, other, query_hidden.shape[1])
     back = lax.all_to_all(sums, "shard", split_axis=0, concat_axis=0, axis_index_groups=groups, tiled=True)

time: 38 us -> 39.3 us (1.034)
  starting transfers between devices: 8.92 us -> 10.2 us
  waiting for transfers between devices: 4.67 us -> 4.23 us
  blocking collectives: 10.1 us -> 10.5 us
    ppermute x9, starting transfers between devices: 8.92 us -> 10.2 us  [swap(): lax.ppermute(value, 'shard', [(i, i ^ distance) for i in range(size)])]
    all_to_all x1, blocking collectives: 10.1 us -> 10.5 us  [per_device(): lax.all_to_all(sums, 'shard', split_axis=0, concat_axis=0, axis_index_gro...]
    ppermute x9, waiting for transfers between devices: 4.67 us -> 4.23 us  [swap(): lax.ppermute(value, 'shard', [(i, i ^ distance) for i in range(size)])]
  transfers between devices with their start and end apart: 9 -> 9, of which waited for: 3 -> 5; matrix products, arithmetic and copies ran while one was open for 0% -> 0% of each run, Pallas kernels for 21% -> 20%
where the time goes in v13:
time: 39.3 us; the launch traced here: 39.1 us
  Pallas kernels  13.5 us (34%)
  blocking collectives  10.5 us (27%)
  starting transfers between devices  10.2 us (26%)
  waiting for transfers between devices  4.23 us (11%)
  between operations  0.7 us (2%)
    all_to_all x1, blocking collectives, per_device(): lax.all_to_all(sums, 'shard', split_axis=0, concat_axis=0, axis_index_gro...  10.5 us
    ppermute x9, starting transfers between devices, swap(): lax.ppermute(value, 'shard', [(i, i ^ distance) for i in range(size)])  10.2 us
    pallas_call x1, Pallas kernels, encode(): pl.pallas_call(kernel, out_shape=(jax.ShapeDtypeStruct((tokens + slots, e...  6.5 us
    pallas_call x1, Pallas kernels, score(): pl.pallas_call(kernel, out_shape=jax.ShapeDtypeStruct((slots, e), F32), i...  4.64 us
    ppermute x9, waiting for transfers between devices, swap(): lax.ppermute(value, 'shard', [(i, i ^ distance) for i in range(size)])  4.23 us
    pallas_call x1, Pallas kernels, mask(): pl.pallas_call(mask_kernel, out_shape=[jax.ShapeDtypeStruct(shape, BF16)]...  1.34 us
    pallas_call x1, Pallas kernels, finish(): pl.pallas_call(finish_kernel, out_shape=(jax.ShapeDtypeStruct(spots.shape...  0.99 us
  transfers between devices with their start and end apart: 9, of which 5 were waited for; matrix products, arithmetic and copies ran while one was open for 0% of the time, Pallas kernels for 20%

profile of v13, /device:TPU:0, one launch (start us, length us, event | category | flops | bytes accessed | tf_op | source)
XLA Modules:
  0.0 39.1 jit_solution(18352538865272014051)
XLA Ops:
  0.6 0.5 %collective-permute-start = (s32[48]{0:T(128)}, s32[48]{0:T(128)S(1)}, u32[]{:S(2)}, u32[]{:S(2)}) collective-permute-start(s32[48]{0:T(128)} %len0_ref.1), channel_id=1, source_target_pairs={{0,1},{1,0},{2,3},{3,2},{4,5},{5,4},{6,7},{7,6},{8,9},{9,8},{10,11... | collective-permute-start | bytes 584 | tf_op jit(solution)/shard_map/ppermute | solution.py:381
  1.2 0.0 copy-start
  1.2 0.0 copy-start.3
  1.2 6.5 %encode.1 = (bf16[144,128]{1,0:T(8,128)(2,1)}, s32[4,64]{1,0:T(4,128)}) custom-call(s32[1]{0:T(128)} %bitcast.refs_0_, s32[4]{0:T(128)} %refs_1_.1, s32[768]{0:T(1024)} %refs_2_.1, s32[4,64]{1,0:T(4,128)} %refs_3_.1, bf16[4,32,768]{2,1,0:T(8,128)(2,1)} %refs_4_.1, bf16[768,3072]{1,0:T(8,128)(2,1)} %refs_5_.1, bf16[3072,768]{1,0:T(8,128)(2,1)} %refs_6_.1, ...), custom_call_target="tpu_custom_call" | custom-call | flops 1207959552 | bytes 9437184 | tf_op jit(solution)/shard_map/encode/pallas_call | solution.py:198
  7.7 0.0 collective-permute-done.len1_ref
  7.7 0.0 copy-done
  7.7 0.0 copy-start.1
  7.7 0.1 collective-permute-start.1
  7.8 4.0 %collective-permute-start.5 = (bf16[144,128]{1,0:T(8,128)(2,1)}, bf16[144,128]{1,0:T(8,128)(2,1)S(1)}, u32[]{:S(2)}, u32[]{:S(2)}) collective-permute-start(bf16[144,128]{1,0:T(8,128)(2,1)} %get-tuple-element.12.refs_3_), channel_id=1, source_target_pairs={{0,8},{1,9},{2,10},{3,11},{4,12},{5,13},{6,14},{7,15},{8,0},{9,1},... | collective-permute-start | bytes 110600 | tf_op jit(solution)/shard_map/ppermute | solution.py:381
  11.8 1.0 %collective-permute-start.2 = (bf16[144,128]{1,0:T(8,128)(2,1)}, bf16[144,128]{1,0:T(8,128)(2,1)S(1)}, u32[]{:S(2)}, u32[]{:S(2)}) collective-permute-start(bf16[144,128]{1,0:T(8,128)(2,1)} %get-tuple-element.12.refs_3_), channel_id=1, source_target_pairs={{0,5},{1,4},{2,7},{3,6},{4,1},{5,0},{6,3},{7,2},{8,13},{9,12},{10,... | collective-permute-start | bytes 110600 | tf_op jit(solution)/shard_map/ppermute | solution.py:381
  12.8 1.2 %collective-permute-done.5.refs_7_ = bf16[144,128]{1,0:T(8,128)(2,1)S(1)} collective-permute-done((bf16[144,128]{1,0:T(8,128)(2,1)}, bf16[144,128]{1,0:T(8,128)(2,1)S(1)}, u32[]{:S(2)}, u32[]{:S(2)}) %collective-permute-start.5) | collective-permute-done | bytes 36896 | tf_op jit(solution)/shard_map/ppermute | solution.py:381
  14.0 0.5 %collective-permute-start.7 = (bf16[144,128]{1,0:T(8,128)(2,1)S(1)}, bf16[144,128]{1,0:T(8,128)(2,1)S(1)}, u32[]{:S(2)}, u32[]{:S(2)}) collective-permute-start(bf16[144,128]{1,0:T(8,128)(2,1)S(1)} %collective-permute-done.5.refs_7_), channel_id=1, source_target_pairs={{0,5},{1,4},{2,7},{3,6},{4,1},{5,0},{6,3},{7,2},{8,13},{9,12},{10,... | collective-permute-start | bytes 110600 | tf_op jit(solution)/shard_map/ppermute | solution.py:381
  14.4 1.2 %collective-permute-done.2.refs_5_ = bf16[144,128]{1,0:T(8,128)(2,1)S(1)} collective-permute-done((bf16[144,128]{1,0:T(8,128)(2,1)}, bf16[144,128]{1,0:T(8,128)(2,1)S(1)}, u32[]{:S(2)}, u32[]{:S(2)}) %collective-permute-start.2) | collective-permute-done | bytes 36896 | tf_op jit(solution)/shard_map/ppermute | solution.py:381
  15.7 1.8 %collective-permute-start.3 = (bf16[144,128]{1,0:T(8,128)(2,1)S(1)}, bf16[144,128]{1,0:T(8,128)(2,1)S(1)}, u32[]{:S(2)}, u32[]{:S(2)}) collective-permute-start(bf16[144,128]{1,0:T(8,128)(2,1)S(1)} %collective-permute-done.2.refs_5_), channel_id=1, source_target_pairs={{0,3},{1,2},{2,1},{3,0},{4,7},{5,6},{6,5},{7,4},{8,11},{9,10},{10,... | collective-permute-start | bytes 110600 | tf_op jit(solution)/shard_map/ppermute | solution.py:381
  17.4 0.0 collective-permute-start.4
  17.5 1.7 %collective-permute-start.6 = (bf16[144,128]{1,0:T(8,128)(2,1)S(1)}, bf16[144,128]{1,0:T(8,128)(2,1)S(1)}, u32[]{:S(2)}, u32[]{:S(2)}) collective-permute-start(bf16[144,128]{1,0:T(8,128)(2,1)S(1)} %collective-permute-done.5.refs_7_), channel_id=1, source_target_pairs={{0,3},{1,2},{2,1},{3,0},{4,7},{5,6},{6,5},{7,4},{8,11},{9,10},{10,... | collective-permute-start | bytes 110600 | tf_op jit(solution)/shard_map/ppermute | solution.py:381
  19.2 0.0 collective-permute-done.7.refs_9_
  19.2 0.6 %collective-permute-start.8 = (bf16[144,128]{1,0:T(8,128)(2,1)S(1)}, bf16[144,128]{1,0:T(8,128)(2,1)S(1)}, u32[]{:S(2)}, u32[]{:S(2)}) collective-permute-start(bf16[144,128]{1,0:T(8,128)(2,1)S(1)} %collective-permute-done.7.refs_9_), channel_id=1, source_target_pairs={{0,3},{1,2},{2,1},{3,0},{4,7},{5,6},{6,5},{7,4},{8,11},{9,10},{10,... | collective-permute-start | bytes 110600 | tf_op jit(solution)/shard_map/ppermute | solution.py:381
  19.7 0.0 collective-permute-done.3._.refs_6_
  19.8 0.0 collective-permute-done.1.pass1_ref
  19.8 0.0 copy-done.3
  19.8 1.3 %mask.1 = (bf16[48,128,128]{2,1,0:T(8,128)(2,1)S(1)}, bf16[48,128,128]{2,1,0:T(8,128)(2,1)S(1)}) custom-call(s32[48]{0:T(128)S(1)} %copy-done.3, s32[48]{0:T(128)S(1)} %collective-permute-done.len1_ref, bf16[48,128,128]{2,1,0:T(8,128)(2,1)S(1)} %copy-done, bf16[48,128,128]{2,1,0:T(8,128)(2,1)S(1)} %collective-permute-done.1.pass1_ref, ...), custom_call_target="tpu_custom_call" | custom-call | flops 12582912 | bytes 6291456 | tf_op jit(solution)/shard_map/mask/pallas_call | solution.py:249
  21.1 0.2 collective-permute-done.4.refs_4_
  21.3 0.8 %collective-permute-done.6.refs_8_ = bf16[144,128]{1,0:T(8,128)(2,1)S(1)} collective-permute-done((bf16[144,128]{1,0:T(8,128)(2,1)S(1)}, bf16[144,128]{1,0:T(8,128)(2,1)S(1)}, u32[]{:S(2)}, u32[]{:S(2)}) %collective-permute-start.6) | collective-permute-done | bytes 36896 | tf_op jit(solution)/shard_map/ppermute | solution.py:381
  22.1 0.8 %collective-permute-done.8.refs_10_ = bf16[144,128]{1,0:T(8,128)(2,1)S(1)} collective-permute-done((bf16[144,128]{1,0:T(8,128)(2,1)S(1)}, bf16[144,128]{1,0:T(8,128)(2,1)S(1)}, u32[]{:S(2)}, u32[]{:S(2)}) %collective-permute-start.8) | collective-permute-done | bytes 36896 | tf_op jit(solution)/shard_map/ppermute | solution.py:381
  23.0 0.0 copy-done.1
  23.0 0.0 copy-start.2
  23.0 4.6 %score.1 = f32[8,128]{1,0:T(8,128)S(1)} custom-call(s32[1]{0:T(128)} %bitcast.refs_0_, bf16[48,128,128]{2,1,0:T(8,128)(2,1)S(1)} %get-tuple-element.13.refs_1_, bf16[48,128,128]{2,1,0:T(8,128)(2,1)S(1)} %get-tuple-element.14.refs_2_, bf16[144,128]{1,0:T(8,128)(2,1)S(1)} %copy-done.1, bf16[144,128]{1,0:T(8,128)(2,1)S(1)} %collective-permute-done.4.refs_4_, ...), custom_call_target="tpu_custom_call" | custom-call | flops 805306368 | bytes 3145728 | tf_op jit(solution)/shard_map/score/pallas_call | solution.py:320
  27.6 10.5 %all_to_all.11 = f32[8,1,128]{2,1,0:T(1,128)S(1)} all-to-all(f32[8,1,128]{2,1,0:T(1,128)S(1)} %bitcast.5), channel_id=1, replica_groups={{0,3,5,6,8,11,13,14},{1,2,4,7,9,10,12,15},{16,19,21,22,24,27,29,30},{17..., dimensions={0} | all-to-all | bytes 8192 | tf_op jit(solution)/shard_map/all_to_all | solution.py:438
  38.1 0.0 copy-done.2
  38.1 1.0 %finish.1 = (f32[4,64]{1,0:T(4,128)}, f32[4,10]{1,0:T(4,128)}) custom-call(f32[8,128]{1,0:T(8,128)S(1)} %bitcast.6, s32[4,64]{1,0:T(4,128)S(1)} %copy-done.2), custom_call_target="tpu_custom_call" | custom-call | tf_op jit(solution)/shard_map/finish/pallas_call | solution.py:366
Async XLA Ops:
  0.6 7.0 %collective-permute-start = (s32[48]{0:T(128)}, s32[48]{0:T(128)S(1)}, u32[]{:S(2)}, u32[]{:S(2)}) collective-permute-start(s32[48]{0:T(128)} %len0_ref.1), channel_id=1, source_target_pairs={{0,1},{1,0},{2,3},{3,2},{4,5},{5,4},{6,7},{7,6},{8,9},{9,8},{10,11... | collective-permute-start | bytes 584 | tf_op jit(solution)/shard_map/ppermute | solution.py:381
  1.2 6.5 %copy-start = (bf16[48,128,128]{2,1,0:T(8,128)(2,1)S(1)}, bf16[48,128,128]{2,1,0:T(8,128)(2,1)}, u32[]{:S(2)}) copy-start(bf16[48,128,128]{2,1,0:T(8,128)(2,1)} %pass0_ref.1) | copy-start | bytes 4718596
  1.2 18.6 %copy-start.3 = (s32[48]{0:T(128)S(1)}, s32[48]{0:T(128)}, u32[]{:S(2)}) copy-start(s32[48]{0:T(128)} %len0_ref.1) | copy-start | bytes 580
  7.7 15.3 %copy-start.1 = (bf16[144,128]{1,0:T(8,128)(2,1)S(1)}, bf16[144,128]{1,0:T(8,128)(2,1)}, u32[]{:S(2)}) copy-start(bf16[144,128]{1,0:T(8,128)(2,1)} %get-tuple-element.12.refs_3_) | copy-start | bytes 110596
  7.7 12.1 %collective-permute-start.1 = (bf16[48,128,128]{2,1,0:T(8,128)(2,1)S(1)}, bf16[48,128,128]{2,1,0:T(8,128)(2,1)S(1)}, u32[]{:S(2)}, u32[]{:S(2)}) collective-permute-start(bf16[48,128,128]{2,1,0:T(8,128)(2,1)S(1)} %copy-done), channel_id=1, source_target_pairs={{0,1},{1,0},{2,3},{3,2},{4,5},{5,4},{6,7},{7,6},{8,9},{9,8},{10,11... | collective-permute-start | bytes 4718600 | tf_op jit(solution)/shard_map/ppermute | solution.py:381
  7.8 6.2 %collective-permute-start.5 = (bf16[144,128]{1,0:T(8,128)(2,1)}, bf16[144,128]{1,0:T(8,128)(2,1)S(1)}, u32[]{:S(2)}, u32[]{:S(2)}) collective-permute-start(bf16[144,128]{1,0:T(8,128)(2,1)} %get-tuple-element.12.refs_3_), channel_id=1, source_target_pairs={{0,8},{1,9},{2,10},{3,11},{4,12},{5,13},{6,14},{7,15},{8,0},{9,1},... | collective-permute-start | bytes 110600 | tf_op jit(solution)/shard_map/ppermute | solution.py:381
  11.8 3.8 %collective-permute-start.2 = (bf16[144,128]{1,0:T(8,128)(2,1)}, bf16[144,128]{1,0:T(8,128)(2,1)S(1)}, u32[]{:S(2)}, u32[]{:S(2)}) collective-permute-start(bf16[144,128]{1,0:T(8,128)(2,1)} %get-tuple-element.12.refs_3_), channel_id=1, source_target_pairs={{0,5},{1,4},{2,7},{3,6},{4,1},{5,0},{6,3},{7,2},{8,13},{9,12},{10,... | collective-permute-start | bytes 110600 | tf_op jit(solution)/shard_map/ppermute | solution.py:381
  14.0 5.2 %collective-permute-start.7 = (bf16[144,128]{1,0:T(8,128)(2,1)S(1)}, bf16[144,128]{1,0:T(8,128)(2,1)S(1)}, u32[]{:S(2)}, u32[]{:S(2)}) collective-permute-start(bf16[144,128]{1,0:T(8,128)(2,1)S(1)} %collective-permute-done.5.refs_7_), channel_id=1, source_target_pairs={{0,5},{1,4},{2,7},{3,6},{4,1},{5,0},{6,3},{7,2},{8,13},{9,12},{10,... | collective-permute-start | bytes 110600 | tf_op jit(solution)/shard_map/ppermute | solution.py:381
  15.7 4.1 %collective-permute-start.3 = (bf16[144,128]{1,0:T(8,128)(2,1)S(1)}, bf16[144,128]{1,0:T(8,128)(2,1)S(1)}, u32[]{:S(2)}, u32[]{:S(2)}) collective-permute-start(bf16[144,128]{1,0:T(8,128)(2,1)S(1)} %collective-permute-done.2.refs_5_), channel_id=1, source_target_pairs={{0,3},{1,2},{2,1},{3,0},{4,7},{5,6},{6,5},{7,4},{8,11},{9,10},{10,... | collective-permute-start | bytes 110600 | tf_op jit(solution)/shard_map/ppermute | solution.py:381
  17.4 3.9 %collective-permute-start.4 = (bf16[144,128]{1,0:T(8,128)(2,1)}, bf16[144,128]{1,0:T(8,128)(2,1)S(1)}, u32[]{:S(2)}, u32[]{:S(2)}) collective-permute-start(bf16[144,128]{1,0:T(8,128)(2,1)} %get-tuple-element.12.refs_3_), channel_id=1, source_target_pairs={{0,3},{1,2},{2,1},{3,0},{4,7},{5,6},{6,5},{7,4},{8,11},{9,10},{10,... | collective-permute-start | bytes 110600 | tf_op jit(solution)/shard_map/ppermute | solution.py:381
  17.5 4.7 %collective-permute-start.6 = (bf16[144,128]{1,0:T(8,128)(2,1)S(1)}, bf16[144,128]{1,0:T(8,128)(2,1)S(1)}, u32[]{:S(2)}, u32[]{:S(2)}) collective-permute-start(bf16[144,128]{1,0:T(8,128)(2,1)S(1)} %collective-permute-done.5.refs_7_), channel_id=1, source_target_pairs={{0,3},{1,2},{2,1},{3,0},{4,7},{5,6},{6,5},{7,4},{8,11},{9,10},{10,... | collective-permute-start | bytes 110600 | tf_op jit(solution)/shard_map/ppermute | solution.py:381
  19.2 3.8 %collective-permute-start.8 = (bf16[144,128]{1,0:T(8,128)(2,1)S(1)}, bf16[144,128]{1,0:T(8,128)(2,1)S(1)}, u32[]{:S(2)}, u32[]{:S(2)}) collective-permute-start(bf16[144,128]{1,0:T(8,128)(2,1)S(1)} %collective-permute-done.7.refs_9_), channel_id=1, source_target_pairs={{0,3},{1,2},{2,1},{3,0},{4,7},{5,6},{6,5},{7,4},{8,11},{9,10},{10,... | collective-permute-start | bytes 110600 | tf_op jit(solution)/shard_map/ppermute | solution.py:381
  23.0 15.2 %copy-start.2 = (s32[4,64]{1,0:T(4,128)S(1)}, s32[4,64]{1,0:T(4,128)}, u32[]{:S(2)}) copy-start(s32[4,64]{1,0:T(4,128)} %get-tuple-element.15.spot_ref) | copy-start | bytes 3076

commit v14 on v13

--- a/solution.py
+++ b/solution.py
@@ -409,6 +409,7 @@
         return swap(value, 2 * distance + color(2 * distance))
 
     me = lax.axis_index("shard").astype(jnp.int32).reshape(1)
+    raw = swap(passage_vectors, 1)
     across = swap(passage_lengths, 1)
     message, spots = encode(
         me,
@@ -424,8 +425,7 @@
         slots,
         color,
     )
-    message, across, raw = lax.optimization_barrier((message, across, passage_vectors))
-    raw = swap(raw, 1)
+    message, across = lax.optimization_barrier((message, across))
 
     got = {0: message}
     distance = slots

time: 39.3 us -> 39.3 us (level)
  no operation moved by 1% of the time
where the time goes in v14:
time: 39.3 us; the launch traced here: 39.1 us
  Pallas kernels  13.4 us (34%)
  blocking collectives  10.5 us (27%)
  starting transfers between devices  10.1 us (26%)
  waiting for transfers between devices  4.32 us (11%)
  between operations  0.7 us (2%)
    all_to_all x1, blocking collectives, per_device(): lax.all_to_all(sums, 'shard', split_axis=0, concat_axis=0, axis_index_gro...  10.5 us
    ppermute x9, starting transfers between devices, swap(): lax.ppermute(value, 'shard', [(i, i ^ distance) for i in range(size)])  10.1 us
    pallas_call x1, Pallas kernels, encode(): pl.pallas_call(kernel, out_shape=(jax.ShapeDtypeStruct((tokens + slots, e...  6.5 us
    pallas_call x1, Pallas kernels, score(): pl.pallas_call(kernel, out_shape=jax.ShapeDtypeStruct((slots, e), F32), i...  4.63 us
    ppermute x9, waiting for transfers between devices, swap(): lax.ppermute(value, 'shard', [(i, i ^ distance) for i in range(size)])  4.32 us
    pallas_call x1, Pallas kernels, mask(): pl.pallas_call(mask_kernel, out_shape=[jax.ShapeDtypeStruct(shape, BF16)]...  1.34 us
    pallas_call x1, Pallas kernels, finish(): pl.pallas_call(finish_kernel, out_shape=(jax.ShapeDtypeStruct(spots.shape...  0.99 us
  transfers between devices with their start and end apart: 9, of which 5 were waited for; matrix products, arithmetic and copies ran while one was open for 0% of the time, Pallas kernels for 20%

profile of v14, /device:TPU:0, one launch (start us, length us, event | category | flops | bytes accessed | tf_op | source)
XLA Modules:
  0.0 39.1 jit_solution(10178828808611313874)
XLA Ops:
  0.6 0.5 %collective-permute-start.1 = (bf16[48,128,128]{2,1,0:T(8,128)(2,1)}, bf16[48,128,128]{2,1,0:T(8,128)(2,1)S(1)}, u32[]{:S(2)}, u32[]{:S(2)}) collective-permute-start(bf16[48,128,128]{2,1,0:T(8,128)(2,1)} %pass0_ref.1), channel_id=1, source_target_pairs={{0,1},{1,0},{2,3},{3,2},{4,5},{5,4},{6,7},{7,6},{8,9},{9,8},{10,11... | collective-permute-start | bytes 4718600 | tf_op jit(solution)/shard_map/ppermute | solution.py:381
  1.2 0.1 collective-permute-start
  1.2 0.0 copy-start
  1.2 0.0 copy-start.3
  1.2 6.5 %encode.1 = (bf16[144,128]{1,0:T(8,128)(2,1)}, s32[4,64]{1,0:T(4,128)}) custom-call(s32[1]{0:T(128)} %bitcast.refs_0_, s32[4]{0:T(128)} %refs_1_.1, s32[768]{0:T(1024)} %refs_2_.1, s32[4,64]{1,0:T(4,128)} %refs_3_.1, bf16[4,32,768]{2,1,0:T(8,128)(2,1)} %refs_4_.1, bf16[768,3072]{1,0:T(8,128)(2,1)} %refs_5_.1, bf16[3072,768]{1,0:T(8,128)(2,1)} %refs_6_.1, ...), custom_call_target="tpu_custom_call" | custom-call | flops 1207959552 | bytes 9437184 | tf_op jit(solution)/shard_map/encode/pallas_call | solution.py:198
  7.7 0.0 collective-permute-done.len1_ref
  7.7 0.0 copy-start.1
  7.8 4.1 %collective-permute-start.5 = (bf16[144,128]{1,0:T(8,128)(2,1)}, bf16[144,128]{1,0:T(8,128)(2,1)S(1)}, u32[]{:S(2)}, u32[]{:S(2)}) collective-permute-start(bf16[144,128]{1,0:T(8,128)(2,1)} %get-tuple-element.10.refs_3_), channel_id=1, source_target_pairs={{0,8},{1,9},{2,10},{3,11},{4,12},{5,13},{6,14},{7,15},{8,0},{9,1},... | collective-permute-start | bytes 110600 | tf_op jit(solution)/shard_map/ppermute | solution.py:381
  11.9 1.0 %collective-permute-start.2 = (bf16[144,128]{1,0:T(8,128)(2,1)}, bf16[144,128]{1,0:T(8,128)(2,1)S(1)}, u32[]{:S(2)}, u32[]{:S(2)}) collective-permute-start(bf16[144,128]{1,0:T(8,128)(2,1)} %get-tuple-element.10.refs_3_), channel_id=1, source_target_pairs={{0,5},{1,4},{2,7},{3,6},{4,1},{5,0},{6,3},{7,2},{8,13},{9,12},{10,... | collective-permute-start | bytes 110600 | tf_op jit(solution)/shard_map/ppermute | solution.py:381
  12.8 1.2 %collective-permute-done.5.refs_7_ = bf16[144,128]{1,0:T(8,128)(2,1)S(1)} collective-permute-done((bf16[144,128]{1,0:T(8,128)(2,1)}, bf16[144,128]{1,0:T(8,128)(2,1)S(1)}, u32[]{:S(2)}, u32[]{:S(2)}) %collective-permute-start.5) | collective-permute-done | bytes 36896 | tf_op jit(solution)/shard_map/ppermute | solution.py:381
  14.0 0.4 %collective-permute-start.7 = (bf16[144,128]{1,0:T(8,128)(2,1)S(1)}, bf16[144,128]{1,0:T(8,128)(2,1)S(1)}, u32[]{:S(2)}, u32[]{:S(2)}) collective-permute-start(bf16[144,128]{1,0:T(8,128)(2,1)S(1)} %collective-permute-done.5.refs_7_), channel_id=1, source_target_pairs={{0,5},{1,4},{2,7},{3,6},{4,1},{5,0},{6,3},{7,2},{8,13},{9,12},{10,... | collective-permute-start | bytes 110600 | tf_op jit(solution)/shard_map/ppermute | solution.py:381
  14.4 1.3 %collective-permute-done.2.refs_5_ = bf16[144,128]{1,0:T(8,128)(2,1)S(1)} collective-permute-done((bf16[144,128]{1,0:T(8,128)(2,1)}, bf16[144,128]{1,0:T(8,128)(2,1)S(1)}, u32[]{:S(2)}, u32[]{:S(2)}) %collective-permute-start.2) | collective-permute-done | bytes 36896 | tf_op jit(solution)/shard_map/ppermute | solution.py:381
  15.7 1.7 %collective-permute-start.3 = (bf16[144,128]{1,0:T(8,128)(2,1)S(1)}, bf16[144,128]{1,0:T(8,128)(2,1)S(1)}, u32[]{:S(2)}, u32[]{:S(2)}) collective-permute-start(bf16[144,128]{1,0:T(8,128)(2,1)S(1)} %collective-permute-done.2.refs_5_), channel_id=1, source_target_pairs={{0,3},{1,2},{2,1},{3,0},{4,7},{5,6},{6,5},{7,4},{8,11},{9,10},{10,... | collective-permute-start | bytes 110600 | tf_op jit(solution)/shard_map/ppermute | solution.py:381
  17.4 0.0 collective-permute-start.4
  17.5 1.7 %collective-permute-start.6 = (bf16[144,128]{1,0:T(8,128)(2,1)S(1)}, bf16[144,128]{1,0:T(8,128)(2,1)S(1)}, u32[]{:S(2)}, u32[]{:S(2)}) collective-permute-start(bf16[144,128]{1,0:T(8,128)(2,1)S(1)} %collective-permute-done.5.refs_7_), channel_id=1, source_target_pairs={{0,3},{1,2},{2,1},{3,0},{4,7},{5,6},{6,5},{7,4},{8,11},{9,10},{10,... | collective-permute-start | bytes 110600 | tf_op jit(solution)/shard_map/ppermute | solution.py:381
  19.2 0.0 collective-permute-done.7.refs_9_
  19.2 0.5 %collective-permute-start.8 = (bf16[144,128]{1,0:T(8,128)(2,1)S(1)}, bf16[144,128]{1,0:T(8,128)(2,1)S(1)}, u32[]{:S(2)}, u32[]{:S(2)}) collective-permute-start(bf16[144,128]{1,0:T(8,128)(2,1)S(1)} %collective-permute-done.7.refs_9_), channel_id=1, source_target_pairs={{0,3},{1,2},{2,1},{3,0},{4,7},{5,6},{6,5},{7,4},{8,11},{9,10},{10,... | collective-permute-start | bytes 110600 | tf_op jit(solution)/shard_map/ppermute | solution.py:381
  19.7 0.0 collective-permute-done.3._.refs_6_
  19.7 0.0 collective-permute-done.1.pass1_ref
  19.7 0.0 copy-done
  19.7 0.0 copy-done.3
  19.7 1.3 %mask.1 = (bf16[48,128,128]{2,1,0:T(8,128)(2,1)S(1)}, bf16[48,128,128]{2,1,0:T(8,128)(2,1)S(1)}) custom-call(s32[48]{0:T(128)S(1)} %copy-done.3, s32[48]{0:T(128)S(1)} %collective-permute-done.len1_ref, bf16[48,128,128]{2,1,0:T(8,128)(2,1)S(1)} %copy-done, bf16[48,128,128]{2,1,0:T(8,128)(2,1)S(1)} %collective-permute-done.1.pass1_ref, ...), custom_call_target="tpu_custom_call" | custom-call | flops 12582912 | bytes 6291456 | tf_op jit(solution)/shard_map/mask/pallas_call | solution.py:249
  21.1 0.3 collective-permute-done.4.refs_4_
  21.3 0.8 %collective-permute-done.6.refs_8_ = bf16[144,128]{1,0:T(8,128)(2,1)S(1)} collective-permute-done((bf16[144,128]{1,0:T(8,128)(2,1)S(1)}, bf16[144,128]{1,0:T(8,128)(2,1)S(1)}, u32[]{:S(2)}, u32[]{:S(2)}) %collective-permute-start.6) | collective-permute-done | bytes 36896 | tf_op jit(solution)/shard_map/ppermute | solution.py:381
  22.1 0.8 %collective-permute-done.8.refs_10_ = bf16[144,128]{1,0:T(8,128)(2,1)S(1)} collective-permute-done((bf16[144,128]{1,0:T(8,128)(2,1)S(1)}, bf16[144,128]{1,0:T(8,128)(2,1)S(1)}, u32[]{:S(2)}, u32[]{:S(2)}) %collective-permute-start.8) | collective-permute-done | bytes 36896 | tf_op jit(solution)/shard_map/ppermute | solution.py:381
  23.0 0.0 copy-done.1
  23.0 0.0 copy-start.2
  23.0 4.6 %score.1 = f32[8,128]{1,0:T(8,128)S(1)} custom-call(s32[1]{0:T(128)} %bitcast.refs_0_, bf16[48,128,128]{2,1,0:T(8,128)(2,1)S(1)} %get-tuple-element.11.refs_1_, bf16[48,128,128]{2,1,0:T(8,128)(2,1)S(1)} %get-tuple-element.12.refs_2_, bf16[144,128]{1,0:T(8,128)(2,1)S(1)} %copy-done.1, bf16[144,128]{1,0:T(8,128)(2,1)S(1)} %collective-permute-done.4.refs_4_, ...), custom_call_target="tpu_custom_call" | custom-call | flops 805306368 | bytes 3145728 | tf_op jit(solution)/shard_map/score/pallas_call | solution.py:320
  27.6 10.5 %all_to_all.11 = f32[8,1,128]{2,1,0:T(1,128)S(1)} all-to-all(f32[8,1,128]{2,1,0:T(1,128)S(1)} %bitcast.5), channel_id=1, replica_groups={{0,3,5,6,8,11,13,14},{1,2,4,7,9,10,12,15},{16,19,21,22,24,27,29,30},{17..., dimensions={0} | all-to-all | bytes 8192 | tf_op jit(solution)/shard_map/all_to_all | solution.py:438
  38.1 0.0 copy-done.2
  38.1 1.0 %finish.1 = (f32[4,64]{1,0:T(4,128)}, f32[4,10]{1,0:T(4,128)}) custom-call(f32[8,128]{1,0:T(8,128)S(1)} %bitcast.6, s32[4,64]{1,0:T(4,128)S(1)} %copy-done.2), custom_call_target="tpu_custom_call" | custom-call | tf_op jit(solution)/shard_map/finish/pallas_call | solution.py:366
Async XLA Ops:
  0.6 19.1 %collective-permute-start.1 = (bf16[48,128,128]{2,1,0:T(8,128)(2,1)}, bf16[48,128,128]{2,1,0:T(8,128)(2,1)S(1)}, u32[]{:S(2)}, u32[]{:S(2)}) collective-permute-start(bf16[48,128,128]{2,1,0:T(8,128)(2,1)} %pass0_ref.1), channel_id=1, source_target_pairs={{0,1},{1,0},{2,3},{3,2},{4,5},{5,4},{6,7},{7,6},{8,9},{9,8},{10,11... | collective-permute-start | bytes 4718600 | tf_op jit(solution)/shard_map/ppermute | solution.py:381
  1.2 6.6 %collective-permute-start = (s32[48]{0:T(128)}, s32[48]{0:T(128)S(1)}, u32[]{:S(2)}, u32[]{:S(2)}) collective-permute-start(s32[48]{0:T(128)} %len0_ref.1), channel_id=1, source_target_pairs={{0,1},{1,0},{2,3},{3,2},{4,5},{5,4},{6,7},{7,6},{8,9},{9,8},{10,11... | collective-permute-start | bytes 584 | tf_op jit(solution)/shard_map/ppermute | solution.py:381
  1.2 18.5 %copy-start = (bf16[48,128,128]{2,1,0:T(8,128)(2,1)S(1)}, bf16[48,128,128]{2,1,0:T(8,128)(2,1)}, u32[]{:S(2)}) copy-start(bf16[48,128,128]{2,1,0:T(8,128)(2,1)} %pass0_ref.1) | copy-start | bytes 4718596
  1.2 18.5 %copy-start.3 = (s32[48]{0:T(128)S(1)}, s32[48]{0:T(128)}, u32[]{:S(2)}) copy-start(s32[48]{0:T(128)} %len0_ref.1) | copy-start | bytes 580
  7.7 15.2 %copy-start.1 = (bf16[144,128]{1,0:T(8,128)(2,1)S(1)}, bf16[144,128]{1,0:T(8,128)(2,1)}, u32[]{:S(2)}) copy-start(bf16[144,128]{1,0:T(8,128)(2,1)} %get-tuple-element.10.refs_3_) | copy-start | bytes 110596
  7.8 6.2 %collective-permute-start.5 = (bf16[144,128]{1,0:T(8,128)(2,1)}, bf16[144,128]{1,0:T(8,128)(2,1)S(1)}, u32[]{:S(2)}, u32[]{:S(2)}) collective-permute-start(bf16[144,128]{1,0:T(8,128)(2,1)} %get-tuple-element.10.refs_3_), channel_id=1, source_target_pairs={{0,8},{1,9},{2,10},{3,11},{4,12},{5,13},{6,14},{7,15},{8,0},{9,1},... | collective-permute-start | bytes 110600 | tf_op jit(solution)/shard_map/ppermute | solution.py:381
  11.9 3.8 %collective-permute-start.2 = (bf16[144,128]{1,0:T(8,128)(2,1)}, bf16[144,128]{1,0:T(8,128)(2,1)S(1)}, u32[]{:S(2)}, u32[]{:S(2)}) collective-permute-start(bf16[144,128]{1,0:T(8,128)(2,1)} %get-tuple-element.10.refs_3_), channel_id=1, source_target_pairs={{0,5},{1,4},{2,7},{3,6},{4,1},{5,0},{6,3},{7,2},{8,13},{9,12},{10,... | collective-permute-start | bytes 110600 | tf_op jit(solution)/shard_map/ppermute | solution.py:381
  14.0 5.2 %collective-permute-start.7 = (bf16[144,128]{1,0:T(8,128)(2,1)S(1)}, bf16[144,128]{1,0:T(8,128)(2,1)S(1)}, u32[]{:S(2)}, u32[]{:S(2)}) collective-permute-start(bf16[144,128]{1,0:T(8,128)(2,1)S(1)} %collective-permute-done.5.refs_7_), channel_id=1, source_target_pairs={{0,5},{1,4},{2,7},{3,6},{4,1},{5,0},{6,3},{7,2},{8,13},{9,12},{10,... | collective-permute-start | bytes 110600 | tf_op jit(solution)/shard_map/ppermute | solution.py:381
  15.7 4.0 %collective-permute-start.3 = (bf16[144,128]{1,0:T(8,128)(2,1)S(1)}, bf16[144,128]{1,0:T(8,128)(2,1)S(1)}, u32[]{:S(2)}, u32[]{:S(2)}) collective-permute-start(bf16[144,128]{1,0:T(8,128)(2,1)S(1)} %collective-permute-done.2.refs_5_), channel_id=1, source_target_pairs={{0,3},{1,2},{2,1},{3,0},{4,7},{5,6},{6,5},{7,4},{8,11},{9,10},{10,... | collective-permute-start | bytes 110600 | tf_op jit(solution)/shard_map/ppermute | solution.py:381
  17.4 3.9 %collective-permute-start.4 = (bf16[144,128]{1,0:T(8,128)(2,1)}, bf16[144,128]{1,0:T(8,128)(2,1)S(1)}, u32[]{:S(2)}, u32[]{:S(2)}) collective-permute-start(bf16[144,128]{1,0:T(8,128)(2,1)} %get-tuple-element.10.refs_3_), channel_id=1, source_target_pairs={{0,3},{1,2},{2,1},{3,0},{4,7},{5,6},{6,5},{7,4},{8,11},{9,10},{10,... | collective-permute-start | bytes 110600 | tf_op jit(solution)/shard_map/ppermute | solution.py:381
  17.5 4.7 %collective-permute-start.6 = (bf16[144,128]{1,0:T(8,128)(2,1)S(1)}, bf16[144,128]{1,0:T(8,128)(2,1)S(1)}, u32[]{:S(2)}, u32[]{:S(2)}) collective-permute-start(bf16[144,128]{1,0:T(8,128)(2,1)S(1)} %collective-permute-done.5.refs_7_), channel_id=1, source_target_pairs={{0,3},{1,2},{2,1},{3,0},{4,7},{5,6},{6,5},{7,4},{8,11},{9,10},{10,... | collective-permute-start | bytes 110600 | tf_op jit(solution)/shard_map/ppermute | solution.py:381
  19.2 3.8 %collective-permute-start.8 = (bf16[144,128]{1,0:T(8,128)(2,1)S(1)}, bf16[144,128]{1,0:T(8,128)(2,1)S(1)}, u32[]{:S(2)}, u32[]{:S(2)}) collective-permute-start(bf16[144,128]{1,0:T(8,128)(2,1)S(1)} %collective-permute-done.7.refs_9_), channel_id=1, source_target_pairs={{0,3},{1,2},{2,1},{3,0},{4,7},{5,6},{6,5},{7,4},{8,11},{9,10},{10,... | collective-permute-start | bytes 110600 | tf_op jit(solution)/shard_map/ppermute | solution.py:381
  23.0 15.2 %copy-start.2 = (s32[4,64]{1,0:T(4,128)S(1)}, s32[4,64]{1,0:T(4,128)}, u32[]{:S(2)}) copy-start(s32[4,64]{1,0:T(4,128)} %get-tuple-element.13.spot_ref) | copy-start | bytes 3076

commit v15 on v12

--- a/solution.py
+++ b/solution.py
@@ -20,6 +20,26 @@
     middle = rest.astype(BF16)
     low = (rest - middle.astype(F32)).astype(BF16)
     return high, middle, low
+
+
+ERF_AS_TANH = (
+    0.7978849414561846,
+    0.0363330845700197,
+    -3.259496904628066e-05,
+    -5.53061960886502e-05,
+    3.964744776164795e-06,
+    -1.3226336338657016e-07,
+    1.7561713006335889e-09,
+)
+
+
+def gelu(value):
+    square = value * value
+    factor = ERF_AS_TANH[-1] * square + ERF_AS_TANH[-2]
+    for coefficient in ERF_AS_TANH[-3::-1]:
+        factor = factor * square + coefficient
+    half = 0.5 * value
+    return half + half * jnp.tanh(value * factor)
 
 
 def mask_into(out_ref, pass_ref, len_ref, first, count):
@@ -143,7 +163,7 @@
         if step >= 2:
             total = total + jnp.dot(active, w2_buf[step - 2], preferred_element_type=F32)
         if 1 <= step <= chunks:
-            active = (0.5 * inner * (1.0 + lax.erf(inner * (0.5 ** 0.5)))).astype(BF16)
+            active = gelu(inner).astype(BF16)
         inner = later
         if step == chunks:
             fetch = pltpu.make_async_copy(table, table_v, table_sem)

time: 38 us -> 38.9 us (1.024)
  Pallas kernels: 13.5 us -> 14.3 us
    pallas_call x1, Pallas kernels: 6.5 us -> 7.35 us  [encode(): pl.pallas_call(kernel, out_shape=(jax.ShapeDtypeStruct((tokens + slots, e...]
  transfers between devices with their start and end apart: 9 -> 9, of which waited for: 3 -> 3; matrix products, arithmetic and copies ran while one was open for 0% -> 0% of each run, Pallas kernels for 21% -> 22%
where the time goes in v15:
time: 38.9 us; the launch traced here: 38.7 us
  Pallas kernels  14.3 us (37%)
  blocking collectives  10.1 us (26%)
  starting transfers between devices  8.94 us (23%)
  waiting for transfers between devices  4.67 us (12%)
  between operations  0.71 us (2%)
    all_to_all x1, blocking collectives, per_device(): lax.all_to_all(sums, 'shard', split_axis=0, concat_axis=0, axis_index_gro...  10.1 us
    ppermute x9, starting transfers between devices, swap(): lax.ppermute(value, 'shard', [(i, i ^ distance) for i in range(size)])  8.94 us
    pallas_call x1, Pallas kernels, encode(): pl.pallas_call(kernel, out_shape=(jax.ShapeDtypeStruct((tokens + slots, e...  7.35 us
    ppermute x9, waiting for transfers between devices, swap(): lax.ppermute(value, 'shard', [(i, i ^ distance) for i in range(size)])  4.67 us
    pallas_call x1, Pallas kernels, score(): pl.pallas_call(kernel, out_shape=jax.ShapeDtypeStruct((slots, e), F32), i...  4.64 us
    pallas_call x1, Pallas kernels, mask(): pl.pallas_call(mask_kernel, out_shape=[jax.ShapeDtypeStruct(shape, BF16)]...  1.34 us
    pallas_call x1, Pallas kernels, finish(): pl.pallas_call(finish_kernel, out_shape=(jax.ShapeDtypeStruct(spots.shape...  0.99 us
  transfers between devices with their start and end apart: 9, of which 3 were waited for; matrix products, arithmetic and copies ran while one was open for 0% of the time, Pallas kernels for 22%

profile of v15, /device:TPU:0, one launch (start us, length us, event | category | flops | bytes accessed | tf_op | source)
XLA Modules:
  0.0 38.7 jit_solution(16503090500033312050)
XLA Ops:
  0.6 0.5 %collective-permute-start = (s32[48]{0:T(128)}, s32[48]{0:T(128)S(1)}, u32[]{:S(2)}, u32[]{:S(2)}) collective-permute-start(s32[48]{0:T(128)} %len0_ref.1), channel_id=1, source_target_pairs={{0,1},{1,0},{2,3},{3,2},{4,5},{5,4},{6,7},{7,6},{8,9},{9,8},{10,11... | collective-permute-start | bytes 584 | tf_op jit(solution)/shard_map/ppermute | solution.py:401
  1.2 0.0 copy-start
  1.2 0.0 copy-start.3
  1.2 7.3 %encode.1 = (bf16[144,128]{1,0:T(8,128)(2,1)}, s32[4,64]{1,0:T(4,128)}) custom-call(s32[1]{0:T(128)} %bitcast.refs_0_, s32[4]{0:T(128)} %refs_1_.1, s32[768]{0:T(1024)} %refs_2_.1, s32[4,64]{1,0:T(4,128)} %refs_3_.1, bf16[4,32,768]{2,1,0:T(8,128)(2,1)} %refs_4_.1, bf16[768,3072]{1,0:T(8,128)(2,1)} %refs_5_.1, bf16[3072,768]{1,0:T(8,128)(2,1)} %refs_6_.1, ...), custom_call_target="tpu_custom_call" | custom-call | flops 1207959552 | bytes 9437184 | tf_op jit(solution)/shard_map/encode/pallas_call | solution.py:218
  8.5 0.0 collective-permute-done.len1_ref
  8.5 0.0 copy-done
  8.5 0.0 copy-start.1
  8.5 0.1 collective-permute-start.1
  8.7 2.7 %collective-permute-start.2 = (bf16[144,128]{1,0:T(8,128)(2,1)}, bf16[144,128]{1,0:T(8,128)(2,1)S(1)}, u32[]{:S(2)}, u32[]{:S(2)}) collective-permute-start(bf16[144,128]{1,0:T(8,128)(2,1)} %get-tuple-element.12.refs_3_), channel_id=1, source_target_pairs={{0,5},{1,4},{2,7},{3,6},{4,1},{5,0},{6,3},{7,2},{8,13},{9,12},{10,... | collective-permute-start | bytes 110600 | tf_op jit(solution)/shard_map/ppermute | solution.py:401
  11.4 2.6 %collective-permute-start.5 = (bf16[144,128]{1,0:T(8,128)(2,1)}, bf16[144,128]{1,0:T(8,128)(2,1)S(1)}, u32[]{:S(2)}, u32[]{:S(2)}) collective-permute-start(bf16[144,128]{1,0:T(8,128)(2,1)} %get-tuple-element.12.refs_3_), channel_id=1, source_target_pairs={{0,8},{1,9},{2,10},{3,11},{4,12},{5,13},{6,14},{7,15},{8,0},{9,1},... | collective-permute-start | bytes 110600 | tf_op jit(solution)/shard_map/ppermute | solution.py:401
  14.0 0.0 collective-permute-start.7
  14.0 0.0 collective-permute-done.2.refs_5_
  14.0 1.5 %collective-permute-start.3 = (bf16[144,128]{1,0:T(8,128)(2,1)S(1)}, bf16[144,128]{1,0:T(8,128)(2,1)S(1)}, u32[]{:S(2)}, u32[]{:S(2)}) collective-permute-start(bf16[144,128]{1,0:T(8,128)(2,1)S(1)} %collective-permute-done.2.refs_5_), channel_id=1, source_target_pairs={{0,3},{1,2},{2,1},{3,0},{4,7},{5,6},{6,5},{7,4},{8,11},{9,10},{10,... | collective-permute-start | bytes 110600 | tf_op jit(solution)/shard_map/ppermute | solution.py:401
  15.5 0.3 collective-permute-start.4
  15.7 1.5 %collective-permute-done.5.refs_7_ = bf16[144,128]{1,0:T(8,128)(2,1)S(1)} collective-permute-done((bf16[144,128]{1,0:T(8,128)(2,1)}, bf16[144,128]{1,0:T(8,128)(2,1)S(1)}, u32[]{:S(2)}, u32[]{:S(2)}) %collective-permute-start.5) | collective-permute-done | bytes 36896 | tf_op jit(solution)/shard_map/ppermute | solution.py:401
  17.2 0.0 collective-permute-start.6
  17.2 2.3 %collective-permute-done.7.refs_9_ = bf16[144,128]{1,0:T(8,128)(2,1)S(1)} collective-permute-done((bf16[144,128]{1,0:T(8,128)(2,1)}, bf16[144,128]{1,0:T(8,128)(2,1)S(1)}, u32[]{:S(2)}, u32[]{:S(2)}) %collective-permute-start.7) | collective-permute-done | bytes 36896 | tf_op jit(solution)/shard_map/ppermute | solution.py:401
  19.5 1.2 %collective-permute-start.8 = (bf16[144,128]{1,0:T(8,128)(2,1)S(1)}, bf16[144,128]{1,0:T(8,128)(2,1)S(1)}, u32[]{:S(2)}, u32[]{:S(2)}) collective-permute-start(bf16[144,128]{1,0:T(8,128)(2,1)S(1)} %collective-permute-done.7.refs_9_), channel_id=1, source_target_pairs={{0,3},{1,2},{2,1},{3,0},{4,7},{5,6},{6,5},{7,4},{8,11},{9,10},{10,... | collective-permute-start | bytes 110600 | tf_op jit(solution)/shard_map/ppermute | solution.py:401
  20.7 0.0 collective-permute-done.3._.refs_6_
  20.7 0.0 collective-permute-done.1.pass1_ref
  20.8 0.0 copy-done.3
  20.8 1.3 %mask.1 = (bf16[48,128,128]{2,1,0:T(8,128)(2,1)S(1)}, bf16[48,128,128]{2,1,0:T(8,128)(2,1)S(1)}) custom-call(s32[48]{0:T(128)S(1)} %copy-done.3, s32[48]{0:T(128)S(1)} %collective-permute-done.len1_ref, bf16[48,128,128]{2,1,0:T(8,128)(2,1)S(1)} %copy-done, bf16[48,128,128]{2,1,0:T(8,128)(2,1)S(1)} %collective-permute-done.1.pass1_ref, ...), custom_call_target="tpu_custom_call" | custom-call | flops 12582912 | bytes 6291456 | tf_op jit(solution)/shard_map/mask/pallas_call | solution.py:269
  22.1 0.0 collective-permute-done.4.refs_4_
  22.1 0.0 collective-permute-done.6.refs_8_
  22.1 0.9 %collective-permute-done.8.refs_10_ = bf16[144,128]{1,0:T(8,128)(2,1)S(1)} collective-permute-done((bf16[144,128]{1,0:T(8,128)(2,1)S(1)}, bf16[144,128]{1,0:T(8,128)(2,1)S(1)}, u32[]{:S(2)}, u32[]{:S(2)}) %collective-permute-start.8) | collective-permute-done | bytes 36896 | tf_op jit(solution)/shard_map/ppermute | solution.py:401
  23.0 0.0 copy-done.1
  23.0 0.0 copy-start.2
  23.0 4.6 %score.1 = f32[8,128]{1,0:T(8,128)S(1)} custom-call(s32[1]{0:T(128)} %bitcast.refs_0_, bf16[48,128,128]{2,1,0:T(8,128)(2,1)S(1)} %get-tuple-element.13.refs_1_, bf16[48,128,128]{2,1,0:T(8,128)(2,1)S(1)} %get-tuple-element.14.refs_2_, bf16[144,128]{1,0:T(8,128)(2,1)S(1)} %copy-done.1, bf16[144,128]{1,0:T(8,128)(2,1)S(1)} %collective-permute-done.4.refs_4_, ...), custom_call_target="tpu_custom_call" | custom-call | flops 805306368 | bytes 3145728 | tf_op jit(solution)/shard_map/score/pallas_call | solution.py:340
  27.7 10.1 %all_to_all.11 = f32[8,1,128]{2,1,0:T(1,128)S(1)} all-to-all(f32[8,1,128]{2,1,0:T(1,128)S(1)} %bitcast.5), channel_id=1, replica_groups={{0,3,5,6,8,11,13,14},{1,2,4,7,9,10,12,15},{16,19,21,22,24,27,29,30},{17..., dimensions={0} | all-to-all | bytes 8192 | tf_op jit(solution)/shard_map/all_to_all | solution.py:454
  37.7 0.0 copy-done.2
  37.7 1.0 %finish.1 = (f32[4,64]{1,0:T(4,128)}, f32[4,10]{1,0:T(4,128)}) custom-call(f32[8,128]{1,0:T(8,128)S(1)} %bitcast.6, s32[4,64]{1,0:T(4,128)S(1)} %copy-done.2), custom_call_target="tpu_custom_call" | custom-call | tf_op jit(solution)/shard_map/finish/pallas_call | solution.py:386
Async XLA Ops:
  0.6 7.9 %collective-permute-start = (s32[48]{0:T(128)}, s32[48]{0:T(128)S(1)}, u32[]{:S(2)}, u32[]{:S(2)}) collective-permute-start(s32[48]{0:T(128)} %len0_ref.1), channel_id=1, source_target_pairs={{0,1},{1,0},{2,3},{3,2},{4,5},{5,4},{6,7},{7,6},{8,9},{9,8},{10,11... | collective-permute-start | bytes 584 | tf_op jit(solution)/shard_map/ppermute | solution.py:401
  1.2 7.4 %copy-start = (bf16[48,128,128]{2,1,0:T(8,128)(2,1)S(1)}, bf16[48,128,128]{2,1,0:T(8,128)(2,1)}, u32[]{:S(2)}) copy-start(bf16[48,128,128]{2,1,0:T(8,128)(2,1)} %pass0_ref.1) | copy-start | bytes 4718596
  1.2 19.6 %copy-start.3 = (s32[48]{0:T(128)S(1)}, s32[48]{0:T(128)}, u32[]{:S(2)}) copy-start(s32[48]{0:T(128)} %len0_ref.1) | copy-start | bytes 580
  8.5 14.5 %copy-start.1 = (bf16[144,128]{1,0:T(8,128)(2,1)S(1)}, bf16[144,128]{1,0:T(8,128)(2,1)}, u32[]{:S(2)}) copy-start(bf16[144,128]{1,0:T(8,128)(2,1)} %get-tuple-element.12.refs_3_) | copy-start | bytes 110596
  8.5 12.2 %collective-permute-start.1 = (bf16[48,128,128]{2,1,0:T(8,128)(2,1)S(1)}, bf16[48,128,128]{2,1,0:T(8,128)(2,1)S(1)}, u32[]{:S(2)}, u32[]{:S(2)}) collective-permute-start(bf16[48,128,128]{2,1,0:T(8,128)(2,1)S(1)} %copy-done), channel_id=1, source_target_pairs={{0,1},{1,0},{2,3},{3,2},{4,5},{5,4},{6,7},{7,6},{8,9},{9,8},{10,11... | collective-permute-start | bytes 4718600 | tf_op jit(solution)/shard_map/ppermute | solution.py:401
  8.7 5.3 %collective-permute-start.2 = (bf16[144,128]{1,0:T(8,128)(2,1)}, bf16[144,128]{1,0:T(8,128)(2,1)S(1)}, u32[]{:S(2)}, u32[]{:S(2)}) collective-permute-start(bf16[144,128]{1,0:T(8,128)(2,1)} %get-tuple-element.12.refs_3_), channel_id=1, source_target_pairs={{0,5},{1,4},{2,7},{3,6},{4,1},{5,0},{6,3},{7,2},{8,13},{9,12},{10,... | collective-permute-start | bytes 110600 | tf_op jit(solution)/shard_map/ppermute | solution.py:401
  11.4 5.9 %collective-permute-start.5 = (bf16[144,128]{1,0:T(8,128)(2,1)}, bf16[144,128]{1,0:T(8,128)(2,1)S(1)}, u32[]{:S(2)}, u32[]{:S(2)}) collective-permute-start(bf16[144,128]{1,0:T(8,128)(2,1)} %get-tuple-element.12.refs_3_), channel_id=1, source_target_pairs={{0,8},{1,9},{2,10},{3,11},{4,12},{5,13},{6,14},{7,15},{8,0},{9,1},... | collective-permute-start | bytes 110600 | tf_op jit(solution)/shard_map/ppermute | solution.py:401
  14.0 5.5 %collective-permute-start.7 = (bf16[144,128]{1,0:T(8,128)(2,1)}, bf16[144,128]{1,0:T(8,128)(2,1)S(1)}, u32[]{:S(2)}, u32[]{:S(2)}) collective-permute-start(bf16[144,128]{1,0:T(8,128)(2,1)} %get-tuple-element.12.refs_3_), channel_id=1, source_target_pairs={{0,13},{1,12},{2,15},{3,14},{4,9},{5,8},{6,11},{7,10},{8,5},{9,4},... | collective-permute-start | bytes 110600 | tf_op jit(solution)/shard_map/ppermute | solution.py:401
  14.0 6.7 %collective-permute-start.3 = (bf16[144,128]{1,0:T(8,128)(2,1)S(1)}, bf16[144,128]{1,0:T(8,128)(2,1)S(1)}, u32[]{:S(2)}, u32[]{:S(2)}) collective-permute-start(bf16[144,128]{1,0:T(8,128)(2,1)S(1)} %collective-permute-done.2.refs_5_), channel_id=1, source_target_pairs={{0,3},{1,2},{2,1},{3,0},{4,7},{5,6},{6,5},{7,4},{8,11},{9,10},{10,... | collective-permute-start | bytes 110600 | tf_op jit(solution)/shard_map/ppermute | solution.py:401
  15.5 6.7 %collective-permute-start.4 = (bf16[144,128]{1,0:T(8,128)(2,1)}, bf16[144,128]{1,0:T(8,128)(2,1)S(1)}, u32[]{:S(2)}, u32[]{:S(2)}) collective-permute-start(bf16[144,128]{1,0:T(8,128)(2,1)} %get-tuple-element.12.refs_3_), channel_id=1, source_target_pairs={{0,3},{1,2},{2,1},{3,0},{4,7},{5,6},{6,5},{7,4},{8,11},{9,10},{10,... | collective-permute-start | bytes 110600 | tf_op jit(solution)/shard_map/ppermute | solution.py:401
  17.2 4.9 %collective-permute-start.6 = (bf16[144,128]{1,0:T(8,128)(2,1)S(1)}, bf16[144,128]{1,0:T(8,128)(2,1)S(1)}, u32[]{:S(2)}, u32[]{:S(2)}) collective-permute-start(bf16[144,128]{1,0:T(8,128)(2,1)S(1)} %collective-permute-done.5.refs_7_), channel_id=1, source_target_pairs={{0,3},{1,2},{2,1},{3,0},{4,7},{5,6},{6,5},{7,4},{8,11},{9,10},{10,... | collective-permute-start | bytes 110600 | tf_op jit(solution)/shard_map/ppermute | solution.py:401
  19.5 3.5 %collective-permute-start.8 = (bf16[144,128]{1,0:T(8,128)(2,1)S(1)}, bf16[144,128]{1,0:T(8,128)(2,1)S(1)}, u32[]{:S(2)}, u32[]{:S(2)}) collective-permute-start(bf16[144,128]{1,0:T(8,128)(2,1)S(1)} %collective-permute-done.7.refs_9_), channel_id=1, source_target_pairs={{0,3},{1,2},{2,1},{3,0},{4,7},{5,6},{6,5},{7,4},{8,11},{9,10},{10,... | collective-permute-start | bytes 110600 | tf_op jit(solution)/shard_map/ppermute | solution.py:401
  23.0 14.7 %copy-start.2 = (s32[4,64]{1,0:T(4,128)S(1)}, s32[4,64]{1,0:T(4,128)}, u32[]{:S(2)}) copy-start(s32[4,64]{1,0:T(4,128)} %get-tuple-element.15.spot_ref) | copy-start | bytes 3076

commit v16 on v12

--- a/solution.py
+++ b/solution.py
@@ -265,6 +265,7 @@
     rows = -(-slots // 16) * 16
     tokens = message - rows
     group = min(slots, 256 // token_count)
+    unroll = 24 if slots == group else 8
     chip = jnp.right_shift(me_ref[0], 1)
     mine = lax.broadcasted_iota(jnp.int32, (rows, lanes), 0) == chip
     for s in range(slots):
@@ -277,11 +278,11 @@
 
     for first, pass_ref in ((half, other_ref), (0, own_ref)):
 
-        def eight(step, carry):
+        def several(step, carry):
             for part in range(slots // group):
                 rows = []
-                for j in range(8):
-                    p = step * 8 + j
+                for j in range(unroll):
+                    p = step * unroll + j
                     picked = jnp.concatenate(
                         [
                             got_refs[s][pl.ds(pl.multiple_of(index[s, first + p], token_count), token_count), :]
@@ -291,13 +292,15 @@
                     )
                     similar = lax.dot_general(pass_ref[p], picked, NT, preferred_element_type=F32)
                     rows.append(jnp.max(similar, axis=0, keepdims=True))
-                best_ref[
-                    pl.ds(pl.multiple_of(first + step * 8, 8), 8),
-                    pl.ds(part * group * token_count, group * token_count),
-                ] = jnp.concatenate(rows, axis=0)
+                    if len(rows) == 8:
+                        best_ref[
+                            pl.ds(pl.multiple_of(first + step * unroll + j - 7, 8), 8),
+                            pl.ds(part * group * token_count, group * token_count),
+                        ] = jnp.concatenate(rows, axis=0)
+                        rows = []
             return carry
 
-        lax.fori_loop(0, half // 8, eight, 0)
+        lax.fori_loop(0, half // unroll, several, 0)
     wide = best_ref.shape[1]
     source = lax.broadcasted_iota(jnp.int32, (slots, wide), 0)
     column = lax.broadcasted_iota(jnp.int32, (slots, wide), 1)

time: 38 us -> 36.6 us (0.963)
  Pallas kernels: 13.5 us -> 12 us
    pallas_call x1, Pallas kernels: 4.64 us -> 3.21 us  [score(): pl.pallas_call(kernel, out_shape=jax.ShapeDtypeStruct((slots, e), F32), i...]
  transfers between devices with their start and end apart: 9 -> 9, of which waited for: 3 -> 3; matrix products, arithmetic and copies ran while one was open for 0% -> 0% of each run, Pallas kernels for 21% -> 22%
where the time goes in v16:
time: 36.6 us; the launch traced here: 36.4 us
  Pallas kernels  12 us (33%)
  blocking collectives  10.1 us (28%)
  starting transfers between devices  8.92 us (24%)
  waiting for transfers between devices  4.67 us (13%)
  between operations  0.71 us (2%)
    all_to_all x1, blocking collectives, per_device(): lax.all_to_all(sums, 'shard', split_axis=0, concat_axis=0, axis_index_gro...  10.1 us
    ppermute x9, starting transfers between devices, swap(): lax.ppermute(value, 'shard', [(i, i ^ distance) for i in range(size)])  8.92 us
    pallas_call x1, Pallas kernels, encode(): pl.pallas_call(kernel, out_shape=(jax.ShapeDtypeStruct((tokens + slots, e...  6.5 us
    ppermute x9, waiting for transfers between devices, swap(): lax.ppermute(value, 'shard', [(i, i ^ distance) for i in range(size)])  4.67 us
    pallas_call x1, Pallas kernels, score(): pl.pallas_call(kernel, out_shape=jax.ShapeDtypeStruct((slots, e), F32), i...  3.21 us
    pallas_call x1, Pallas kernels, mask(): pl.pallas_call(mask_kernel, out_shape=[jax.ShapeDtypeStruct(shape, BF16)]...  1.34 us
    pallas_call x1, Pallas kernels, finish(): pl.pallas_call(finish_kernel, out_shape=(jax.ShapeDtypeStruct(spots.shape...  0.99 us
  transfers between devices with their start and end apart: 9, of which 3 were waited for; matrix products, arithmetic and copies ran while one was open for 0% of the time, Pallas kernels for 22%

profile of v16, /device:TPU:0, one launch (start us, length us, event | category | flops | bytes accessed | tf_op | source)
XLA Modules:
  0.0 36.4 jit_solution(9785438192703252681)
XLA Ops:
  0.6 0.5 %collective-permute-start = (s32[48]{0:T(128)}, s32[48]{0:T(128)S(1)}, u32[]{:S(2)}, u32[]{:S(2)}) collective-permute-start(s32[48]{0:T(128)} %len0_ref.1), channel_id=1, source_target_pairs={{0,1},{1,0},{2,3},{3,2},{4,5},{5,4},{6,7},{7,6},{8,9},{9,8},{10,11... | collective-permute-start | bytes 584 | tf_op jit(solution)/shard_map/ppermute | solution.py:384
  1.2 0.0 copy-start
  1.2 0.0 copy-start.3
  1.2 6.5 %encode.1 = (bf16[144,128]{1,0:T(8,128)(2,1)}, s32[4,64]{1,0:T(4,128)}) custom-call(s32[1]{0:T(128)} %bitcast.refs_0_, s32[4]{0:T(128)} %refs_1_.1, s32[768]{0:T(1024)} %refs_2_.1, s32[4,64]{1,0:T(4,128)} %refs_3_.1, bf16[4,32,768]{2,1,0:T(8,128)(2,1)} %refs_4_.1, bf16[768,3072]{1,0:T(8,128)(2,1)} %refs_5_.1, bf16[3072,768]{1,0:T(8,128)(2,1)} %refs_6_.1, ...), custom_call_target="tpu_custom_call" | custom-call | flops 1207959552 | bytes 9437184 | tf_op jit(solution)/shard_map/encode/pallas_call | solution.py:198
  7.7 0.0 collective-permute-done.len1_ref
  7.7 0.0 copy-done
  7.7 0.0 copy-start.1
  7.7 0.1 collective-permute-start.1
  7.8 2.7 %collective-permute-start.2 = (bf16[144,128]{1,0:T(8,128)(2,1)}, bf16[144,128]{1,0:T(8,128)(2,1)S(1)}, u32[]{:S(2)}, u32[]{:S(2)}) collective-permute-start(bf16[144,128]{1,0:T(8,128)(2,1)} %get-tuple-element.12.refs_3_), channel_id=1, source_target_pairs={{0,5},{1,4},{2,7},{3,6},{4,1},{5,0},{6,3},{7,2},{8,13},{9,12},{10,... | collective-permute-start | bytes 110600 | tf_op jit(solution)/shard_map/ppermute | solution.py:384
  10.5 2.6 %collective-permute-start.5 = (bf16[144,128]{1,0:T(8,128)(2,1)}, bf16[144,128]{1,0:T(8,128)(2,1)S(1)}, u32[]{:S(2)}, u32[]{:S(2)}) collective-permute-start(bf16[144,128]{1,0:T(8,128)(2,1)} %get-tuple-element.12.refs_3_), channel_id=1, source_target_pairs={{0,8},{1,9},{2,10},{3,11},{4,12},{5,13},{6,14},{7,15},{8,0},{9,1},... | collective-permute-start | bytes 110600 | tf_op jit(solution)/shard_map/ppermute | solution.py:384
  13.1 0.0 collective-permute-start.7
  13.1 0.0 collective-permute-done.2.refs_5_
  13.1 1.5 %collective-permute-start.3 = (bf16[144,128]{1,0:T(8,128)(2,1)S(1)}, bf16[144,128]{1,0:T(8,128)(2,1)S(1)}, u32[]{:S(2)}, u32[]{:S(2)}) collective-permute-start(bf16[144,128]{1,0:T(8,128)(2,1)S(1)} %collective-permute-done.2.refs_5_), channel_id=1, source_target_pairs={{0,3},{1,2},{2,1},{3,0},{4,7},{5,6},{6,5},{7,4},{8,11},{9,10},{10,... | collective-permute-start | bytes 110600 | tf_op jit(solution)/shard_map/ppermute | solution.py:384
  14.6 0.3 collective-permute-start.4
  14.9 1.5 %collective-permute-done.5.refs_7_ = bf16[144,128]{1,0:T(8,128)(2,1)S(1)} collective-permute-done((bf16[144,128]{1,0:T(8,128)(2,1)}, bf16[144,128]{1,0:T(8,128)(2,1)S(1)}, u32[]{:S(2)}, u32[]{:S(2)}) %collective-permute-start.5) | collective-permute-done | bytes 36896 | tf_op jit(solution)/shard_map/ppermute | solution.py:384
  16.4 0.0 collective-permute-start.6
  16.4 2.3 %collective-permute-done.7.refs_9_ = bf16[144,128]{1,0:T(8,128)(2,1)S(1)} collective-permute-done((bf16[144,128]{1,0:T(8,128)(2,1)}, bf16[144,128]{1,0:T(8,128)(2,1)S(1)}, u32[]{:S(2)}, u32[]{:S(2)}) %collective-permute-start.7) | collective-permute-done | bytes 36896 | tf_op jit(solution)/shard_map/ppermute | solution.py:384
  18.6 1.2 %collective-permute-start.8 = (bf16[144,128]{1,0:T(8,128)(2,1)S(1)}, bf16[144,128]{1,0:T(8,128)(2,1)S(1)}, u32[]{:S(2)}, u32[]{:S(2)}) collective-permute-start(bf16[144,128]{1,0:T(8,128)(2,1)S(1)} %collective-permute-done.7.refs_9_), channel_id=1, source_target_pairs={{0,3},{1,2},{2,1},{3,0},{4,7},{5,6},{6,5},{7,4},{8,11},{9,10},{10,... | collective-permute-start | bytes 110600 | tf_op jit(solution)/shard_map/ppermute | solution.py:384
  19.9 0.0 collective-permute-done.3._.refs_6_
  19.9 0.0 collective-permute-done.1.pass1_ref
  19.9 0.0 copy-done.3
  19.9 1.3 %mask.1 = (bf16[48,128,128]{2,1,0:T(8,128)(2,1)S(1)}, bf16[48,128,128]{2,1,0:T(8,128)(2,1)S(1)}) custom-call(s32[48]{0:T(128)S(1)} %copy-done.3, s32[48]{0:T(128)S(1)} %collective-permute-done.len1_ref, bf16[48,128,128]{2,1,0:T(8,128)(2,1)S(1)} %copy-done, bf16[48,128,128]{2,1,0:T(8,128)(2,1)S(1)} %collective-permute-done.1.pass1_ref, ...), custom_call_target="tpu_custom_call" | custom-call | flops 12582912 | bytes 6291456 | tf_op jit(solution)/shard_map/mask/pallas_call | solution.py:249
  21.2 0.0 collective-permute-done.4.refs_4_
  21.2 0.0 collective-permute-done.6.refs_8_
  21.3 0.9 %collective-permute-done.8.refs_10_ = bf16[144,128]{1,0:T(8,128)(2,1)S(1)} collective-permute-done((bf16[144,128]{1,0:T(8,128)(2,1)S(1)}, bf16[144,128]{1,0:T(8,128)(2,1)S(1)}, u32[]{:S(2)}, u32[]{:S(2)}) %collective-permute-start.8) | collective-permute-done | bytes 36896 | tf_op jit(solution)/shard_map/ppermute | solution.py:384
  22.1 0.0 copy-done.1
  22.1 0.0 copy-start.2
  22.1 3.2 %score.1 = f32[8,128]{1,0:T(8,128)S(1)} custom-call(s32[1]{0:T(128)} %bitcast.refs_0_, bf16[48,128,128]{2,1,0:T(8,128)(2,1)S(1)} %get-tuple-element.13.refs_1_, bf16[48,128,128]{2,1,0:T(8,128)(2,1)S(1)} %get-tuple-element.14.refs_2_, bf16[144,128]{1,0:T(8,128)(2,1)S(1)} %copy-done.1, bf16[144,128]{1,0:T(8,128)(2,1)S(1)} %collective-permute-done.4.refs_4_, ...), custom_call_target="tpu_custom_call" | custom-call | flops 805306368 | bytes 3145728 | tf_op jit(solution)/shard_map/score/pallas_call | solution.py:323
  25.4 10.1 %all_to_all.11 = f32[8,1,128]{2,1,0:T(1,128)S(1)} all-to-all(f32[8,1,128]{2,1,0:T(1,128)S(1)} %bitcast.5), channel_id=1, replica_groups={{0,3,5,6,8,11,13,14},{1,2,4,7,9,10,12,15},{16,19,21,22,24,27,29,30},{17..., dimensions={0} | all-to-all | bytes 8192 | tf_op jit(solution)/shard_map/all_to_all | solution.py:437
  35.4 0.0 copy-done.2
  35.4 1.0 %finish.1 = (f32[4,64]{1,0:T(4,128)}, f32[4,10]{1,0:T(4,128)}) custom-call(f32[8,128]{1,0:T(8,128)S(1)} %bitcast.6, s32[4,64]{1,0:T(4,128)S(1)} %copy-done.2), custom_call_target="tpu_custom_call" | custom-call | tf_op jit(solution)/shard_map/finish/pallas_call | solution.py:369
Async XLA Ops:
  0.6 7.0 %collective-permute-start = (s32[48]{0:T(128)}, s32[48]{0:T(128)S(1)}, u32[]{:S(2)}, u32[]{:S(2)}) collective-permute-start(s32[48]{0:T(128)} %len0_ref.1), channel_id=1, source_target_pairs={{0,1},{1,0},{2,3},{3,2},{4,5},{5,4},{6,7},{7,6},{8,9},{9,8},{10,11... | collective-permute-start | bytes 584 | tf_op jit(solution)/shard_map/ppermute | solution.py:384
  1.2 6.5 %copy-start = (bf16[48,128,128]{2,1,0:T(8,128)(2,1)S(1)}, bf16[48,128,128]{2,1,0:T(8,128)(2,1)}, u32[]{:S(2)}) copy-start(bf16[48,128,128]{2,1,0:T(8,128)(2,1)} %pass0_ref.1) | copy-start | bytes 4718596
  1.2 18.7 %copy-start.3 = (s32[48]{0:T(128)S(1)}, s32[48]{0:T(128)}, u32[]{:S(2)}) copy-start(s32[48]{0:T(128)} %len0_ref.1) | copy-start | bytes 580
  7.7 14.4 %copy-start.1 = (bf16[144,128]{1,0:T(8,128)(2,1)S(1)}, bf16[144,128]{1,0:T(8,128)(2,1)}, u32[]{:S(2)}) copy-start(bf16[144,128]{1,0:T(8,128)(2,1)} %get-tuple-element.12.refs_3_) | copy-start | bytes 110596
  7.7 12.2 %collective-permute-start.1 = (bf16[48,128,128]{2,1,0:T(8,128)(2,1)S(1)}, bf16[48,128,128]{2,1,0:T(8,128)(2,1)S(1)}, u32[]{:S(2)}, u32[]{:S(2)}) collective-permute-start(bf16[48,128,128]{2,1,0:T(8,128)(2,1)S(1)} %copy-done), channel_id=1, source_target_pairs={{0,1},{1,0},{2,3},{3,2},{4,5},{5,4},{6,7},{7,6},{8,9},{9,8},{10,11... | collective-permute-start | bytes 4718600 | tf_op jit(solution)/shard_map/ppermute | solution.py:384
  7.8 5.3 %collective-permute-start.2 = (bf16[144,128]{1,0:T(8,128)(2,1)}, bf16[144,128]{1,0:T(8,128)(2,1)S(1)}, u32[]{:S(2)}, u32[]{:S(2)}) collective-permute-start(bf16[144,128]{1,0:T(8,128)(2,1)} %get-tuple-element.12.refs_3_), channel_id=1, source_target_pairs={{0,5},{1,4},{2,7},{3,6},{4,1},{5,0},{6,3},{7,2},{8,13},{9,12},{10,... | collective-permute-start | bytes 110600 | tf_op jit(solution)/shard_map/ppermute | solution.py:384
  10.5 5.9 %collective-permute-start.5 = (bf16[144,128]{1,0:T(8,128)(2,1)}, bf16[144,128]{1,0:T(8,128)(2,1)S(1)}, u32[]{:S(2)}, u32[]{:S(2)}) collective-permute-start(bf16[144,128]{1,0:T(8,128)(2,1)} %get-tuple-element.12.refs_3_), channel_id=1, source_target_pairs={{0,8},{1,9},{2,10},{3,11},{4,12},{5,13},{6,14},{7,15},{8,0},{9,1},... | collective-permute-start | bytes 110600 | tf_op jit(solution)/shard_map/ppermute | solution.py:384
  13.1 5.5 %collective-permute-start.7 = (bf16[144,128]{1,0:T(8,128)(2,1)}, bf16[144,128]{1,0:T(8,128)(2,1)S(1)}, u32[]{:S(2)}, u32[]{:S(2)}) collective-permute-start(bf16[144,128]{1,0:T(8,128)(2,1)} %get-tuple-element.12.refs_3_), channel_id=1, source_target_pairs={{0,13},{1,12},{2,15},{3,14},{4,9},{5,8},{6,11},{7,10},{8,5},{9,4},... | collective-permute-start | bytes 110600 | tf_op jit(solution)/shard_map/ppermute | solution.py:384
  13.1 6.8 %collective-permute-start.3 = (bf16[144,128]{1,0:T(8,128)(2,1)S(1)}, bf16[144,128]{1,0:T(8,128)(2,1)S(1)}, u32[]{:S(2)}, u32[]{:S(2)}) collective-permute-start(bf16[144,128]{1,0:T(8,128)(2,1)S(1)} %collective-permute-done.2.refs_5_), channel_id=1, source_target_pairs={{0,3},{1,2},{2,1},{3,0},{4,7},{5,6},{6,5},{7,4},{8,11},{9,10},{10,... | collective-permute-start | bytes 110600 | tf_op jit(solution)/shard_map/ppermute | solution.py:384
  14.6 6.6 %collective-permute-start.4 = (bf16[144,128]{1,0:T(8,128)(2,1)}, bf16[144,128]{1,0:T(8,128)(2,1)S(1)}, u32[]{:S(2)}, u32[]{:S(2)}) collective-permute-start(bf16[144,128]{1,0:T(8,128)(2,1)} %get-tuple-element.12.refs_3_), channel_id=1, source_target_pairs={{0,3},{1,2},{2,1},{3,0},{4,7},{5,6},{6,5},{7,4},{8,11},{9,10},{10,... | collective-permute-start | bytes 110600 | tf_op jit(solution)/shard_map/ppermute | solution.py:384
  16.4 4.9 %collective-permute-start.6 = (bf16[144,128]{1,0:T(8,128)(2,1)S(1)}, bf16[144,128]{1,0:T(8,128)(2,1)S(1)}, u32[]{:S(2)}, u32[]{:S(2)}) collective-permute-start(bf16[144,128]{1,0:T(8,128)(2,1)S(1)} %collective-permute-done.5.refs_7_), channel_id=1, source_target_pairs={{0,3},{1,2},{2,1},{3,0},{4,7},{5,6},{6,5},{7,4},{8,11},{9,10},{10,... | collective-permute-start | bytes 110600 | tf_op jit(solution)/shard_map/ppermute | solution.py:384
  18.6 3.5 %collective-permute-start.8 = (bf16[144,128]{1,0:T(8,128)(2,1)S(1)}, bf16[144,128]{1,0:T(8,128)(2,1)S(1)}, u32[]{:S(2)}, u32[]{:S(2)}) collective-permute-start(bf16[144,128]{1,0:T(8,128)(2,1)S(1)} %collective-permute-done.7.refs_9_), channel_id=1, source_target_pairs={{0,3},{1,2},{2,1},{3,0},{4,7},{5,6},{6,5},{7,4},{8,11},{9,10},{10,... | collective-permute-start | bytes 110600 | tf_op jit(solution)/shard_map/ppermute | solution.py:384
  22.1 13.3 %copy-start.2 = (s32[4,64]{1,0:T(4,128)S(1)}, s32[4,64]{1,0:T(4,128)}, u32[]{:S(2)}) copy-start(s32[4,64]{1,0:T(4,128)} %get-tuple-element.15.spot_ref) | copy-start | bytes 3076

commit v17 on v16

--- a/solution.py
+++ b/solution.py
@@ -188,7 +188,7 @@
     e = embed_weight.shape[1]
     slots = -(-slots // 16) * 16
     assert 2 * half <= e == 128
-    chunks = 6
+    chunks = 4
     width = ff // chunks
     tokens = query_count * token_count
 
@@ -265,7 +265,7 @@
     rows = -(-slots // 16) * 16
     tokens = message - rows
     group = min(slots, 256 // token_count)
-    unroll = 24 if slots == group else 8
+    unroll = half if slots == group else 8
     chip = jnp.right_shift(me_ref[0], 1)
     mine = lax.broadcasted_iota(jnp.int32, (rows, lanes), 0) == chip
     for s in range(slots):

time: 36.6 us -> 35.2 us (0.962)
  Pallas kernels: 12 us -> 10.7 us
    pallas_call x1, Pallas kernels: 6.5 us -> 5.69 us  [encode(): pl.pallas_call(kernel, out_shape=(jax.ShapeDtypeStruct((tokens + slots, e...]
    pallas_call x1, Pallas kernels: 3.21 us -> 2.64 us  [score(): pl.pallas_call(kernel, out_shape=jax.ShapeDtypeStruct((slots, e), F32), i...]
  transfers between devices with their start and end apart: 9 -> 9, of which waited for: 3 -> 3; matrix products, arithmetic and copies ran while one was open for 0% -> 0% of each run, Pallas kernels for 22% -> 20%
where the time goes in v17:
time: 35.2 us; the launch traced here: 35 us
  Pallas kernels  10.7 us (30%)
  blocking collectives  10.1 us (29%)
  starting transfers between devices  8.93 us (25%)
  waiting for transfers between devices  4.66 us (13%)
  between operations  0.71 us (2%)
    all_to_all x1, blocking collectives, per_device(): lax.all_to_all(sums, 'shard', split_axis=0, concat_axis=0, axis_index_gro...  10.1 us
    ppermute x9, starting transfers between devices, swap(): lax.ppermute(value, 'shard', [(i, i ^ distance) for i in range(size)])  8.93 us
    pallas_call x1, Pallas kernels, encode(): pl.pallas_call(kernel, out_shape=(jax.ShapeDtypeStruct((tokens + slots, e...  5.69 us
    ppermute x9, waiting for transfers between devices, swap(): lax.ppermute(value, 'shard', [(i, i ^ distance) for i in range(size)])  4.66 us
    pallas_call x1, Pallas kernels, score(): pl.pallas_call(kernel, out_shape=jax.ShapeDtypeStruct((slots, e), F32), i...  2.64 us
    pallas_call x1, Pallas kernels, mask(): pl.pallas_call(mask_kernel, out_shape=[jax.ShapeDtypeStruct(shape, BF16)]...  1.34 us
    pallas_call x1, Pallas kernels, finish(): pl.pallas_call(finish_kernel, out_shape=(jax.ShapeDtypeStruct(spots.shape...  0.99 us
  transfers between devices with their start and end apart: 9, of which 3 were waited for; matrix products, arithmetic and copies ran while one was open for 0% of the time, Pallas kernels for 20%

profile of v17, /device:TPU:0, one launch (start us, length us, event | category | flops | bytes accessed | tf_op | source)
XLA Modules:
  0.0 35.0 jit_solution(694459280446619010)
XLA Ops:
  0.6 0.5 %collective-permute-start = (s32[48]{0:T(128)}, s32[48]{0:T(128)S(1)}, u32[]{:S(2)}, u32[]{:S(2)}) collective-permute-start(s32[48]{0:T(128)} %len0_ref.1), channel_id=1, source_target_pairs={{0,1},{1,0},{2,3},{3,2},{4,5},{5,4},{6,7},{7,6},{8,9},{9,8},{10,11... | collective-permute-start | bytes 584 | tf_op jit(solution)/shard_map/ppermute | solution.py:384
  1.2 0.0 copy-start
  1.2 0.0 copy-start.3
  1.2 5.7 %encode.1 = (bf16[144,128]{1,0:T(8,128)(2,1)}, s32[4,64]{1,0:T(4,128)}) custom-call(s32[1]{0:T(128)} %bitcast.refs_0_, s32[4]{0:T(128)} %refs_1_.1, s32[768]{0:T(1024)} %refs_2_.1, s32[4,64]{1,0:T(4,128)} %refs_3_.1, bf16[4,32,768]{2,1,0:T(8,128)(2,1)} %refs_4_.1, bf16[768,3072]{1,0:T(8,128)(2,1)} %refs_5_.1, bf16[3072,768]{1,0:T(8,128)(2,1)} %refs_6_.1, ...), custom_call_target="tpu_custom_call" | custom-call | flops 1207959552 | bytes 9437184 | tf_op jit(solution)/shard_map/encode/pallas_call | solution.py:198
  6.9 0.0 collective-permute-done.len1_ref
  6.9 0.0 copy-done
  6.9 0.0 copy-start.1
  6.9 0.1 collective-permute-start.1
  7.0 2.7 %collective-permute-start.2 = (bf16[144,128]{1,0:T(8,128)(2,1)}, bf16[144,128]{1,0:T(8,128)(2,1)S(1)}, u32[]{:S(2)}, u32[]{:S(2)}) collective-permute-start(bf16[144,128]{1,0:T(8,128)(2,1)} %get-tuple-element.12.refs_3_), channel_id=1, source_target_pairs={{0,5},{1,4},{2,7},{3,6},{4,1},{5,0},{6,3},{7,2},{8,13},{9,12},{10,... | collective-permute-start | bytes 110600 | tf_op jit(solution)/shard_map/ppermute | solution.py:384
  9.7 2.6 %collective-permute-start.5 = (bf16[144,128]{1,0:T(8,128)(2,1)}, bf16[144,128]{1,0:T(8,128)(2,1)S(1)}, u32[]{:S(2)}, u32[]{:S(2)}) collective-permute-start(bf16[144,128]{1,0:T(8,128)(2,1)} %get-tuple-element.12.refs_3_), channel_id=1, source_target_pairs={{0,8},{1,9},{2,10},{3,11},{4,12},{5,13},{6,14},{7,15},{8,0},{9,1},... | collective-permute-start | bytes 110600 | tf_op jit(solution)/shard_map/ppermute | solution.py:384
  12.3 0.0 collective-permute-start.7
  12.3 0.0 collective-permute-done.2.refs_5_
  12.3 1.5 %collective-permute-start.3 = (bf16[144,128]{1,0:T(8,128)(2,1)S(1)}, bf16[144,128]{1,0:T(8,128)(2,1)S(1)}, u32[]{:S(2)}, u32[]{:S(2)}) collective-permute-start(bf16[144,128]{1,0:T(8,128)(2,1)S(1)} %collective-permute-done.2.refs_5_), channel_id=1, source_target_pairs={{0,3},{1,2},{2,1},{3,0},{4,7},{5,6},{6,5},{7,4},{8,11},{9,10},{10,... | collective-permute-start | bytes 110600 | tf_op jit(solution)/shard_map/ppermute | solution.py:384
  13.8 0.3 collective-permute-start.4
  14.1 1.5 %collective-permute-done.5.refs_7_ = bf16[144,128]{1,0:T(8,128)(2,1)S(1)} collective-permute-done((bf16[144,128]{1,0:T(8,128)(2,1)}, bf16[144,128]{1,0:T(8,128)(2,1)S(1)}, u32[]{:S(2)}, u32[]{:S(2)}) %collective-permute-start.5) | collective-permute-done | bytes 36896 | tf_op jit(solution)/shard_map/ppermute | solution.py:384
  15.6 0.0 collective-permute-start.6
  15.6 2.3 %collective-permute-done.7.refs_9_ = bf16[144,128]{1,0:T(8,128)(2,1)S(1)} collective-permute-done((bf16[144,128]{1,0:T(8,128)(2,1)}, bf16[144,128]{1,0:T(8,128)(2,1)S(1)}, u32[]{:S(2)}, u32[]{:S(2)}) %collective-permute-start.7) | collective-permute-done | bytes 36896 | tf_op jit(solution)/shard_map/ppermute | solution.py:384
  17.8 1.2 %collective-permute-start.8 = (bf16[144,128]{1,0:T(8,128)(2,1)S(1)}, bf16[144,128]{1,0:T(8,128)(2,1)S(1)}, u32[]{:S(2)}, u32[]{:S(2)}) collective-permute-start(bf16[144,128]{1,0:T(8,128)(2,1)S(1)} %collective-permute-done.7.refs_9_), channel_id=1, source_target_pairs={{0,3},{1,2},{2,1},{3,0},{4,7},{5,6},{6,5},{7,4},{8,11},{9,10},{10,... | collective-permute-start | bytes 110600 | tf_op jit(solution)/shard_map/ppermute | solution.py:384
  19.1 0.0 collective-permute-done.3._.refs_6_
  19.1 0.0 collective-permute-done.1.pass1_ref
  19.1 0.0 copy-done.3
  19.1 1.3 %mask.1 = (bf16[48,128,128]{2,1,0:T(8,128)(2,1)S(1)}, bf16[48,128,128]{2,1,0:T(8,128)(2,1)S(1)}) custom-call(s32[48]{0:T(128)S(1)} %copy-done.3, s32[48]{0:T(128)S(1)} %collective-permute-done.len1_ref, bf16[48,128,128]{2,1,0:T(8,128)(2,1)S(1)} %copy-done, bf16[48,128,128]{2,1,0:T(8,128)(2,1)S(1)} %collective-permute-done.1.pass1_ref, ...), custom_call_target="tpu_custom_call" | custom-call | flops 12582912 | bytes 6291456 | tf_op jit(solution)/shard_map/mask/pallas_call | solution.py:249
  20.4 0.0 collective-permute-done.4.refs_4_
  20.4 0.0 collective-permute-done.6.refs_8_
  20.5 0.9 %collective-permute-done.8.refs_10_ = bf16[144,128]{1,0:T(8,128)(2,1)S(1)} collective-permute-done((bf16[144,128]{1,0:T(8,128)(2,1)S(1)}, bf16[144,128]{1,0:T(8,128)(2,1)S(1)}, u32[]{:S(2)}, u32[]{:S(2)}) %collective-permute-start.8) | collective-permute-done | bytes 36896 | tf_op jit(solution)/shard_map/ppermute | solution.py:384
  21.3 0.0 copy-done.1
  21.3 0.0 copy-start.2
  21.3 2.6 %score.1 = f32[8,128]{1,0:T(8,128)S(1)} custom-call(s32[1]{0:T(128)} %bitcast.refs_0_, bf16[48,128,128]{2,1,0:T(8,128)(2,1)S(1)} %get-tuple-element.13.refs_1_, bf16[48,128,128]{2,1,0:T(8,128)(2,1)S(1)} %get-tuple-element.14.refs_2_, bf16[144,128]{1,0:T(8,128)(2,1)S(1)} %copy-done.1, bf16[144,128]{1,0:T(8,128)(2,1)S(1)} %collective-permute-done.4.refs_4_, ...), custom_call_target="tpu_custom_call" | custom-call | flops 805306368 | bytes 3145728 | tf_op jit(solution)/shard_map/score/pallas_call | solution.py:323
  24.0 10.1 %all_to_all.11 = f32[8,1,128]{2,1,0:T(1,128)S(1)} all-to-all(f32[8,1,128]{2,1,0:T(1,128)S(1)} %bitcast.5), channel_id=1, replica_groups={{0,3,5,6,8,11,13,14},{1,2,4,7,9,10,12,15},{16,19,21,22,24,27,29,30},{17..., dimensions={0} | all-to-all | bytes 8192 | tf_op jit(solution)/shard_map/all_to_all | solution.py:437
  34.0 0.0 copy-done.2
  34.0 1.0 %finish.1 = (f32[4,64]{1,0:T(4,128)}, f32[4,10]{1,0:T(4,128)}) custom-call(f32[8,128]{1,0:T(8,128)S(1)} %bitcast.6, s32[4,64]{1,0:T(4,128)S(1)} %copy-done.2), custom_call_target="tpu_custom_call" | custom-call | tf_op jit(solution)/shard_map/finish/pallas_call | solution.py:369
Async XLA Ops:
  0.6 6.2 %collective-permute-start = (s32[48]{0:T(128)}, s32[48]{0:T(128)S(1)}, u32[]{:S(2)}, u32[]{:S(2)}) collective-permute-start(s32[48]{0:T(128)} %len0_ref.1), channel_id=1, source_target_pairs={{0,1},{1,0},{2,3},{3,2},{4,5},{5,4},{6,7},{7,6},{8,9},{9,8},{10,11... | collective-permute-start | bytes 584 | tf_op jit(solution)/shard_map/ppermute | solution.py:384
  1.2 5.7 %copy-start = (bf16[48,128,128]{2,1,0:T(8,128)(2,1)S(1)}, bf16[48,128,128]{2,1,0:T(8,128)(2,1)}, u32[]{:S(2)}) copy-start(bf16[48,128,128]{2,1,0:T(8,128)(2,1)} %pass0_ref.1) | copy-start | bytes 4718596
  1.2 17.9 %copy-start.3 = (s32[48]{0:T(128)S(1)}, s32[48]{0:T(128)}, u32[]{:S(2)}) copy-start(s32[48]{0:T(128)} %len0_ref.1) | copy-start | bytes 580
  6.9 14.4 %copy-start.1 = (bf16[144,128]{1,0:T(8,128)(2,1)S(1)}, bf16[144,128]{1,0:T(8,128)(2,1)}, u32[]{:S(2)}) copy-start(bf16[144,128]{1,0:T(8,128)(2,1)} %get-tuple-element.12.refs_3_) | copy-start | bytes 110596
  6.9 12.2 %collective-permute-start.1 = (bf16[48,128,128]{2,1,0:T(8,128)(2,1)S(1)}, bf16[48,128,128]{2,1,0:T(8,128)(2,1)S(1)}, u32[]{:S(2)}, u32[]{:S(2)}) collective-permute-start(bf16[48,128,128]{2,1,0:T(8,128)(2,1)S(1)} %copy-done), channel_id=1, source_target_pairs={{0,1},{1,0},{2,3},{3,2},{4,5},{5,4},{6,7},{7,6},{8,9},{9,8},{10,11... | collective-permute-start | bytes 4718600 | tf_op jit(solution)/shard_map/ppermute | solution.py:384
  7.0 5.3 %collective-permute-start.2 = (bf16[144,128]{1,0:T(8,128)(2,1)}, bf16[144,128]{1,0:T(8,128)(2,1)S(1)}, u32[]{:S(2)}, u32[]{:S(2)}) collective-permute-start(bf16[144,128]{1,0:T(8,128)(2,1)} %get-tuple-element.12.refs_3_), channel_id=1, source_target_pairs={{0,5},{1,4},{2,7},{3,6},{4,1},{5,0},{6,3},{7,2},{8,13},{9,12},{10,... | collective-permute-start | bytes 110600 | tf_op jit(solution)/shard_map/ppermute | solution.py:384
  9.7 5.9 %collective-permute-start.5 = (bf16[144,128]{1,0:T(8,128)(2,1)}, bf16[144,128]{1,0:T(8,128)(2,1)S(1)}, u32[]{:S(2)}, u32[]{:S(2)}) collective-permute-start(bf16[144,128]{1,0:T(8,128)(2,1)} %get-tuple-element.12.refs_3_), channel_id=1, source_target_pairs={{0,8},{1,9},{2,10},{3,11},{4,12},{5,13},{6,14},{7,15},{8,0},{9,1},... | collective-permute-start | bytes 110600 | tf_op jit(solution)/shard_map/ppermute | solution.py:384
  12.3 5.5 %collective-permute-start.7 = (bf16[144,128]{1,0:T(8,128)(2,1)}, bf16[144,128]{1,0:T(8,128)(2,1)S(1)}, u32[]{:S(2)}, u32[]{:S(2)}) collective-permute-start(bf16[144,128]{1,0:T(8,128)(2,1)} %get-tuple-element.12.refs_3_), channel_id=1, source_target_pairs={{0,13},{1,12},{2,15},{3,14},{4,9},{5,8},{6,11},{7,10},{8,5},{9,4},... | collective-permute-start | bytes 110600 | tf_op jit(solution)/shard_map/ppermute | solution.py:384
  12.3 6.8 %collective-permute-start.3 = (bf16[144,128]{1,0:T(8,128)(2,1)S(1)}, bf16[144,128]{1,0:T(8,128)(2,1)S(1)}, u32[]{:S(2)}, u32[]{:S(2)}) collective-permute-start(bf16[144,128]{1,0:T(8,128)(2,1)S(1)} %collective-permute-done.2.refs_5_), channel_id=1, source_target_pairs={{0,3},{1,2},{2,1},{3,0},{4,7},{5,6},{6,5},{7,4},{8,11},{9,10},{10,... | collective-permute-start | bytes 110600 | tf_op jit(solution)/shard_map/ppermute | solution.py:384
  13.8 6.7 %collective-permute-start.4 = (bf16[144,128]{1,0:T(8,128)(2,1)}, bf16[144,128]{1,0:T(8,128)(2,1)S(1)}, u32[]{:S(2)}, u32[]{:S(2)}) collective-permute-start(bf16[144,128]{1,0:T(8,128)(2,1)} %get-tuple-element.12.refs_3_), channel_id=1, source_target_pairs={{0,3},{1,2},{2,1},{3,0},{4,7},{5,6},{6,5},{7,4},{8,11},{9,10},{10,... | collective-permute-start | bytes 110600 | tf_op jit(solution)/shard_map/ppermute | solution.py:384
  15.6 4.9 %collective-permute-start.6 = (bf16[144,128]{1,0:T(8,128)(2,1)S(1)}, bf16[144,128]{1,0:T(8,128)(2,1)S(1)}, u32[]{:S(2)}, u32[]{:S(2)}) collective-permute-start(bf16[144,128]{1,0:T(8,128)(2,1)S(1)} %collective-permute-done.5.refs_7_), channel_id=1, source_target_pairs={{0,3},{1,2},{2,1},{3,0},{4,7},{5,6},{6,5},{7,4},{8,11},{9,10},{10,... | collective-permute-start | bytes 110600 | tf_op jit(solution)/shard_map/ppermute | solution.py:384
  17.8 3.5 %collective-permute-start.8 = (bf16[144,128]{1,0:T(8,128)(2,1)S(1)}, bf16[144,128]{1,0:T(8,128)(2,1)S(1)}, u32[]{:S(2)}, u32[]{:S(2)}) collective-permute-start(bf16[144,128]{1,0:T(8,128)(2,1)S(1)} %collective-permute-done.7.refs_9_), channel_id=1, source_target_pairs={{0,3},{1,2},{2,1},{3,0},{4,7},{5,6},{6,5},{7,4},{8,11},{9,10},{10,... | collective-permute-start | bytes 110600 | tf_op jit(solution)/shard_map/ppermute | solution.py:384
  21.3 12.7 %copy-start.2 = (s32[4,64]{1,0:T(4,128)S(1)}, s32[4,64]{1,0:T(4,128)}, u32[]{:S(2)}) copy-start(s32[4,64]{1,0:T(4,128)} %get-tuple-element.15.spot_ref) | copy-start | bytes 3076

commit v18 on v17

--- a/solution.py
+++ b/solution.py
@@ -34,7 +34,7 @@
         for p in range(first, first + count):
             mask(p, 0)
     else:
-        lax.fori_loop(first, first + count, mask, 0, unroll=8)
+        lax.fori_loop(first, first + count, mask, 0, unroll=16)
 
 
 def encode_kernel(
@@ -188,7 +188,7 @@
     e = embed_weight.shape[1]
     slots = -(-slots // 16) * 16
     assert 2 * half <= e == 128
-    chunks = 4
+    chunks = 3
     width = ff // chunks
     tokens = query_count * token_count
 
@@ -300,7 +300,10 @@
                         rows = []
             return carry
 
-        lax.fori_loop(0, half // unroll, several, 0)
+        if unroll == half:
+            several(0, 0)
+        else:
+            lax.fori_loop(0, half // unroll, several, 0)
     wide = best_ref.shape[1]
     source = lax.broadcasted_iota(jnp.int32, (slots, wide), 0)
     column = lax.broadcasted_iota(jnp.int32, (slots, wide), 1)

time: 35.2 us -> 35.3 us (level)
  no operation moved by 1% of the time
where the time goes in v18:
time: 35.3 us; the launch traced here: 35.1 us
  Pallas kernels  10.7 us (30%)
  blocking collectives  10.1 us (29%)
  starting transfers between devices  8.93 us (25%)
  waiting for transfers between devices  4.68 us (13%)
  between operations  0.71 us (2%)
    all_to_all x1, blocking collectives, per_device(): lax.all_to_all(sums, 'shard', split_axis=0, concat_axis=0, axis_index_gro...  10.1 us
    ppermute x9, starting transfers between devices, swap(): lax.ppermute(value, 'shard', [(i, i ^ distance) for i in range(size)])  8.93 us
    pallas_call x1, Pallas kernels, encode(): pl.pallas_call(kernel, out_shape=(jax.ShapeDtypeStruct((tokens + slots, e...  5.78 us
    ppermute x9, waiting for transfers between devices, swap(): lax.ppermute(value, 'shard', [(i, i ^ distance) for i in range(size)])  4.68 us
    pallas_call x1, Pallas kernels, score(): pl.pallas_call(kernel, out_shape=jax.ShapeDtypeStruct((slots, e), F32), i...  2.64 us
    pallas_call x1, Pallas kernels, mask(): pl.pallas_call(mask_kernel, out_shape=[jax.ShapeDtypeStruct(shape, BF16)]...  1.31 us
    pallas_call x1, Pallas kernels, finish(): pl.pallas_call(finish_kernel, out_shape=(jax.ShapeDtypeStruct(spots.shape...  0.99 us
  transfers between devices with their start and end apart: 9, of which 3 were waited for; matrix products, arithmetic and copies ran while one was open for 0% of the time, Pallas kernels for 20%

profile of v18, /device:TPU:0, one launch (start us, length us, event | category | flops | bytes accessed | tf_op | source)
XLA Modules:
  0.0 35.1 jit_solution(3749304471091878652)
XLA Ops:
  0.6 0.5 %collective-permute-start = (s32[48]{0:T(128)}, s32[48]{0:T(128)S(1)}, u32[]{:S(2)}, u32[]{:S(2)}) collective-permute-start(s32[48]{0:T(128)} %len0_ref.1), channel_id=1, source_target_pairs={{0,1},{1,0},{2,3},{3,2},{4,5},{5,4},{6,7},{7,6},{8,9},{9,8},{10,11... | collective-permute-start | bytes 584 | tf_op jit(solution)/shard_map/ppermute | solution.py:387
  1.2 0.0 copy-start
  1.2 0.0 copy-start.3
  1.2 5.8 %encode.1 = (bf16[144,128]{1,0:T(8,128)(2,1)}, s32[4,64]{1,0:T(4,128)}) custom-call(s32[1]{0:T(128)} %bitcast.refs_0_, s32[4]{0:T(128)} %refs_1_.1, s32[768]{0:T(1024)} %refs_2_.1, s32[4,64]{1,0:T(4,128)} %refs_3_.1, bf16[4,32,768]{2,1,0:T(8,128)(2,1)} %refs_4_.1, bf16[768,3072]{1,0:T(8,128)(2,1)} %refs_5_.1, bf16[3072,768]{1,0:T(8,128)(2,1)} %refs_6_.1, ...), custom_call_target="tpu_custom_call" | custom-call | flops 1207959552 | bytes 9437184 | tf_op jit(solution)/shard_map/encode/pallas_call | solution.py:198
  6.9 0.0 collective-permute-done.len1_ref
  7.0 0.0 copy-done
  7.0 0.0 copy-start.1
  7.0 0.1 collective-permute-start.1
  7.1 2.7 %collective-permute-start.2 = (bf16[144,128]{1,0:T(8,128)(2,1)}, bf16[144,128]{1,0:T(8,128)(2,1)S(1)}, u32[]{:S(2)}, u32[]{:S(2)}) collective-permute-start(bf16[144,128]{1,0:T(8,128)(2,1)} %get-tuple-element.12.refs_3_), channel_id=1, source_target_pairs={{0,5},{1,4},{2,7},{3,6},{4,1},{5,0},{6,3},{7,2},{8,13},{9,12},{10,... | collective-permute-start | bytes 110600 | tf_op jit(solution)/shard_map/ppermute | solution.py:387
  9.8 2.6 %collective-permute-start.5 = (bf16[144,128]{1,0:T(8,128)(2,1)}, bf16[144,128]{1,0:T(8,128)(2,1)S(1)}, u32[]{:S(2)}, u32[]{:S(2)}) collective-permute-start(bf16[144,128]{1,0:T(8,128)(2,1)} %get-tuple-element.12.refs_3_), channel_id=1, source_target_pairs={{0,8},{1,9},{2,10},{3,11},{4,12},{5,13},{6,14},{7,15},{8,0},{9,1},... | collective-permute-start | bytes 110600 | tf_op jit(solution)/shard_map/ppermute | solution.py:387
  12.4 0.0 collective-permute-start.7
  12.4 0.0 collective-permute-done.2.refs_5_
  12.4 1.5 %collective-permute-start.3 = (bf16[144,128]{1,0:T(8,128)(2,1)S(1)}, bf16[144,128]{1,0:T(8,128)(2,1)S(1)}, u32[]{:S(2)}, u32[]{:S(2)}) collective-permute-start(bf16[144,128]{1,0:T(8,128)(2,1)S(1)} %collective-permute-done.2.refs_5_), channel_id=1, source_target_pairs={{0,3},{1,2},{2,1},{3,0},{4,7},{5,6},{6,5},{7,4},{8,11},{9,10},{10,... | collective-permute-start | bytes 110600 | tf_op jit(solution)/shard_map/ppermute | solution.py:387
  13.9 0.3 collective-permute-start.4
  14.1 1.5 %collective-permute-done.5.refs_7_ = bf16[144,128]{1,0:T(8,128)(2,1)S(1)} collective-permute-done((bf16[144,128]{1,0:T(8,128)(2,1)}, bf16[144,128]{1,0:T(8,128)(2,1)S(1)}, u32[]{:S(2)}, u32[]{:S(2)}) %collective-permute-start.5) | collective-permute-done | bytes 36896 | tf_op jit(solution)/shard_map/ppermute | solution.py:387
  15.7 0.0 collective-permute-start.6
  15.7 2.2 %collective-permute-done.7.refs_9_ = bf16[144,128]{1,0:T(8,128)(2,1)S(1)} collective-permute-done((bf16[144,128]{1,0:T(8,128)(2,1)}, bf16[144,128]{1,0:T(8,128)(2,1)S(1)}, u32[]{:S(2)}, u32[]{:S(2)}) %collective-permute-start.7) | collective-permute-done | bytes 36896 | tf_op jit(solution)/shard_map/ppermute | solution.py:387
  17.9 1.2 %collective-permute-start.8 = (bf16[144,128]{1,0:T(8,128)(2,1)S(1)}, bf16[144,128]{1,0:T(8,128)(2,1)S(1)}, u32[]{:S(2)}, u32[]{:S(2)}) collective-permute-start(bf16[144,128]{1,0:T(8,128)(2,1)S(1)} %collective-permute-done.7.refs_9_), channel_id=1, source_target_pairs={{0,3},{1,2},{2,1},{3,0},{4,7},{5,6},{6,5},{7,4},{8,11},{9,10},{10,... | collective-permute-start | bytes 110600 | tf_op jit(solution)/shard_map/ppermute | solution.py:387
  19.2 0.0 collective-permute-done.3._.refs_6_
  19.2 0.0 collective-permute-done.1.pass1_ref
  19.2 0.0 copy-done.3
  19.2 1.3 %mask.1 = (bf16[48,128,128]{2,1,0:T(8,128)(2,1)S(1)}, bf16[48,128,128]{2,1,0:T(8,128)(2,1)S(1)}) custom-call(s32[48]{0:T(128)S(1)} %copy-done.3, s32[48]{0:T(128)S(1)} %collective-permute-done.len1_ref, bf16[48,128,128]{2,1,0:T(8,128)(2,1)S(1)} %copy-done, bf16[48,128,128]{2,1,0:T(8,128)(2,1)S(1)} %collective-permute-done.1.pass1_ref, ...), custom_call_target="tpu_custom_call" | custom-call | flops 12582912 | bytes 6291456 | tf_op jit(solution)/shard_map/mask/pallas_call | solution.py:249
  20.5 0.0 collective-permute-done.4.refs_4_
  20.5 0.0 collective-permute-done.6.refs_8_
  20.5 0.9 %collective-permute-done.8.refs_10_ = bf16[144,128]{1,0:T(8,128)(2,1)S(1)} collective-permute-done((bf16[144,128]{1,0:T(8,128)(2,1)S(1)}, bf16[144,128]{1,0:T(8,128)(2,1)S(1)}, u32[]{:S(2)}, u32[]{:S(2)}) %collective-permute-start.8) | collective-permute-done | bytes 36896 | tf_op jit(solution)/shard_map/ppermute | solution.py:387
  21.4 0.0 copy-done.1
  21.4 0.0 copy-start.2
  21.4 2.6 %score.1 = f32[8,128]{1,0:T(8,128)S(1)} custom-call(s32[1]{0:T(128)} %bitcast.refs_0_, bf16[48,128,128]{2,1,0:T(8,128)(2,1)S(1)} %get-tuple-element.13.refs_1_, bf16[48,128,128]{2,1,0:T(8,128)(2,1)S(1)} %get-tuple-element.14.refs_2_, bf16[144,128]{1,0:T(8,128)(2,1)S(1)} %copy-done.1, bf16[144,128]{1,0:T(8,128)(2,1)S(1)} %collective-permute-done.4.refs_4_, ...), custom_call_target="tpu_custom_call" | custom-call | flops 805306368 | bytes 3145728 | tf_op jit(solution)/shard_map/score/pallas_call | solution.py:326
  24.1 10.1 %all_to_all.11 = f32[8,1,128]{2,1,0:T(1,128)S(1)} all-to-all(f32[8,1,128]{2,1,0:T(1,128)S(1)} %bitcast.5), channel_id=1, replica_groups={{0,3,5,6,8,11,13,14},{1,2,4,7,9,10,12,15},{16,19,21,22,24,27,29,30},{17..., dimensions={0} | all-to-all | bytes 8192 | tf_op jit(solution)/shard_map/all_to_all | solution.py:440
  34.1 0.0 copy-done.2
  34.1 1.0 %finish.1 = (f32[4,64]{1,0:T(4,128)}, f32[4,10]{1,0:T(4,128)}) custom-call(f32[8,128]{1,0:T(8,128)S(1)} %bitcast.6, s32[4,64]{1,0:T(4,128)S(1)} %copy-done.2), custom_call_target="tpu_custom_call" | custom-call | tf_op jit(solution)/shard_map/finish/pallas_call | solution.py:372
Async XLA Ops:
  0.6 6.3 %collective-permute-start = (s32[48]{0:T(128)}, s32[48]{0:T(128)S(1)}, u32[]{:S(2)}, u32[]{:S(2)}) collective-permute-start(s32[48]{0:T(128)} %len0_ref.1), channel_id=1, source_target_pairs={{0,1},{1,0},{2,3},{3,2},{4,5},{5,4},{6,7},{7,6},{8,9},{9,8},{10,11... | collective-permute-start | bytes 584 | tf_op jit(solution)/shard_map/ppermute | solution.py:387
  1.2 5.8 %copy-start = (bf16[48,128,128]{2,1,0:T(8,128)(2,1)S(1)}, bf16[48,128,128]{2,1,0:T(8,128)(2,1)}, u32[]{:S(2)}) copy-start(bf16[48,128,128]{2,1,0:T(8,128)(2,1)} %pass0_ref.1) | copy-start | bytes 4718596
  1.2 18.0 %copy-start.3 = (s32[48]{0:T(128)S(1)}, s32[48]{0:T(128)}, u32[]{:S(2)}) copy-start(s32[48]{0:T(128)} %len0_ref.1) | copy-start | bytes 580
  7.0 14.4 %copy-start.1 = (bf16[144,128]{1,0:T(8,128)(2,1)S(1)}, bf16[144,128]{1,0:T(8,128)(2,1)}, u32[]{:S(2)}) copy-start(bf16[144,128]{1,0:T(8,128)(2,1)} %get-tuple-element.12.refs_3_) | copy-start | bytes 110596
  7.0 12.2 %collective-permute-start.1 = (bf16[48,128,128]{2,1,0:T(8,128)(2,1)S(1)}, bf16[48,128,128]{2,1,0:T(8,128)(2,1)S(1)}, u32[]{:S(2)}, u32[]{:S(2)}) collective-permute-start(bf16[48,128,128]{2,1,0:T(8,128)(2,1)S(1)} %copy-done), channel_id=1, source_target_pairs={{0,1},{1,0},{2,3},{3,2},{4,5},{5,4},{6,7},{7,6},{8,9},{9,8},{10,11... | collective-permute-start | bytes 4718600 | tf_op jit(solution)/shard_map/ppermute | solution.py:387
  7.1 5.3 %collective-permute-start.2 = (bf16[144,128]{1,0:T(8,128)(2,1)}, bf16[144,128]{1,0:T(8,128)(2,1)S(1)}, u32[]{:S(2)}, u32[]{:S(2)}) collective-permute-start(bf16[144,128]{1,0:T(8,128)(2,1)} %get-tuple-element.12.refs_3_), channel_id=1, source_target_pairs={{0,5},{1,4},{2,7},{3,6},{4,1},{5,0},{6,3},{7,2},{8,13},{9,12},{10,... | collective-permute-start | bytes 110600 | tf_op jit(solution)/shard_map/ppermute | solution.py:387
  9.8 5.9 %collective-permute-start.5 = (bf16[144,128]{1,0:T(8,128)(2,1)}, bf16[144,128]{1,0:T(8,128)(2,1)S(1)}, u32[]{:S(2)}, u32[]{:S(2)}) collective-permute-start(bf16[144,128]{1,0:T(8,128)(2,1)} %get-tuple-element.12.refs_3_), channel_id=1, source_target_pairs={{0,8},{1,9},{2,10},{3,11},{4,12},{5,13},{6,14},{7,15},{8,0},{9,1},... | collective-permute-start | bytes 110600 | tf_op jit(solution)/shard_map/ppermute | solution.py:387
  12.4 5.5 %collective-permute-start.7 = (bf16[144,128]{1,0:T(8,128)(2,1)}, bf16[144,128]{1,0:T(8,128)(2,1)S(1)}, u32[]{:S(2)}, u32[]{:S(2)}) collective-permute-start(bf16[144,128]{1,0:T(8,128)(2,1)} %get-tuple-element.12.refs_3_), channel_id=1, source_target_pairs={{0,13},{1,12},{2,15},{3,14},{4,9},{5,8},{6,11},{7,10},{8,5},{9,4},... | collective-permute-start | bytes 110600 | tf_op jit(solution)/shard_map/ppermute | solution.py:387
  12.4 6.8 %collective-permute-start.3 = (bf16[144,128]{1,0:T(8,128)(2,1)S(1)}, bf16[144,128]{1,0:T(8,128)(2,1)S(1)}, u32[]{:S(2)}, u32[]{:S(2)}) collective-permute-start(bf16[144,128]{1,0:T(8,128)(2,1)S(1)} %collective-permute-done.2.refs_5_), channel_id=1, source_target_pairs={{0,3},{1,2},{2,1},{3,0},{4,7},{5,6},{6,5},{7,4},{8,11},{9,10},{10,... | collective-permute-start | bytes 110600 | tf_op jit(solution)/shard_map/ppermute | solution.py:387
  13.9 6.6 %collective-permute-start.4 = (bf16[144,128]{1,0:T(8,128)(2,1)}, bf16[144,128]{1,0:T(8,128)(2,1)S(1)}, u32[]{:S(2)}, u32[]{:S(2)}) collective-permute-start(bf16[144,128]{1,0:T(8,128)(2,1)} %get-tuple-element.12.refs_3_), channel_id=1, source_target_pairs={{0,3},{1,2},{2,1},{3,0},{4,7},{5,6},{6,5},{7,4},{8,11},{9,10},{10,... | collective-permute-start | bytes 110600 | tf_op jit(solution)/shard_map/ppermute | solution.py:387
  15.7 4.8 %collective-permute-start.6 = (bf16[144,128]{1,0:T(8,128)(2,1)S(1)}, bf16[144,128]{1,0:T(8,128)(2,1)S(1)}, u32[]{:S(2)}, u32[]{:S(2)}) collective-permute-start(bf16[144,128]{1,0:T(8,128)(2,1)S(1)} %collective-permute-done.5.refs_7_), channel_id=1, source_target_pairs={{0,3},{1,2},{2,1},{3,0},{4,7},{5,6},{6,5},{7,4},{8,11},{9,10},{10,... | collective-permute-start | bytes 110600 | tf_op jit(solution)/shard_map/ppermute | solution.py:387
  17.9 3.5 %collective-permute-start.8 = (bf16[144,128]{1,0:T(8,128)(2,1)S(1)}, bf16[144,128]{1,0:T(8,128)(2,1)S(1)}, u32[]{:S(2)}, u32[]{:S(2)}) collective-permute-start(bf16[144,128]{1,0:T(8,128)(2,1)S(1)} %collective-permute-done.7.refs_9_), channel_id=1, source_target_pairs={{0,3},{1,2},{2,1},{3,0},{4,7},{5,6},{6,5},{7,4},{8,11},{9,10},{10,... | collective-permute-start | bytes 110600 | tf_op jit(solution)/shard_map/ppermute | solution.py:387
  21.4 12.7 %copy-start.2 = (s32[4,64]{1,0:T(4,128)S(1)}, s32[4,64]{1,0:T(4,128)}, u32[]{:S(2)}) copy-start(s32[4,64]{1,0:T(4,128)} %get-tuple-element.15.spot_ref) | copy-start | bytes 3076

commit v19 on v18

--- a/solution.py
+++ b/solution.py
@@ -188,7 +188,7 @@
     e = embed_weight.shape[1]
     slots = -(-slots // 16) * 16
     assert 2 * half <= e == 128
-    chunks = 3
+    chunks = 4
     width = ff // chunks
     tokens = query_count * token_count
 
@@ -257,7 +257,8 @@
     )(*lengths, *passages, late)
 
 
-def score_kernel(slots, token_count, me_ref, own_ref, other_ref, *refs):
+def score_kernel(order, token_count, me_ref, own_ref, other_ref, *refs):
+    slots = len(order)
     got_refs = refs[:slots]
     out_ref, best_ref, index_v, index, sem = refs[slots:]
     message, lanes = got_refs[0].shape
@@ -312,16 +313,16 @@
     total = sum(lax.dot_general(ones, part, NT, preferred_element_type=F32) for part in split3(best_ref[...]))
     out_ref[...] = jnp.zeros(out_ref.shape, F32)
     for s in range(slots):
-        out_ref[pl.ds(jnp.bitwise_xor(chip, s), 1), pl.ds(0, 2 * half)] = total[s:s + 1]
-
-
-def score(me, got, own, other, token_count):
+        out_ref[pl.ds(jnp.bitwise_xor(chip, order[s]), 1), pl.ds(0, 2 * half)] = total[s:s + 1]
+
+
+def score(me, got, order, own, other, token_count):
     half, plen, e = own.shape
     passage_count = 2 * half
     slots = len(got)
 
     def kernel(*refs):
-        score_kernel(slots, token_count, *refs)
+        score_kernel(order, token_count, *refs)
 
     return pl.pallas_call(
         kernel,
@@ -341,7 +342,7 @@
             transcendentals=0,
         ),
         name="score",
-    )(me, own, other, *got)
+    )(me, own, other, *[got[s] for s in order])
 
 
 def finish_kernel(got_ref, spot_ref, scores_ref, best_ref):
@@ -435,8 +436,9 @@
 
     line = [message] + [send(message, d) for d in range(slots - inner, 0, -inner)][::-1]
     got = [line[s // inner] if s % inner == 0 else send(line[s // inner], s % inner) for s in range(slots)]
-    own, other = mask((passage_lengths, across), (passage_vectors, raw), got[inner + 1])
-    sums = score(me, got, own, other, query_hidden.shape[1])
+    own, other = mask((passage_lengths, across), (passage_vectors, raw), got[-1])
+    order = [z + y for z in [0, *range(slots - inner, 0, -inner)] for y in range(inner)]
+    sums = score(me, got, order, own, other, query_hidden.shape[1])
     back = lax.all_to_all(sums, "shard", split_axis=0, concat_axis=0, axis_index_groups=groups, tiled=True)
     return finish(back, spots)
 

time: 35.3 us -> 35.9 us (1.017)
  blocking collectives: 10.1 us -> 11.1 us
  waiting for transfers between devices: 4.68 us -> 4.06 us
    all_to_all x1, blocking collectives: 10.1 us -> 11.1 us  [per_device(): lax.all_to_all(sums, 'shard', split_axis=0, concat_axis=0, axis_index_gro...]
    ppermute x9, waiting for transfers between devices: 4.68 us -> 4.06 us  [swap(): lax.ppermute(value, 'shard', [(i, i ^ distance) for i in range(size)])]
  transfers between devices with their start and end apart: 9 -> 9, of which waited for: 3 -> 4; matrix products, arithmetic and copies ran while one was open for 0% -> 0% of each run, Pallas kernels for 20% -> 20%
where the time goes in v19:
time: 35.9 us; the launch traced here: 35.7 us
  blocking collectives  11.1 us (31%)
  Pallas kernels  10.6 us (30%)
  starting transfers between devices  9.23 us (26%)
  waiting for transfers between devices  4.06 us (11%)
  between operations  0.7 us (2%)
    all_to_all x1, blocking collectives, per_device(): lax.all_to_all(sums, 'shard', split_axis=0, concat_axis=0, axis_index_gro...  11.1 us
    ppermute x9, starting transfers between devices, swap(): lax.ppermute(value, 'shard', [(i, i ^ distance) for i in range(size)])  9.23 us
    pallas_call x1, Pallas kernels, encode(): pl.pallas_call(kernel, out_shape=(jax.ShapeDtypeStruct((tokens + slots, e...  5.69 us
    ppermute x9, waiting for transfers between devices, swap(): lax.ppermute(value, 'shard', [(i, i ^ distance) for i in range(size)])  4.06 us
    pallas_call x1, Pallas kernels, score(): pl.pallas_call(kernel, out_shape=jax.ShapeDtypeStruct((slots, e), F32), i...  2.63 us
    pallas_call x1, Pallas kernels, mask(): pl.pallas_call(mask_kernel, out_shape=[jax.ShapeDtypeStruct(shape, BF16)]...  1.31 us
    pallas_call x1, Pallas kernels, finish(): pl.pallas_call(finish_kernel, out_shape=(jax.ShapeDtypeStruct(spots.shape...  0.99 us
  transfers between devices with their start and end apart: 9, of which 4 were waited for; matrix products, arithmetic and copies ran while one was open for 0% of the time, Pallas kernels for 20%

profile of v19, /device:TPU:0, one launch (start us, length us, event | category | flops | bytes accessed | tf_op | source)
XLA Modules:
  0.0 35.7 jit_solution(11566006354144051933)
XLA Ops:
  0.6 0.5 %collective-permute-start = (s32[48]{0:T(128)}, s32[48]{0:T(128)S(1)}, u32[]{:S(2)}, u32[]{:S(2)}) collective-permute-start(s32[48]{0:T(128)} %len0_ref.1), channel_id=1, source_target_pairs={{0,1},{1,0},{2,3},{3,2},{4,5},{5,4},{6,7},{7,6},{8,9},{9,8},{10,11... | collective-permute-start | bytes 584 | tf_op jit(solution)/shard_map/ppermute | solution.py:388
  1.2 0.0 copy-start
  1.2 0.0 copy-start.3
  1.2 5.7 %encode.1 = (bf16[144,128]{1,0:T(8,128)(2,1)}, s32[4,64]{1,0:T(4,128)}) custom-call(s32[1]{0:T(128)} %bitcast.refs_0_, s32[4]{0:T(128)} %refs_1_.1, s32[768]{0:T(1024)} %refs_2_.1, s32[4,64]{1,0:T(4,128)} %refs_3_.1, bf16[4,32,768]{2,1,0:T(8,128)(2,1)} %refs_4_.1, bf16[768,3072]{1,0:T(8,128)(2,1)} %refs_5_.1, bf16[3072,768]{1,0:T(8,128)(2,1)} %refs_6_.1, ...), custom_call_target="tpu_custom_call" | custom-call | flops 1207959552 | bytes 9437184 | tf_op jit(solution)/shard_map/encode/pallas_call | solution.py:198
  6.9 0.0 collective-permute-done.len1_ref
  6.9 0.0 copy-done
  6.9 0.0 copy-start.1
  6.9 0.1 collective-permute-start.1
  7.0 4.7 %collective-permute-start.2 = (bf16[144,128]{1,0:T(8,128)(2,1)}, bf16[144,128]{1,0:T(8,128)(2,1)S(1)}, u32[]{:S(2)}, u32[]{:S(2)}) collective-permute-start(bf16[144,128]{1,0:T(8,128)(2,1)} %get-tuple-element.12.refs_3_), channel_id=1, source_target_pairs={{0,13},{1,12},{2,15},{3,14},{4,9},{5,8},{6,11},{7,10},{8,5},{9,4},... | collective-permute-start | bytes 110600 | tf_op jit(solution)/shard_map/ppermute | solution.py:388
  11.7 0.0 collective-permute-start.5
  11.7 0.4 %collective-permute-start.7 = (bf16[144,128]{1,0:T(8,128)(2,1)}, bf16[144,128]{1,0:T(8,128)(2,1)S(1)}, u32[]{:S(2)}, u32[]{:S(2)}) collective-permute-start(bf16[144,128]{1,0:T(8,128)(2,1)} %get-tuple-element.12.refs_3_), channel_id=1, source_target_pairs={{0,5},{1,4},{2,7},{3,6},{4,1},{5,0},{6,3},{7,2},{8,13},{9,12},{10,... | collective-permute-start | bytes 110600 | tf_op jit(solution)/shard_map/ppermute | solution.py:388
  12.1 1.8 %collective-permute-done.2.refs_5_ = bf16[144,128]{1,0:T(8,128)(2,1)S(1)} collective-permute-done((bf16[144,128]{1,0:T(8,128)(2,1)}, bf16[144,128]{1,0:T(8,128)(2,1)S(1)}, u32[]{:S(2)}, u32[]{:S(2)}) %collective-permute-start.2) | collective-permute-done | bytes 36896 | tf_op jit(solution)/shard_map/ppermute | solution.py:388
  14.0 1.3 %collective-permute-start.3 = (bf16[144,128]{1,0:T(8,128)(2,1)S(1)}, bf16[144,128]{1,0:T(8,128)(2,1)S(1)}, u32[]{:S(2)}, u32[]{:S(2)}) collective-permute-start(bf16[144,128]{1,0:T(8,128)(2,1)S(1)} %collective-permute-done.2.refs_5_), channel_id=1, source_target_pairs={{0,3},{1,2},{2,1},{3,0},{4,7},{5,6},{6,5},{7,4},{8,11},{9,10},{10,... | collective-permute-start | bytes 110600 | tf_op jit(solution)/shard_map/ppermute | solution.py:388
  15.2 0.5 %collective-permute-start.4 = (bf16[144,128]{1,0:T(8,128)(2,1)}, bf16[144,128]{1,0:T(8,128)(2,1)S(1)}, u32[]{:S(2)}, u32[]{:S(2)}) collective-permute-start(bf16[144,128]{1,0:T(8,128)(2,1)} %get-tuple-element.12.refs_3_), channel_id=1, source_target_pairs={{0,3},{1,2},{2,1},{3,0},{4,7},{5,6},{6,5},{7,4},{8,11},{9,10},{10,... | collective-permute-start | bytes 110600 | tf_op jit(solution)/shard_map/ppermute | solution.py:388
  15.7 1.1 %collective-permute-done.5.refs_7_ = bf16[144,128]{1,0:T(8,128)(2,1)S(1)} collective-permute-done((bf16[144,128]{1,0:T(8,128)(2,1)}, bf16[144,128]{1,0:T(8,128)(2,1)S(1)}, u32[]{:S(2)}, u32[]{:S(2)}) %collective-permute-start.5) | collective-permute-done | bytes 36896 | tf_op jit(solution)/shard_map/ppermute | solution.py:388
  16.8 0.5 %collective-permute-start.6 = (bf16[144,128]{1,0:T(8,128)(2,1)S(1)}, bf16[144,128]{1,0:T(8,128)(2,1)S(1)}, u32[]{:S(2)}, u32[]{:S(2)}) collective-permute-start(bf16[144,128]{1,0:T(8,128)(2,1)S(1)} %collective-permute-done.5.refs_7_), channel_id=1, source_target_pairs={{0,3},{1,2},{2,1},{3,0},{4,7},{5,6},{6,5},{7,4},{8,11},{9,10},{10,... | collective-permute-start | bytes 110600 | tf_op jit(solution)/shard_map/ppermute | solution.py:388
  17.3 0.0 collective-permute-done.7.refs_9_
  17.3 1.3 %collective-permute-start.8 = (bf16[144,128]{1,0:T(8,128)(2,1)S(1)}, bf16[144,128]{1,0:T(8,128)(2,1)S(1)}, u32[]{:S(2)}, u32[]{:S(2)}) collective-permute-start(bf16[144,128]{1,0:T(8,128)(2,1)S(1)} %collective-permute-done.7.refs_9_), channel_id=1, source_target_pairs={{0,3},{1,2},{2,1},{3,0},{4,7},{5,6},{6,5},{7,4},{8,11},{9,10},{10,... | collective-permute-start | bytes 110600 | tf_op jit(solution)/shard_map/ppermute | solution.py:388
  18.6 0.0 collective-permute-done.3._.refs_6_
  18.6 0.0 collective-permute-done.1.pass1_ref
  18.6 0.0 copy-done.3
  18.6 1.3 %mask.1 = (bf16[48,128,128]{2,1,0:T(8,128)(2,1)S(1)}, bf16[48,128,128]{2,1,0:T(8,128)(2,1)S(1)}) custom-call(s32[48]{0:T(128)S(1)} %copy-done.3, s32[48]{0:T(128)S(1)} %collective-permute-done.len1_ref, bf16[48,128,128]{2,1,0:T(8,128)(2,1)S(1)} %copy-done, bf16[48,128,128]{2,1,0:T(8,128)(2,1)S(1)} %collective-permute-done.1.pass1_ref, ...), custom_call_target="tpu_custom_call" | custom-call | flops 12582912 | bytes 6291456 | tf_op jit(solution)/shard_map/mask/pallas_call | solution.py:249
  19.9 0.0 collective-permute-done.4.refs_4_
  19.9 0.6 %collective-permute-done.6.refs_8_ = bf16[144,128]{1,0:T(8,128)(2,1)S(1)} collective-permute-done((bf16[144,128]{1,0:T(8,128)(2,1)S(1)}, bf16[144,128]{1,0:T(8,128)(2,1)S(1)}, u32[]{:S(2)}, u32[]{:S(2)}) %collective-permute-start.6) | collective-permute-done | bytes 36896 | tf_op jit(solution)/shard_map/ppermute | solution.py:388
  20.5 0.5 %collective-permute-done.8.refs_10_ = bf16[144,128]{1,0:T(8,128)(2,1)S(1)} collective-permute-done((bf16[144,128]{1,0:T(8,128)(2,1)S(1)}, bf16[144,128]{1,0:T(8,128)(2,1)S(1)}, u32[]{:S(2)}, u32[]{:S(2)}) %collective-permute-start.8) | collective-permute-done | bytes 36896 | tf_op jit(solution)/shard_map/ppermute | solution.py:388
  21.0 0.0 copy-done.1
  21.0 0.0 copy-start.2
  21.0 2.6 %score.1 = f32[8,128]{1,0:T(8,128)S(1)} custom-call(s32[1]{0:T(128)} %bitcast.refs_0_, bf16[48,128,128]{2,1,0:T(8,128)(2,1)S(1)} %get-tuple-element.13.refs_1_, bf16[48,128,128]{2,1,0:T(8,128)(2,1)S(1)} %get-tuple-element.14.refs_2_, bf16[144,128]{1,0:T(8,128)(2,1)S(1)} %copy-done.1, bf16[144,128]{1,0:T(8,128)(2,1)S(1)} %collective-permute-done.4.refs_4_, ...), custom_call_target="tpu_custom_call" | custom-call | flops 805306368 | bytes 3145728 | tf_op jit(solution)/shard_map/score/pallas_call | solution.py:327
  23.6 11.1 %all_to_all.11 = f32[8,1,128]{2,1,0:T(1,128)S(1)} all-to-all(f32[8,1,128]{2,1,0:T(1,128)S(1)} %bitcast.5), channel_id=1, replica_groups={{0,3,5,6,8,11,13,14},{1,2,4,7,9,10,12,15},{16,19,21,22,24,27,29,30},{17..., dimensions={0} | all-to-all | bytes 8192 | tf_op jit(solution)/shard_map/all_to_all | solution.py:442
  34.7 0.0 copy-done.2
  34.7 1.0 %finish.1 = (f32[4,64]{1,0:T(4,128)}, f32[4,10]{1,0:T(4,128)}) custom-call(f32[8,128]{1,0:T(8,128)S(1)} %bitcast.6, s32[4,64]{1,0:T(4,128)S(1)} %copy-done.2), custom_call_target="tpu_custom_call" | custom-call | tf_op jit(solution)/shard_map/finish/pallas_call | solution.py:373
Async XLA Ops:
  0.6 6.2 %collective-permute-start = (s32[48]{0:T(128)}, s32[48]{0:T(128)S(1)}, u32[]{:S(2)}, u32[]{:S(2)}) collective-permute-start(s32[48]{0:T(128)} %len0_ref.1), channel_id=1, source_target_pairs={{0,1},{1,0},{2,3},{3,2},{4,5},{5,4},{6,7},{7,6},{8,9},{9,8},{10,11... | collective-permute-start | bytes 584 | tf_op jit(solution)/shard_map/ppermute | solution.py:388
  1.2 5.7 %copy-start = (bf16[48,128,128]{2,1,0:T(8,128)(2,1)S(1)}, bf16[48,128,128]{2,1,0:T(8,128)(2,1)}, u32[]{:S(2)}) copy-start(bf16[48,128,128]{2,1,0:T(8,128)(2,1)} %pass0_ref.1) | copy-start | bytes 4718596
  1.2 17.4 %copy-start.3 = (s32[48]{0:T(128)S(1)}, s32[48]{0:T(128)}, u32[]{:S(2)}) copy-start(s32[48]{0:T(128)} %len0_ref.1) | copy-start | bytes 580
  6.9 14.1 %copy-start.1 = (bf16[144,128]{1,0:T(8,128)(2,1)S(1)}, bf16[144,128]{1,0:T(8,128)(2,1)}, u32[]{:S(2)}) copy-start(bf16[144,128]{1,0:T(8,128)(2,1)} %get-tuple-element.12.refs_3_) | copy-start | bytes 110596
  6.9 11.7 %collective-permute-start.1 = (bf16[48,128,128]{2,1,0:T(8,128)(2,1)S(1)}, bf16[48,128,128]{2,1,0:T(8,128)(2,1)S(1)}, u32[]{:S(2)}, u32[]{:S(2)}) collective-permute-start(bf16[48,128,128]{2,1,0:T(8,128)(2,1)S(1)} %copy-done), channel_id=1, source_target_pairs={{0,1},{1,0},{2,3},{3,2},{4,5},{5,4},{6,7},{7,6},{8,9},{9,8},{10,11... | collective-permute-start | bytes 4718600 | tf_op jit(solution)/shard_map/ppermute | solution.py:388
  7.0 6.9 %collective-permute-start.2 = (bf16[144,128]{1,0:T(8,128)(2,1)}, bf16[144,128]{1,0:T(8,128)(2,1)S(1)}, u32[]{:S(2)}, u32[]{:S(2)}) collective-permute-start(bf16[144,128]{1,0:T(8,128)(2,1)} %get-tuple-element.12.refs_3_), channel_id=1, source_target_pairs={{0,13},{1,12},{2,15},{3,14},{4,9},{5,8},{6,11},{7,10},{8,5},{9,4},... | collective-permute-start | bytes 110600 | tf_op jit(solution)/shard_map/ppermute | solution.py:388
  11.7 5.1 %collective-permute-start.5 = (bf16[144,128]{1,0:T(8,128)(2,1)}, bf16[144,128]{1,0:T(8,128)(2,1)S(1)}, u32[]{:S(2)}, u32[]{:S(2)}) collective-permute-start(bf16[144,128]{1,0:T(8,128)(2,1)} %get-tuple-element.12.refs_3_), channel_id=1, source_target_pairs={{0,8},{1,9},{2,10},{3,11},{4,12},{5,13},{6,14},{7,15},{8,0},{9,1},... | collective-permute-start | bytes 110600 | tf_op jit(solution)/shard_map/ppermute | solution.py:388
  11.7 5.6 %collective-permute-start.7 = (bf16[144,128]{1,0:T(8,128)(2,1)}, bf16[144,128]{1,0:T(8,128)(2,1)S(1)}, u32[]{:S(2)}, u32[]{:S(2)}) collective-permute-start(bf16[144,128]{1,0:T(8,128)(2,1)} %get-tuple-element.12.refs_3_), channel_id=1, source_target_pairs={{0,5},{1,4},{2,7},{3,6},{4,1},{5,0},{6,3},{7,2},{8,13},{9,12},{10,... | collective-permute-start | bytes 110600 | tf_op jit(solution)/shard_map/ppermute | solution.py:388
  14.0 4.6 %collective-permute-start.3 = (bf16[144,128]{1,0:T(8,128)(2,1)S(1)}, bf16[144,128]{1,0:T(8,128)(2,1)S(1)}, u32[]{:S(2)}, u32[]{:S(2)}) collective-permute-start(bf16[144,128]{1,0:T(8,128)(2,1)S(1)} %collective-permute-done.2.refs_5_), channel_id=1, source_target_pairs={{0,3},{1,2},{2,1},{3,0},{4,7},{5,6},{6,5},{7,4},{8,11},{9,10},{10,... | collective-permute-start | bytes 110600 | tf_op jit(solution)/shard_map/ppermute | solution.py:388
  15.2 4.7 %collective-permute-start.4 = (bf16[144,128]{1,0:T(8,128)(2,1)}, bf16[144,128]{1,0:T(8,128)(2,1)S(1)}, u32[]{:S(2)}, u32[]{:S(2)}) collective-permute-start(bf16[144,128]{1,0:T(8,128)(2,1)} %get-tuple-element.12.refs_3_), channel_id=1, source_target_pairs={{0,3},{1,2},{2,1},{3,0},{4,7},{5,6},{6,5},{7,4},{8,11},{9,10},{10,... | collective-permute-start | bytes 110600 | tf_op jit(solution)/shard_map/ppermute | solution.py:388
  16.8 3.7 %collective-permute-start.6 = (bf16[144,128]{1,0:T(8,128)(2,1)S(1)}, bf16[144,128]{1,0:T(8,128)(2,1)S(1)}, u32[]{:S(2)}, u32[]{:S(2)}) collective-permute-start(bf16[144,128]{1,0:T(8,128)(2,1)S(1)} %collective-permute-done.5.refs_7_), channel_id=1, source_target_pairs={{0,3},{1,2},{2,1},{3,0},{4,7},{5,6},{6,5},{7,4},{8,11},{9,10},{10,... | collective-permute-start | bytes 110600 | tf_op jit(solution)/shard_map/ppermute | solution.py:388
  17.3 3.7 %collective-permute-start.8 = (bf16[144,128]{1,0:T(8,128)(2,1)S(1)}, bf16[144,128]{1,0:T(8,128)(2,1)S(1)}, u32[]{:S(2)}, u32[]{:S(2)}) collective-permute-start(bf16[144,128]{1,0:T(8,128)(2,1)S(1)} %collective-permute-done.7.refs_9_), channel_id=1, source_target_pairs={{0,3},{1,2},{2,1},{3,0},{4,7},{5,6},{6,5},{7,4},{8,11},{9,10},{10,... | collective-permute-start | bytes 110600 | tf_op jit(solution)/shard_map/ppermute | solution.py:388
  21.0 13.7 %copy-start.2 = (s32[4,64]{1,0:T(4,128)S(1)}, s32[4,64]{1,0:T(4,128)}, u32[]{:S(2)}) copy-start(s32[4,64]{1,0:T(4,128)} %get-tuple-element.15.spot_ref) | copy-start | bytes 3076

commit v20 on v19

--- a/solution.py
+++ b/solution.py
@@ -436,7 +436,7 @@
 
     line = [message] + [send(message, d) for d in range(slots - inner, 0, -inner)][::-1]
     got = [line[s // inner] if s % inner == 0 else send(line[s // inner], s % inner) for s in range(slots)]
-    own, other = mask((passage_lengths, across), (passage_vectors, raw), got[-1])
+    own, other = mask((passage_lengths, across), (passage_vectors, raw), got[inner + 1])
     order = [z + y for z in [0, *range(slots - inner, 0, -inner)] for y in range(inner)]
     sums = score(me, got, order, own, other, query_hidden.shape[1])
     back = lax.all_to_all(sums, "shard", split_axis=0, concat_axis=0, axis_index_groups=groups, tiled=True)

time: 35.9 us -> 35.8 us (level)
  blocking collectives: 11.1 us -> 10.5 us
    all_to_all x1, blocking collectives: 11.1 us -> 10.5 us  [per_device(): lax.all_to_all(sums, 'shard', split_axis=0, concat_axis=0, axis_index_gro...]
  transfers between devices with their start and end apart: 9 -> 9, of which waited for: 4 -> 3; matrix products, arithmetic and copies ran while one was open for 0% -> 0% of each run, Pallas kernels for 20% -> 20%
where the time goes in v20:
time: 35.8 us; the launch traced here: 35.6 us
  Pallas kernels  10.7 us (30%)
  blocking collectives  10.5 us (29%)
  starting transfers between devices  9.3 us (26%)
  waiting for transfers between devices  4.41 us (12%)
  between operations  0.71 us (2%)
    all_to_all x1, blocking collectives, per_device(): lax.all_to_all(sums, 'shard', split_axis=0, concat_axis=0, axis_index_gro...  10.5 us
    ppermute x9, starting transfers between devices, swap(): lax.ppermute(value, 'shard', [(i, i ^ distance) for i in range(size)])  9.3 us
    pallas_call x1, Pallas kernels, encode(): pl.pallas_call(kernel, out_shape=(jax.ShapeDtypeStruct((tokens + slots, e...  5.69 us
    ppermute x9, waiting for transfers between devices, swap(): lax.ppermute(value, 'shard', [(i, i ^ distance) for i in range(size)])  4.41 us
    pallas_call x1, Pallas kernels, score(): pl.pallas_call(kernel, out_shape=jax.ShapeDtypeStruct((slots, e), F32), i...  2.68 us
    pallas_call x1, Pallas kernels, mask(): pl.pallas_call(mask_kernel, out_shape=[jax.ShapeDtypeStruct(shape, BF16)]...  1.31 us
    pallas_call x1, Pallas kernels, finish(): pl.pallas_call(finish_kernel, out_shape=(jax.ShapeDtypeStruct(spots.shape...  0.99 us
  transfers between devices with their start and end apart: 9, of which 3 were waited for; matrix products, arithmetic and copies ran while one was open for 0% of the time, Pallas kernels for 20%

profile of v20, /device:TPU:0, one launch (start us, length us, event | category | flops | bytes accessed | tf_op | source)
XLA Modules:
  0.0 35.6 jit_solution(10363721623076501783)
XLA Ops:
  0.6 0.5 %collective-permute-start = (s32[48]{0:T(128)}, s32[48]{0:T(128)S(1)}, u32[]{:S(2)}, u32[]{:S(2)}) collective-permute-start(s32[48]{0:T(128)} %len0_ref.1), channel_id=1, source_target_pairs={{0,1},{1,0},{2,3},{3,2},{4,5},{5,4},{6,7},{7,6},{8,9},{9,8},{10,11... | collective-permute-start | bytes 584 | tf_op jit(solution)/shard_map/ppermute | solution.py:388
  1.2 0.0 copy-start
  1.2 0.0 copy-start.3
  1.2 5.7 %encode.1 = (bf16[144,128]{1,0:T(8,128)(2,1)}, s32[4,64]{1,0:T(4,128)}) custom-call(s32[1]{0:T(128)} %bitcast.refs_0_, s32[4]{0:T(128)} %refs_1_.1, s32[768]{0:T(1024)} %refs_2_.1, s32[4,64]{1,0:T(4,128)} %refs_3_.1, bf16[4,32,768]{2,1,0:T(8,128)(2,1)} %refs_4_.1, bf16[768,3072]{1,0:T(8,128)(2,1)} %refs_5_.1, bf16[3072,768]{1,0:T(8,128)(2,1)} %refs_6_.1, ...), custom_call_target="tpu_custom_call" | custom-call | flops 1207959552 | bytes 9437184 | tf_op jit(solution)/shard_map/encode/pallas_call | solution.py:198
  6.9 0.0 collective-permute-done.len1_ref
  6.9 0.0 copy-done
  6.9 0.0 copy-start.1
  6.9 0.1 collective-permute-start.1
  7.0 2.7 %collective-permute-start.2 = (bf16[144,128]{1,0:T(8,128)(2,1)}, bf16[144,128]{1,0:T(8,128)(2,1)S(1)}, u32[]{:S(2)}, u32[]{:S(2)}) collective-permute-start(bf16[144,128]{1,0:T(8,128)(2,1)} %get-tuple-element.12.refs_3_), channel_id=1, source_target_pairs={{0,5},{1,4},{2,7},{3,6},{4,1},{5,0},{6,3},{7,2},{8,13},{9,12},{10,... | collective-permute-start | bytes 110600 | tf_op jit(solution)/shard_map/ppermute | solution.py:388
  9.7 2.5 %collective-permute-start.5 = (bf16[144,128]{1,0:T(8,128)(2,1)}, bf16[144,128]{1,0:T(8,128)(2,1)S(1)}, u32[]{:S(2)}, u32[]{:S(2)}) collective-permute-start(bf16[144,128]{1,0:T(8,128)(2,1)} %get-tuple-element.12.refs_3_), channel_id=1, source_target_pairs={{0,13},{1,12},{2,15},{3,14},{4,9},{5,8},{6,11},{7,10},{8,5},{9,4},... | collective-permute-start | bytes 110600 | tf_op jit(solution)/shard_map/ppermute | solution.py:388
  12.2 0.1 collective-permute-start.7
  12.3 0.0 collective-permute-done.2.refs_9_
  12.3 1.3 %collective-permute-start.3 = (bf16[144,128]{1,0:T(8,128)(2,1)S(1)}, bf16[144,128]{1,0:T(8,128)(2,1)S(1)}, u32[]{:S(2)}, u32[]{:S(2)}) collective-permute-start(bf16[144,128]{1,0:T(8,128)(2,1)S(1)} %collective-permute-done.2.refs_9_), channel_id=1, source_target_pairs={{0,3},{1,2},{2,1},{3,0},{4,7},{5,6},{6,5},{7,4},{8,11},{9,10},{10,... | collective-permute-start | bytes 110600 | tf_op jit(solution)/shard_map/ppermute | solution.py:388
  13.6 0.5 %collective-permute-start.4 = (bf16[144,128]{1,0:T(8,128)(2,1)}, bf16[144,128]{1,0:T(8,128)(2,1)S(1)}, u32[]{:S(2)}, u32[]{:S(2)}) collective-permute-start(bf16[144,128]{1,0:T(8,128)(2,1)} %get-tuple-element.12.refs_3_), channel_id=1, source_target_pairs={{0,3},{1,2},{2,1},{3,0},{4,7},{5,6},{6,5},{7,4},{8,11},{9,10},{10,... | collective-permute-start | bytes 110600 | tf_op jit(solution)/shard_map/ppermute | solution.py:388
  14.1 1.0 %collective-permute-done.5.refs_5_ = bf16[144,128]{1,0:T(8,128)(2,1)S(1)} collective-permute-done((bf16[144,128]{1,0:T(8,128)(2,1)}, bf16[144,128]{1,0:T(8,128)(2,1)S(1)}, u32[]{:S(2)}, u32[]{:S(2)}) %collective-permute-start.5) | collective-permute-done | bytes 36896 | tf_op jit(solution)/shard_map/ppermute | solution.py:388
  15.1 1.6 %collective-permute-start.6 = (bf16[144,128]{1,0:T(8,128)(2,1)S(1)}, bf16[144,128]{1,0:T(8,128)(2,1)S(1)}, u32[]{:S(2)}, u32[]{:S(2)}) collective-permute-start(bf16[144,128]{1,0:T(8,128)(2,1)S(1)} %collective-permute-done.5.refs_5_), channel_id=1, source_target_pairs={{0,3},{1,2},{2,1},{3,0},{4,7},{5,6},{6,5},{7,4},{8,11},{9,10},{10,... | collective-permute-start | bytes 110600 | tf_op jit(solution)/shard_map/ppermute | solution.py:388
  16.7 1.0 %collective-permute-done.7.refs_7_ = bf16[144,128]{1,0:T(8,128)(2,1)S(1)} collective-permute-done((bf16[144,128]{1,0:T(8,128)(2,1)}, bf16[144,128]{1,0:T(8,128)(2,1)S(1)}, u32[]{:S(2)}, u32[]{:S(2)}) %collective-permute-start.7) | collective-permute-done | bytes 36896 | tf_op jit(solution)/shard_map/ppermute | solution.py:388
  17.7 0.0 collective-permute-start.8
  17.7 0.0 collective-permute-done.3._.refs_10_
  17.7 0.0 collective-permute-done.1.pass1_ref
  17.8 0.0 copy-done.3
  17.8 1.3 %mask.1 = (bf16[48,128,128]{2,1,0:T(8,128)(2,1)S(1)}, bf16[48,128,128]{2,1,0:T(8,128)(2,1)S(1)}) custom-call(s32[48]{0:T(128)S(1)} %copy-done.3, s32[48]{0:T(128)S(1)} %collective-permute-done.len1_ref, bf16[48,128,128]{2,1,0:T(8,128)(2,1)S(1)} %copy-done, bf16[48,128,128]{2,1,0:T(8,128)(2,1)S(1)} %collective-permute-done.1.pass1_ref, ...), custom_call_target="tpu_custom_call" | custom-call | flops 12582912 | bytes 6291456 | tf_op jit(solution)/shard_map/mask/pallas_call | solution.py:249
  19.1 0.0 collective-permute-done.4.refs_4_
  19.1 0.0 collective-permute-done.6.refs_6_
  19.1 2.3 %collective-permute-done.8.refs_8_ = bf16[144,128]{1,0:T(8,128)(2,1)S(1)} collective-permute-done((bf16[144,128]{1,0:T(8,128)(2,1)S(1)}, bf16[144,128]{1,0:T(8,128)(2,1)S(1)}, u32[]{:S(2)}, u32[]{:S(2)}) %collective-permute-start.8) | collective-permute-done | bytes 36896 | tf_op jit(solution)/shard_map/ppermute | solution.py:388
  21.4 0.0 copy-done.1
  21.4 0.0 copy-start.2
  21.4 2.7 %score.1 = f32[8,128]{1,0:T(8,128)S(1)} custom-call(s32[1]{0:T(128)} %bitcast.refs_0_, bf16[48,128,128]{2,1,0:T(8,128)(2,1)S(1)} %get-tuple-element.13.refs_1_, bf16[48,128,128]{2,1,0:T(8,128)(2,1)S(1)} %get-tuple-element.14.refs_2_, bf16[144,128]{1,0:T(8,128)(2,1)S(1)} %copy-done.1, bf16[144,128]{1,0:T(8,128)(2,1)S(1)} %collective-permute-done.4.refs_4_, ...), custom_call_target="tpu_custom_call" | custom-call | flops 805306368 | bytes 3145728 | tf_op jit(solution)/shard_map/score/pallas_call | solution.py:327
  24.1 10.5 %all_to_all.11 = f32[8,1,128]{2,1,0:T(1,128)S(1)} all-to-all(f32[8,1,128]{2,1,0:T(1,128)S(1)} %bitcast.5), channel_id=1, replica_groups={{0,3,5,6,8,11,13,14},{1,2,4,7,9,10,12,15},{16,19,21,22,24,27,29,30},{17..., dimensions={0} | all-to-all | bytes 8192 | tf_op jit(solution)/shard_map/all_to_all | solution.py:442
  34.6 0.0 copy-done.2
  34.6 1.0 %finish.1 = (f32[4,64]{1,0:T(4,128)}, f32[4,10]{1,0:T(4,128)}) custom-call(f32[8,128]{1,0:T(8,128)S(1)} %bitcast.6, s32[4,64]{1,0:T(4,128)S(1)} %copy-done.2), custom_call_target="tpu_custom_call" | custom-call | tf_op jit(solution)/shard_map/finish/pallas_call | solution.py:373
Async XLA Ops:
  0.6 6.2 %collective-permute-start = (s32[48]{0:T(128)}, s32[48]{0:T(128)S(1)}, u32[]{:S(2)}, u32[]{:S(2)}) collective-permute-start(s32[48]{0:T(128)} %len0_ref.1), channel_id=1, source_target_pairs={{0,1},{1,0},{2,3},{3,2},{4,5},{5,4},{6,7},{7,6},{8,9},{9,8},{10,11... | collective-permute-start | bytes 584 | tf_op jit(solution)/shard_map/ppermute | solution.py:388
  1.2 5.7 %copy-start = (bf16[48,128,128]{2,1,0:T(8,128)(2,1)S(1)}, bf16[48,128,128]{2,1,0:T(8,128)(2,1)}, u32[]{:S(2)}) copy-start(bf16[48,128,128]{2,1,0:T(8,128)(2,1)} %pass0_ref.1) | copy-start | bytes 4718596
  1.2 16.6 %copy-start.3 = (s32[48]{0:T(128)S(1)}, s32[48]{0:T(128)}, u32[]{:S(2)}) copy-start(s32[48]{0:T(128)} %len0_ref.1) | copy-start | bytes 580
  6.9 14.5 %copy-start.1 = (bf16[144,128]{1,0:T(8,128)(2,1)S(1)}, bf16[144,128]{1,0:T(8,128)(2,1)}, u32[]{:S(2)}) copy-start(bf16[144,128]{1,0:T(8,128)(2,1)} %get-tuple-element.12.refs_3_) | copy-start | bytes 110596
  6.9 10.9 %collective-permute-start.1 = (bf16[48,128,128]{2,1,0:T(8,128)(2,1)S(1)}, bf16[48,128,128]{2,1,0:T(8,128)(2,1)S(1)}, u32[]{:S(2)}, u32[]{:S(2)}) collective-permute-start(bf16[48,128,128]{2,1,0:T(8,128)(2,1)S(1)} %copy-done), channel_id=1, source_target_pairs={{0,1},{1,0},{2,3},{3,2},{4,5},{5,4},{6,7},{7,6},{8,9},{9,8},{10,11... | collective-permute-start | bytes 4718600 | tf_op jit(solution)/shard_map/ppermute | solution.py:388
  7.0 5.3 %collective-permute-start.2 = (bf16[144,128]{1,0:T(8,128)(2,1)}, bf16[144,128]{1,0:T(8,128)(2,1)S(1)}, u32[]{:S(2)}, u32[]{:S(2)}) collective-permute-start(bf16[144,128]{1,0:T(8,128)(2,1)} %get-tuple-element.12.refs_3_), channel_id=1, source_target_pairs={{0,5},{1,4},{2,7},{3,6},{4,1},{5,0},{6,3},{7,2},{8,13},{9,12},{10,... | collective-permute-start | bytes 110600 | tf_op jit(solution)/shard_map/ppermute | solution.py:388
  9.7 5.4 %collective-permute-start.5 = (bf16[144,128]{1,0:T(8,128)(2,1)}, bf16[144,128]{1,0:T(8,128)(2,1)S(1)}, u32[]{:S(2)}, u32[]{:S(2)}) collective-permute-start(bf16[144,128]{1,0:T(8,128)(2,1)} %get-tuple-element.12.refs_3_), channel_id=1, source_target_pairs={{0,13},{1,12},{2,15},{3,14},{4,9},{5,8},{6,11},{7,10},{8,5},{9,4},... | collective-permute-start | bytes 110600 | tf_op jit(solution)/shard_map/ppermute | solution.py:388
  12.2 5.5 %collective-permute-start.7 = (bf16[144,128]{1,0:T(8,128)(2,1)}, bf16[144,128]{1,0:T(8,128)(2,1)S(1)}, u32[]{:S(2)}, u32[]{:S(2)}) collective-permute-start(bf16[144,128]{1,0:T(8,128)(2,1)} %get-tuple-element.12.refs_3_), channel_id=1, source_target_pairs={{0,8},{1,9},{2,10},{3,11},{4,12},{5,13},{6,14},{7,15},{8,0},{9,1},... | collective-permute-start | bytes 110600 | tf_op jit(solution)/shard_map/ppermute | solution.py:388
  12.3 5.4 %collective-permute-start.3 = (bf16[144,128]{1,0:T(8,128)(2,1)S(1)}, bf16[144,128]{1,0:T(8,128)(2,1)S(1)}, u32[]{:S(2)}, u32[]{:S(2)}) collective-permute-start(bf16[144,128]{1,0:T(8,128)(2,1)S(1)} %collective-permute-done.2.refs_9_), channel_id=1, source_target_pairs={{0,3},{1,2},{2,1},{3,0},{4,7},{5,6},{6,5},{7,4},{8,11},{9,10},{10,... | collective-permute-start | bytes 110600 | tf_op jit(solution)/shard_map/ppermute | solution.py:388
  13.6 5.5 %collective-permute-start.4 = (bf16[144,128]{1,0:T(8,128)(2,1)}, bf16[144,128]{1,0:T(8,128)(2,1)S(1)}, u32[]{:S(2)}, u32[]{:S(2)}) collective-permute-start(bf16[144,128]{1,0:T(8,128)(2,1)} %get-tuple-element.12.refs_3_), channel_id=1, source_target_pairs={{0,3},{1,2},{2,1},{3,0},{4,7},{5,6},{6,5},{7,4},{8,11},{9,10},{10,... | collective-permute-start | bytes 110600 | tf_op jit(solution)/shard_map/ppermute | solution.py:388
  15.1 4.0 %collective-permute-start.6 = (bf16[144,128]{1,0:T(8,128)(2,1)S(1)}, bf16[144,128]{1,0:T(8,128)(2,1)S(1)}, u32[]{:S(2)}, u32[]{:S(2)}) collective-permute-start(bf16[144,128]{1,0:T(8,128)(2,1)S(1)} %collective-permute-done.5.refs_5_), channel_id=1, source_target_pairs={{0,3},{1,2},{2,1},{3,0},{4,7},{5,6},{6,5},{7,4},{8,11},{9,10},{10,... | collective-permute-start | bytes 110600 | tf_op jit(solution)/shard_map/ppermute | solution.py:388
  17.7 3.7 %collective-permute-start.8 = (bf16[144,128]{1,0:T(8,128)(2,1)S(1)}, bf16[144,128]{1,0:T(8,128)(2,1)S(1)}, u32[]{:S(2)}, u32[]{:S(2)}) collective-permute-start(bf16[144,128]{1,0:T(8,128)(2,1)S(1)} %collective-permute-done.7.refs_7_), channel_id=1, source_target_pairs={{0,3},{1,2},{2,1},{3,0},{4,7},{5,6},{6,5},{7,4},{8,11},{9,10},{10,... | collective-permute-start | bytes 110600 | tf_op jit(solution)/shard_map/ppermute | solution.py:388
  21.4 13.2 %copy-start.2 = (s32[4,64]{1,0:T(4,128)S(1)}, s32[4,64]{1,0:T(4,128)}, u32[]{:S(2)}) copy-start(s32[4,64]{1,0:T(4,128)} %get-tuple-element.15.spot_ref) | copy-start | bytes 3076

commit v21 on v20

--- a/solution.py
+++ b/solution.py
@@ -128,22 +128,20 @@
     small[0].wait()
     x = x_ref[...].reshape(query_count * token_count, width_in)
     total = x.astype(F32)
-    inner = active = None
-    for step in range(chunks + 2):
+    inner = None
+    for step in range(chunks + 1):
         if step < chunks:
             copies[step][0].wait()
-        if step >= 2:
-            copies[step - 2][1].wait()
         if step == 1:
             small[2].wait()
             placed.wait()
         if step >= 1:
+            copies[step - 1][1].wait()
             enter()
         later = jnp.dot(x, w1_buf[step], preferred_element_type=F32) if step < chunks else None
-        if step >= 2:
-            total = total + jnp.dot(active, w2_buf[step - 2], preferred_element_type=F32)
-        if 1 <= step <= chunks:
+        if step >= 1:
             active = (0.5 * inner * (1.0 + lax.erf(inner * (0.5 ** 0.5)))).astype(BF16)
+            total = total + jnp.dot(active, w2_buf[step - 1], preferred_element_type=F32)
         inner = later
         if step == chunks:
             fetch = pltpu.make_async_copy(table, table_v, table_sem)

time: 35.8 us -> 35.8 us (level)
  no operation moved by 1% of the time
where the time goes in v21:
time: 35.8 us; the launch traced here: 35.6 us
  Pallas kernels  10.7 us (30%)
  blocking collectives  10.5 us (29%)
  starting transfers between devices  9.29 us (26%)
  waiting for transfers between devices  4.41 us (12%)
  between operations  0.71 us (2%)
    all_to_all x1, blocking collectives, per_device(): lax.all_to_all(sums, 'shard', split_axis=0, concat_axis=0, axis_index_gro...  10.5 us
    ppermute x9, starting transfers between devices, swap(): lax.ppermute(value, 'shard', [(i, i ^ distance) for i in range(size)])  9.29 us
    pallas_call x1, Pallas kernels, encode(): pl.pallas_call(kernel, out_shape=(jax.ShapeDtypeStruct((tokens + slots, e...  5.71 us
    ppermute x9, waiting for transfers between devices, swap(): lax.ppermute(value, 'shard', [(i, i ^ distance) for i in range(size)])  4.41 us
    pallas_call x1, Pallas kernels, score(): pl.pallas_call(kernel, out_shape=jax.ShapeDtypeStruct((slots, e), F32), i...  2.68 us
    pallas_call x1, Pallas kernels, mask(): pl.pallas_call(mask_kernel, out_shape=[jax.ShapeDtypeStruct(shape, BF16)]...  1.31 us
    pallas_call x1, Pallas kernels, finish(): pl.pallas_call(finish_kernel, out_shape=(jax.ShapeDtypeStruct(spots.shape...  0.99 us
  transfers between devices with their start and end apart: 9, of which 3 were waited for; matrix products, arithmetic and copies ran while one was open for 0% of the time, Pallas kernels for 20%

profile of v21, /device:TPU:0, one launch (start us, length us, event | category | flops | bytes accessed | tf_op | source)
XLA Modules:
  0.0 35.6 jit_solution(1891292035512166324)
XLA Ops:
  0.6 0.5 %collective-permute-start = (s32[48]{0:T(128)}, s32[48]{0:T(128)S(1)}, u32[]{:S(2)}, u32[]{:S(2)}) collective-permute-start(s32[48]{0:T(128)} %len0_ref.1), channel_id=1, source_target_pairs={{0,1},{1,0},{2,3},{3,2},{4,5},{5,4},{6,7},{7,6},{8,9},{9,8},{10,11... | collective-permute-start | bytes 584 | tf_op jit(solution)/shard_map/ppermute | solution.py:386
  1.2 0.0 copy-start
  1.2 0.0 copy-start.3
  1.2 5.7 %encode.1 = (bf16[144,128]{1,0:T(8,128)(2,1)}, s32[4,64]{1,0:T(4,128)}) custom-call(s32[1]{0:T(128)} %bitcast.refs_0_, s32[4]{0:T(128)} %refs_1_.1, s32[768]{0:T(1024)} %refs_2_.1, s32[4,64]{1,0:T(4,128)} %refs_3_.1, bf16[4,32,768]{2,1,0:T(8,128)(2,1)} %refs_4_.1, bf16[768,3072]{1,0:T(8,128)(2,1)} %refs_5_.1, bf16[3072,768]{1,0:T(8,128)(2,1)} %refs_6_.1, ...), custom_call_target="tpu_custom_call" | custom-call | flops 1207959552 | bytes 9437184 | tf_op jit(solution)/shard_map/encode/pallas_call | solution.py:196
  6.9 0.0 collective-permute-done.len1_ref
  6.9 0.0 copy-done
  6.9 0.0 copy-start.1
  6.9 0.1 collective-permute-start.1
  7.0 2.7 %collective-permute-start.2 = (bf16[144,128]{1,0:T(8,128)(2,1)}, bf16[144,128]{1,0:T(8,128)(2,1)S(1)}, u32[]{:S(2)}, u32[]{:S(2)}) collective-permute-start(bf16[144,128]{1,0:T(8,128)(2,1)} %get-tuple-element.12.refs_3_), channel_id=1, source_target_pairs={{0,5},{1,4},{2,7},{3,6},{4,1},{5,0},{6,3},{7,2},{8,13},{9,12},{10,... | collective-permute-start | bytes 110600 | tf_op jit(solution)/shard_map/ppermute | solution.py:386
  9.7 2.5 %collective-permute-start.5 = (bf16[144,128]{1,0:T(8,128)(2,1)}, bf16[144,128]{1,0:T(8,128)(2,1)S(1)}, u32[]{:S(2)}, u32[]{:S(2)}) collective-permute-start(bf16[144,128]{1,0:T(8,128)(2,1)} %get-tuple-element.12.refs_3_), channel_id=1, source_target_pairs={{0,13},{1,12},{2,15},{3,14},{4,9},{5,8},{6,11},{7,10},{8,5},{9,4},... | collective-permute-start | bytes 110600 | tf_op jit(solution)/shard_map/ppermute | solution.py:386
  12.3 0.1 collective-permute-start.7
  12.3 0.0 collective-permute-done.2.refs_9_
  12.3 1.3 %collective-permute-start.3 = (bf16[144,128]{1,0:T(8,128)(2,1)S(1)}, bf16[144,128]{1,0:T(8,128)(2,1)S(1)}, u32[]{:S(2)}, u32[]{:S(2)}) collective-permute-start(bf16[144,128]{1,0:T(8,128)(2,1)S(1)} %collective-permute-done.2.refs_9_), channel_id=1, source_target_pairs={{0,3},{1,2},{2,1},{3,0},{4,7},{5,6},{6,5},{7,4},{8,11},{9,10},{10,... | collective-permute-start | bytes 110600 | tf_op jit(solution)/shard_map/ppermute | solution.py:386
  13.6 0.5 %collective-permute-start.4 = (bf16[144,128]{1,0:T(8,128)(2,1)}, bf16[144,128]{1,0:T(8,128)(2,1)S(1)}, u32[]{:S(2)}, u32[]{:S(2)}) collective-permute-start(bf16[144,128]{1,0:T(8,128)(2,1)} %get-tuple-element.12.refs_3_), channel_id=1, source_target_pairs={{0,3},{1,2},{2,1},{3,0},{4,7},{5,6},{6,5},{7,4},{8,11},{9,10},{10,... | collective-permute-start | bytes 110600 | tf_op jit(solution)/shard_map/ppermute | solution.py:386
  14.1 1.0 %collective-permute-done.5.refs_5_ = bf16[144,128]{1,0:T(8,128)(2,1)S(1)} collective-permute-done((bf16[144,128]{1,0:T(8,128)(2,1)}, bf16[144,128]{1,0:T(8,128)(2,1)S(1)}, u32[]{:S(2)}, u32[]{:S(2)}) %collective-permute-start.5) | collective-permute-done | bytes 36896 | tf_op jit(solution)/shard_map/ppermute | solution.py:386
  15.1 1.6 %collective-permute-start.6 = (bf16[144,128]{1,0:T(8,128)(2,1)S(1)}, bf16[144,128]{1,0:T(8,128)(2,1)S(1)}, u32[]{:S(2)}, u32[]{:S(2)}) collective-permute-start(bf16[144,128]{1,0:T(8,128)(2,1)S(1)} %collective-permute-done.5.refs_5_), channel_id=1, source_target_pairs={{0,3},{1,2},{2,1},{3,0},{4,7},{5,6},{6,5},{7,4},{8,11},{9,10},{10,... | collective-permute-start | bytes 110600 | tf_op jit(solution)/shard_map/ppermute | solution.py:386
  16.7 1.0 %collective-permute-done.7.refs_7_ = bf16[144,128]{1,0:T(8,128)(2,1)S(1)} collective-permute-done((bf16[144,128]{1,0:T(8,128)(2,1)}, bf16[144,128]{1,0:T(8,128)(2,1)S(1)}, u32[]{:S(2)}, u32[]{:S(2)}) %collective-permute-start.7) | collective-permute-done | bytes 36896 | tf_op jit(solution)/shard_map/ppermute | solution.py:386
  17.7 0.0 collective-permute-start.8
  17.8 0.0 collective-permute-done.3._.refs_10_
  17.8 0.0 collective-permute-done.1.pass1_ref
  17.8 0.0 copy-done.3
  17.8 1.3 %mask.1 = (bf16[48,128,128]{2,1,0:T(8,128)(2,1)S(1)}, bf16[48,128,128]{2,1,0:T(8,128)(2,1)S(1)}) custom-call(s32[48]{0:T(128)S(1)} %copy-done.3, s32[48]{0:T(128)S(1)} %collective-permute-done.len1_ref, bf16[48,128,128]{2,1,0:T(8,128)(2,1)S(1)} %copy-done, bf16[48,128,128]{2,1,0:T(8,128)(2,1)S(1)} %collective-permute-done.1.pass1_ref, ...), custom_call_target="tpu_custom_call" | custom-call | flops 12582912 | bytes 6291456 | tf_op jit(solution)/shard_map/mask/pallas_call | solution.py:247
  19.1 0.0 collective-permute-done.4.refs_4_
  19.1 0.0 collective-permute-done.6.refs_6_
  19.1 2.3 %collective-permute-done.8.refs_8_ = bf16[144,128]{1,0:T(8,128)(2,1)S(1)} collective-permute-done((bf16[144,128]{1,0:T(8,128)(2,1)S(1)}, bf16[144,128]{1,0:T(8,128)(2,1)S(1)}, u32[]{:S(2)}, u32[]{:S(2)}) %collective-permute-start.8) | collective-permute-done | bytes 36896 | tf_op jit(solution)/shard_map/ppermute | solution.py:386
  21.4 0.0 copy-done.1
  21.4 0.0 copy-start.2
  21.4 2.7 %score.1 = f32[8,128]{1,0:T(8,128)S(1)} custom-call(s32[1]{0:T(128)} %bitcast.refs_0_, bf16[48,128,128]{2,1,0:T(8,128)(2,1)S(1)} %get-tuple-element.13.refs_1_, bf16[48,128,128]{2,1,0:T(8,128)(2,1)S(1)} %get-tuple-element.14.refs_2_, bf16[144,128]{1,0:T(8,128)(2,1)S(1)} %copy-done.1, bf16[144,128]{1,0:T(8,128)(2,1)S(1)} %collective-permute-done.4.refs_4_, ...), custom_call_target="tpu_custom_call" | custom-call | flops 805306368 | bytes 3145728 | tf_op jit(solution)/shard_map/score/pallas_call | solution.py:325
  24.1 10.5 %all_to_all.11 = f32[8,1,128]{2,1,0:T(1,128)S(1)} all-to-all(f32[8,1,128]{2,1,0:T(1,128)S(1)} %bitcast.5), channel_id=1, replica_groups={{0,3,5,6,8,11,13,14},{1,2,4,7,9,10,12,15},{16,19,21,22,24,27,29,30},{17..., dimensions={0} | all-to-all | bytes 8192 | tf_op jit(solution)/shard_map/all_to_all | solution.py:440
  34.6 0.0 copy-done.2
  34.6 1.0 %finish.1 = (f32[4,64]{1,0:T(4,128)}, f32[4,10]{1,0:T(4,128)}) custom-call(f32[8,128]{1,0:T(8,128)S(1)} %bitcast.6, s32[4,64]{1,0:T(4,128)S(1)} %copy-done.2), custom_call_target="tpu_custom_call" | custom-call | tf_op jit(solution)/shard_map/finish/pallas_call | solution.py:371
Async XLA Ops:
  0.6 6.2 %collective-permute-start = (s32[48]{0:T(128)}, s32[48]{0:T(128)S(1)}, u32[]{:S(2)}, u32[]{:S(2)}) collective-permute-start(s32[48]{0:T(128)} %len0_ref.1), channel_id=1, source_target_pairs={{0,1},{1,0},{2,3},{3,2},{4,5},{5,4},{6,7},{7,6},{8,9},{9,8},{10,11... | collective-permute-start | bytes 584 | tf_op jit(solution)/shard_map/ppermute | solution.py:386
  1.2 5.7 %copy-start = (bf16[48,128,128]{2,1,0:T(8,128)(2,1)S(1)}, bf16[48,128,128]{2,1,0:T(8,128)(2,1)}, u32[]{:S(2)}) copy-start(bf16[48,128,128]{2,1,0:T(8,128)(2,1)} %pass0_ref.1) | copy-start | bytes 4718596
  1.2 16.6 %copy-start.3 = (s32[48]{0:T(128)S(1)}, s32[48]{0:T(128)}, u32[]{:S(2)}) copy-start(s32[48]{0:T(128)} %len0_ref.1) | copy-start | bytes 580
  6.9 14.5 %copy-start.1 = (bf16[144,128]{1,0:T(8,128)(2,1)S(1)}, bf16[144,128]{1,0:T(8,128)(2,1)}, u32[]{:S(2)}) copy-start(bf16[144,128]{1,0:T(8,128)(2,1)} %get-tuple-element.12.refs_3_) | copy-start | bytes 110596
  6.9 10.9 %collective-permute-start.1 = (bf16[48,128,128]{2,1,0:T(8,128)(2,1)S(1)}, bf16[48,128,128]{2,1,0:T(8,128)(2,1)S(1)}, u32[]{:S(2)}, u32[]{:S(2)}) collective-permute-start(bf16[48,128,128]{2,1,0:T(8,128)(2,1)S(1)} %copy-done), channel_id=1, source_target_pairs={{0,1},{1,0},{2,3},{3,2},{4,5},{5,4},{6,7},{7,6},{8,9},{9,8},{10,11... | collective-permute-start | bytes 4718600 | tf_op jit(solution)/shard_map/ppermute | solution.py:386
  7.0 5.3 %collective-permute-start.2 = (bf16[144,128]{1,0:T(8,128)(2,1)}, bf16[144,128]{1,0:T(8,128)(2,1)S(1)}, u32[]{:S(2)}, u32[]{:S(2)}) collective-permute-start(bf16[144,128]{1,0:T(8,128)(2,1)} %get-tuple-element.12.refs_3_), channel_id=1, source_target_pairs={{0,5},{1,4},{2,7},{3,6},{4,1},{5,0},{6,3},{7,2},{8,13},{9,12},{10,... | collective-permute-start | bytes 110600 | tf_op jit(solution)/shard_map/ppermute | solution.py:386
  9.7 5.4 %collective-permute-start.5 = (bf16[144,128]{1,0:T(8,128)(2,1)}, bf16[144,128]{1,0:T(8,128)(2,1)S(1)}, u32[]{:S(2)}, u32[]{:S(2)}) collective-permute-start(bf16[144,128]{1,0:T(8,128)(2,1)} %get-tuple-element.12.refs_3_), channel_id=1, source_target_pairs={{0,13},{1,12},{2,15},{3,14},{4,9},{5,8},{6,11},{7,10},{8,5},{9,4},... | collective-permute-start | bytes 110600 | tf_op jit(solution)/shard_map/ppermute | solution.py:386
  12.3 5.5 %collective-permute-start.7 = (bf16[144,128]{1,0:T(8,128)(2,1)}, bf16[144,128]{1,0:T(8,128)(2,1)S(1)}, u32[]{:S(2)}, u32[]{:S(2)}) collective-permute-start(bf16[144,128]{1,0:T(8,128)(2,1)} %get-tuple-element.12.refs_3_), channel_id=1, source_target_pairs={{0,8},{1,9},{2,10},{3,11},{4,12},{5,13},{6,14},{7,15},{8,0},{9,1},... | collective-permute-start | bytes 110600 | tf_op jit(solution)/shard_map/ppermute | solution.py:386
  12.3 5.4 %collective-permute-start.3 = (bf16[144,128]{1,0:T(8,128)(2,1)S(1)}, bf16[144,128]{1,0:T(8,128)(2,1)S(1)}, u32[]{:S(2)}, u32[]{:S(2)}) collective-permute-start(bf16[144,128]{1,0:T(8,128)(2,1)S(1)} %collective-permute-done.2.refs_9_), channel_id=1, source_target_pairs={{0,3},{1,2},{2,1},{3,0},{4,7},{5,6},{6,5},{7,4},{8,11},{9,10},{10,... | collective-permute-start | bytes 110600 | tf_op jit(solution)/shard_map/ppermute | solution.py:386
  13.6 5.5 %collective-permute-start.4 = (bf16[144,128]{1,0:T(8,128)(2,1)}, bf16[144,128]{1,0:T(8,128)(2,1)S(1)}, u32[]{:S(2)}, u32[]{:S(2)}) collective-permute-start(bf16[144,128]{1,0:T(8,128)(2,1)} %get-tuple-element.12.refs_3_), channel_id=1, source_target_pairs={{0,3},{1,2},{2,1},{3,0},{4,7},{5,6},{6,5},{7,4},{8,11},{9,10},{10,... | collective-permute-start | bytes 110600 | tf_op jit(solution)/shard_map/ppermute | solution.py:386
  15.1 4.0 %collective-permute-start.6 = (bf16[144,128]{1,0:T(8,128)(2,1)S(1)}, bf16[144,128]{1,0:T(8,128)(2,1)S(1)}, u32[]{:S(2)}, u32[]{:S(2)}) collective-permute-start(bf16[144,128]{1,0:T(8,128)(2,1)S(1)} %collective-permute-done.5.refs_5_), channel_id=1, source_target_pairs={{0,3},{1,2},{2,1},{3,0},{4,7},{5,6},{6,5},{7,4},{8,11},{9,10},{10,... | collective-permute-start | bytes 110600 | tf_op jit(solution)/shard_map/ppermute | solution.py:386
  17.7 3.7 %collective-permute-start.8 = (bf16[144,128]{1,0:T(8,128)(2,1)S(1)}, bf16[144,128]{1,0:T(8,128)(2,1)S(1)}, u32[]{:S(2)}, u32[]{:S(2)}) collective-permute-start(bf16[144,128]{1,0:T(8,128)(2,1)S(1)} %collective-permute-done.7.refs_7_), channel_id=1, source_target_pairs={{0,3},{1,2},{2,1},{3,0},{4,7},{5,6},{6,5},{7,4},{8,11},{9,10},{10,... | collective-permute-start | bytes 110600 | tf_op jit(solution)/shard_map/ppermute | solution.py:386
  21.4 13.2 %copy-start.2 = (s32[4,64]{1,0:T(4,128)S(1)}, s32[4,64]{1,0:T(4,128)}, u32[]{:S(2)}) copy-start(s32[4,64]{1,0:T(4,128)} %get-tuple-element.15.spot_ref) | copy-start | bytes 3076

commit v22 on v18

--- a/solution.py
+++ b/solution.py
@@ -100,9 +100,9 @@
     for c in range(2, chunks):
         copies[c][0].start()
         copies[c - 1][1].start()
-    copies[-1][1].start()
     for copy in small[3:]:
         copy.start()
+    copies[-1][1].start()
     clear.wait()
     small[1].wait()
     row = row_ref[...]
@@ -132,11 +132,15 @@
     for step in range(chunks + 2):
         if step < chunks:
             copies[step][0].wait()
-        if step >= 2:
-            copies[step - 2][1].wait()
         if step == 1:
             small[2].wait()
             placed.wait()
+        if step == chunks + 1:
+            for copy in small[3:]:
+                copy.wait()
+            fetch.wait()
+        if step >= 2:
+            copies[step - 2][1].wait()
         if step >= 1:
             enter()
         later = jnp.dot(x, w1_buf[step], preferred_element_type=F32) if step < chunks else None
@@ -149,8 +153,6 @@
             fetch = pltpu.make_async_copy(table, table_v, table_sem)
             fetch.start()
 
-    for copy in small[3:]:
-        copy.wait()
     centered = total - jnp.mean(total, axis=-1, keepdims=True)
     variance = jnp.mean(jnp.square(centered), axis=-1, keepdims=True)
     layer_out = (centered * lax.rsqrt(variance + 1e-12) * gain_ref[...].reshape(1, width_in)).astype(BF16)
@@ -162,7 +164,6 @@
         padded = (token >= i * token_count + lens_ref[i]) & (token < (i + 1) * token_count)
         vectors = jnp.where(padded, 0.0, vectors)
     vectors = vectors.astype(BF16)
-    fetch.wait()
     tokens = query_count * token_count
     wanted = table_v[...].astype(F32).astype(BF16)
     out_ref[pl.ds(0, tokens), :] = vectors
@@ -188,7 +189,7 @@
     e = embed_weight.shape[1]
     slots = -(-slots // 16) * 16
     assert 2 * half <= e == 128
-    chunks = 3
+    chunks = 4
     width = ff // chunks
     tokens = query_count * token_count
 

time: 35.3 us -> 35.7 us (1.011)
  Pallas kernels: 10.7 us -> 11.2 us
    pallas_call x1, Pallas kernels: 5.78 us -> 6.23 us  [encode(): pl.pallas_call(kernel, out_shape=(jax.ShapeDtypeStruct((tokens + slots, e...]
  transfers between devices with their start and end apart: 9 -> 9, of which waited for: 3 -> 3; matrix products, arithmetic and copies ran while one was open for 0% -> 0% of each run, Pallas kernels for 20% -> 21%
where the time goes in v22:
time: 35.7 us; the launch traced here: 35.6 us
  Pallas kernels  11.2 us (31%)
  blocking collectives  10.1 us (28%)
  starting transfers between devices  8.93 us (25%)
  waiting for transfers between devices  4.69 us (13%)
  between operations  0.71 us (2%)
    all_to_all x1, blocking collectives, per_device(): lax.all_to_all(sums, 'shard', split_axis=0, concat_axis=0, axis_index_gro...  10.1 us
    ppermute x9, starting transfers between devices, swap(): lax.ppermute(value, 'shard', [(i, i ^ distance) for i in range(size)])  8.93 us
    pallas_call x1, Pallas kernels, encode(): pl.pallas_call(kernel, out_shape=(jax.ShapeDtypeStruct((tokens + slots, e...  6.23 us
    ppermute x9, waiting for transfers between devices, swap(): lax.ppermute(value, 'shard', [(i, i ^ distance) for i in range(size)])  4.69 us
    pallas_call x1, Pallas kernels, score(): pl.pallas_call(kernel, out_shape=jax.ShapeDtypeStruct((slots, e), F32), i...  2.64 us
    pallas_call x1, Pallas kernels, mask(): pl.pallas_call(mask_kernel, out_shape=[jax.ShapeDtypeStruct(shape, BF16)]...  1.31 us
    pallas_call x1, Pallas kernels, finish(): pl.pallas_call(finish_kernel, out_shape=(jax.ShapeDtypeStruct(spots.shape...  0.99 us
  transfers between devices with their start and end apart: 9, of which 3 were waited for; matrix products, arithmetic and copies ran while one was open for 0% of the time, Pallas kernels for 21%

profile of v22, /device:TPU:0, one launch (start us, length us, event | category | flops | bytes accessed | tf_op | source)
XLA Modules:
  0.0 35.6 jit_solution(10068239324387653767)
XLA Ops:
  0.6 0.5 %collective-permute-start = (s32[48]{0:T(128)}, s32[48]{0:T(128)S(1)}, u32[]{:S(2)}, u32[]{:S(2)}) collective-permute-start(s32[48]{0:T(128)} %len0_ref.1), channel_id=1, source_target_pairs={{0,1},{1,0},{2,3},{3,2},{4,5},{5,4},{6,7},{7,6},{8,9},{9,8},{10,11... | collective-permute-start | bytes 584 | tf_op jit(solution)/shard_map/ppermute | solution.py:388
  1.2 0.0 copy-start
  1.2 0.0 copy-start.3
  1.2 6.2 %encode.1 = (bf16[144,128]{1,0:T(8,128)(2,1)}, s32[4,64]{1,0:T(4,128)}) custom-call(s32[1]{0:T(128)} %bitcast.refs_0_, s32[4]{0:T(128)} %refs_1_.1, s32[768]{0:T(1024)} %refs_2_.1, s32[4,64]{1,0:T(4,128)} %refs_3_.1, bf16[4,32,768]{2,1,0:T(8,128)(2,1)} %refs_4_.1, bf16[768,3072]{1,0:T(8,128)(2,1)} %refs_5_.1, bf16[3072,768]{1,0:T(8,128)(2,1)} %refs_6_.1, ...), custom_call_target="tpu_custom_call" | custom-call | flops 1207959552 | bytes 9437184 | tf_op jit(solution)/shard_map/encode/pallas_call | solution.py:199
  7.4 0.0 collective-permute-done.len1_ref
  7.4 0.0 copy-done
  7.4 0.0 copy-start.1
  7.4 0.1 collective-permute-start.1
  7.6 2.7 %collective-permute-start.2 = (bf16[144,128]{1,0:T(8,128)(2,1)}, bf16[144,128]{1,0:T(8,128)(2,1)S(1)}, u32[]{:S(2)}, u32[]{:S(2)}) collective-permute-start(bf16[144,128]{1,0:T(8,128)(2,1)} %get-tuple-element.12.refs_3_), channel_id=1, source_target_pairs={{0,5},{1,4},{2,7},{3,6},{4,1},{5,0},{6,3},{7,2},{8,13},{9,12},{10,... | collective-permute-start | bytes 110600 | tf_op jit(solution)/shard_map/ppermute | solution.py:388
  10.3 2.6 %collective-permute-start.5 = (bf16[144,128]{1,0:T(8,128)(2,1)}, bf16[144,128]{1,0:T(8,128)(2,1)S(1)}, u32[]{:S(2)}, u32[]{:S(2)}) collective-permute-start(bf16[144,128]{1,0:T(8,128)(2,1)} %get-tuple-element.12.refs_3_), channel_id=1, source_target_pairs={{0,8},{1,9},{2,10},{3,11},{4,12},{5,13},{6,14},{7,15},{8,0},{9,1},... | collective-permute-start | bytes 110600 | tf_op jit(solution)/shard_map/ppermute | solution.py:388
  12.8 0.0 collective-permute-start.7
  12.8 0.0 collective-permute-done.2.refs_5_
  12.9 1.5 %collective-permute-start.3 = (bf16[144,128]{1,0:T(8,128)(2,1)S(1)}, bf16[144,128]{1,0:T(8,128)(2,1)S(1)}, u32[]{:S(2)}, u32[]{:S(2)}) collective-permute-start(bf16[144,128]{1,0:T(8,128)(2,1)S(1)} %collective-permute-done.2.refs_5_), channel_id=1, source_target_pairs={{0,3},{1,2},{2,1},{3,0},{4,7},{5,6},{6,5},{7,4},{8,11},{9,10},{10,... | collective-permute-start | bytes 110600 | tf_op jit(solution)/shard_map/ppermute | solution.py:388
  14.3 0.3 collective-permute-start.4
  14.6 1.5 %collective-permute-done.5.refs_7_ = bf16[144,128]{1,0:T(8,128)(2,1)S(1)} collective-permute-done((bf16[144,128]{1,0:T(8,128)(2,1)}, bf16[144,128]{1,0:T(8,128)(2,1)S(1)}, u32[]{:S(2)}, u32[]{:S(2)}) %collective-permute-start.5) | collective-permute-done | bytes 36896 | tf_op jit(solution)/shard_map/ppermute | solution.py:388
  16.1 0.0 collective-permute-start.6
  16.1 2.3 %collective-permute-done.7.refs_9_ = bf16[144,128]{1,0:T(8,128)(2,1)S(1)} collective-permute-done((bf16[144,128]{1,0:T(8,128)(2,1)}, bf16[144,128]{1,0:T(8,128)(2,1)S(1)}, u32[]{:S(2)}, u32[]{:S(2)}) %collective-permute-start.7) | collective-permute-done | bytes 36896 | tf_op jit(solution)/shard_map/ppermute | solution.py:388
  18.4 1.2 %collective-permute-start.8 = (bf16[144,128]{1,0:T(8,128)(2,1)S(1)}, bf16[144,128]{1,0:T(8,128)(2,1)S(1)}, u32[]{:S(2)}, u32[]{:S(2)}) collective-permute-start(bf16[144,128]{1,0:T(8,128)(2,1)S(1)} %collective-permute-done.7.refs_9_), channel_id=1, source_target_pairs={{0,3},{1,2},{2,1},{3,0},{4,7},{5,6},{6,5},{7,4},{8,11},{9,10},{10,... | collective-permute-start | bytes 110600 | tf_op jit(solution)/shard_map/ppermute | solution.py:388
  19.6 0.0 collective-permute-done.3._.refs_6_
  19.6 0.0 collective-permute-done.1.pass1_ref
  19.6 0.0 copy-done.3
  19.6 1.3 %mask.1 = (bf16[48,128,128]{2,1,0:T(8,128)(2,1)S(1)}, bf16[48,128,128]{2,1,0:T(8,128)(2,1)S(1)}) custom-call(s32[48]{0:T(128)S(1)} %copy-done.3, s32[48]{0:T(128)S(1)} %collective-permute-done.len1_ref, bf16[48,128,128]{2,1,0:T(8,128)(2,1)S(1)} %copy-done, bf16[48,128,128]{2,1,0:T(8,128)(2,1)S(1)} %collective-permute-done.1.pass1_ref, ...), custom_call_target="tpu_custom_call" | custom-call | flops 12582912 | bytes 6291456 | tf_op jit(solution)/shard_map/mask/pallas_call | solution.py:250
  20.9 0.0 collective-permute-done.4.refs_4_
  20.9 0.0 collective-permute-done.6.refs_8_
  21.0 0.9 %collective-permute-done.8.refs_10_ = bf16[144,128]{1,0:T(8,128)(2,1)S(1)} collective-permute-done((bf16[144,128]{1,0:T(8,128)(2,1)S(1)}, bf16[144,128]{1,0:T(8,128)(2,1)S(1)}, u32[]{:S(2)}, u32[]{:S(2)}) %collective-permute-start.8) | collective-permute-done | bytes 36896 | tf_op jit(solution)/shard_map/ppermute | solution.py:388
  21.9 0.0 copy-done.1
  21.9 0.0 copy-start.2
  21.9 2.6 %score.1 = f32[8,128]{1,0:T(8,128)S(1)} custom-call(s32[1]{0:T(128)} %bitcast.refs_0_, bf16[48,128,128]{2,1,0:T(8,128)(2,1)S(1)} %get-tuple-element.13.refs_1_, bf16[48,128,128]{2,1,0:T(8,128)(2,1)S(1)} %get-tuple-element.14.refs_2_, bf16[144,128]{1,0:T(8,128)(2,1)S(1)} %copy-done.1, bf16[144,128]{1,0:T(8,128)(2,1)S(1)} %collective-permute-done.4.refs_4_, ...), custom_call_target="tpu_custom_call" | custom-call | flops 805306368 | bytes 3145728 | tf_op jit(solution)/shard_map/score/pallas_call | solution.py:327
  24.5 10.1 %all_to_all.11 = f32[8,1,128]{2,1,0:T(1,128)S(1)} all-to-all(f32[8,1,128]{2,1,0:T(1,128)S(1)} %bitcast.5), channel_id=1, replica_groups={{0,3,5,6,8,11,13,14},{1,2,4,7,9,10,12,15},{16,19,21,22,24,27,29,30},{17..., dimensions={0} | all-to-all | bytes 8192 | tf_op jit(solution)/shard_map/all_to_all | solution.py:441
  34.6 0.0 copy-done.2
  34.6 1.0 %finish.1 = (f32[4,64]{1,0:T(4,128)}, f32[4,10]{1,0:T(4,128)}) custom-call(f32[8,128]{1,0:T(8,128)S(1)} %bitcast.6, s32[4,64]{1,0:T(4,128)S(1)} %copy-done.2), custom_call_target="tpu_custom_call" | custom-call | tf_op jit(solution)/shard_map/finish/pallas_call | solution.py:373
Async XLA Ops:
  0.6 6.8 %collective-permute-start = (s32[48]{0:T(128)}, s32[48]{0:T(128)S(1)}, u32[]{:S(2)}, u32[]{:S(2)}) collective-permute-start(s32[48]{0:T(128)} %len0_ref.1), channel_id=1, source_target_pairs={{0,1},{1,0},{2,3},{3,2},{4,5},{5,4},{6,7},{7,6},{8,9},{9,8},{10,11... | collective-permute-start | bytes 584 | tf_op jit(solution)/shard_map/ppermute | solution.py:388
  1.2 6.3 %copy-start = (bf16[48,128,128]{2,1,0:T(8,128)(2,1)S(1)}, bf16[48,128,128]{2,1,0:T(8,128)(2,1)}, u32[]{:S(2)}) copy-start(bf16[48,128,128]{2,1,0:T(8,128)(2,1)} %pass0_ref.1) | copy-start | bytes 4718596
  1.2 18.5 %copy-start.3 = (s32[48]{0:T(128)S(1)}, s32[48]{0:T(128)}, u32[]{:S(2)}) copy-start(s32[48]{0:T(128)} %len0_ref.1) | copy-start | bytes 580
  7.4 14.4 %copy-start.1 = (bf16[144,128]{1,0:T(8,128)(2,1)S(1)}, bf16[144,128]{1,0:T(8,128)(2,1)}, u32[]{:S(2)}) copy-start(bf16[144,128]{1,0:T(8,128)(2,1)} %get-tuple-element.12.refs_3_) | copy-start | bytes 110596
  7.4 12.2 %collective-permute-start.1 = (bf16[48,128,128]{2,1,0:T(8,128)(2,1)S(1)}, bf16[48,128,128]{2,1,0:T(8,128)(2,1)S(1)}, u32[]{:S(2)}, u32[]{:S(2)}) collective-permute-start(bf16[48,128,128]{2,1,0:T(8,128)(2,1)S(1)} %copy-done), channel_id=1, source_target_pairs={{0,1},{1,0},{2,3},{3,2},{4,5},{5,4},{6,7},{7,6},{8,9},{9,8},{10,11... | collective-permute-start | bytes 4718600 | tf_op jit(solution)/shard_map/ppermute | solution.py:388
  7.6 5.3 %collective-permute-start.2 = (bf16[144,128]{1,0:T(8,128)(2,1)}, bf16[144,128]{1,0:T(8,128)(2,1)S(1)}, u32[]{:S(2)}, u32[]{:S(2)}) collective-permute-start(bf16[144,128]{1,0:T(8,128)(2,1)} %get-tuple-element.12.refs_3_), channel_id=1, source_target_pairs={{0,5},{1,4},{2,7},{3,6},{4,1},{5,0},{6,3},{7,2},{8,13},{9,12},{10,... | collective-permute-start | bytes 110600 | tf_op jit(solution)/shard_map/ppermute | solution.py:388
  10.3 5.9 %collective-permute-start.5 = (bf16[144,128]{1,0:T(8,128)(2,1)}, bf16[144,128]{1,0:T(8,128)(2,1)S(1)}, u32[]{:S(2)}, u32[]{:S(2)}) collective-permute-start(bf16[144,128]{1,0:T(8,128)(2,1)} %get-tuple-element.12.refs_3_), channel_id=1, source_target_pairs={{0,8},{1,9},{2,10},{3,11},{4,12},{5,13},{6,14},{7,15},{8,0},{9,1},... | collective-permute-start | bytes 110600 | tf_op jit(solution)/shard_map/ppermute | solution.py:388
  12.8 5.5 %collective-permute-start.7 = (bf16[144,128]{1,0:T(8,128)(2,1)}, bf16[144,128]{1,0:T(8,128)(2,1)S(1)}, u32[]{:S(2)}, u32[]{:S(2)}) collective-permute-start(bf16[144,128]{1,0:T(8,128)(2,1)} %get-tuple-element.12.refs_3_), channel_id=1, source_target_pairs={{0,13},{1,12},{2,15},{3,14},{4,9},{5,8},{6,11},{7,10},{8,5},{9,4},... | collective-permute-start | bytes 110600 | tf_op jit(solution)/shard_map/ppermute | solution.py:388
  12.9 6.8 %collective-permute-start.3 = (bf16[144,128]{1,0:T(8,128)(2,1)S(1)}, bf16[144,128]{1,0:T(8,128)(2,1)S(1)}, u32[]{:S(2)}, u32[]{:S(2)}) collective-permute-start(bf16[144,128]{1,0:T(8,128)(2,1)S(1)} %collective-permute-done.2.refs_5_), channel_id=1, source_target_pairs={{0,3},{1,2},{2,1},{3,0},{4,7},{5,6},{6,5},{7,4},{8,11},{9,10},{10,... | collective-permute-start | bytes 110600 | tf_op jit(solution)/shard_map/ppermute | solution.py:388
  14.3 6.6 %collective-permute-start.4 = (bf16[144,128]{1,0:T(8,128)(2,1)}, bf16[144,128]{1,0:T(8,128)(2,1)S(1)}, u32[]{:S(2)}, u32[]{:S(2)}) collective-permute-start(bf16[144,128]{1,0:T(8,128)(2,1)} %get-tuple-element.12.refs_3_), channel_id=1, source_target_pairs={{0,3},{1,2},{2,1},{3,0},{4,7},{5,6},{6,5},{7,4},{8,11},{9,10},{10,... | collective-permute-start | bytes 110600 | tf_op jit(solution)/shard_map/ppermute | solution.py:388
  16.1 4.8 %collective-permute-start.6 = (bf16[144,128]{1,0:T(8,128)(2,1)S(1)}, bf16[144,128]{1,0:T(8,128)(2,1)S(1)}, u32[]{:S(2)}, u32[]{:S(2)}) collective-permute-start(bf16[144,128]{1,0:T(8,128)(2,1)S(1)} %collective-permute-done.5.refs_7_), channel_id=1, source_target_pairs={{0,3},{1,2},{2,1},{3,0},{4,7},{5,6},{6,5},{7,4},{8,11},{9,10},{10,... | collective-permute-start | bytes 110600 | tf_op jit(solution)/shard_map/ppermute | solution.py:388
  18.4 3.5 %collective-permute-start.8 = (bf16[144,128]{1,0:T(8,128)(2,1)S(1)}, bf16[144,128]{1,0:T(8,128)(2,1)S(1)}, u32[]{:S(2)}, u32[]{:S(2)}) collective-permute-start(bf16[144,128]{1,0:T(8,128)(2,1)S(1)} %collective-permute-done.7.refs_9_), channel_id=1, source_target_pairs={{0,3},{1,2},{2,1},{3,0},{4,7},{5,6},{6,5},{7,4},{8,11},{9,10},{10,... | collective-permute-start | bytes 110600 | tf_op jit(solution)/shard_map/ppermute | solution.py:388
  21.9 12.7 %copy-start.2 = (s32[4,64]{1,0:T(4,128)S(1)}, s32[4,64]{1,0:T(4,128)}, u32[]{:S(2)}) copy-start(s32[4,64]{1,0:T(4,128)} %get-tuple-element.15.spot_ref) | copy-start | bytes 3076

commit v23 on v22

--- a/solution.py
+++ b/solution.py
@@ -135,10 +135,9 @@
         if step == 1:
             small[2].wait()
             placed.wait()
-        if step == chunks + 1:
+        if step == chunks:
             for copy in small[3:]:
                 copy.wait()
-            fetch.wait()
         if step >= 2:
             copies[step - 2][1].wait()
         if step >= 1:
@@ -165,6 +164,7 @@
         vectors = jnp.where(padded, 0.0, vectors)
     vectors = vectors.astype(BF16)
     tokens = query_count * token_count
+    fetch.wait()
     wanted = table_v[...].astype(F32).astype(BF16)
     out_ref[pl.ds(0, tokens), :] = vectors
     out_ref[pl.ds(tokens, slots), :] = wanted

time: 35.7 us -> 35.2 us (0.986)
  Pallas kernels: 11.2 us -> 10.6 us
    pallas_call x1, Pallas kernels: 6.23 us -> 5.65 us  [encode(): pl.pallas_call(kernel, out_shape=(jax.ShapeDtypeStruct((tokens + slots, e...]
  transfers between devices with their start and end apart: 9 -> 9, of which waited for: 3 -> 3; matrix products, arithmetic and copies ran while one was open for 0% -> 0% of each run, Pallas kernels for 21% -> 20%
where the time goes in v23:
time: 35.2 us; the launch traced here: 35 us
  Pallas kernels  10.6 us (30%)
  blocking collectives  10.1 us (29%)
  starting transfers between devices  8.93 us (25%)
  waiting for transfers between devices  4.69 us (13%)
  between operations  0.71 us (2%)
    all_to_all x1, blocking collectives, per_device(): lax.all_to_all(sums, 'shard', split_axis=0, concat_axis=0, axis_index_gro...  10.1 us
    ppermute x9, starting transfers between devices, swap(): lax.ppermute(value, 'shard', [(i, i ^ distance) for i in range(size)])  8.93 us
    pallas_call x1, Pallas kernels, encode(): pl.pallas_call(kernel, out_shape=(jax.ShapeDtypeStruct((tokens + slots, e...  5.65 us
    ppermute x9, waiting for transfers between devices, swap(): lax.ppermute(value, 'shard', [(i, i ^ distance) for i in range(size)])  4.69 us
    pallas_call x1, Pallas kernels, score(): pl.pallas_call(kernel, out_shape=jax.ShapeDtypeStruct((slots, e), F32), i...  2.64 us
    pallas_call x1, Pallas kernels, mask(): pl.pallas_call(mask_kernel, out_shape=[jax.ShapeDtypeStruct(shape, BF16)]...  1.31 us
    pallas_call x1, Pallas kernels, finish(): pl.pallas_call(finish_kernel, out_shape=(jax.ShapeDtypeStruct(spots.shape...  0.99 us
  transfers between devices with their start and end apart: 9, of which 3 were waited for; matrix products, arithmetic and copies ran while one was open for 0% of the time, Pallas kernels for 20%

profile of v23, /device:TPU:0, one launch (start us, length us, event | category | flops | bytes accessed | tf_op | source)
XLA Modules:
  0.0 35.0 jit_solution(4443798427878391018)
XLA Ops:
  0.6 0.5 %collective-permute-start = (s32[48]{0:T(128)}, s32[48]{0:T(128)S(1)}, u32[]{:S(2)}, u32[]{:S(2)}) collective-permute-start(s32[48]{0:T(128)} %len0_ref.1), channel_id=1, source_target_pairs={{0,1},{1,0},{2,3},{3,2},{4,5},{5,4},{6,7},{7,6},{8,9},{9,8},{10,11... | collective-permute-start | bytes 584 | tf_op jit(solution)/shard_map/ppermute | solution.py:388
  1.2 0.0 copy-start
  1.2 0.0 copy-start.3
  1.2 5.6 %encode.1 = (bf16[144,128]{1,0:T(8,128)(2,1)}, s32[4,64]{1,0:T(4,128)}) custom-call(s32[1]{0:T(128)} %bitcast.refs_0_, s32[4]{0:T(128)} %refs_1_.1, s32[768]{0:T(1024)} %refs_2_.1, s32[4,64]{1,0:T(4,128)} %refs_3_.1, bf16[4,32,768]{2,1,0:T(8,128)(2,1)} %refs_4_.1, bf16[768,3072]{1,0:T(8,128)(2,1)} %refs_5_.1, bf16[3072,768]{1,0:T(8,128)(2,1)} %refs_6_.1, ...), custom_call_target="tpu_custom_call" | custom-call | flops 1207959552 | bytes 9437184 | tf_op jit(solution)/shard_map/encode/pallas_call | solution.py:199
  6.8 0.0 collective-permute-done.len1_ref
  6.8 0.0 copy-done
  6.8 0.0 copy-start.1
  6.8 0.1 collective-permute-start.1
  7.0 2.7 %collective-permute-start.2 = (bf16[144,128]{1,0:T(8,128)(2,1)}, bf16[144,128]{1,0:T(8,128)(2,1)S(1)}, u32[]{:S(2)}, u32[]{:S(2)}) collective-permute-start(bf16[144,128]{1,0:T(8,128)(2,1)} %get-tuple-element.12.refs_3_), channel_id=1, source_target_pairs={{0,5},{1,4},{2,7},{3,6},{4,1},{5,0},{6,3},{7,2},{8,13},{9,12},{10,... | collective-permute-start | bytes 110600 | tf_op jit(solution)/shard_map/ppermute | solution.py:388
  9.7 2.6 %collective-permute-start.5 = (bf16[144,128]{1,0:T(8,128)(2,1)}, bf16[144,128]{1,0:T(8,128)(2,1)S(1)}, u32[]{:S(2)}, u32[]{:S(2)}) collective-permute-start(bf16[144,128]{1,0:T(8,128)(2,1)} %get-tuple-element.12.refs_3_), channel_id=1, source_target_pairs={{0,8},{1,9},{2,10},{3,11},{4,12},{5,13},{6,14},{7,15},{8,0},{9,1},... | collective-permute-start | bytes 110600 | tf_op jit(solution)/shard_map/ppermute | solution.py:388
  12.3 0.0 collective-permute-start.7
  12.3 0.0 collective-permute-done.2.refs_5_
  12.3 1.5 %collective-permute-start.3 = (bf16[144,128]{1,0:T(8,128)(2,1)S(1)}, bf16[144,128]{1,0:T(8,128)(2,1)S(1)}, u32[]{:S(2)}, u32[]{:S(2)}) collective-permute-start(bf16[144,128]{1,0:T(8,128)(2,1)S(1)} %collective-permute-done.2.refs_5_), channel_id=1, source_target_pairs={{0,3},{1,2},{2,1},{3,0},{4,7},{5,6},{6,5},{7,4},{8,11},{9,10},{10,... | collective-permute-start | bytes 110600 | tf_op jit(solution)/shard_map/ppermute | solution.py:388
  13.7 0.3 collective-permute-start.4
  14.0 1.5 %collective-permute-done.5.refs_7_ = bf16[144,128]{1,0:T(8,128)(2,1)S(1)} collective-permute-done((bf16[144,128]{1,0:T(8,128)(2,1)}, bf16[144,128]{1,0:T(8,128)(2,1)S(1)}, u32[]{:S(2)}, u32[]{:S(2)}) %collective-permute-start.5) | collective-permute-done | bytes 36896 | tf_op jit(solution)/shard_map/ppermute | solution.py:388
  15.5 0.0 collective-permute-start.6
  15.5 2.3 %collective-permute-done.7.refs_9_ = bf16[144,128]{1,0:T(8,128)(2,1)S(1)} collective-permute-done((bf16[144,128]{1,0:T(8,128)(2,1)}, bf16[144,128]{1,0:T(8,128)(2,1)S(1)}, u32[]{:S(2)}, u32[]{:S(2)}) %collective-permute-start.7) | collective-permute-done | bytes 36896 | tf_op jit(solution)/shard_map/ppermute | solution.py:388
  17.8 1.2 %collective-permute-start.8 = (bf16[144,128]{1,0:T(8,128)(2,1)S(1)}, bf16[144,128]{1,0:T(8,128)(2,1)S(1)}, u32[]{:S(2)}, u32[]{:S(2)}) collective-permute-start(bf16[144,128]{1,0:T(8,128)(2,1)S(1)} %collective-permute-done.7.refs_9_), channel_id=1, source_target_pairs={{0,3},{1,2},{2,1},{3,0},{4,7},{5,6},{6,5},{7,4},{8,11},{9,10},{10,... | collective-permute-start | bytes 110600 | tf_op jit(solution)/shard_map/ppermute | solution.py:388
  19.0 0.0 collective-permute-done.3._.refs_6_
  19.0 0.0 collective-permute-done.1.pass1_ref
  19.0 0.0 copy-done.3
  19.0 1.3 %mask.1 = (bf16[48,128,128]{2,1,0:T(8,128)(2,1)S(1)}, bf16[48,128,128]{2,1,0:T(8,128)(2,1)S(1)}) custom-call(s32[48]{0:T(128)S(1)} %copy-done.3, s32[48]{0:T(128)S(1)} %collective-permute-done.len1_ref, bf16[48,128,128]{2,1,0:T(8,128)(2,1)S(1)} %copy-done, bf16[48,128,128]{2,1,0:T(8,128)(2,1)S(1)} %collective-permute-done.1.pass1_ref, ...), custom_call_target="tpu_custom_call" | custom-call | flops 12582912 | bytes 6291456 | tf_op jit(solution)/shard_map/mask/pallas_call | solution.py:250
  20.4 0.0 collective-permute-done.4.refs_4_
  20.4 0.0 collective-permute-done.6.refs_8_
  20.4 0.9 %collective-permute-done.8.refs_10_ = bf16[144,128]{1,0:T(8,128)(2,1)S(1)} collective-permute-done((bf16[144,128]{1,0:T(8,128)(2,1)S(1)}, bf16[144,128]{1,0:T(8,128)(2,1)S(1)}, u32[]{:S(2)}, u32[]{:S(2)}) %collective-permute-start.8) | collective-permute-done | bytes 36896 | tf_op jit(solution)/shard_map/ppermute | solution.py:388
  21.3 0.0 copy-done.1
  21.3 0.0 copy-start.2
  21.3 2.6 %score.1 = f32[8,128]{1,0:T(8,128)S(1)} custom-call(s32[1]{0:T(128)} %bitcast.refs_0_, bf16[48,128,128]{2,1,0:T(8,128)(2,1)S(1)} %get-tuple-element.13.refs_1_, bf16[48,128,128]{2,1,0:T(8,128)(2,1)S(1)} %get-tuple-element.14.refs_2_, bf16[144,128]{1,0:T(8,128)(2,1)S(1)} %copy-done.1, bf16[144,128]{1,0:T(8,128)(2,1)S(1)} %collective-permute-done.4.refs_4_, ...), custom_call_target="tpu_custom_call" | custom-call | flops 805306368 | bytes 3145728 | tf_op jit(solution)/shard_map/score/pallas_call | solution.py:327
  23.9 10.1 %all_to_all.11 = f32[8,1,128]{2,1,0:T(1,128)S(1)} all-to-all(f32[8,1,128]{2,1,0:T(1,128)S(1)} %bitcast.5), channel_id=1, replica_groups={{0,3,5,6,8,11,13,14},{1,2,4,7,9,10,12,15},{16,19,21,22,24,27,29,30},{17..., dimensions={0} | all-to-all | bytes 8192 | tf_op jit(solution)/shard_map/all_to_all | solution.py:441
  34.0 0.0 copy-done.2
  34.0 1.0 %finish.1 = (f32[4,64]{1,0:T(4,128)}, f32[4,10]{1,0:T(4,128)}) custom-call(f32[8,128]{1,0:T(8,128)S(1)} %bitcast.6, s32[4,64]{1,0:T(4,128)S(1)} %copy-done.2), custom_call_target="tpu_custom_call" | custom-call | tf_op jit(solution)/shard_map/finish/pallas_call | solution.py:373
Async XLA Ops:
  0.6 6.2 %collective-permute-start = (s32[48]{0:T(128)}, s32[48]{0:T(128)S(1)}, u32[]{:S(2)}, u32[]{:S(2)}) collective-permute-start(s32[48]{0:T(128)} %len0_ref.1), channel_id=1, source_target_pairs={{0,1},{1,0},{2,3},{3,2},{4,5},{5,4},{6,7},{7,6},{8,9},{9,8},{10,11... | collective-permute-start | bytes 584 | tf_op jit(solution)/shard_map/ppermute | solution.py:388
  1.2 5.7 %copy-start = (bf16[48,128,128]{2,1,0:T(8,128)(2,1)S(1)}, bf16[48,128,128]{2,1,0:T(8,128)(2,1)}, u32[]{:S(2)}) copy-start(bf16[48,128,128]{2,1,0:T(8,128)(2,1)} %pass0_ref.1) | copy-start | bytes 4718596
  1.2 17.9 %copy-start.3 = (s32[48]{0:T(128)S(1)}, s32[48]{0:T(128)}, u32[]{:S(2)}) copy-start(s32[48]{0:T(128)} %len0_ref.1) | copy-start | bytes 580
  6.8 14.4 %copy-start.1 = (bf16[144,128]{1,0:T(8,128)(2,1)S(1)}, bf16[144,128]{1,0:T(8,128)(2,1)}, u32[]{:S(2)}) copy-start(bf16[144,128]{1,0:T(8,128)(2,1)} %get-tuple-element.12.refs_3_) | copy-start | bytes 110596
  6.8 12.2 %collective-permute-start.1 = (bf16[48,128,128]{2,1,0:T(8,128)(2,1)S(1)}, bf16[48,128,128]{2,1,0:T(8,128)(2,1)S(1)}, u32[]{:S(2)}, u32[]{:S(2)}) collective-permute-start(bf16[48,128,128]{2,1,0:T(8,128)(2,1)S(1)} %copy-done), channel_id=1, source_target_pairs={{0,1},{1,0},{2,3},{3,2},{4,5},{5,4},{6,7},{7,6},{8,9},{9,8},{10,11... | collective-permute-start | bytes 4718600 | tf_op jit(solution)/shard_map/ppermute | solution.py:388
  7.0 5.3 %collective-permute-start.2 = (bf16[144,128]{1,0:T(8,128)(2,1)}, bf16[144,128]{1,0:T(8,128)(2,1)S(1)}, u32[]{:S(2)}, u32[]{:S(2)}) collective-permute-start(bf16[144,128]{1,0:T(8,128)(2,1)} %get-tuple-element.12.refs_3_), channel_id=1, source_target_pairs={{0,5},{1,4},{2,7},{3,6},{4,1},{5,0},{6,3},{7,2},{8,13},{9,12},{10,... | collective-permute-start | bytes 110600 | tf_op jit(solution)/shard_map/ppermute | solution.py:388
  9.7 5.9 %collective-permute-start.5 = (bf16[144,128]{1,0:T(8,128)(2,1)}, bf16[144,128]{1,0:T(8,128)(2,1)S(1)}, u32[]{:S(2)}, u32[]{:S(2)}) collective-permute-start(bf16[144,128]{1,0:T(8,128)(2,1)} %get-tuple-element.12.refs_3_), channel_id=1, source_target_pairs={{0,8},{1,9},{2,10},{3,11},{4,12},{5,13},{6,14},{7,15},{8,0},{9,1},... | collective-permute-start | bytes 110600 | tf_op jit(solution)/shard_map/ppermute | solution.py:388
  12.3 5.5 %collective-permute-start.7 = (bf16[144,128]{1,0:T(8,128)(2,1)}, bf16[144,128]{1,0:T(8,128)(2,1)S(1)}, u32[]{:S(2)}, u32[]{:S(2)}) collective-permute-start(bf16[144,128]{1,0:T(8,128)(2,1)} %get-tuple-element.12.refs_3_), channel_id=1, source_target_pairs={{0,13},{1,12},{2,15},{3,14},{4,9},{5,8},{6,11},{7,10},{8,5},{9,4},... | collective-permute-start | bytes 110600 | tf_op jit(solution)/shard_map/ppermute | solution.py:388
  12.3 6.8 %collective-permute-start.3 = (bf16[144,128]{1,0:T(8,128)(2,1)S(1)}, bf16[144,128]{1,0:T(8,128)(2,1)S(1)}, u32[]{:S(2)}, u32[]{:S(2)}) collective-permute-start(bf16[144,128]{1,0:T(8,128)(2,1)S(1)} %collective-permute-done.2.refs_5_), channel_id=1, source_target_pairs={{0,3},{1,2},{2,1},{3,0},{4,7},{5,6},{6,5},{7,4},{8,11},{9,10},{10,... | collective-permute-start | bytes 110600 | tf_op jit(solution)/shard_map/ppermute | solution.py:388
  13.7 6.6 %collective-permute-start.4 = (bf16[144,128]{1,0:T(8,128)(2,1)}, bf16[144,128]{1,0:T(8,128)(2,1)S(1)}, u32[]{:S(2)}, u32[]{:S(2)}) collective-permute-start(bf16[144,128]{1,0:T(8,128)(2,1)} %get-tuple-element.12.refs_3_), channel_id=1, source_target_pairs={{0,3},{1,2},{2,1},{3,0},{4,7},{5,6},{6,5},{7,4},{8,11},{9,10},{10,... | collective-permute-start | bytes 110600 | tf_op jit(solution)/shard_map/ppermute | solution.py:388
  15.5 4.8 %collective-permute-start.6 = (bf16[144,128]{1,0:T(8,128)(2,1)S(1)}, bf16[144,128]{1,0:T(8,128)(2,1)S(1)}, u32[]{:S(2)}, u32[]{:S(2)}) collective-permute-start(bf16[144,128]{1,0:T(8,128)(2,1)S(1)} %collective-permute-done.5.refs_7_), channel_id=1, source_target_pairs={{0,3},{1,2},{2,1},{3,0},{4,7},{5,6},{6,5},{7,4},{8,11},{9,10},{10,... | collective-permute-start | bytes 110600 | tf_op jit(solution)/shard_map/ppermute | solution.py:388
  17.8 3.5 %collective-permute-start.8 = (bf16[144,128]{1,0:T(8,128)(2,1)S(1)}, bf16[144,128]{1,0:T(8,128)(2,1)S(1)}, u32[]{:S(2)}, u32[]{:S(2)}) collective-permute-start(bf16[144,128]{1,0:T(8,128)(2,1)S(1)} %collective-permute-done.7.refs_9_), channel_id=1, source_target_pairs={{0,3},{1,2},{2,1},{3,0},{4,7},{5,6},{6,5},{7,4},{8,11},{9,10},{10,... | collective-permute-start | bytes 110600 | tf_op jit(solution)/shard_map/ppermute | solution.py:388
  21.3 12.7 %copy-start.2 = (s32[4,64]{1,0:T(4,128)S(1)}, s32[4,64]{1,0:T(4,128)}, u32[]{:S(2)}) copy-start(s32[4,64]{1,0:T(4,128)} %get-tuple-element.15.spot_ref) | copy-start | bytes 3076

commit v24 on v23

--- a/solution.py
+++ b/solution.py
@@ -348,18 +348,21 @@
 def finish_kernel(got_ref, spot_ref, scores_ref, best_ref):
     slots, lanes = got_ref.shape
     query_count, cand_count = scores_ref.shape
-    parts = split3(got_ref[...])
-    slot_iota = lax.broadcasted_iota(jnp.int32, (slots, cand_count), 0) * lanes
-    lane_iota = lax.broadcasted_iota(jnp.int32, (lanes, cand_count), 0)
+    parts = jnp.concatenate([part.astype(F32) for part in split3(got_ref[...])], axis=0).astype(BF16)
+    spots = jnp.concatenate([spot_ref[i:i + 1, :] for i in range(query_count)], axis=1)
+    entry_count = query_count * cand_count
+    lane = jnp.bitwise_and(spots, lanes - 1)
+    lane_iota = lax.broadcasted_iota(jnp.int32, (lanes, entry_count), 0)
+    slot_iota = lax.broadcasted_iota(jnp.int32, (slots, entry_count), 0) * lanes
+    onehot = jnp.where(lane_iota == lane, 1.0, 0.0).astype(BF16)
+    picked = jnp.dot(parts, onehot, preferred_element_type=F32)
+    picked = picked[:slots] + picked[slots:2 * slots] + picked[2 * slots:]
+    picked = jnp.sum(jnp.where(slot_iota == spots - lane, picked, 0.0), axis=0, keepdims=True)
     row_iota = lax.broadcasted_iota(jnp.int32, (cand_count, cand_count), 0)
     col_iota = lax.broadcasted_iota(jnp.int32, (cand_count, cand_count), 1)
     place = lax.broadcasted_iota(jnp.int32, (cand_count, 128), 1)
     for i in range(query_count):
-        spot = spot_ref[i:i + 1, :]
-        lane = jnp.bitwise_and(spot, lanes - 1)
-        onehot = jnp.where(lane_iota == lane, 1.0, 0.0).astype(BF16)
-        picked = sum(jnp.dot(part, onehot, preferred_element_type=F32) for part in parts)
-        score_row = jnp.sum(jnp.where(slot_iota == spot - lane, picked, 0.0), axis=0, keepdims=True)
+        score_row = picked[:, i * cand_count:(i + 1) * cand_count]
         scores_ref[i:i + 1, :] = score_row
         across = jnp.broadcast_to(score_row, (cand_count, cand_count))
         score_col = jnp.sum(jnp.where(row_iota == col_iota, across, 0.0), axis=1, keepdims=True)

time: 35.2 us -> 35.3 us (level)
  no operation moved by 1% of the time
where the time goes in v24:
time: 35.3 us; the launch traced here: 35.1 us
  Pallas kernels  10.7 us (30%)
  blocking collectives  10.1 us (29%)
  starting transfers between devices  8.93 us (25%)
  waiting for transfers between devices  4.69 us (13%)
  between operations  0.71 us (2%)
    all_to_all x1, blocking collectives, per_device(): lax.all_to_all(sums, 'shard', split_axis=0, concat_axis=0, axis_index_gro...  10.1 us
    ppermute x9, starting transfers between devices, swap(): lax.ppermute(value, 'shard', [(i, i ^ distance) for i in range(size)])  8.93 us
    pallas_call x1, Pallas kernels, encode(): pl.pallas_call(kernel, out_shape=(jax.ShapeDtypeStruct((tokens + slots, e...  5.65 us
    ppermute x9, waiting for transfers between devices, swap(): lax.ppermute(value, 'shard', [(i, i ^ distance) for i in range(size)])  4.69 us
    pallas_call x1, Pallas kernels, score(): pl.pallas_call(kernel, out_shape=jax.ShapeDtypeStruct((slots, e), F32), i...  2.64 us
    pallas_call x1, Pallas kernels, mask(): pl.pallas_call(mask_kernel, out_shape=[jax.ShapeDtypeStruct(shape, BF16)]...  1.31 us
    pallas_call x1, Pallas kernels, finish(): pl.pallas_call(finish_kernel, out_shape=(jax.ShapeDtypeStruct(spots.shape...  1.13 us
  transfers between devices with their start and end apart: 9, of which 3 were waited for; matrix products, arithmetic and copies ran while one was open for 0% of the time, Pallas kernels for 20%

profile of v24, /device:TPU:0, one launch (start us, length us, event | category | flops | bytes accessed | tf_op | source)
XLA Modules:
  0.0 35.1 jit_solution(1557289700375122025)
XLA Ops:
  0.6 0.5 %collective-permute-start = (s32[48]{0:T(128)}, s32[48]{0:T(128)S(1)}, u32[]{:S(2)}, u32[]{:S(2)}) collective-permute-start(s32[48]{0:T(128)} %len0_ref.1), channel_id=1, source_target_pairs={{0,1},{1,0},{2,3},{3,2},{4,5},{5,4},{6,7},{7,6},{8,9},{9,8},{10,11... | collective-permute-start | bytes 584 | tf_op jit(solution)/shard_map/ppermute | solution.py:391
  1.2 0.0 copy-start
  1.2 0.0 copy-start.3
  1.2 5.6 %encode.1 = (bf16[144,128]{1,0:T(8,128)(2,1)}, s32[4,64]{1,0:T(4,128)}) custom-call(s32[1]{0:T(128)} %bitcast.refs_0_, s32[4]{0:T(128)} %refs_1_.1, s32[768]{0:T(1024)} %refs_2_.1, s32[4,64]{1,0:T(4,128)} %refs_3_.1, bf16[4,32,768]{2,1,0:T(8,128)(2,1)} %refs_4_.1, bf16[768,3072]{1,0:T(8,128)(2,1)} %refs_5_.1, bf16[3072,768]{1,0:T(8,128)(2,1)} %refs_6_.1, ...), custom_call_target="tpu_custom_call" | custom-call | flops 1207959552 | bytes 9437184 | tf_op jit(solution)/shard_map/encode/pallas_call | solution.py:199
  6.8 0.0 collective-permute-done.len1_ref
  6.8 0.0 copy-done
  6.8 0.0 copy-start.1
  6.8 0.1 collective-permute-start.1
  7.0 2.7 %collective-permute-start.2 = (bf16[144,128]{1,0:T(8,128)(2,1)}, bf16[144,128]{1,0:T(8,128)(2,1)S(1)}, u32[]{:S(2)}, u32[]{:S(2)}) collective-permute-start(bf16[144,128]{1,0:T(8,128)(2,1)} %get-tuple-element.12.refs_3_), channel_id=1, source_target_pairs={{0,5},{1,4},{2,7},{3,6},{4,1},{5,0},{6,3},{7,2},{8,13},{9,12},{10,... | collective-permute-start | bytes 110600 | tf_op jit(solution)/shard_map/ppermute | solution.py:391
  9.7 2.6 %collective-permute-start.5 = (bf16[144,128]{1,0:T(8,128)(2,1)}, bf16[144,128]{1,0:T(8,128)(2,1)S(1)}, u32[]{:S(2)}, u32[]{:S(2)}) collective-permute-start(bf16[144,128]{1,0:T(8,128)(2,1)} %get-tuple-element.12.refs_3_), channel_id=1, source_target_pairs={{0,8},{1,9},{2,10},{3,11},{4,12},{5,13},{6,14},{7,15},{8,0},{9,1},... | collective-permute-start | bytes 110600 | tf_op jit(solution)/shard_map/ppermute | solution.py:391
  12.3 0.0 collective-permute-start.7
  12.3 0.0 collective-permute-done.2.refs_5_
  12.3 1.5 %collective-permute-start.3 = (bf16[144,128]{1,0:T(8,128)(2,1)S(1)}, bf16[144,128]{1,0:T(8,128)(2,1)S(1)}, u32[]{:S(2)}, u32[]{:S(2)}) collective-permute-start(bf16[144,128]{1,0:T(8,128)(2,1)S(1)} %collective-permute-done.2.refs_5_), channel_id=1, source_target_pairs={{0,3},{1,2},{2,1},{3,0},{4,7},{5,6},{6,5},{7,4},{8,11},{9,10},{10,... | collective-permute-start | bytes 110600 | tf_op jit(solution)/shard_map/ppermute | solution.py:391
  13.7 0.3 collective-permute-start.4
  14.0 1.5 %collective-permute-done.5.refs_7_ = bf16[144,128]{1,0:T(8,128)(2,1)S(1)} collective-permute-done((bf16[144,128]{1,0:T(8,128)(2,1)}, bf16[144,128]{1,0:T(8,128)(2,1)S(1)}, u32[]{:S(2)}, u32[]{:S(2)}) %collective-permute-start.5) | collective-permute-done | bytes 36896 | tf_op jit(solution)/shard_map/ppermute | solution.py:391
  15.5 0.0 collective-permute-start.6
  15.5 2.3 %collective-permute-done.7.refs_9_ = bf16[144,128]{1,0:T(8,128)(2,1)S(1)} collective-permute-done((bf16[144,128]{1,0:T(8,128)(2,1)}, bf16[144,128]{1,0:T(8,128)(2,1)S(1)}, u32[]{:S(2)}, u32[]{:S(2)}) %collective-permute-start.7) | collective-permute-done | bytes 36896 | tf_op jit(solution)/shard_map/ppermute | solution.py:391
  17.8 1.2 %collective-permute-start.8 = (bf16[144,128]{1,0:T(8,128)(2,1)S(1)}, bf16[144,128]{1,0:T(8,128)(2,1)S(1)}, u32[]{:S(2)}, u32[]{:S(2)}) collective-permute-start(bf16[144,128]{1,0:T(8,128)(2,1)S(1)} %collective-permute-done.7.refs_9_), channel_id=1, source_target_pairs={{0,3},{1,2},{2,1},{3,0},{4,7},{5,6},{6,5},{7,4},{8,11},{9,10},{10,... | collective-permute-start | bytes 110600 | tf_op jit(solution)/shard_map/ppermute | solution.py:391
  19.0 0.0 collective-permute-done.3._.refs_6_
  19.0 0.0 collective-permute-done.1.pass1_ref
  19.0 0.0 copy-done.3
  19.0 1.3 %mask.1 = (bf16[48,128,128]{2,1,0:T(8,128)(2,1)S(1)}, bf16[48,128,128]{2,1,0:T(8,128)(2,1)S(1)}) custom-call(s32[48]{0:T(128)S(1)} %copy-done.3, s32[48]{0:T(128)S(1)} %collective-permute-done.len1_ref, bf16[48,128,128]{2,1,0:T(8,128)(2,1)S(1)} %copy-done, bf16[48,128,128]{2,1,0:T(8,128)(2,1)S(1)} %collective-permute-done.1.pass1_ref, ...), custom_call_target="tpu_custom_call" | custom-call | flops 12582912 | bytes 6291456 | tf_op jit(solution)/shard_map/mask/pallas_call | solution.py:250
  20.4 0.0 collective-permute-done.4.refs_4_
  20.4 0.0 collective-permute-done.6.refs_8_
  20.4 0.9 %collective-permute-done.8.refs_10_ = bf16[144,128]{1,0:T(8,128)(2,1)S(1)} collective-permute-done((bf16[144,128]{1,0:T(8,128)(2,1)S(1)}, bf16[144,128]{1,0:T(8,128)(2,1)S(1)}, u32[]{:S(2)}, u32[]{:S(2)}) %collective-permute-start.8) | collective-permute-done | bytes 36896 | tf_op jit(solution)/shard_map/ppermute | solution.py:391
  21.3 0.0 copy-done.1
  21.3 0.0 copy-start.2
  21.3 2.6 %score.1 = f32[8,128]{1,0:T(8,128)S(1)} custom-call(s32[1]{0:T(128)} %bitcast.refs_0_, bf16[48,128,128]{2,1,0:T(8,128)(2,1)S(1)} %get-tuple-element.13.refs_1_, bf16[48,128,128]{2,1,0:T(8,128)(2,1)S(1)} %get-tuple-element.14.refs_2_, bf16[144,128]{1,0:T(8,128)(2,1)S(1)} %copy-done.1, bf16[144,128]{1,0:T(8,128)(2,1)S(1)} %collective-permute-done.4.refs_4_, ...), custom_call_target="tpu_custom_call" | custom-call | flops 805306368 | bytes 3145728 | tf_op jit(solution)/shard_map/score/pallas_call | solution.py:327
  23.9 10.1 %all_to_all.11 = f32[8,1,128]{2,1,0:T(1,128)S(1)} all-to-all(f32[8,1,128]{2,1,0:T(1,128)S(1)} %bitcast.5), channel_id=1, replica_groups={{0,3,5,6,8,11,13,14},{1,2,4,7,9,10,12,15},{16,19,21,22,24,27,29,30},{17..., dimensions={0} | all-to-all | bytes 8192 | tf_op jit(solution)/shard_map/all_to_all | solution.py:444
  34.0 0.0 copy-done.2
  34.0 1.1 %finish.1 = (f32[4,64]{1,0:T(4,128)}, f32[4,10]{1,0:T(4,128)}) custom-call(f32[8,128]{1,0:T(8,128)S(1)} %bitcast.6, s32[4,64]{1,0:T(4,128)S(1)} %copy-done.2), custom_call_target="tpu_custom_call" | custom-call | tf_op jit(solution)/shard_map/finish/pallas_call | solution.py:376
Async XLA Ops:
  0.6 6.2 %collective-permute-start = (s32[48]{0:T(128)}, s32[48]{0:T(128)S(1)}, u32[]{:S(2)}, u32[]{:S(2)}) collective-permute-start(s32[48]{0:T(128)} %len0_ref.1), channel_id=1, source_target_pairs={{0,1},{1,0},{2,3},{3,2},{4,5},{5,4},{6,7},{7,6},{8,9},{9,8},{10,11... | collective-permute-start | bytes 584 | tf_op jit(solution)/shard_map/ppermute | solution.py:391
  1.2 5.7 %copy-start = (bf16[48,128,128]{2,1,0:T(8,128)(2,1)S(1)}, bf16[48,128,128]{2,1,0:T(8,128)(2,1)}, u32[]{:S(2)}) copy-start(bf16[48,128,128]{2,1,0:T(8,128)(2,1)} %pass0_ref.1) | copy-start | bytes 4718596
  1.2 17.9 %copy-start.3 = (s32[48]{0:T(128)S(1)}, s32[48]{0:T(128)}, u32[]{:S(2)}) copy-start(s32[48]{0:T(128)} %len0_ref.1) | copy-start | bytes 580
  6.8 14.4 %copy-start.1 = (bf16[144,128]{1,0:T(8,128)(2,1)S(1)}, bf16[144,128]{1,0:T(8,128)(2,1)}, u32[]{:S(2)}) copy-start(bf16[144,128]{1,0:T(8,128)(2,1)} %get-tuple-element.12.refs_3_) | copy-start | bytes 110596
  6.8 12.2 %collective-permute-start.1 = (bf16[48,128,128]{2,1,0:T(8,128)(2,1)S(1)}, bf16[48,128,128]{2,1,0:T(8,128)(2,1)S(1)}, u32[]{:S(2)}, u32[]{:S(2)}) collective-permute-start(bf16[48,128,128]{2,1,0:T(8,128)(2,1)S(1)} %copy-done), channel_id=1, source_target_pairs={{0,1},{1,0},{2,3},{3,2},{4,5},{5,4},{6,7},{7,6},{8,9},{9,8},{10,11... | collective-permute-start | bytes 4718600 | tf_op jit(solution)/shard_map/ppermute | solution.py:391
  7.0 5.3 %collective-permute-start.2 = (bf16[144,128]{1,0:T(8,128)(2,1)}, bf16[144,128]{1,0:T(8,128)(2,1)S(1)}, u32[]{:S(2)}, u32[]{:S(2)}) collective-permute-start(bf16[144,128]{1,0:T(8,128)(2,1)} %get-tuple-element.12.refs_3_), channel_id=1, source_target_pairs={{0,5},{1,4},{2,7},{3,6},{4,1},{5,0},{6,3},{7,2},{8,13},{9,12},{10,... | collective-permute-start | bytes 110600 | tf_op jit(solution)/shard_map/ppermute | solution.py:391
  9.7 5.9 %collective-permute-start.5 = (bf16[144,128]{1,0:T(8,128)(2,1)}, bf16[144,128]{1,0:T(8,128)(2,1)S(1)}, u32[]{:S(2)}, u32[]{:S(2)}) collective-permute-start(bf16[144,128]{1,0:T(8,128)(2,1)} %get-tuple-element.12.refs_3_), channel_id=1, source_target_pairs={{0,8},{1,9},{2,10},{3,11},{4,12},{5,13},{6,14},{7,15},{8,0},{9,1},... | collective-permute-start | bytes 110600 | tf_op jit(solution)/shard_map/ppermute | solution.py:391
  12.3 5.5 %collective-permute-start.7 = (bf16[144,128]{1,0:T(8,128)(2,1)}, bf16[144,128]{1,0:T(8,128)(2,1)S(1)}, u32[]{:S(2)}, u32[]{:S(2)}) collective-permute-start(bf16[144,128]{1,0:T(8,128)(2,1)} %get-tuple-element.12.refs_3_), channel_id=1, source_target_pairs={{0,13},{1,12},{2,15},{3,14},{4,9},{5,8},{6,11},{7,10},{8,5},{9,4},... | collective-permute-start | bytes 110600 | tf_op jit(solution)/shard_map/ppermute | solution.py:391
  12.3 6.8 %collective-permute-start.3 = (bf16[144,128]{1,0:T(8,128)(2,1)S(1)}, bf16[144,128]{1,0:T(8,128)(2,1)S(1)}, u32[]{:S(2)}, u32[]{:S(2)}) collective-permute-start(bf16[144,128]{1,0:T(8,128)(2,1)S(1)} %collective-permute-done.2.refs_5_), channel_id=1, source_target_pairs={{0,3},{1,2},{2,1},{3,0},{4,7},{5,6},{6,5},{7,4},{8,11},{9,10},{10,... | collective-permute-start | bytes 110600 | tf_op jit(solution)/shard_map/ppermute | solution.py:391
  13.7 6.6 %collective-permute-start.4 = (bf16[144,128]{1,0:T(8,128)(2,1)}, bf16[144,128]{1,0:T(8,128)(2,1)S(1)}, u32[]{:S(2)}, u32[]{:S(2)}) collective-permute-start(bf16[144,128]{1,0:T(8,128)(2,1)} %get-tuple-element.12.refs_3_), channel_id=1, source_target_pairs={{0,3},{1,2},{2,1},{3,0},{4,7},{5,6},{6,5},{7,4},{8,11},{9,10},{10,... | collective-permute-start | bytes 110600 | tf_op jit(solution)/shard_map/ppermute | solution.py:391
  15.5 4.8 %collective-permute-start.6 = (bf16[144,128]{1,0:T(8,128)(2,1)S(1)}, bf16[144,128]{1,0:T(8,128)(2,1)S(1)}, u32[]{:S(2)}, u32[]{:S(2)}) collective-permute-start(bf16[144,128]{1,0:T(8,128)(2,1)S(1)} %collective-permute-done.5.refs_7_), channel_id=1, source_target_pairs={{0,3},{1,2},{2,1},{3,0},{4,7},{5,6},{6,5},{7,4},{8,11},{9,10},{10,... | collective-permute-start | bytes 110600 | tf_op jit(solution)/shard_map/ppermute | solution.py:391
  17.8 3.5 %collective-permute-start.8 = (bf16[144,128]{1,0:T(8,128)(2,1)S(1)}, bf16[144,128]{1,0:T(8,128)(2,1)S(1)}, u32[]{:S(2)}, u32[]{:S(2)}) collective-permute-start(bf16[144,128]{1,0:T(8,128)(2,1)S(1)} %collective-permute-done.7.refs_9_), channel_id=1, source_target_pairs={{0,3},{1,2},{2,1},{3,0},{4,7},{5,6},{6,5},{7,4},{8,11},{9,10},{10,... | collective-permute-start | bytes 110600 | tf_op jit(solution)/shard_map/ppermute | solution.py:391
  21.3 12.7 %copy-start.2 = (s32[4,64]{1,0:T(4,128)S(1)}, s32[4,64]{1,0:T(4,128)}, u32[]{:S(2)}) copy-start(s32[4,64]{1,0:T(4,128)} %get-tuple-element.15.spot_ref) | copy-start | bytes 3076

commit v25 on v23

--- a/solution.py
+++ b/solution.py
@@ -258,7 +258,7 @@
     )(*lengths, *passages, late)
 
 
-def score_kernel(slots, token_count, me_ref, own_ref, other_ref, *refs):
+def score_kernel(slots, middle, token_count, me_ref, own_ref, other_ref, *refs):
     got_refs = refs[:slots]
     out_ref, best_ref, index_v, index, sem = refs[slots:]
     message, lanes = got_refs[0].shape
@@ -313,16 +313,16 @@
     total = sum(lax.dot_general(ones, part, NT, preferred_element_type=F32) for part in split3(best_ref[...]))
     out_ref[...] = jnp.zeros(out_ref.shape, F32)
     for s in range(slots):
-        out_ref[pl.ds(jnp.bitwise_xor(chip, s), 1), pl.ds(0, 2 * half)] = total[s:s + 1]
-
-
-def score(me, got, own, other, token_count):
+        out_ref[pl.ds(jnp.bitwise_xor(chip, s ^ middle), 1), pl.ds(0, 2 * half)] = total[s:s + 1]
+
+
+def score(me, got, own, other, middle, token_count):
     half, plen, e = own.shape
     passage_count = 2 * half
     slots = len(got)
 
     def kernel(*refs):
-        score_kernel(slots, token_count, *refs)
+        score_kernel(slots, middle, token_count, *refs)
 
     return pl.pallas_call(
         kernel,
@@ -345,7 +345,7 @@
     )(me, own, other, *got)
 
 
-def finish_kernel(got_ref, spot_ref, scores_ref, best_ref):
+def finish_kernel(middle, got_ref, spot_ref, scores_ref, best_ref):
     slots, lanes = got_ref.shape
     query_count, cand_count = scores_ref.shape
     parts = split3(got_ref[...])
@@ -355,7 +355,7 @@
     col_iota = lax.broadcasted_iota(jnp.int32, (cand_count, cand_count), 1)
     place = lax.broadcasted_iota(jnp.int32, (cand_count, 128), 1)
     for i in range(query_count):
-        spot = spot_ref[i:i + 1, :]
+        spot = jnp.bitwise_xor(spot_ref[i:i + 1, :], middle * lanes)
         lane = jnp.bitwise_and(spot, lanes - 1)
         onehot = jnp.where(lane_iota == lane, 1.0, 0.0).astype(BF16)
         picked = sum(jnp.dot(part, onehot, preferred_element_type=F32) for part in parts)
@@ -369,9 +369,12 @@
         best_ref[i:i + 1, :] = ordered[:, :TOPN]
 
 
-def finish(got, spots):
+def finish(got, spots, middle):
+    def kernel(*refs):
+        finish_kernel(middle, *refs)
+
     return pl.pallas_call(
-        finish_kernel,
+        kernel,
         out_shape=(
             jax.ShapeDtypeStruct(spots.shape, F32),
             jax.ShapeDtypeStruct((spots.shape[0], TOPN), F32),
@@ -410,7 +413,8 @@
     def color(index):
         return (index ^ (index >> 1) ^ (index >> shift)) & 1
 
-    groups = [[i for i in range(size) if color(i) == c] for c in range(2)]
+    middle = inner * (slots // inner // 2 - 1)
+    groups = [[2 * (p ^ middle) + (c ^ color(2 * (p ^ middle))) for p in range(slots)] for c in range(2)]
 
     def send(value, distance):
         return swap(value, 2 * distance + color(2 * distance))
@@ -437,9 +441,9 @@
     line = [message] + [send(message, d) for d in range(slots - inner, 0, -inner)][::-1]
     got = [line[s // inner] if s % inner == 0 else send(line[s // inner], s % inner) for s in range(slots)]
     own, other = mask((passage_lengths, across), (passage_vectors, raw), got[inner + 1])
-    sums = score(me, got, own, other, query_hidden.shape[1])
+    sums = score(me, got, own, other, middle, query_hidden.shape[1])
     back = lax.all_to_all(sums, "shard", split_axis=0, concat_axis=0, axis_index_groups=groups, tiled=True)
-    return finish(back, spots)
+    return finish(back, spots, middle)
 
 
 def solution(mesh):

time: 35.2 us -> 34 us (0.966)
  blocking collectives: 10.1 us -> 8.87 us
    all_to_all x1, blocking collectives: 10.1 us -> 8.87 us  [per_device(): lax.all_to_all(sums, 'shard', split_axis=0, concat_axis=0, axis_index_gro...]
  transfers between devices with their start and end apart: 9 -> 9, of which waited for: 3 -> 3; matrix products, arithmetic and copies ran while one was open for 0% -> 0% of each run, Pallas kernels for 20% -> 21%
where the time goes in v25:
time: 34 us; the launch traced here: 33.8 us
  Pallas kernels  10.6 us (31%)
  starting transfers between devices  8.93 us (26%)
  blocking collectives  8.87 us (26%)
  waiting for transfers between devices  4.69 us (14%)
  between operations  0.71 us (2%)
    ppermute x9, starting transfers between devices, swap(): lax.ppermute(value, 'shard', [(i, i ^ distance) for i in range(size)])  8.93 us
    all_to_all x1, blocking collectives, per_device(): lax.all_to_all(sums, 'shard', split_axis=0, concat_axis=0, axis_index_gro...  8.87 us
    pallas_call x1, Pallas kernels, encode(): pl.pallas_call(kernel, out_shape=(jax.ShapeDtypeStruct((tokens + slots, e...  5.65 us
    ppermute x9, waiting for transfers between devices, swap(): lax.ppermute(value, 'shard', [(i, i ^ distance) for i in range(size)])  4.69 us
    pallas_call x1, Pallas kernels, score(): pl.pallas_call(kernel, out_shape=jax.ShapeDtypeStruct((slots, e), F32), i...  2.64 us
    pallas_call x1, Pallas kernels, mask(): pl.pallas_call(mask_kernel, out_shape=[jax.ShapeDtypeStruct(shape, BF16)]...  1.31 us
    pallas_call x1, Pallas kernels, finish(): pl.pallas_call(kernel, out_shape=(jax.ShapeDtypeStruct(spots.shape, F32),...  0.99 us
  transfers between devices with their start and end apart: 9, of which 3 were waited for; matrix products, arithmetic and copies ran while one was open for 0% of the time, Pallas kernels for 21%

profile of v25, /device:TPU:0, one launch (start us, length us, event | category | flops | bytes accessed | tf_op | source)
XLA Modules:
  0.0 33.8 jit_solution(13448354176253522493)
XLA Ops:
  0.6 0.5 %collective-permute-start = (s32[48]{0:T(128)}, s32[48]{0:T(128)S(1)}, u32[]{:S(2)}, u32[]{:S(2)}) collective-permute-start(s32[48]{0:T(128)} %len0_ref.1), channel_id=1, source_target_pairs={{0,1},{1,0},{2,3},{3,2},{4,5},{5,4},{6,7},{7,6},{8,9},{9,8},{10,11... | collective-permute-start | bytes 584 | tf_op jit(solution)/shard_map/ppermute | solution.py:391
  1.2 0.0 copy-start
  1.2 0.0 copy-start.3
  1.2 5.6 %encode.1 = (bf16[144,128]{1,0:T(8,128)(2,1)}, s32[4,64]{1,0:T(4,128)}) custom-call(s32[1]{0:T(128)} %bitcast.refs_0_, s32[4]{0:T(128)} %refs_1_.1, s32[768]{0:T(1024)} %refs_2_.1, s32[4,64]{1,0:T(4,128)} %refs_3_.1, bf16[4,32,768]{2,1,0:T(8,128)(2,1)} %refs_4_.1, bf16[768,3072]{1,0:T(8,128)(2,1)} %refs_5_.1, bf16[3072,768]{1,0:T(8,128)(2,1)} %refs_6_.1, ...), custom_call_target="tpu_custom_call" | custom-call | flops 1207959552 | bytes 9437184 | tf_op jit(solution)/shard_map/encode/pallas_call | solution.py:199
  6.8 0.0 collective-permute-done.len1_ref
  6.8 0.0 copy-done
  6.8 0.0 copy-start.1
  6.8 0.1 collective-permute-start.1
  7.0 2.7 %collective-permute-start.2 = (bf16[144,128]{1,0:T(8,128)(2,1)}, bf16[144,128]{1,0:T(8,128)(2,1)S(1)}, u32[]{:S(2)}, u32[]{:S(2)}) collective-permute-start(bf16[144,128]{1,0:T(8,128)(2,1)} %get-tuple-element.12.refs_3_), channel_id=1, source_target_pairs={{0,5},{1,4},{2,7},{3,6},{4,1},{5,0},{6,3},{7,2},{8,13},{9,12},{10,... | collective-permute-start | bytes 110600 | tf_op jit(solution)/shard_map/ppermute | solution.py:391
  9.7 2.6 %collective-permute-start.5 = (bf16[144,128]{1,0:T(8,128)(2,1)}, bf16[144,128]{1,0:T(8,128)(2,1)S(1)}, u32[]{:S(2)}, u32[]{:S(2)}) collective-permute-start(bf16[144,128]{1,0:T(8,128)(2,1)} %get-tuple-element.12.refs_3_), channel_id=1, source_target_pairs={{0,8},{1,9},{2,10},{3,11},{4,12},{5,13},{6,14},{7,15},{8,0},{9,1},... | collective-permute-start | bytes 110600 | tf_op jit(solution)/shard_map/ppermute | solution.py:391
  12.3 0.0 collective-permute-start.7
  12.3 0.0 collective-permute-done.2.refs_5_
  12.3 1.5 %collective-permute-start.3 = (bf16[144,128]{1,0:T(8,128)(2,1)S(1)}, bf16[144,128]{1,0:T(8,128)(2,1)S(1)}, u32[]{:S(2)}, u32[]{:S(2)}) collective-permute-start(bf16[144,128]{1,0:T(8,128)(2,1)S(1)} %collective-permute-done.2.refs_5_), channel_id=1, source_target_pairs={{0,3},{1,2},{2,1},{3,0},{4,7},{5,6},{6,5},{7,4},{8,11},{9,10},{10,... | collective-permute-start | bytes 110600 | tf_op jit(solution)/shard_map/ppermute | solution.py:391
  13.7 0.3 collective-permute-start.4
  14.0 1.5 %collective-permute-done.5.refs_7_ = bf16[144,128]{1,0:T(8,128)(2,1)S(1)} collective-permute-done((bf16[144,128]{1,0:T(8,128)(2,1)}, bf16[144,128]{1,0:T(8,128)(2,1)S(1)}, u32[]{:S(2)}, u32[]{:S(2)}) %collective-permute-start.5) | collective-permute-done | bytes 36896 | tf_op jit(solution)/shard_map/ppermute | solution.py:391
  15.5 0.0 collective-permute-start.6
  15.5 2.3 %collective-permute-done.7.refs_9_ = bf16[144,128]{1,0:T(8,128)(2,1)S(1)} collective-permute-done((bf16[144,128]{1,0:T(8,128)(2,1)}, bf16[144,128]{1,0:T(8,128)(2,1)S(1)}, u32[]{:S(2)}, u32[]{:S(2)}) %collective-permute-start.7) | collective-permute-done | bytes 36896 | tf_op jit(solution)/shard_map/ppermute | solution.py:391
  17.8 1.2 %collective-permute-start.8 = (bf16[144,128]{1,0:T(8,128)(2,1)S(1)}, bf16[144,128]{1,0:T(8,128)(2,1)S(1)}, u32[]{:S(2)}, u32[]{:S(2)}) collective-permute-start(bf16[144,128]{1,0:T(8,128)(2,1)S(1)} %collective-permute-done.7.refs_9_), channel_id=1, source_target_pairs={{0,3},{1,2},{2,1},{3,0},{4,7},{5,6},{6,5},{7,4},{8,11},{9,10},{10,... | collective-permute-start | bytes 110600 | tf_op jit(solution)/shard_map/ppermute | solution.py:391
  19.0 0.0 collective-permute-done.3._.refs_6_
  19.0 0.0 collective-permute-done.1.pass1_ref
  19.0 0.0 copy-done.3
  19.0 1.3 %mask.1 = (bf16[48,128,128]{2,1,0:T(8,128)(2,1)S(1)}, bf16[48,128,128]{2,1,0:T(8,128)(2,1)S(1)}) custom-call(s32[48]{0:T(128)S(1)} %copy-done.3, s32[48]{0:T(128)S(1)} %collective-permute-done.len1_ref, bf16[48,128,128]{2,1,0:T(8,128)(2,1)S(1)} %copy-done, bf16[48,128,128]{2,1,0:T(8,128)(2,1)S(1)} %collective-permute-done.1.pass1_ref, ...), custom_call_target="tpu_custom_call" | custom-call | flops 12582912 | bytes 6291456 | tf_op jit(solution)/shard_map/mask/pallas_call | solution.py:250
  20.4 0.0 collective-permute-done.4.refs_4_
  20.4 0.0 collective-permute-done.6.refs_8_
  20.4 0.9 %collective-permute-done.8.refs_10_ = bf16[144,128]{1,0:T(8,128)(2,1)S(1)} collective-permute-done((bf16[144,128]{1,0:T(8,128)(2,1)S(1)}, bf16[144,128]{1,0:T(8,128)(2,1)S(1)}, u32[]{:S(2)}, u32[]{:S(2)}) %collective-permute-start.8) | collective-permute-done | bytes 36896 | tf_op jit(solution)/shard_map/ppermute | solution.py:391
  21.3 0.0 copy-done.1
  21.3 0.0 copy-start.2
  21.3 2.6 %score.1 = f32[8,128]{1,0:T(8,128)S(1)} custom-call(s32[1]{0:T(128)} %bitcast.refs_0_, bf16[48,128,128]{2,1,0:T(8,128)(2,1)S(1)} %get-tuple-element.13.refs_1_, bf16[48,128,128]{2,1,0:T(8,128)(2,1)S(1)} %get-tuple-element.14.refs_2_, bf16[144,128]{1,0:T(8,128)(2,1)S(1)} %copy-done.1, bf16[144,128]{1,0:T(8,128)(2,1)S(1)} %collective-permute-done.4.refs_4_, ...), custom_call_target="tpu_custom_call" | custom-call | flops 805306368 | bytes 3145728 | tf_op jit(solution)/shard_map/score/pallas_call | solution.py:327
  23.9 8.9 %all_to_all.11 = f32[8,1,128]{2,1,0:T(1,128)S(1)} all-to-all(f32[8,1,128]{2,1,0:T(1,128)S(1)} %bitcast.5), channel_id=1, replica_groups={{5,6,0,3,13,14,8,11},{4,7,1,2,12,15,9,10},{21,22,16,19,29,30,24,27},{20..., dimensions={0} | all-to-all | bytes 8192 | tf_op jit(solution)/shard_map/all_to_all | solution.py:445
  32.8 0.0 copy-done.2
  32.8 1.0 %finish.1 = (f32[4,64]{1,0:T(4,128)}, f32[4,10]{1,0:T(4,128)}) custom-call(f32[8,128]{1,0:T(8,128)S(1)} %bitcast.6, s32[4,64]{1,0:T(4,128)S(1)} %copy-done.2), custom_call_target="tpu_custom_call" | custom-call | tf_op jit(solution)/shard_map/finish/pallas_call | solution.py:376
Async XLA Ops:
  0.6 6.2 %collective-permute-start = (s32[48]{0:T(128)}, s32[48]{0:T(128)S(1)}, u32[]{:S(2)}, u32[]{:S(2)}) collective-permute-start(s32[48]{0:T(128)} %len0_ref.1), channel_id=1, source_target_pairs={{0,1},{1,0},{2,3},{3,2},{4,5},{5,4},{6,7},{7,6},{8,9},{9,8},{10,11... | collective-permute-start | bytes 584 | tf_op jit(solution)/shard_map/ppermute | solution.py:391
  1.2 5.7 %copy-start = (bf16[48,128,128]{2,1,0:T(8,128)(2,1)S(1)}, bf16[48,128,128]{2,1,0:T(8,128)(2,1)}, u32[]{:S(2)}) copy-start(bf16[48,128,128]{2,1,0:T(8,128)(2,1)} %pass0_ref.1) | copy-start | bytes 4718596
  1.2 17.9 %copy-start.3 = (s32[48]{0:T(128)S(1)}, s32[48]{0:T(128)}, u32[]{:S(2)}) copy-start(s32[48]{0:T(128)} %len0_ref.1) | copy-start | bytes 580
  6.8 14.4 %copy-start.1 = (bf16[144,128]{1,0:T(8,128)(2,1)S(1)}, bf16[144,128]{1,0:T(8,128)(2,1)}, u32[]{:S(2)}) copy-start(bf16[144,128]{1,0:T(8,128)(2,1)} %get-tuple-element.12.refs_3_) | copy-start | bytes 110596
  6.8 12.2 %collective-permute-start.1 = (bf16[48,128,128]{2,1,0:T(8,128)(2,1)S(1)}, bf16[48,128,128]{2,1,0:T(8,128)(2,1)S(1)}, u32[]{:S(2)}, u32[]{:S(2)}) collective-permute-start(bf16[48,128,128]{2,1,0:T(8,128)(2,1)S(1)} %copy-done), channel_id=1, source_target_pairs={{0,1},{1,0},{2,3},{3,2},{4,5},{5,4},{6,7},{7,6},{8,9},{9,8},{10,11... | collective-permute-start | bytes 4718600 | tf_op jit(solution)/shard_map/ppermute | solution.py:391
  7.0 5.3 %collective-permute-start.2 = (bf16[144,128]{1,0:T(8,128)(2,1)}, bf16[144,128]{1,0:T(8,128)(2,1)S(1)}, u32[]{:S(2)}, u32[]{:S(2)}) collective-permute-start(bf16[144,128]{1,0:T(8,128)(2,1)} %get-tuple-element.12.refs_3_), channel_id=1, source_target_pairs={{0,5},{1,4},{2,7},{3,6},{4,1},{5,0},{6,3},{7,2},{8,13},{9,12},{10,... | collective-permute-start | bytes 110600 | tf_op jit(solution)/shard_map/ppermute | solution.py:391
  9.7 5.9 %collective-permute-start.5 = (bf16[144,128]{1,0:T(8,128)(2,1)}, bf16[144,128]{1,0:T(8,128)(2,1)S(1)}, u32[]{:S(2)}, u32[]{:S(2)}) collective-permute-start(bf16[144,128]{1,0:T(8,128)(2,1)} %get-tuple-element.12.refs_3_), channel_id=1, source_target_pairs={{0,8},{1,9},{2,10},{3,11},{4,12},{5,13},{6,14},{7,15},{8,0},{9,1},... | collective-permute-start | bytes 110600 | tf_op jit(solution)/shard_map/ppermute | solution.py:391
  12.3 5.5 %collective-permute-start.7 = (bf16[144,128]{1,0:T(8,128)(2,1)}, bf16[144,128]{1,0:T(8,128)(2,1)S(1)}, u32[]{:S(2)}, u32[]{:S(2)}) collective-permute-start(bf16[144,128]{1,0:T(8,128)(2,1)} %get-tuple-element.12.refs_3_), channel_id=1, source_target_pairs={{0,13},{1,12},{2,15},{3,14},{4,9},{5,8},{6,11},{7,10},{8,5},{9,4},... | collective-permute-start | bytes 110600 | tf_op jit(solution)/shard_map/ppermute | solution.py:391
  12.3 6.8 %collective-permute-start.3 = (bf16[144,128]{1,0:T(8,128)(2,1)S(1)}, bf16[144,128]{1,0:T(8,128)(2,1)S(1)}, u32[]{:S(2)}, u32[]{:S(2)}) collective-permute-start(bf16[144,128]{1,0:T(8,128)(2,1)S(1)} %collective-permute-done.2.refs_5_), channel_id=1, source_target_pairs={{0,3},{1,2},{2,1},{3,0},{4,7},{5,6},{6,5},{7,4},{8,11},{9,10},{10,... | collective-permute-start | bytes 110600 | tf_op jit(solution)/shard_map/ppermute | solution.py:391
  13.7 6.6 %collective-permute-start.4 = (bf16[144,128]{1,0:T(8,128)(2,1)}, bf16[144,128]{1,0:T(8,128)(2,1)S(1)}, u32[]{:S(2)}, u32[]{:S(2)}) collective-permute-start(bf16[144,128]{1,0:T(8,128)(2,1)} %get-tuple-element.12.refs_3_), channel_id=1, source_target_pairs={{0,3},{1,2},{2,1},{3,0},{4,7},{5,6},{6,5},{7,4},{8,11},{9,10},{10,... | collective-permute-start | bytes 110600 | tf_op jit(solution)/shard_map/ppermute | solution.py:391
  15.5 4.8 %collective-permute-start.6 = (bf16[144,128]{1,0:T(8,128)(2,1)S(1)}, bf16[144,128]{1,0:T(8,128)(2,1)S(1)}, u32[]{:S(2)}, u32[]{:S(2)}) collective-permute-start(bf16[144,128]{1,0:T(8,128)(2,1)S(1)} %collective-permute-done.5.refs_7_), channel_id=1, source_target_pairs={{0,3},{1,2},{2,1},{3,0},{4,7},{5,6},{6,5},{7,4},{8,11},{9,10},{10,... | collective-permute-start | bytes 110600 | tf_op jit(solution)/shard_map/ppermute | solution.py:391
  17.8 3.5 %collective-permute-start.8 = (bf16[144,128]{1,0:T(8,128)(2,1)S(1)}, bf16[144,128]{1,0:T(8,128)(2,1)S(1)}, u32[]{:S(2)}, u32[]{:S(2)}) collective-permute-start(bf16[144,128]{1,0:T(8,128)(2,1)S(1)} %collective-permute-done.7.refs_9_), channel_id=1, source_target_pairs={{0,3},{1,2},{2,1},{3,0},{4,7},{5,6},{6,5},{7,4},{8,11},{9,10},{10,... | collective-permute-start | bytes 110600 | tf_op jit(solution)/shard_map/ppermute | solution.py:391
  21.3 11.5 %copy-start.2 = (s32[4,64]{1,0:T(4,128)S(1)}, s32[4,64]{1,0:T(4,128)}, u32[]{:S(2)}) copy-start(s32[4,64]{1,0:T(4,128)} %get-tuple-element.15.refs_1_) | copy-start | bytes 3076

commit v26 on v25

--- a/solution.py
+++ b/solution.py
@@ -17,9 +17,9 @@
 def split3(value):
     high = value.astype(BF16)
     rest = value - high.astype(F32)
-    middle = rest.astype(BF16)
-    low = (rest - middle.astype(F32)).astype(BF16)
-    return high, middle, low
+    leader = rest.astype(BF16)
+    low = (rest - leader.astype(F32)).astype(BF16)
+    return high, leader, low
 
 
 def mask_into(out_ref, pass_ref, len_ref, first, count):
@@ -258,7 +258,7 @@
     )(*lengths, *passages, late)
 
 
-def score_kernel(slots, middle, token_count, me_ref, own_ref, other_ref, *refs):
+def score_kernel(slots, leader, token_count, me_ref, own_ref, other_ref, *refs):
     got_refs = refs[:slots]
     out_ref, best_ref, index_v, index, sem = refs[slots:]
     message, lanes = got_refs[0].shape
@@ -313,16 +313,16 @@
     total = sum(lax.dot_general(ones, part, NT, preferred_element_type=F32) for part in split3(best_ref[...]))
     out_ref[...] = jnp.zeros(out_ref.shape, F32)
     for s in range(slots):
-        out_ref[pl.ds(jnp.bitwise_xor(chip, s ^ middle), 1), pl.ds(0, 2 * half)] = total[s:s + 1]
-
-
-def score(me, got, own, other, middle, token_count):
+        out_ref[pl.ds(jnp.bitwise_xor(chip, s ^ leader), 1), pl.ds(0, 2 * half)] = total[s:s + 1]
+
+
+def score(me, got, own, other, leader, token_count):
     half, plen, e = own.shape
     passage_count = 2 * half
     slots = len(got)
 
     def kernel(*refs):
-        score_kernel(slots, middle, token_count, *refs)
+        score_kernel(slots, leader, token_count, *refs)
 
     return pl.pallas_call(
         kernel,
@@ -345,7 +345,7 @@
     )(me, own, other, *got)
 
 
-def finish_kernel(middle, got_ref, spot_ref, scores_ref, best_ref):
+def finish_kernel(leader, got_ref, spot_ref, scores_ref, best_ref):
     slots, lanes = got_ref.shape
     query_count, cand_count = scores_ref.shape
     parts = split3(got_ref[...])
@@ -355,7 +355,7 @@
     col_iota = lax.broadcasted_iota(jnp.int32, (cand_count, cand_count), 1)
     place = lax.broadcasted_iota(jnp.int32, (cand_count, 128), 1)
     for i in range(query_count):
-        spot = jnp.bitwise_xor(spot_ref[i:i + 1, :], middle * lanes)
+        spot = jnp.bitwise_xor(spot_ref[i:i + 1, :], leader * lanes)
         lane = jnp.bitwise_and(spot, lanes - 1)
         onehot = jnp.where(lane_iota == lane, 1.0, 0.0).astype(BF16)
         picked = sum(jnp.dot(part, onehot, preferred_element_type=F32) for part in parts)
@@ -369,9 +369,9 @@
         best_ref[i:i + 1, :] = ordered[:, :TOPN]
 
 
-def finish(got, spots, middle):
+def finish(got, spots, leader):
     def kernel(*refs):
-        finish_kernel(middle, *refs)
+        finish_kernel(leader, *refs)
 
     return pl.pallas_call(
         kernel,
@@ -413,8 +413,8 @@
     def color(index):
         return (index ^ (index >> 1) ^ (index >> shift)) & 1
 
-    middle = inner * (slots // inner // 2 - 1)
-    groups = [[2 * (p ^ middle) + (c ^ color(2 * (p ^ middle))) for p in range(slots)] for c in range(2)]
+    leader = slots - inner
+    groups = [[2 * (p ^ leader) + (c ^ color(2 * (p ^ leader))) for p in range(slots)] for c in range(2)]
 
     def send(value, distance):
         return swap(value, 2 * distance + color(2 * distance))
@@ -441,9 +441,9 @@
     line = [message] + [send(message, d) for d in range(slots - inner, 0, -inner)][::-1]
     got = [line[s // inner] if s % inner == 0 else send(line[s // inner], s % inner) for s in range(slots)]
     own, other = mask((passage_lengths, across), (passage_vectors, raw), got[inner + 1])
-    sums = score(me, got, own, other, middle, query_hidden.shape[1])
+    sums = score(me, got, own, other, leader, query_hidden.shape[1])
     back = lax.all_to_all(sums, "shard", split_axis=0, concat_axis=0, axis_index_groups=groups, tiled=True)
-    return finish(back, spots, middle)
+    return finish(back, spots, leader)
 
 
 def solution(mesh):

time: 34 us -> 33.6 us (0.988)
  blocking collectives: 8.87 us -> 8.5 us
    all_to_all x1, blocking collectives: 8.87 us -> 8.5 us  [per_device(): lax.all_to_all(sums, 'shard', split_axis=0, concat_axis=0, axis_index_gro...]
where the time goes in v26:
time: 33.6 us; the launch traced here: 33.4 us
  Pallas kernels  10.6 us (32%)
  starting transfers between devices  8.93 us (27%)
  blocking collectives  8.5 us (25%)
  waiting for transfers between devices  4.69 us (14%)
  between operations  0.71 us (2%)
    ppermute x9, starting transfers between devices, swap(): lax.ppermute(value, 'shard', [(i, i ^ distance) for i in range(size)])  8.93 us
    all_to_all x1, blocking collectives, per_device(): lax.all_to_all(sums, 'shard', split_axis=0, concat_axis=0, axis_index_gro...  8.5 us
    pallas_call x1, Pallas kernels, encode(): pl.pallas_call(kernel, out_shape=(jax.ShapeDtypeStruct((tokens + slots, e...  5.65 us
    ppermute x9, waiting for transfers between devices, swap(): lax.ppermute(value, 'shard', [(i, i ^ distance) for i in range(size)])  4.69 us
    pallas_call x1, Pallas kernels, score(): pl.pallas_call(kernel, out_shape=jax.ShapeDtypeStruct((slots, e), F32), i...  2.64 us
    pallas_call x1, Pallas kernels, mask(): pl.pallas_call(mask_kernel, out_shape=[jax.ShapeDtypeStruct(shape, BF16)]...  1.31 us
    pallas_call x1, Pallas kernels, finish(): pl.pallas_call(kernel, out_shape=(jax.ShapeDtypeStruct(spots.shape, F32),...  0.99 us
  transfers between devices with their start and end apart: 9, of which 3 were waited for; matrix products, arithmetic and copies ran while one was open for 0% of the time, Pallas kernels for 21%

profile of v26, /device:TPU:0, one launch (start us, length us, event | category | flops | bytes accessed | tf_op | source)
XLA Modules:
  0.0 33.4 jit_solution(4421814932591153639)
XLA Ops:
  0.6 0.5 %collective-permute-start = (s32[48]{0:T(128)}, s32[48]{0:T(128)S(1)}, u32[]{:S(2)}, u32[]{:S(2)}) collective-permute-start(s32[48]{0:T(128)} %len0_ref.1), channel_id=1, source_target_pairs={{0,1},{1,0},{2,3},{3,2},{4,5},{5,4},{6,7},{7,6},{8,9},{9,8},{10,11... | collective-permute-start | bytes 584 | tf_op jit(solution)/shard_map/ppermute | solution.py:391
  1.2 0.0 copy-start
  1.2 0.0 copy-start.3
  1.2 5.6 %encode.1 = (bf16[144,128]{1,0:T(8,128)(2,1)}, s32[4,64]{1,0:T(4,128)}) custom-call(s32[1]{0:T(128)} %bitcast.refs_0_, s32[4]{0:T(128)} %refs_1_.1, s32[768]{0:T(1024)} %refs_2_.1, s32[4,64]{1,0:T(4,128)} %refs_3_.1, bf16[4,32,768]{2,1,0:T(8,128)(2,1)} %refs_4_.1, bf16[768,3072]{1,0:T(8,128)(2,1)} %refs_5_.1, bf16[3072,768]{1,0:T(8,128)(2,1)} %refs_6_.1, ...), custom_call_target="tpu_custom_call" | custom-call | flops 1207959552 | bytes 9437184 | tf_op jit(solution)/shard_map/encode/pallas_call | solution.py:199
  6.8 0.0 collective-permute-done.len1_ref
  6.8 0.0 copy-done
  6.8 0.0 copy-start.1
  6.8 0.1 collective-permute-start.1
  7.0 2.7 %collective-permute-start.2 = (bf16[144,128]{1,0:T(8,128)(2,1)}, bf16[144,128]{1,0:T(8,128)(2,1)S(1)}, u32[]{:S(2)}, u32[]{:S(2)}) collective-permute-start(bf16[144,128]{1,0:T(8,128)(2,1)} %get-tuple-element.12.refs_3_), channel_id=1, source_target_pairs={{0,5},{1,4},{2,7},{3,6},{4,1},{5,0},{6,3},{7,2},{8,13},{9,12},{10,... | collective-permute-start | bytes 110600 | tf_op jit(solution)/shard_map/ppermute | solution.py:391
  9.7 2.6 %collective-permute-start.5 = (bf16[144,128]{1,0:T(8,128)(2,1)}, bf16[144,128]{1,0:T(8,128)(2,1)S(1)}, u32[]{:S(2)}, u32[]{:S(2)}) collective-permute-start(bf16[144,128]{1,0:T(8,128)(2,1)} %get-tuple-element.12.refs_3_), channel_id=1, source_target_pairs={{0,8},{1,9},{2,10},{3,11},{4,12},{5,13},{6,14},{7,15},{8,0},{9,1},... | collective-permute-start | bytes 110600 | tf_op jit(solution)/shard_map/ppermute | solution.py:391
  12.3 0.0 collective-permute-start.7
  12.3 0.0 collective-permute-done.2.refs_5_
  12.3 1.5 %collective-permute-start.3 = (bf16[144,128]{1,0:T(8,128)(2,1)S(1)}, bf16[144,128]{1,0:T(8,128)(2,1)S(1)}, u32[]{:S(2)}, u32[]{:S(2)}) collective-permute-start(bf16[144,128]{1,0:T(8,128)(2,1)S(1)} %collective-permute-done.2.refs_5_), channel_id=1, source_target_pairs={{0,3},{1,2},{2,1},{3,0},{4,7},{5,6},{6,5},{7,4},{8,11},{9,10},{10,... | collective-permute-start | bytes 110600 | tf_op jit(solution)/shard_map/ppermute | solution.py:391
  13.7 0.3 collective-permute-start.4
  14.0 1.5 %collective-permute-done.5.refs_7_ = bf16[144,128]{1,0:T(8,128)(2,1)S(1)} collective-permute-done((bf16[144,128]{1,0:T(8,128)(2,1)}, bf16[144,128]{1,0:T(8,128)(2,1)S(1)}, u32[]{:S(2)}, u32[]{:S(2)}) %collective-permute-start.5) | collective-permute-done | bytes 36896 | tf_op jit(solution)/shard_map/ppermute | solution.py:391
  15.5 0.0 collective-permute-start.6
  15.5 2.3 %collective-permute-done.7.refs_9_ = bf16[144,128]{1,0:T(8,128)(2,1)S(1)} collective-permute-done((bf16[144,128]{1,0:T(8,128)(2,1)}, bf16[144,128]{1,0:T(8,128)(2,1)S(1)}, u32[]{:S(2)}, u32[]{:S(2)}) %collective-permute-start.7) | collective-permute-done | bytes 36896 | tf_op jit(solution)/shard_map/ppermute | solution.py:391
  17.8 1.2 %collective-permute-start.8 = (bf16[144,128]{1,0:T(8,128)(2,1)S(1)}, bf16[144,128]{1,0:T(8,128)(2,1)S(1)}, u32[]{:S(2)}, u32[]{:S(2)}) collective-permute-start(bf16[144,128]{1,0:T(8,128)(2,1)S(1)} %collective-permute-done.7.refs_9_), channel_id=1, source_target_pairs={{0,3},{1,2},{2,1},{3,0},{4,7},{5,6},{6,5},{7,4},{8,11},{9,10},{10,... | collective-permute-start | bytes 110600 | tf_op jit(solution)/shard_map/ppermute | solution.py:391
  19.0 0.0 collective-permute-done.3._.refs_6_
  19.0 0.0 collective-permute-done.1.pass1_ref
  19.0 0.0 copy-done.3
  19.0 1.3 %mask.1 = (bf16[48,128,128]{2,1,0:T(8,128)(2,1)S(1)}, bf16[48,128,128]{2,1,0:T(8,128)(2,1)S(1)}) custom-call(s32[48]{0:T(128)S(1)} %copy-done.3, s32[48]{0:T(128)S(1)} %collective-permute-done.len1_ref, bf16[48,128,128]{2,1,0:T(8,128)(2,1)S(1)} %copy-done, bf16[48,128,128]{2,1,0:T(8,128)(2,1)S(1)} %collective-permute-done.1.pass1_ref, ...), custom_call_target="tpu_custom_call" | custom-call | flops 12582912 | bytes 6291456 | tf_op jit(solution)/shard_map/mask/pallas_call | solution.py:250
  20.4 0.0 collective-permute-done.4.refs_4_
  20.4 0.0 collective-permute-done.6.refs_8_
  20.4 0.9 %collective-permute-done.8.refs_10_ = bf16[144,128]{1,0:T(8,128)(2,1)S(1)} collective-permute-done((bf16[144,128]{1,0:T(8,128)(2,1)S(1)}, bf16[144,128]{1,0:T(8,128)(2,1)S(1)}, u32[]{:S(2)}, u32[]{:S(2)}) %collective-permute-start.8) | collective-permute-done | bytes 36896 | tf_op jit(solution)/shard_map/ppermute | solution.py:391
  21.3 0.0 copy-done.1
  21.3 0.0 copy-start.2
  21.3 2.6 %score.1 = f32[8,128]{1,0:T(8,128)S(1)} custom-call(s32[1]{0:T(128)} %bitcast.refs_0_, bf16[48,128,128]{2,1,0:T(8,128)(2,1)S(1)} %get-tuple-element.13.refs_1_, bf16[48,128,128]{2,1,0:T(8,128)(2,1)S(1)} %get-tuple-element.14.refs_2_, bf16[144,128]{1,0:T(8,128)(2,1)S(1)} %copy-done.1, bf16[144,128]{1,0:T(8,128)(2,1)S(1)} %collective-permute-done.4.refs_4_, ...), custom_call_target="tpu_custom_call" | custom-call | flops 805306368 | bytes 3145728 | tf_op jit(solution)/shard_map/score/pallas_call | solution.py:327
  23.9 8.5 %all_to_all.11 = f32[8,1,128]{2,1,0:T(1,128)S(1)} all-to-all(f32[8,1,128]{2,1,0:T(1,128)S(1)} %bitcast.5), channel_id=1, replica_groups={{13,14,8,11,5,6,0,3},{12,15,9,10,4,7,1,2},{29,30,24,27,21,22,16,19},{28..., dimensions={0} | all-to-all | bytes 8192 | tf_op jit(solution)/shard_map/all_to_all | solution.py:445
  32.4 0.0 copy-done.2
  32.4 1.0 %finish.1 = (f32[4,64]{1,0:T(4,128)}, f32[4,10]{1,0:T(4,128)}) custom-call(f32[8,128]{1,0:T(8,128)S(1)} %bitcast.6, s32[4,64]{1,0:T(4,128)S(1)} %copy-done.2), custom_call_target="tpu_custom_call" | custom-call | tf_op jit(solution)/shard_map/finish/pallas_call | solution.py:376
Async XLA Ops:
  0.6 6.2 %collective-permute-start = (s32[48]{0:T(128)}, s32[48]{0:T(128)S(1)}, u32[]{:S(2)}, u32[]{:S(2)}) collective-permute-start(s32[48]{0:T(128)} %len0_ref.1), channel_id=1, source_target_pairs={{0,1},{1,0},{2,3},{3,2},{4,5},{5,4},{6,7},{7,6},{8,9},{9,8},{10,11... | collective-permute-start | bytes 584 | tf_op jit(solution)/shard_map/ppermute | solution.py:391
  1.2 5.7 %copy-start = (bf16[48,128,128]{2,1,0:T(8,128)(2,1)S(1)}, bf16[48,128,128]{2,1,0:T(8,128)(2,1)}, u32[]{:S(2)}) copy-start(bf16[48,128,128]{2,1,0:T(8,128)(2,1)} %pass0_ref.1) | copy-start | bytes 4718596
  1.2 17.9 %copy-start.3 = (s32[48]{0:T(128)S(1)}, s32[48]{0:T(128)}, u32[]{:S(2)}) copy-start(s32[48]{0:T(128)} %len0_ref.1) | copy-start | bytes 580
  6.8 14.4 %copy-start.1 = (bf16[144,128]{1,0:T(8,128)(2,1)S(1)}, bf16[144,128]{1,0:T(8,128)(2,1)}, u32[]{:S(2)}) copy-start(bf16[144,128]{1,0:T(8,128)(2,1)} %get-tuple-element.12.refs_3_) | copy-start | bytes 110596
  6.8 12.2 %collective-permute-start.1 = (bf16[48,128,128]{2,1,0:T(8,128)(2,1)S(1)}, bf16[48,128,128]{2,1,0:T(8,128)(2,1)S(1)}, u32[]{:S(2)}, u32[]{:S(2)}) collective-permute-start(bf16[48,128,128]{2,1,0:T(8,128)(2,1)S(1)} %copy-done), channel_id=1, source_target_pairs={{0,1},{1,0},{2,3},{3,2},{4,5},{5,4},{6,7},{7,6},{8,9},{9,8},{10,11... | collective-permute-start | bytes 4718600 | tf_op jit(solution)/shard_map/ppermute | solution.py:391
  7.0 5.3 %collective-permute-start.2 = (bf16[144,128]{1,0:T(8,128)(2,1)}, bf16[144,128]{1,0:T(8,128)(2,1)S(1)}, u32[]{:S(2)}, u32[]{:S(2)}) collective-permute-start(bf16[144,128]{1,0:T(8,128)(2,1)} %get-tuple-element.12.refs_3_), channel_id=1, source_target_pairs={{0,5},{1,4},{2,7},{3,6},{4,1},{5,0},{6,3},{7,2},{8,13},{9,12},{10,... | collective-permute-start | bytes 110600 | tf_op jit(solution)/shard_map/ppermute | solution.py:391
  9.7 5.9 %collective-permute-start.5 = (bf16[144,128]{1,0:T(8,128)(2,1)}, bf16[144,128]{1,0:T(8,128)(2,1)S(1)}, u32[]{:S(2)}, u32[]{:S(2)}) collective-permute-start(bf16[144,128]{1,0:T(8,128)(2,1)} %get-tuple-element.12.refs_3_), channel_id=1, source_target_pairs={{0,8},{1,9},{2,10},{3,11},{4,12},{5,13},{6,14},{7,15},{8,0},{9,1},... | collective-permute-start | bytes 110600 | tf_op jit(solution)/shard_map/ppermute | solution.py:391
  12.3 5.5 %collective-permute-start.7 = (bf16[144,128]{1,0:T(8,128)(2,1)}, bf16[144,128]{1,0:T(8,128)(2,1)S(1)}, u32[]{:S(2)}, u32[]{:S(2)}) collective-permute-start(bf16[144,128]{1,0:T(8,128)(2,1)} %get-tuple-element.12.refs_3_), channel_id=1, source_target_pairs={{0,13},{1,12},{2,15},{3,14},{4,9},{5,8},{6,11},{7,10},{8,5},{9,4},... | collective-permute-start | bytes 110600 | tf_op jit(solution)/shard_map/ppermute | solution.py:391
  12.3 6.8 %collective-permute-start.3 = (bf16[144,128]{1,0:T(8,128)(2,1)S(1)}, bf16[144,128]{1,0:T(8,128)(2,1)S(1)}, u32[]{:S(2)}, u32[]{:S(2)}) collective-permute-start(bf16[144,128]{1,0:T(8,128)(2,1)S(1)} %collective-permute-done.2.refs_5_), channel_id=1, source_target_pairs={{0,3},{1,2},{2,1},{3,0},{4,7},{5,6},{6,5},{7,4},{8,11},{9,10},{10,... | collective-permute-start | bytes 110600 | tf_op jit(solution)/shard_map/ppermute | solution.py:391
  13.7 6.6 %collective-permute-start.4 = (bf16[144,128]{1,0:T(8,128)(2,1)}, bf16[144,128]{1,0:T(8,128)(2,1)S(1)}, u32[]{:S(2)}, u32[]{:S(2)}) collective-permute-start(bf16[144,128]{1,0:T(8,128)(2,1)} %get-tuple-element.12.refs_3_), channel_id=1, source_target_pairs={{0,3},{1,2},{2,1},{3,0},{4,7},{5,6},{6,5},{7,4},{8,11},{9,10},{10,... | collective-permute-start | bytes 110600 | tf_op jit(solution)/shard_map/ppermute | solution.py:391
  15.5 4.8 %collective-permute-start.6 = (bf16[144,128]{1,0:T(8,128)(2,1)S(1)}, bf16[144,128]{1,0:T(8,128)(2,1)S(1)}, u32[]{:S(2)}, u32[]{:S(2)}) collective-permute-start(bf16[144,128]{1,0:T(8,128)(2,1)S(1)} %collective-permute-done.5.refs_7_), channel_id=1, source_target_pairs={{0,3},{1,2},{2,1},{3,0},{4,7},{5,6},{6,5},{7,4},{8,11},{9,10},{10,... | collective-permute-start | bytes 110600 | tf_op jit(solution)/shard_map/ppermute | solution.py:391
  17.8 3.5 %collective-permute-start.8 = (bf16[144,128]{1,0:T(8,128)(2,1)S(1)}, bf16[144,128]{1,0:T(8,128)(2,1)S(1)}, u32[]{:S(2)}, u32[]{:S(2)}) collective-permute-start(bf16[144,128]{1,0:T(8,128)(2,1)S(1)} %collective-permute-done.7.refs_9_), channel_id=1, source_target_pairs={{0,3},{1,2},{2,1},{3,0},{4,7},{5,6},{6,5},{7,4},{8,11},{9,10},{10,... | collective-permute-start | bytes 110600 | tf_op jit(solution)/shard_map/ppermute | solution.py:391
  21.3 11.2 %copy-start.2 = (s32[4,64]{1,0:T(4,128)S(1)}, s32[4,64]{1,0:T(4,128)}, u32[]{:S(2)}) copy-start(s32[4,64]{1,0:T(4,128)} %get-tuple-element.15.refs_1_) | copy-start | bytes 3076

commit v27 on v26

--- a/solution.py
+++ b/solution.py
@@ -17,9 +17,9 @@
 def split3(value):
     high = value.astype(BF16)
     rest = value - high.astype(F32)
-    leader = rest.astype(BF16)
-    low = (rest - leader.astype(F32)).astype(BF16)
-    return high, leader, low
+    middle = rest.astype(BF16)
+    low = (rest - middle.astype(F32)).astype(BF16)
+    return high, middle, low
 
 
 def mask_into(out_ref, pass_ref, len_ref, first, count):
@@ -413,7 +413,7 @@
     def color(index):
         return (index ^ (index >> 1) ^ (index >> shift)) & 1
 
-    leader = slots - inner
+    leader = inner * (slots // inner // 2)
     groups = [[2 * (p ^ leader) + (c ^ color(2 * (p ^ leader))) for p in range(slots)] for c in range(2)]
 
     def send(value, distance):

time: 33.6 us -> 33.9 us (level)
  no operation moved by 1% of the time
where the time goes in v27:
time: 33.9 us; the launch traced here: 33.7 us
  Pallas kernels  10.6 us (31%)
  starting transfers between devices  8.93 us (26%)
  blocking collectives  8.8 us (26%)
  waiting for transfers between devices  4.69 us (14%)
  between operations  0.71 us (2%)
    ppermute x9, starting transfers between devices, swap(): lax.ppermute(value, 'shard', [(i, i ^ distance) for i in range(size)])  8.93 us
    all_to_all x1, blocking collectives, per_device(): lax.all_to_all(sums, 'shard', split_axis=0, concat_axis=0, axis_index_gro...  8.8 us
    pallas_call x1, Pallas kernels, encode(): pl.pallas_call(kernel, out_shape=(jax.ShapeDtypeStruct((tokens + slots, e...  5.65 us
    ppermute x9, waiting for transfers between devices, swap(): lax.ppermute(value, 'shard', [(i, i ^ distance) for i in range(size)])  4.69 us
    pallas_call x1, Pallas kernels, score(): pl.pallas_call(kernel, out_shape=jax.ShapeDtypeStruct((slots, e), F32), i...  2.64 us
    pallas_call x1, Pallas kernels, mask(): pl.pallas_call(mask_kernel, out_shape=[jax.ShapeDtypeStruct(shape, BF16)]...  1.31 us
    pallas_call x1, Pallas kernels, finish(): pl.pallas_call(kernel, out_shape=(jax.ShapeDtypeStruct(spots.shape, F32),...  0.99 us
  transfers between devices with their start and end apart: 9, of which 3 were waited for; matrix products, arithmetic and copies ran while one was open for 0% of the time, Pallas kernels for 21%

profile of v27, /device:TPU:0, one launch (start us, length us, event | category | flops | bytes accessed | tf_op | source)
XLA Modules:
  0.0 33.7 jit_solution(12439181611625596307)
XLA Ops:
  0.6 0.5 %collective-permute-start = (s32[48]{0:T(128)}, s32[48]{0:T(128)S(1)}, u32[]{:S(2)}, u32[]{:S(2)}) collective-permute-start(s32[48]{0:T(128)} %len0_ref.1), channel_id=1, source_target_pairs={{0,1},{1,0},{2,3},{3,2},{4,5},{5,4},{6,7},{7,6},{8,9},{9,8},{10,11... | collective-permute-start | bytes 584 | tf_op jit(solution)/shard_map/ppermute | solution.py:391
  1.2 0.0 copy-start
  1.2 0.0 copy-start.3
  1.2 5.6 %encode.1 = (bf16[144,128]{1,0:T(8,128)(2,1)}, s32[4,64]{1,0:T(4,128)}) custom-call(s32[1]{0:T(128)} %bitcast.refs_0_, s32[4]{0:T(128)} %refs_1_.1, s32[768]{0:T(1024)} %refs_2_.1, s32[4,64]{1,0:T(4,128)} %refs_3_.1, bf16[4,32,768]{2,1,0:T(8,128)(2,1)} %refs_4_.1, bf16[768,3072]{1,0:T(8,128)(2,1)} %refs_5_.1, bf16[3072,768]{1,0:T(8,128)(2,1)} %refs_6_.1, ...), custom_call_target="tpu_custom_call" | custom-call | flops 1207959552 | bytes 9437184 | tf_op jit(solution)/shard_map/encode/pallas_call | solution.py:199
  6.8 0.0 collective-permute-done.len1_ref
  6.8 0.0 copy-done
  6.8 0.0 copy-start.1
  6.8 0.1 collective-permute-start.1
  7.0 2.7 %collective-permute-start.2 = (bf16[144,128]{1,0:T(8,128)(2,1)}, bf16[144,128]{1,0:T(8,128)(2,1)S(1)}, u32[]{:S(2)}, u32[]{:S(2)}) collective-permute-start(bf16[144,128]{1,0:T(8,128)(2,1)} %get-tuple-element.12.refs_3_), channel_id=1, source_target_pairs={{0,5},{1,4},{2,7},{3,6},{4,1},{5,0},{6,3},{7,2},{8,13},{9,12},{10,... | collective-permute-start | bytes 110600 | tf_op jit(solution)/shard_map/ppermute | solution.py:391
  9.7 2.6 %collective-permute-start.5 = (bf16[144,128]{1,0:T(8,128)(2,1)}, bf16[144,128]{1,0:T(8,128)(2,1)S(1)}, u32[]{:S(2)}, u32[]{:S(2)}) collective-permute-start(bf16[144,128]{1,0:T(8,128)(2,1)} %get-tuple-element.12.refs_3_), channel_id=1, source_target_pairs={{0,8},{1,9},{2,10},{3,11},{4,12},{5,13},{6,14},{7,15},{8,0},{9,1},... | collective-permute-start | bytes 110600 | tf_op jit(solution)/shard_map/ppermute | solution.py:391
  12.3 0.0 collective-permute-start.7
  12.3 0.0 collective-permute-done.2.refs_5_
  12.3 1.5 %collective-permute-start.3 = (bf16[144,128]{1,0:T(8,128)(2,1)S(1)}, bf16[144,128]{1,0:T(8,128)(2,1)S(1)}, u32[]{:S(2)}, u32[]{:S(2)}) collective-permute-start(bf16[144,128]{1,0:T(8,128)(2,1)S(1)} %collective-permute-done.2.refs_5_), channel_id=1, source_target_pairs={{0,3},{1,2},{2,1},{3,0},{4,7},{5,6},{6,5},{7,4},{8,11},{9,10},{10,... | collective-permute-start | bytes 110600 | tf_op jit(solution)/shard_map/ppermute | solution.py:391
  13.7 0.3 collective-permute-start.4
  14.0 1.5 %collective-permute-done.5.refs_7_ = bf16[144,128]{1,0:T(8,128)(2,1)S(1)} collective-permute-done((bf16[144,128]{1,0:T(8,128)(2,1)}, bf16[144,128]{1,0:T(8,128)(2,1)S(1)}, u32[]{:S(2)}, u32[]{:S(2)}) %collective-permute-start.5) | collective-permute-done | bytes 36896 | tf_op jit(solution)/shard_map/ppermute | solution.py:391
  15.5 0.0 collective-permute-start.6
  15.5 2.3 %collective-permute-done.7.refs_9_ = bf16[144,128]{1,0:T(8,128)(2,1)S(1)} collective-permute-done((bf16[144,128]{1,0:T(8,128)(2,1)}, bf16[144,128]{1,0:T(8,128)(2,1)S(1)}, u32[]{:S(2)}, u32[]{:S(2)}) %collective-permute-start.7) | collective-permute-done | bytes 36896 | tf_op jit(solution)/shard_map/ppermute | solution.py:391
  17.8 1.2 %collective-permute-start.8 = (bf16[144,128]{1,0:T(8,128)(2,1)S(1)}, bf16[144,128]{1,0:T(8,128)(2,1)S(1)}, u32[]{:S(2)}, u32[]{:S(2)}) collective-permute-start(bf16[144,128]{1,0:T(8,128)(2,1)S(1)} %collective-permute-done.7.refs_9_), channel_id=1, source_target_pairs={{0,3},{1,2},{2,1},{3,0},{4,7},{5,6},{6,5},{7,4},{8,11},{9,10},{10,... | collective-permute-start | bytes 110600 | tf_op jit(solution)/shard_map/ppermute | solution.py:391
  19.0 0.0 collective-permute-done.3._.refs_6_
  19.0 0.0 collective-permute-done.1.pass1_ref
  19.0 0.0 copy-done.3
  19.0 1.3 %mask.1 = (bf16[48,128,128]{2,1,0:T(8,128)(2,1)S(1)}, bf16[48,128,128]{2,1,0:T(8,128)(2,1)S(1)}) custom-call(s32[48]{0:T(128)S(1)} %copy-done.3, s32[48]{0:T(128)S(1)} %collective-permute-done.len1_ref, bf16[48,128,128]{2,1,0:T(8,128)(2,1)S(1)} %copy-done, bf16[48,128,128]{2,1,0:T(8,128)(2,1)S(1)} %collective-permute-done.1.pass1_ref, ...), custom_call_target="tpu_custom_call" | custom-call | flops 12582912 | bytes 6291456 | tf_op jit(solution)/shard_map/mask/pallas_call | solution.py:250
  20.4 0.0 collective-permute-done.4.refs_4_
  20.4 0.0 collective-permute-done.6.refs_8_
  20.4 0.9 %collective-permute-done.8.refs_10_ = bf16[144,128]{1,0:T(8,128)(2,1)S(1)} collective-permute-done((bf16[144,128]{1,0:T(8,128)(2,1)S(1)}, bf16[144,128]{1,0:T(8,128)(2,1)S(1)}, u32[]{:S(2)}, u32[]{:S(2)}) %collective-permute-start.8) | collective-permute-done | bytes 36896 | tf_op jit(solution)/shard_map/ppermute | solution.py:391
  21.3 0.0 copy-done.1
  21.3 0.0 copy-start.2
  21.3 2.6 %score.1 = f32[8,128]{1,0:T(8,128)S(1)} custom-call(s32[1]{0:T(128)} %bitcast.refs_0_, bf16[48,128,128]{2,1,0:T(8,128)(2,1)S(1)} %get-tuple-element.13.refs_1_, bf16[48,128,128]{2,1,0:T(8,128)(2,1)S(1)} %get-tuple-element.14.refs_2_, bf16[144,128]{1,0:T(8,128)(2,1)S(1)} %copy-done.1, bf16[144,128]{1,0:T(8,128)(2,1)S(1)} %collective-permute-done.4.refs_4_, ...), custom_call_target="tpu_custom_call" | custom-call | flops 805306368 | bytes 3145728 | tf_op jit(solution)/shard_map/score/pallas_call | solution.py:327
  23.9 8.8 %all_to_all.11 = f32[8,1,128]{2,1,0:T(1,128)S(1)} all-to-all(f32[8,1,128]{2,1,0:T(1,128)S(1)} %bitcast.5), channel_id=1, replica_groups={{8,11,13,14,0,3,5,6},{9,10,12,15,1,2,4,7},{24,27,29,30,16,19,21,22},{25..., dimensions={0} | all-to-all | bytes 8192 | tf_op jit(solution)/shard_map/all_to_all | solution.py:445
  32.7 0.0 copy-done.2
  32.7 1.0 %finish.1 = (f32[4,64]{1,0:T(4,128)}, f32[4,10]{1,0:T(4,128)}) custom-call(f32[8,128]{1,0:T(8,128)S(1)} %bitcast.6, s32[4,64]{1,0:T(4,128)S(1)} %copy-done.2), custom_call_target="tpu_custom_call" | custom-call | tf_op jit(solution)/shard_map/finish/pallas_call | solution.py:376
Async XLA Ops:
  0.6 6.2 %collective-permute-start = (s32[48]{0:T(128)}, s32[48]{0:T(128)S(1)}, u32[]{:S(2)}, u32[]{:S(2)}) collective-permute-start(s32[48]{0:T(128)} %len0_ref.1), channel_id=1, source_target_pairs={{0,1},{1,0},{2,3},{3,2},{4,5},{5,4},{6,7},{7,6},{8,9},{9,8},{10,11... | collective-permute-start | bytes 584 | tf_op jit(solution)/shard_map/ppermute | solution.py:391
  1.2 5.7 %copy-start = (bf16[48,128,128]{2,1,0:T(8,128)(2,1)S(1)}, bf16[48,128,128]{2,1,0:T(8,128)(2,1)}, u32[]{:S(2)}) copy-start(bf16[48,128,128]{2,1,0:T(8,128)(2,1)} %pass0_ref.1) | copy-start | bytes 4718596
  1.2 17.9 %copy-start.3 = (s32[48]{0:T(128)S(1)}, s32[48]{0:T(128)}, u32[]{:S(2)}) copy-start(s32[48]{0:T(128)} %len0_ref.1) | copy-start | bytes 580
  6.8 14.4 %copy-start.1 = (bf16[144,128]{1,0:T(8,128)(2,1)S(1)}, bf16[144,128]{1,0:T(8,128)(2,1)}, u32[]{:S(2)}) copy-start(bf16[144,128]{1,0:T(8,128)(2,1)} %get-tuple-element.12.refs_3_) | copy-start | bytes 110596
  6.8 12.2 %collective-permute-start.1 = (bf16[48,128,128]{2,1,0:T(8,128)(2,1)S(1)}, bf16[48,128,128]{2,1,0:T(8,128)(2,1)S(1)}, u32[]{:S(2)}, u32[]{:S(2)}) collective-permute-start(bf16[48,128,128]{2,1,0:T(8,128)(2,1)S(1)} %copy-done), channel_id=1, source_target_pairs={{0,1},{1,0},{2,3},{3,2},{4,5},{5,4},{6,7},{7,6},{8,9},{9,8},{10,11... | collective-permute-start | bytes 4718600 | tf_op jit(solution)/shard_map/ppermute | solution.py:391
  7.0 5.3 %collective-permute-start.2 = (bf16[144,128]{1,0:T(8,128)(2,1)}, bf16[144,128]{1,0:T(8,128)(2,1)S(1)}, u32[]{:S(2)}, u32[]{:S(2)}) collective-permute-start(bf16[144,128]{1,0:T(8,128)(2,1)} %get-tuple-element.12.refs_3_), channel_id=1, source_target_pairs={{0,5},{1,4},{2,7},{3,6},{4,1},{5,0},{6,3},{7,2},{8,13},{9,12},{10,... | collective-permute-start | bytes 110600 | tf_op jit(solution)/shard_map/ppermute | solution.py:391
  9.7 5.9 %collective-permute-start.5 = (bf16[144,128]{1,0:T(8,128)(2,1)}, bf16[144,128]{1,0:T(8,128)(2,1)S(1)}, u32[]{:S(2)}, u32[]{:S(2)}) collective-permute-start(bf16[144,128]{1,0:T(8,128)(2,1)} %get-tuple-element.12.refs_3_), channel_id=1, source_target_pairs={{0,8},{1,9},{2,10},{3,11},{4,12},{5,13},{6,14},{7,15},{8,0},{9,1},... | collective-permute-start | bytes 110600 | tf_op jit(solution)/shard_map/ppermute | solution.py:391
  12.3 5.5 %collective-permute-start.7 = (bf16[144,128]{1,0:T(8,128)(2,1)}, bf16[144,128]{1,0:T(8,128)(2,1)S(1)}, u32[]{:S(2)}, u32[]{:S(2)}) collective-permute-start(bf16[144,128]{1,0:T(8,128)(2,1)} %get-tuple-element.12.refs_3_), channel_id=1, source_target_pairs={{0,13},{1,12},{2,15},{3,14},{4,9},{5,8},{6,11},{7,10},{8,5},{9,4},... | collective-permute-start | bytes 110600 | tf_op jit(solution)/shard_map/ppermute | solution.py:391
  12.3 6.8 %collective-permute-start.3 = (bf16[144,128]{1,0:T(8,128)(2,1)S(1)}, bf16[144,128]{1,0:T(8,128)(2,1)S(1)}, u32[]{:S(2)}, u32[]{:S(2)}) collective-permute-start(bf16[144,128]{1,0:T(8,128)(2,1)S(1)} %collective-permute-done.2.refs_5_), channel_id=1, source_target_pairs={{0,3},{1,2},{2,1},{3,0},{4,7},{5,6},{6,5},{7,4},{8,11},{9,10},{10,... | collective-permute-start | bytes 110600 | tf_op jit(solution)/shard_map/ppermute | solution.py:391
  13.7 6.6 %collective-permute-start.4 = (bf16[144,128]{1,0:T(8,128)(2,1)}, bf16[144,128]{1,0:T(8,128)(2,1)S(1)}, u32[]{:S(2)}, u32[]{:S(2)}) collective-permute-start(bf16[144,128]{1,0:T(8,128)(2,1)} %get-tuple-element.12.refs_3_), channel_id=1, source_target_pairs={{0,3},{1,2},{2,1},{3,0},{4,7},{5,6},{6,5},{7,4},{8,11},{9,10},{10,... | collective-permute-start | bytes 110600 | tf_op jit(solution)/shard_map/ppermute | solution.py:391
  15.5 4.8 %collective-permute-start.6 = (bf16[144,128]{1,0:T(8,128)(2,1)S(1)}, bf16[144,128]{1,0:T(8,128)(2,1)S(1)}, u32[]{:S(2)}, u32[]{:S(2)}) collective-permute-start(bf16[144,128]{1,0:T(8,128)(2,1)S(1)} %collective-permute-done.5.refs_7_), channel_id=1, source_target_pairs={{0,3},{1,2},{2,1},{3,0},{4,7},{5,6},{6,5},{7,4},{8,11},{9,10},{10,... | collective-permute-start | bytes 110600 | tf_op jit(solution)/shard_map/ppermute | solution.py:391
  17.8 3.5 %collective-permute-start.8 = (bf16[144,128]{1,0:T(8,128)(2,1)S(1)}, bf16[144,128]{1,0:T(8,128)(2,1)S(1)}, u32[]{:S(2)}, u32[]{:S(2)}) collective-permute-start(bf16[144,128]{1,0:T(8,128)(2,1)S(1)} %collective-permute-done.7.refs_9_), channel_id=1, source_target_pairs={{0,3},{1,2},{2,1},{3,0},{4,7},{5,6},{6,5},{7,4},{8,11},{9,10},{10,... | collective-permute-start | bytes 110600 | tf_op jit(solution)/shard_map/ppermute | solution.py:391
  21.3 11.5 %copy-start.2 = (s32[4,64]{1,0:T(4,128)S(1)}, s32[4,64]{1,0:T(4,128)}, u32[]{:S(2)}) copy-start(s32[4,64]{1,0:T(4,128)} %get-tuple-element.15.refs_1_) | copy-start | bytes 3076

commit v28 on v27

--- a/solution.py
+++ b/solution.py
@@ -413,7 +413,7 @@
     def color(index):
         return (index ^ (index >> 1) ^ (index >> shift)) & 1
 
-    leader = inner * (slots // inner // 2)
+    leader = slots - 1
     groups = [[2 * (p ^ leader) + (c ^ color(2 * (p ^ leader))) for p in range(slots)] for c in range(2)]
 
     def send(value, distance):

time: 33.9 us -> 33.2 us (0.979)
  blocking collectives: 8.8 us -> 8.09 us
    all_to_all x1, blocking collectives: 8.8 us -> 8.09 us  [per_device(): lax.all_to_all(sums, 'shard', split_axis=0, concat_axis=0, axis_index_gro...]
where the time goes in v28:
time: 33.2 us; the launch traced here: 33 us
  Pallas kernels  10.6 us (32%)
  starting transfers between devices  8.93 us (27%)
  blocking collectives  8.09 us (24%)
  waiting for transfers between devices  4.69 us (14%)
  between operations  0.71 us (2%)
    ppermute x9, starting transfers between devices, swap(): lax.ppermute(value, 'shard', [(i, i ^ distance) for i in range(size)])  8.93 us
    all_to_all x1, blocking collectives, per_device(): lax.all_to_all(sums, 'shard', split_axis=0, concat_axis=0, axis_index_gro...  8.09 us
    pallas_call x1, Pallas kernels, encode(): pl.pallas_call(kernel, out_shape=(jax.ShapeDtypeStruct((tokens + slots, e...  5.65 us
    ppermute x9, waiting for transfers between devices, swap(): lax.ppermute(value, 'shard', [(i, i ^ distance) for i in range(size)])  4.69 us
    pallas_call x1, Pallas kernels, score(): pl.pallas_call(kernel, out_shape=jax.ShapeDtypeStruct((slots, e), F32), i...  2.64 us
    pallas_call x1, Pallas kernels, mask(): pl.pallas_call(mask_kernel, out_shape=[jax.ShapeDtypeStruct(shape, BF16)]...  1.31 us
    pallas_call x1, Pallas kernels, finish(): pl.pallas_call(kernel, out_shape=(jax.ShapeDtypeStruct(spots.shape, F32),...  0.99 us
  transfers between devices with their start and end apart: 9, of which 3 were waited for; matrix products, arithmetic and copies ran while one was open for 0% of the time, Pallas kernels for 21%

profile of v28, /device:TPU:0, one launch (start us, length us, event | category | flops | bytes accessed | tf_op | source)
XLA Modules:
  0.0 33.0 jit_solution(5207117992765385154)
XLA Ops:
  0.6 0.5 %collective-permute-start = (s32[48]{0:T(128)}, s32[48]{0:T(128)S(1)}, u32[]{:S(2)}, u32[]{:S(2)}) collective-permute-start(s32[48]{0:T(128)} %len0_ref.1), channel_id=1, source_target_pairs={{0,1},{1,0},{2,3},{3,2},{4,5},{5,4},{6,7},{7,6},{8,9},{9,8},{10,11... | collective-permute-start | bytes 584 | tf_op jit(solution)/shard_map/ppermute | solution.py:391
  1.2 0.0 copy-start
  1.2 0.0 copy-start.3
  1.2 5.6 %encode.1 = (bf16[144,128]{1,0:T(8,128)(2,1)}, s32[4,64]{1,0:T(4,128)}) custom-call(s32[1]{0:T(128)} %bitcast.refs_0_, s32[4]{0:T(128)} %refs_1_.1, s32[768]{0:T(1024)} %refs_2_.1, s32[4,64]{1,0:T(4,128)} %refs_3_.1, bf16[4,32,768]{2,1,0:T(8,128)(2,1)} %refs_4_.1, bf16[768,3072]{1,0:T(8,128)(2,1)} %refs_5_.1, bf16[3072,768]{1,0:T(8,128)(2,1)} %refs_6_.1, ...), custom_call_target="tpu_custom_call" | custom-call | flops 1207959552 | bytes 9437184 | tf_op jit(solution)/shard_map/encode/pallas_call | solution.py:199
  6.8 0.0 collective-permute-done.len1_ref
  6.8 0.0 copy-done
  6.8 0.0 copy-start.1
  6.8 0.1 collective-permute-start.1
  7.0 2.7 %collective-permute-start.2 = (bf16[144,128]{1,0:T(8,128)(2,1)}, bf16[144,128]{1,0:T(8,128)(2,1)S(1)}, u32[]{:S(2)}, u32[]{:S(2)}) collective-permute-start(bf16[144,128]{1,0:T(8,128)(2,1)} %get-tuple-element.12.refs_3_), channel_id=1, source_target_pairs={{0,5},{1,4},{2,7},{3,6},{4,1},{5,0},{6,3},{7,2},{8,13},{9,12},{10,... | collective-permute-start | bytes 110600 | tf_op jit(solution)/shard_map/ppermute | solution.py:391
  9.7 2.6 %collective-permute-start.5 = (bf16[144,128]{1,0:T(8,128)(2,1)}, bf16[144,128]{1,0:T(8,128)(2,1)S(1)}, u32[]{:S(2)}, u32[]{:S(2)}) collective-permute-start(bf16[144,128]{1,0:T(8,128)(2,1)} %get-tuple-element.12.refs_3_), channel_id=1, source_target_pairs={{0,8},{1,9},{2,10},{3,11},{4,12},{5,13},{6,14},{7,15},{8,0},{9,1},... | collective-permute-start | bytes 110600 | tf_op jit(solution)/shard_map/ppermute | solution.py:391
  12.3 0.0 collective-permute-start.7
  12.3 0.0 collective-permute-done.2.refs_5_
  12.3 1.5 %collective-permute-start.3 = (bf16[144,128]{1,0:T(8,128)(2,1)S(1)}, bf16[144,128]{1,0:T(8,128)(2,1)S(1)}, u32[]{:S(2)}, u32[]{:S(2)}) collective-permute-start(bf16[144,128]{1,0:T(8,128)(2,1)S(1)} %collective-permute-done.2.refs_5_), channel_id=1, source_target_pairs={{0,3},{1,2},{2,1},{3,0},{4,7},{5,6},{6,5},{7,4},{8,11},{9,10},{10,... | collective-permute-start | bytes 110600 | tf_op jit(solution)/shard_map/ppermute | solution.py:391
  13.7 0.3 collective-permute-start.4
  14.0 1.5 %collective-permute-done.5.refs_7_ = bf16[144,128]{1,0:T(8,128)(2,1)S(1)} collective-permute-done((bf16[144,128]{1,0:T(8,128)(2,1)}, bf16[144,128]{1,0:T(8,128)(2,1)S(1)}, u32[]{:S(2)}, u32[]{:S(2)}) %collective-permute-start.5) | collective-permute-done | bytes 36896 | tf_op jit(solution)/shard_map/ppermute | solution.py:391
  15.5 0.0 collective-permute-start.6
  15.5 2.3 %collective-permute-done.7.refs_9_ = bf16[144,128]{1,0:T(8,128)(2,1)S(1)} collective-permute-done((bf16[144,128]{1,0:T(8,128)(2,1)}, bf16[144,128]{1,0:T(8,128)(2,1)S(1)}, u32[]{:S(2)}, u32[]{:S(2)}) %collective-permute-start.7) | collective-permute-done | bytes 36896 | tf_op jit(solution)/shard_map/ppermute | solution.py:391
  17.8 1.2 %collective-permute-start.8 = (bf16[144,128]{1,0:T(8,128)(2,1)S(1)}, bf16[144,128]{1,0:T(8,128)(2,1)S(1)}, u32[]{:S(2)}, u32[]{:S(2)}) collective-permute-start(bf16[144,128]{1,0:T(8,128)(2,1)S(1)} %collective-permute-done.7.refs_9_), channel_id=1, source_target_pairs={{0,3},{1,2},{2,1},{3,0},{4,7},{5,6},{6,5},{7,4},{8,11},{9,10},{10,... | collective-permute-start | bytes 110600 | tf_op jit(solution)/shard_map/ppermute | solution.py:391
  19.0 0.0 collective-permute-done.3._.refs_6_
  19.0 0.0 collective-permute-done.1.pass1_ref
  19.0 0.0 copy-done.3
  19.0 1.3 %mask.1 = (bf16[48,128,128]{2,1,0:T(8,128)(2,1)S(1)}, bf16[48,128,128]{2,1,0:T(8,128)(2,1)S(1)}) custom-call(s32[48]{0:T(128)S(1)} %copy-done.3, s32[48]{0:T(128)S(1)} %collective-permute-done.len1_ref, bf16[48,128,128]{2,1,0:T(8,128)(2,1)S(1)} %copy-done, bf16[48,128,128]{2,1,0:T(8,128)(2,1)S(1)} %collective-permute-done.1.pass1_ref, ...), custom_call_target="tpu_custom_call" | custom-call | flops 12582912 | bytes 6291456 | tf_op jit(solution)/shard_map/mask/pallas_call | solution.py:250
  20.4 0.0 collective-permute-done.4.refs_4_
  20.4 0.0 collective-permute-done.6.refs_8_
  20.4 0.9 %collective-permute-done.8.refs_10_ = bf16[144,128]{1,0:T(8,128)(2,1)S(1)} collective-permute-done((bf16[144,128]{1,0:T(8,128)(2,1)S(1)}, bf16[144,128]{1,0:T(8,128)(2,1)S(1)}, u32[]{:S(2)}, u32[]{:S(2)}) %collective-permute-start.8) | collective-permute-done | bytes 36896 | tf_op jit(solution)/shard_map/ppermute | solution.py:391
  21.3 0.0 copy-done.1
  21.3 0.0 copy-start.2
  21.3 2.6 %score.1 = f32[8,128]{1,0:T(8,128)S(1)} custom-call(s32[1]{0:T(128)} %bitcast.refs_0_, bf16[48,128,128]{2,1,0:T(8,128)(2,1)S(1)} %get-tuple-element.13.refs_1_, bf16[48,128,128]{2,1,0:T(8,128)(2,1)S(1)} %get-tuple-element.14.refs_2_, bf16[144,128]{1,0:T(8,128)(2,1)S(1)} %copy-done.1, bf16[144,128]{1,0:T(8,128)(2,1)S(1)} %collective-permute-done.4.refs_4_, ...), custom_call_target="tpu_custom_call" | custom-call | flops 805306368 | bytes 3145728 | tf_op jit(solution)/shard_map/score/pallas_call | solution.py:327
  23.9 8.1 %all_to_all.11 = f32[8,1,128]{2,1,0:T(1,128)S(1)} all-to-all(f32[8,1,128]{2,1,0:T(1,128)S(1)} %bitcast.5), channel_id=1, replica_groups={{14,13,11,8,6,5,3,0},{15,12,10,9,7,4,2,1},{30,29,27,24,22,21,19,16},{31..., dimensions={0} | all-to-all | bytes 8192 | tf_op jit(solution)/shard_map/all_to_all | solution.py:445
  32.0 0.0 copy-done.2
  32.0 1.0 %finish.1 = (f32[4,64]{1,0:T(4,128)}, f32[4,10]{1,0:T(4,128)}) custom-call(f32[8,128]{1,0:T(8,128)S(1)} %bitcast.6, s32[4,64]{1,0:T(4,128)S(1)} %copy-done.2), custom_call_target="tpu_custom_call" | custom-call | tf_op jit(solution)/shard_map/finish/pallas_call | solution.py:376
Async XLA Ops:
  0.6 6.2 %collective-permute-start = (s32[48]{0:T(128)}, s32[48]{0:T(128)S(1)}, u32[]{:S(2)}, u32[]{:S(2)}) collective-permute-start(s32[48]{0:T(128)} %len0_ref.1), channel_id=1, source_target_pairs={{0,1},{1,0},{2,3},{3,2},{4,5},{5,4},{6,7},{7,6},{8,9},{9,8},{10,11... | collective-permute-start | bytes 584 | tf_op jit(solution)/shard_map/ppermute | solution.py:391
  1.2 5.7 %copy-start = (bf16[48,128,128]{2,1,0:T(8,128)(2,1)S(1)}, bf16[48,128,128]{2,1,0:T(8,128)(2,1)}, u32[]{:S(2)}) copy-start(bf16[48,128,128]{2,1,0:T(8,128)(2,1)} %pass0_ref.1) | copy-start | bytes 4718596
  1.2 17.9 %copy-start.3 = (s32[48]{0:T(128)S(1)}, s32[48]{0:T(128)}, u32[]{:S(2)}) copy-start(s32[48]{0:T(128)} %len0_ref.1) | copy-start | bytes 580
  6.8 14.4 %copy-start.1 = (bf16[144,128]{1,0:T(8,128)(2,1)S(1)}, bf16[144,128]{1,0:T(8,128)(2,1)}, u32[]{:S(2)}) copy-start(bf16[144,128]{1,0:T(8,128)(2,1)} %get-tuple-element.12.refs_3_) | copy-start | bytes 110596
  6.8 12.2 %collective-permute-start.1 = (bf16[48,128,128]{2,1,0:T(8,128)(2,1)S(1)}, bf16[48,128,128]{2,1,0:T(8,128)(2,1)S(1)}, u32[]{:S(2)}, u32[]{:S(2)}) collective-permute-start(bf16[48,128,128]{2,1,0:T(8,128)(2,1)S(1)} %copy-done), channel_id=1, source_target_pairs={{0,1},{1,0},{2,3},{3,2},{4,5},{5,4},{6,7},{7,6},{8,9},{9,8},{10,11... | collective-permute-start | bytes 4718600 | tf_op jit(solution)/shard_map/ppermute | solution.py:391
  7.0 5.3 %collective-permute-start.2 = (bf16[144,128]{1,0:T(8,128)(2,1)}, bf16[144,128]{1,0:T(8,128)(2,1)S(1)}, u32[]{:S(2)}, u32[]{:S(2)}) collective-permute-start(bf16[144,128]{1,0:T(8,128)(2,1)} %get-tuple-element.12.refs_3_), channel_id=1, source_target_pairs={{0,5},{1,4},{2,7},{3,6},{4,1},{5,0},{6,3},{7,2},{8,13},{9,12},{10,... | collective-permute-start | bytes 110600 | tf_op jit(solution)/shard_map/ppermute | solution.py:391
  9.7 5.9 %collective-permute-start.5 = (bf16[144,128]{1,0:T(8,128)(2,1)}, bf16[144,128]{1,0:T(8,128)(2,1)S(1)}, u32[]{:S(2)}, u32[]{:S(2)}) collective-permute-start(bf16[144,128]{1,0:T(8,128)(2,1)} %get-tuple-element.12.refs_3_), channel_id=1, source_target_pairs={{0,8},{1,9},{2,10},{3,11},{4,12},{5,13},{6,14},{7,15},{8,0},{9,1},... | collective-permute-start | bytes 110600 | tf_op jit(solution)/shard_map/ppermute | solution.py:391
  12.3 5.5 %collective-permute-start.7 = (bf16[144,128]{1,0:T(8,128)(2,1)}, bf16[144,128]{1,0:T(8,128)(2,1)S(1)}, u32[]{:S(2)}, u32[]{:S(2)}) collective-permute-start(bf16[144,128]{1,0:T(8,128)(2,1)} %get-tuple-element.12.refs_3_), channel_id=1, source_target_pairs={{0,13},{1,12},{2,15},{3,14},{4,9},{5,8},{6,11},{7,10},{8,5},{9,4},... | collective-permute-start | bytes 110600 | tf_op jit(solution)/shard_map/ppermute | solution.py:391
  12.3 6.8 %collective-permute-start.3 = (bf16[144,128]{1,0:T(8,128)(2,1)S(1)}, bf16[144,128]{1,0:T(8,128)(2,1)S(1)}, u32[]{:S(2)}, u32[]{:S(2)}) collective-permute-start(bf16[144,128]{1,0:T(8,128)(2,1)S(1)} %collective-permute-done.2.refs_5_), channel_id=1, source_target_pairs={{0,3},{1,2},{2,1},{3,0},{4,7},{5,6},{6,5},{7,4},{8,11},{9,10},{10,... | collective-permute-start | bytes 110600 | tf_op jit(solution)/shard_map/ppermute | solution.py:391
  13.7 6.6 %collective-permute-start.4 = (bf16[144,128]{1,0:T(8,128)(2,1)}, bf16[144,128]{1,0:T(8,128)(2,1)S(1)}, u32[]{:S(2)}, u32[]{:S(2)}) collective-permute-start(bf16[144,128]{1,0:T(8,128)(2,1)} %get-tuple-element.12.refs_3_), channel_id=1, source_target_pairs={{0,3},{1,2},{2,1},{3,0},{4,7},{5,6},{6,5},{7,4},{8,11},{9,10},{10,... | collective-permute-start | bytes 110600 | tf_op jit(solution)/shard_map/ppermute | solution.py:391
  15.5 4.8 %collective-permute-start.6 = (bf16[144,128]{1,0:T(8,128)(2,1)S(1)}, bf16[144,128]{1,0:T(8,128)(2,1)S(1)}, u32[]{:S(2)}, u32[]{:S(2)}) collective-permute-start(bf16[144,128]{1,0:T(8,128)(2,1)S(1)} %collective-permute-done.5.refs_7_), channel_id=1, source_target_pairs={{0,3},{1,2},{2,1},{3,0},{4,7},{5,6},{6,5},{7,4},{8,11},{9,10},{10,... | collective-permute-start | bytes 110600 | tf_op jit(solution)/shard_map/ppermute | solution.py:391
  17.8 3.5 %collective-permute-start.8 = (bf16[144,128]{1,0:T(8,128)(2,1)S(1)}, bf16[144,128]{1,0:T(8,128)(2,1)S(1)}, u32[]{:S(2)}, u32[]{:S(2)}) collective-permute-start(bf16[144,128]{1,0:T(8,128)(2,1)S(1)} %collective-permute-done.7.refs_9_), channel_id=1, source_target_pairs={{0,3},{1,2},{2,1},{3,0},{4,7},{5,6},{6,5},{7,4},{8,11},{9,10},{10,... | collective-permute-start | bytes 110600 | tf_op jit(solution)/shard_map/ppermute | solution.py:391
  21.3 10.7 %copy-start.2 = (s32[4,64]{1,0:T(4,128)S(1)}, s32[4,64]{1,0:T(4,128)}, u32[]{:S(2)}) copy-start(s32[4,64]{1,0:T(4,128)} %get-tuple-element.15.refs_1_) | copy-start | bytes 3076
